TPU v7x, 32 devices: a whole 2x2x4 slice. The times are simulated.
32 devices in a mesh: dp: 8 (over y, x, core), chan: 4 (over z).
Axes of the slice: x: 2, y: 2, z: 4, core: 2. Of those that a mesh axis runs over, the one named last changes fastest.
Arguments:
- features: bfloat16 [8, 32, 32, 512], P('dp', None, None, 'chan'), may hold values from -6 to 6
- z_table: float32 [1024, 512], replicated, may hold values from -6 to 6
- seeds: int32 [8, 2], P('dp'), may hold values from 0 to 1023
- crossover: int32 [8], P('dp'), may hold values from 0 to 2
- counted: int32 [8], P('dp'), may hold values from 0 to 1, as said below
- head: bfloat16 [3, 1024], replicated, may hold values from -0.109375 to 0.109375
- w_avg: float32 [512], replicated, may hold values from -4 to 4
- map_w: float32 [8, 512, 512], P(None, 'dp'), may hold values from -0.25 to 0.25
- map_w_mom: float32 [8, 512, 512], P(None, 'dp'), may hold values from -0.125 to 0.125
- map_w_ema: float32 [8, 512, 512], P(None, 'dp'), may hold values from -0.25 to 0.25
- map_b: float32 [8, 512], replicated, may hold values from -4 to 4
- map_b_mom: float32 [8, 512], replicated, may hold values from -0.25 to 0.25
- map_b_ema: float32 [8, 512], replicated, may hold values from -4 to 4
- aff_w: float32 [2, 512, 512], P(None, None, 'chan'), may hold values from -0.25 to 0.25
- aff_w_mom: float32 [2, 512, 512], P(None, None, 'chan'), may hold values from -0.078125 to 0.078125
- aff_w_ema: float32 [2, 512, 512], P(None, None, 'chan'), may hold values from -0.25 to 0.25
- chan_bias: float32 [3, 512], P(None, 'chan'), may hold values from 0.5 to 1.5
- chan_bias_mom: float32 [3, 512], P(None, 'chan'), may hold values from -0.15625 to 0.15625
- chan_bias_ema: float32 [3, 512], P(None, 'chan'), may hold values from 0.5 to 1.5
- conv_w: float32 [3, 3, 512, 512], P(None, None, None, 'chan'), may hold values from -0.09375 to 0.09375
- conv_w_mom: float32 [3, 3, 512, 512], P(None, None, None, 'chan'), may hold values from -0.15625 to 0.15625
- conv_w_ema: float32 [3, 3, 512, 512], P(None, None, None, 'chan'), may hold values from -0.09375 to 0.09375
- rgb_w: float32 [3, 512], P(None, 'chan'), may hold values from -0.25 to 0.25
- rgb_w_mom: float32 [3, 512], P(None, 'chan'), may hold values from -3 to 3
- rgb_w_ema: float32 [3, 512], P(None, 'chan'), may hold values from -0.25 to 0.25
Outputs:
- map_w_new: float32 [8, 512, 512], P(None, 'dp')
- map_w_mom_new: float32 [8, 512, 512], P(None, 'dp')
- map_w_ema_new: float32 [8, 512, 512], P(None, 'dp')
- map_w_copy: bfloat16 [8, 512, 512], P(None, 'dp')
- map_b_new: float32 [8, 512], replicated
- map_b_mom_new: float32 [8, 512], replicated
- map_b_ema_new: float32 [8, 512], replicated
- map_b_copy: bfloat16 [8, 512], replicated
- aff_w_new: float32 [2, 512, 512], P(None, None, 'chan')
- aff_w_mom_new: float32 [2, 512, 512], P(None, None, 'chan')
- aff_w_ema_new: float32 [2, 512, 512], P(None, None, 'chan')
- aff_w_copy: bfloat16 [2, 512, 512], P(None, None, 'chan')
- chan_bias_new: float32 [3, 512], P(None, 'chan')
- chan_bias_mom_new: float32 [3, 512], P(None, 'chan')
- chan_bias_ema_new: float32 [3, 512], P(None, 'chan')
- chan_bias_copy: bfloat16 [3, 512], P(None, 'chan')
- conv_w_new: float32 [3, 3, 512, 512], P(None, None, None, 'chan')
- conv_w_mom_new: float32 [3, 3, 512, 512], P(None, None, None, 'chan')
- conv_w_ema_new: float32 [3, 3, 512, 512], P(None, None, None, 'chan')
- conv_w_copy: bfloat16 [3, 3, 512, 512], P(None, None, None, 'chan')
- rgb_w_new: float32 [3, 512], P(None, 'chan')
- rgb_w_mom_new: float32 [3, 512], P(None, 'chan')
- rgb_w_ema_new: float32 [3, 512], P(None, 'chan')
- rgb_w_copy: bfloat16 [3, 512], P(None, 'chan')
- w_avg_new: float32 [512], replicated
- loss_sum: float32 [], replicated
- loss_count: float32 [], replicated
Inputs may be any that keep to these rules, and one draw needn't show every extreme that they name: `counted`: the chance that a sample counts rises from a quarter to three quarters along the samples; the last sample always counts.
All inputs are finite; a program needn't handle non-finite values.
Results may differ from a plain program's by a relative error of at most 0.012.
Values may be sent and summed in bfloat16 or wider, within the bound.
No kernel may reach another device: no remote copies, remote signals or barrier semaphores. Data moves between devices by JAX's collectives and lax.ppermute only.
A program may use at most 128 MiB of HBM per device.

v0:
```python
import jax
import jax.numpy as jnp
from jax import lax
from jax.sharding import PartitionSpec as P

MOMENTUM = 0.9
EMA_DECAY = 0.95
AVERAGE_BETA = 0.5
HIGHEST_PRECISION = lax.Precision.HIGHEST


def silu_slope(preact):
    sigmoid_pre = jax.nn.sigmoid(preact)
    return sigmoid_pre * (1.0 + preact * (1.0 - sigmoid_pre))


def advance(param, moment, average, grad, rate):
    moment_new = MOMENTUM * moment + grad
    param_new = param - rate * (grad + MOMENTUM * moment_new)
    average_new = EMA_DECAY * average + (1.0 - EMA_DECAY) * param_new
    return (param_new, moment_new, average_new, param_new.astype(jnp.bfloat16))


def local(
    features,
    z_table,
    seeds,
    crossover,
    counted,
    head,
    w_avg,
    map_w,
    map_w_mom,
    map_w_ema,
    map_b,
    map_b_mom,
    map_b_ema,
    aff_w,
    aff_w_mom,
    aff_w_ema,
    chan_bias,
    chan_bias_mom,
    chan_bias_ema,
    conv_w,
    conv_w_mom,
    conv_w_ema,
    rgb_w,
    rgb_w_mom,
    rgb_w_ema,
):
    samples = features.shape[0]
    grid_side = features.shape[1]
    local_width = features.shape[3]
    width = z_table.shape[1]
    map_depth = map_w.shape[0]
    specs = ("NHWC", "HWIO", "NHWC")
    map_full = lax.all_gather(map_w.astype(jnp.bfloat16), "dp", axis=1, tiled=True)
    latents = jnp.take(z_table, seeds.reshape(-1), axis=0)
    hidden = latents * lax.rsqrt(jnp.mean(latents * latents, axis=1, keepdims=True) + 1e-08)
    inputs_low = []
    preacts = []
    for layer_index in range(map_depth):
        hidden_low = hidden.astype(jnp.bfloat16)
        preact = (
            jnp.dot(hidden_low, map_full[layer_index], preferred_element_type=jnp.float32)
            + map_b[layer_index]
        )
        inputs_low.append(hidden_low)
        preacts.append(preact)
        hidden = jax.nn.silu(preact)
    pair_low = hidden.astype(jnp.bfloat16).reshape(samples, 2, width)
    choose = crossover[:, None] > jnp.arange(2, dtype=jnp.int32)[None, :]
    picked = jnp.where(choose[:, :, None], pair_low[:, 0:1, :], pair_low[:, 1:2, :])
    affine_low = aff_w.astype(jnp.bfloat16)
    style = (
        jnp.einsum("sjc,jcd->sjd", picked, affine_low, preferred_element_type=jnp.float32)
        + chan_bias[None, :2, :]
    )
    style_low = style.astype(jnp.bfloat16)
    whole_x, whole_style = (
        lax.all_gather(features, "chan", axis=3, tiled=True),
        lax.all_gather(style_low[:, 0], "chan", axis=1, tiled=True),
    )
    style_full = whole_style.astype(jnp.float32)
    modulated = (whole_x.astype(jnp.float32) * style_full[:, None, None, :]).astype(jnp.bfloat16)
    kernel = conv_w.astype(jnp.bfloat16)
    conv_out = lax.conv_general_dilated(
        modulated,
        kernel,
        (1, 1),
        "SAME",
        dimension_numbers=specs,
        preferred_element_type=jnp.float32,
    )
    kernel_wide = kernel.astype(jnp.float32)
    kernel_sq = jnp.sum(kernel_wide * kernel_wide, axis=(0, 1))
    style_sq = style_full * style_full
    demod = lax.rsqrt(jnp.dot(style_sq, kernel_sq, precision=HIGHEST_PRECISION) + 1e-08)
    scaled = conv_out * demod[:, None, None, :] + chan_bias[2]
    activated = jax.nn.silu(scaled)
    colour_style = style_low[:, 1].astype(jnp.float32)
    act_mod = (activated * colour_style[:, None, None, :]).astype(jnp.bfloat16)
    head_map = head.reshape(3, grid_side, grid_side)
    colour_low = rgb_w.astype(jnp.bfloat16)
    colour_wide = colour_low.astype(jnp.float32)
    mixed = jnp.einsum("chw,shwo->sco", head_map, act_mod, preferred_element_type=jnp.float32)
    logit = lax.psum(jnp.sum(mixed * colour_wide[None], axis=(1, 2)), "chan")
    weight_mask = counted.astype(jnp.float32)
    local_loss = jnp.sum(weight_mask * jax.nn.softplus(-logit))
    local_count = jnp.sum(weight_mask)
    w_total = jnp.sum(hidden, axis=0)
    w_sum, count_sum, loss_sum = lax.psum((w_total, local_count, local_loss), "dp")
    g_logit = -weight_mask * jax.nn.sigmoid(-logit)
    g_colour = jnp.einsum("s,sco->co", g_logit, mixed, precision=HIGHEST_PRECISION)
    pixel_kernel = jnp.einsum(
        "chw,co->hwo", head_map, colour_low, preferred_element_type=jnp.float32
    )
    g_act_mod = g_logit[:, None, None, None] * pixel_kernel[None]
    g_colour_style = jnp.sum(g_act_mod * activated, axis=(1, 2))
    g_scaled = g_act_mod * colour_style[:, None, None, :] * silu_slope(scaled)
    g_conv_bias = jnp.sum(g_scaled, axis=(0, 1, 2))
    g_demod = jnp.sum(g_scaled * conv_out, axis=(1, 2))
    g_conv_out = (g_scaled * demod[:, None, None, :]).astype(jnp.bfloat16)
    factor = g_demod * demod * demod * demod
    g_kernel_sq = -0.5 * jnp.dot(style_sq.T, factor, precision=HIGHEST_PRECISION)
    g_style_demod = -style_full * jnp.dot(factor, kernel_sq.T, precision=HIGHEST_PRECISION)
    padded = jnp.pad(modulated, ((0, 0), (1, 1), (1, 1), (0, 0)))
    tap_grads = []
    for row_tap in range(3):
        for col_tap in range(3):
            window = padded[:, row_tap : row_tap + grid_side, col_tap : col_tap + grid_side, :]
            tap_grads.append(
                jnp.einsum("shwi,shwo->io", window, g_conv_out, preferred_element_type=jnp.float32)
            )
    g_kernel = (
        jnp.stack(tap_grads).reshape(3, 3, width, local_width) + 2.0 * kernel_wide * g_kernel_sq
    )
    g_padded = jnp.pad(g_conv_out, ((0, 0), (1, 1), (1, 1), (0, 0)))
    total = jnp.zeros(
        (local_width * lax.axis_size("chan"), samples * grid_side * grid_side), jnp.float32
    )
    for row_tap in range(3):
        for col_tap in range(3):
            window = g_padded[
                :, 2 - row_tap : 2 - row_tap + grid_side, 2 - col_tap : 2 - col_tap + grid_side, :
            ].reshape(-1, local_width)
            total = total + lax.dot_general(
                kernel[row_tap, col_tap],
                window,
                (((1,), (1,)), ((), ())),
                preferred_element_type=jnp.float32,
            )
    own_grad = lax.psum_scatter(
        total.astype(jnp.bfloat16), "chan", scatter_dimension=0, tiled=True
    ).astype(jnp.float32)
    own_inputs = features.reshape(samples, grid_side * grid_side, local_width).astype(jnp.float32)
    g_x_own = jnp.einsum(
        "spi,isp->si",
        own_inputs,
        own_grad.reshape(local_width, samples, grid_side * grid_side),
        precision=HIGHEST_PRECISION,
    )
    g_conv_style = (
        lax.psum_scatter(g_style_demod, "chan", scatter_dimension=1, tiled=True) + g_x_own
    )
    g_style = jnp.stack([g_conv_style, g_colour_style], axis=1)
    g_affine = jnp.einsum(
        "sjc,sjd->jcd", picked.astype(jnp.float32), g_style, precision=HIGHEST_PRECISION
    )
    g_affine_bias = jnp.sum(g_style, axis=0)
    g_picked = lax.psum(
        jnp.einsum(
            "sjd,jcd->sjc", g_style, affine_low.astype(jnp.float32), precision=HIGHEST_PRECISION
        ),
        "chan",
    )
    first_grad = jnp.sum(jnp.where(choose[:, :, None], g_picked, 0.0), axis=1)
    second_grad = jnp.sum(jnp.where(choose[:, :, None], 0.0, g_picked), axis=1)
    g_hidden = jnp.stack([first_grad, second_grad], axis=1).reshape(samples * 2, width)
    pre_grads = []
    bias_grads = []
    for layer_index in reversed(range(map_depth)):
        g_preact = g_hidden * silu_slope(preacts[layer_index])
        pre_grads.append(g_preact)
        bias_grads.append(jnp.sum(g_preact, axis=0))
        if layer_index > 0:
            g_hidden = jnp.dot(
                g_preact, map_full[layer_index].astype(jnp.float32).T, precision=HIGHEST_PRECISION
            )
    pre_stack = jnp.stack(pre_grads[::-1])
    input_stack = jnp.stack(inputs_low)
    weight_terms = jnp.einsum(
        "lri,lro->lio", input_stack.astype(jnp.float32), pre_stack, precision=HIGHEST_PRECISION
    )
    g_map_own = lax.psum_scatter(weight_terms, "dp", scatter_dimension=1, tiled=True)
    g_map_bias = jnp.stack(bias_grads[::-1])
    g_bias_all = jnp.concatenate([g_affine_bias, g_conv_bias[None]], axis=0)
    g_affine_sum, g_bias_sum, g_kernel_sum, g_colour_sum, g_map_bias_sum = lax.psum(
        (g_affine, g_bias_all, g_kernel, g_colour, g_map_bias), "dp"
    )
    inverse = 1.0 / count_sum
    outputs = advance(map_w, map_w_mom, map_w_ema, g_map_own * inverse, 30.0)
    outputs = outputs + advance(map_b, map_b_mom, map_b_ema, g_map_bias_sum * inverse, 30.0)
    outputs = outputs + advance(aff_w, aff_w_mom, aff_w_ema, g_affine_sum * inverse, 30.0)
    outputs = outputs + advance(chan_bias, chan_bias_mom, chan_bias_ema, g_bias_sum * inverse, 50.0)
    outputs = outputs + advance(conv_w, conv_w_mom, conv_w_ema, g_kernel_sum * inverse, 5.0)
    outputs = outputs + advance(rgb_w, rgb_w_mom, rgb_w_ema, g_colour_sum * inverse, 1.0)
    total_samples = samples * lax.axis_size("dp")
    w_avg_new = w_avg + (1.0 - AVERAGE_BETA) * (w_sum / (2.0 * total_samples) - w_avg)
    return outputs + (w_avg_new, loss_sum, count_sum)


def solution(mesh):
    in_specs = (
        P("dp", None, None, "chan"),
        P(),
        P("dp", None),
        P("dp"),
        P("dp"),
        P(),
        P(),
        P(None, "dp", None),
        P(None, "dp", None),
        P(None, "dp", None),
        P(),
        P(),
        P(),
        P(None, None, "chan"),
        P(None, None, "chan"),
        P(None, None, "chan"),
        P(None, "chan"),
        P(None, "chan"),
        P(None, "chan"),
        P(None, None, None, "chan"),
        P(None, None, None, "chan"),
        P(None, None, None, "chan"),
        P(None, "chan"),
        P(None, "chan"),
        P(None, "chan"),
    )
    out_specs = (
        P(None, "dp", None),
        P(None, "dp", None),
        P(None, "dp", None),
        P(None, "dp", None),
        P(),
        P(),
        P(),
        P(),
        P(None, None, "chan"),
        P(None, None, "chan"),
        P(None, None, "chan"),
        P(None, None, "chan"),
        P(None, "chan"),
        P(None, "chan"),
        P(None, "chan"),
        P(None, "chan"),
        P(None, None, None, "chan"),
        P(None, None, None, "chan"),
        P(None, None, None, "chan"),
        P(None, None, None, "chan"),
        P(None, "chan"),
        P(None, "chan"),
        P(None, "chan"),
        P(None, "chan"),
        P(),
        P(),
        P(),
    )
    return jax.shard_map(local, mesh=mesh, in_specs=in_specs, out_specs=out_specs, check_vma=False)
```

profile of v0, /device:TPU:1, one launch (start us, length us, event | category | flops | bytes accessed | tf_op | source)
XLA Modules:
  0.0 325.7 jit_solution(12845988517904657122)
XLA Ops:
  7.3 2.2 convert_element_type.127
  11.3 2.0 fusion.1
  14.7 35.2 %all-gather.4.cloned.1.call-done = bf16[8,512,512]{2,1,0:T(8,128)(2,1)} async-done(((bf16[8,64,512]{2,1,0:T(8,128)(2,1)}), bf16[8,512,512]{2,1,0:T(8,128)(2,1)}) %all-gather.4.cloned.1.call-update) | async-done | bytes 4194320 | tf_op jit(solution)/shard_map/all_gather | solution.py:57
  49.8 1.3 constant_dynamic-update-slice_fusion.6
  51.1 1.3 constant_dynamic-update-slice_fusion.5
  60.2 9.8 %all-gather = bf16[1,1,512]{2,1,0:T(2,128)(2,1)S(1)} all-gather(bf16[1,1,128]{2,1,0:T(2,128)(2,1)S(1)} %get-tuple-element.91), channel_id=2, replica_groups=mesh['dp'=8,'chan'=4] {'chan'}, dimensions={2}, use_global_device_ids=true | all-gather | bytes 1280 | tf_op jit(solution)/shard_map/all_gather | solution.py:82
  70.3 9.6 %all-gather.6.cloned.1.call-done = bf16[1,32,32,512]{3,2,1,0:T(8,128)(2,1)} async-done(((bf16[1,32,32,128]{3,2,1,0:T(8,128)(2,1)}), bf16[1,32,32,512]{3,2,1,0:T(8,128)(2,1)}) %all-gather.6.cloned.1.call-update) | async-done | bytes 1048592 | tf_op jit(solution)/shard_map/all_gather | solution.py:81
  79.9 1.4 fusion.141
  83.0 4.2 %multiply_convert_fusion.1 = (bf16[32,8,5,128]{3,1,2,0:T(8,128)(2,1)S(1)}, f32[32,8,5,128]{3,1,2,0:T(8,128)S(1)}, f32[32,8,5,128]{3,1,2,0:T(8,128)S(1)}, f32[32,8,5,128]{3,1,2,0:T(8,128)}) fusion(f32[128]{0:T(128)S(1)} %get-tuple-element.92, f32[128]{0:T(128)S(1)} %slice_bitcast_fusion.41, f32[128]{0:T(128)S(1)} %fusion.24, ...), kind=kOutput, calls=%fused_computation.81 | convolution fusion | flops 1486127104 | bytes 5244456 | tf_op jit(solution)/shard_map/conv_general_dilated | solution.py:87
  88.8 8.3 %psum.70 = f32[1]{0:T(128)} all-reduce(f32[1]{0:T(128)} %bitcast.50), channel_id=1, replica_groups=mesh['dp'=8,'chan'=4] {'chan'}, use_global_device_ids=true, to_apply=%region_3.4 | all-reduce | flops 1 | bytes 8 | tf_op jit(solution)/shard_map/psum | solution.py:107
  109.5 1.3 copy.105
  111.0 2.5 fusion.20
  120.6 3.4 %fusion.2 = f32[3,3,512,128]{3,2,1,0:T(8,128)} fusion(f32[3,3,512,128]{3,2,1,0:T(8,128)} %bitcast.398, bf16[3,3,512,128]{3,2,1,0:T(8,128)(2,1)S(1)} %get-tuple-element.68, f32[512,128]{1,0:T(8,128)S(1)} %multiply_multiply_fusion), kind=kLoop, calls=%fused_computation.6 | loop fusion | flops 1769472 | bytes 6160384 | tf_op jit(solution)/shard_map/add | solution.py:136
  124.9 25.1 %reduce-scatter.12.cloned.1.call-done = bf16[128,1024]{1,0:T(8,128)(2,1)} async-done(((bf16[512,1024]{1,0:T(8,128)(2,1)}), bf16[128,1024]{1,0:T(8,128)(2,1)}) %reduce-scatter.12.cloned.1.call-update) | async-done | bytes 262160
  151.6 7.6 %psum.71 = f32[1,2,512]{2,1,0:T(2,128)S(1)} all-reduce(f32[1,2,512]{2,1,0:T(2,128)S(1)} %bitcast.416), channel_id=1, replica_groups=mesh['dp'=8,'chan'=4] {'chan'}, use_global_device_ids=true, to_apply=%region_8.9 | all-reduce | flops 1024 | bytes 8192 | tf_op jit(solution)/shard_map/psum | solution.py:171
  159.3 1.6 fusion.117
  160.9 1.6 fusion.116
  162.5 1.6 fusion.115
  164.1 1.6 fusion.114
  165.6 1.6 fusion.113
  167.2 1.6 fusion.112
  168.8 1.6 constant_dynamic-update-slice_fusion.15
  171.7 5.7 %fusion.118 = f32[8,512,512]{2,1,0:T(8,128)} fusion(bf16[8,2,512]{2,1,0:T(2,128)(2,1)S(1)} %get-tuple-element.105, f32[8,2,512]{2,1,0:T(2,128)S(1)} %constant_dynamic-update-slice_fusion.8), kind=kOutput, calls=%fused_computation.262 | convolution fusion | flops 50331648 | bytes 8437760 | tf_op jit(solution)/shard_map/lri,lro->lio/dot_general | solution.py:192
  178.6 24.0 %all-reduce.2 = (f32[]{:T(128)}, f32[8,512]{1,0:T(8,128)S(1)}, f32[3,128]{1,0:T(4,128)S(1)}, f32[3,128]{1,0:T(4,128)S(1)}, f32[512]{0:T(512)S(1)}, /*index=5*/f32[]{:T(128)}) all-reduce(f32[]{:T(128)} %bitcast.104, f32[8,512]{1,0:T(8,128)S(1)} %stack.158, ...), channel_id=1, replica_groups=mesh['dp'=8,'chan'=4] {'dp'}, use_global_device_ids=true, to_apply=%region_12.13 | all-reduce | flops 5378 | bytes 43024 | tf_op jit(solution)/shard_map/psum | solution.py:112
  206.9 32.3 %all-reduce.6.cloned.1.call-done = (f32[2,512,128]{2,1,0:T(8,128)}, f32[3,3,512,128]{3,2,1,0:T(8,128)}) async-done(((f32[2,512,128]{2,1,0:T(8,128)}, f32[3,3,512,128]{3,2,1,0:T(8,128)}), (f32[2,512,128]{2,1,0:T(8,128)}, f32[3,3,512,128]{3,2,1,0:T(8,128)})) %all-reduce.6.cloned.1.call-update) | async-done | bytes 2883600 | tf_op jit(solution)/shard_map/psum | solution.py:198
  239.2 2.2 fusion.103
  242.4 5.1 %fusion.101 = (bf16[3,3,512,128]{3,2,1,0:T(8,128)(2,1)}, f32[3,3,512,128]{3,2,1,0:T(8,128)S(1)}, f32[3,3,512,128]{3,2,1,0:T(8,128)}) fusion(f32[3,3,512,128]{3,2,1,0:T(8,128)} %param.44, f32[3,3,512,128]{3,2,1,0:T(8,128)S(1)} %copy-done.8, f32[]{:T(128)S(6)} %div.64, f32[3,3,512,128]{3,2,1,0:T(8,128)} %param.45), kind=kLoop, calls=%fused_computation.248 | loop fusion | flops 4718592 | bytes 12976132 | tf_op jit(solution)/shard_map/convert_element_type | solution.py:21
  247.5 1.4 copy-done.2
  248.9 1.8 multiply_add_fusion
  250.7 63.7 %reduce-scatter.8.cloned.1.call-done = f32[8,64,512]{2,1,0:T(8,128)} async-done(((f32[8,512,512]{2,1,0:T(8,128)}), f32[8,64,512]{2,1,0:T(8,128)}) %reduce-scatter.8.cloned.1.call-update) | async-done | bytes 1048592 | tf_op jit(solution)/shard_map/reduce_scatter | solution.py:195
  314.3 3.2 fusion.105
  317.6 1.3 multiply_add_fusion.2
  (168 shorter events, 40.5 us)
Async XLA Ops:
  7.2 3.2 copy-start
  7.2 3.1 copy-start.30
  7.2 4.0 %copy-start.17 = (f32[8,512]{1,0:T(8,128)S(1)}, f32[8,512]{1,0:T(8,128)}, u32[]{:S(2)}) copy-start(f32[8,512]{1,0:T(8,128)} %param.35) | copy-start | bytes 49156
  7.2 42.6 %all-gather.4.cloned.1.call-start = ((), (), s32[]{:S(2)}) async-start(), calls=%async_computation.3 | async-start | bytes 4718592 | tf_op jit(solution)/shard_map/all_gather | solution.py:57
  9.5 4.4 %copy-start.24 = (f32[3,128]{1,0:T(4,128)S(1)}, f32[3,128]{1,0:T(4,128)}, u32[]{:S(2)}) copy-start(f32[3,128]{1,0:T(4,128)} %param.41) | copy-start | bytes 4612
  9.5 4.4 %copy-start.23 = (bf16[3,1024]{1,0:T(4,128)(2,1)S(1)}, bf16[3,1024]{1,0:T(4,128)(2,1)}, u32[]{:S(2)}) copy-start(bf16[3,1024]{1,0:T(4,128)(2,1)} %param.30) | copy-start | bytes 18436
  9.5 70.4 %all-gather.6.cloned.1.call-start = ((), (), s32[]{:S(2)}) async-start(), calls=%async_computation.4 | async-start | bytes 1310720 | tf_op jit(solution)/shard_map/all_gather | solution.py:81
  10.3 113.7 %reduce-scatter.10.cloned.1.call-start = ((), (), s32[]{:S(2)}) async-start(), calls=%async_computation.6 | async-start | bytes 327680
  51.1 8.9 %copy-start.3 = (f32[2,512,128]{2,1,0:T(8,128)S(1)}, f32[2,512,128]{2,1,0:T(8,128)}, u32[]{:S(2)}) copy-start(f32[2,512,128]{2,1,0:T(8,128)} %param.38) | copy-start | bytes 1572868
  101.5 48.4 %reduce-scatter.12.cloned.1.call-start = ((), (), s32[]{:S(2)}) async-start(), calls=%async_computation.7 | async-start | bytes 1310720
  110.8 2.7 copy-start.12
  110.8 128.4 %all-reduce.6.cloned.1.call-start = ((), (), s32[]{:S(2)}) async-start(), calls=%async_computation.8 | async-start | bytes 5767168 | tf_op jit(solution)/shard_map/psum | solution.py:198
  120.6 30.5 %copy-start.13 = (bf16[1,32,32,128]{3,2,1,0:T(8,128)(2,1)S(1)}, bf16[1,32,32,128]{3,2,1,0:T(8,128)(2,1)}, u32[]{:S(2)}) copy-start(bf16[1,32,32,128]{3,2,1,0:T(8,128)(2,1)} %param.25) | copy-start | bytes 786436
  171.4 142.9 %reduce-scatter.8.cloned.1.call-start = ((), (), s32[]{:S(2)}) async-start(), calls=%async_computation.5 | async-start | bytes 9437184 | tf_op jit(solution)/shard_map/reduce_scatter | solution.py:195
  177.4 25.9 %copy-start.25 = (f32[3,128]{1,0:T(4,128)S(1)}, f32[3,128]{1,0:T(4,128)}, u32[]{:S(2)}) copy-start(f32[3,128]{1,0:T(4,128)} %param.48) | copy-start | bytes 4612
  177.4 25.9 %copy-start.26 = (f32[3,128]{1,0:T(4,128)S(1)}, f32[3,128]{1,0:T(4,128)}, u32[]{:S(2)}) copy-start(f32[3,128]{1,0:T(4,128)} %param.42) | copy-start | bytes 4612
  177.4 26.5 %copy-start.27 = (f32[3,128]{1,0:T(4,128)S(1)}, f32[3,128]{1,0:T(4,128)}, u32[]{:S(2)}) copy-start(f32[3,128]{1,0:T(4,128)} %param.43) | copy-start | bytes 4612
  177.5 27.1 %copy-start.28 = (f32[3,128]{1,0:T(4,128)S(1)}, f32[3,128]{1,0:T(4,128)}, u32[]{:S(2)}) copy-start(f32[3,128]{1,0:T(4,128)} %param.49) | copy-start | bytes 4612
  177.5 27.6 %copy-start.29 = (f32[512]{0:T(512)S(1)}, f32[512]{0:T(512)}, u32[]{:S(2)}) copy-start(f32[512]{0:T(512)} %param.31) | copy-start | bytes 6148
  177.5 28.2 %copy-start.19 = (f32[8,512]{1,0:T(8,128)S(1)}, f32[8,512]{1,0:T(8,128)}, u32[]{:S(2)}) copy-start(f32[8,512]{1,0:T(8,128)} %param.36) | copy-start | bytes 49156
  177.5 28.8 %copy-start.18 = (f32[8,512]{1,0:T(8,128)S(1)}, f32[8,512]{1,0:T(8,128)}, u32[]{:S(2)}) copy-start(f32[8,512]{1,0:T(8,128)} %param.37) | copy-start | bytes 49156
  177.5 61.7 %copy-start.15 = (f32[2,512,128]{2,1,0:T(8,128)S(1)}, f32[2,512,128]{2,1,0:T(8,128)}, u32[]{:S(2)}) copy-start(f32[2,512,128]{2,1,0:T(8,128)} %param.39) | copy-start | bytes 1572868
  177.5 63.9 %copy-start.14 = (f32[2,512,128]{2,1,0:T(8,128)S(1)}, f32[2,512,128]{2,1,0:T(8,128)}, u32[]{:S(2)}) copy-start(f32[2,512,128]{2,1,0:T(8,128)} %param.40) | copy-start | bytes 1572868
  203.9 43.5 %copy-start.21 = (f32[3,128]{1,0:T(4,128)}, f32[3,128]{1,0:T(4,128)S(1)}, u32[]{:S(2)}) copy-start(f32[3,128]{1,0:T(4,128)S(1)} %get-tuple-element.42) | copy-start | bytes 4612
  203.9 43.5 %copy-start.22 = (f32[3,128]{1,0:T(4,128)}, f32[3,128]{1,0:T(4,128)S(1)}, u32[]{:S(2)}) copy-start(f32[3,128]{1,0:T(4,128)S(1)} %get-tuple-element.126) | copy-start | bytes 4612
  206.3 41.2 %copy-start.16 = (f32[8,512]{1,0:T(8,128)}, f32[8,512]{1,0:T(8,128)S(1)}, u32[]{:S(2)}) copy-start(f32[8,512]{1,0:T(8,128)S(1)} %get-tuple-element.54) | copy-start | bytes 49156
  239.2 3.2 copy-start.8
  241.4 6.1 %copy-start.9 = (f32[2,512,128]{2,1,0:T(8,128)}, f32[2,512,128]{2,1,0:T(8,128)S(1)}, u32[]{:S(2)}) copy-start(f32[2,512,128]{2,1,0:T(8,128)S(1)} %get-tuple-element.51) | copy-start | bytes 1572868
  242.4 6.5 %copy-start.7 = (f32[3,3,512,128]{3,2,1,0:T(8,128)S(1)}, f32[3,3,512,128]{3,2,1,0:T(8,128)}, u32[]{:S(2)}) copy-start(f32[3,3,512,128]{3,2,1,0:T(8,128)} %param.46) | copy-start | bytes 7077892
  248.9 65.5 %copy-start.6 = (f32[8,64,512]{2,1,0:T(8,128)S(1)}, f32[8,64,512]{2,1,0:T(8,128)}, u32[]{:S(2)}) copy-start(f32[8,64,512]{2,1,0:T(8,128)} %param.32) | copy-start | bytes 3145732
  314.3 3.2 copy-start.10
  314.3 4.5 %copy-start.1 = (f32[1024,512]{1,0:T(8,128)S(1)}, f32[1024,512]{1,0:T(8,128)}, u32[]{:S(2)}) copy-start(f32[1024,512]{1,0:T(8,128)} %param.26) | copy-start | bytes 6291460
  (6 other events, 7.9 us)
Sparse Core Ops, SparseCore 0:
  10.6 39.2 all-gather.3
  51.4 28.4 all-gather.5
  101.6 18.5 reduce-scatter.9
  123.1 26.8 reduce-scatter.11
  171.5 67.6 all-reduce.5
  242.9 71.3 reduce-scatter.7
where the time goes:
time: 328 us; the launch traced here: 326 us
  waiting for transfers between devices  167 us (51%)
  matrix products  49.9 us (15%)
  blocking collectives  49.8 us (15%)
  other arithmetic  29.6 us (9%)
  between operations  18.4 us (6%)
  local copies, waits for them, and re-layouts  10.8 us (3%)
    reduce_scatter x1, waiting for transfers between devices, local(): lax.psum_scatter(weight_terms, 'dp', scatter_dimension=1, tiled=True)  63.7 us
    all_gather x1, waiting for transfers between devices, local(): lax.all_gather(map_w.astype(jnp.bfloat16), 'dp', axis=1, tiled=True)  35.2 us
    psum x1, waiting for transfers between devices, local(): lax.psum((g_affine, g_bias_all, g_kernel, g_colour, g_map_bias), 'dp')  32.3 us
    unnamed x8, waiting for transfers between devices  25.8 us
    psum x1, blocking collectives, local(): lax.psum((w_total, local_count, local_loss), 'dp')  24 us
    dot_general x9, matrix products, local(): jnp.einsum('shwi,shwo->io', window, g_conv_out, preferred_element_type=jn...  12 us
    convert_element_type x5, other arithmetic, advance(): return (param_new, moment_new, average_new, param_new.astype(jnp.bfloat16))  11.7 us
    dot_general x7, matrix products, local(): jnp.dot(g_preact, map_full[layer_index].astype(jnp.float32).T, precision=...  11 us
  transfers between devices with their start and end apart: 6, of which 5 were waited for; matrix products, arithmetic and copies ran while one was open for 17% of the time, Pallas kernels for 0%

commit v1 on v0

v1 whole, which is shorter than its diff:
```python
import functools

import jax
import jax.numpy as jnp
from jax import lax
from jax.experimental import pallas as pl
from jax.experimental.pallas import tpu as pltpu
from jax.sharding import PartitionSpec as P

MOMENTUM = 0.9
EMA_DECAY = 0.95
AVERAGE_BETA = 0.5
BF16 = jnp.bfloat16
F32 = jnp.float32
TAPS = 9
LANES = 128
COUNT_ROWS = 32
VMEM = pl.BlockSpec(memory_space=pltpu.VMEM)
SMEM = pl.BlockSpec(memory_space=pltpu.SMEM)
HBM = pl.BlockSpec(memory_space=pl.ANY)


def shape(dims, dtype):
    return jax.ShapeDtypeStruct(dims, dtype)


def params(mib):
    return pltpu.CompilerParams(vmem_limit_bytes=mib * 1024 * 1024)


def swap(value, axis, distance):
    return lax.ppermute(
        value, axis, [(i, i ^ distance) for i in range(lax.axis_size(axis))]
    )


def spread(value, axis):
    size = lax.axis_size(axis)
    parts = [value] * size
    for k in range(2, size, 2):
        parts[k] = swap(value, axis, k)
    for k in range(0, size, 2):
        parts[k + 1] = swap(parts[k], axis, 1)
    return parts


def spread_direct(value, axis):
    return [value] + [swap(value, axis, k) for k in range(1, lax.axis_size(axis))]


def silu_slope(preact):
    sig = jax.nn.sigmoid(preact)
    return sig * (1.0 + preact * (1.0 - sig))


def pieces(value, count):
    out = []
    for _ in range(count):
        part = value.astype(BF16)
        out.append(part)
        value = value - part.astype(F32)
    return out


def advance(param, moment, average, grad, rate):
    moment_new = MOMENTUM * moment + grad
    param_new = param - rate * (grad + MOMENTUM * moment_new)
    average_new = EMA_DECAY * average + (1.0 - EMA_DECAY) * param_new
    return param_new, moment_new, average_new, param_new.astype(BF16)


def dot(a, b):
    return jnp.dot(a, b, preferred_element_type=F32)


def dot_nt(a, b):
    return lax.dot_general(a, b, (((1,), (1,)), ((), ())), preferred_element_type=F32)


def dot_tn(a, b):
    return lax.dot_general(a, b, (((0,), (0,)), ((), ())), preferred_element_type=F32)


def prepare_kernel(where, map_w, aff_w, bias, map_low, aff_part):
    map_low[...] = map_w[...].astype(BF16)
    half = aff_part.shape[0] - 16
    start = pl.multiple_of(lax.rem(where[0], 2) * half, half)
    aff_part[pl.ds(0, half), :] = aff_w[0, pl.ds(start, half), :].astype(BF16)
    hi, mid, lo = pieces(bias[0:1, :], 3)
    rows = jnp.concatenate(
        [hi.astype(F32), mid.astype(F32), lo.astype(F32), jnp.zeros((13, LANES), F32)], axis=0
    )
    aff_part[pl.ds(half, 16), :] = rows.astype(BF16)


def main_kernel(n_dp, n_ch, samples, side, *refs):
    refs = list(refs)

    def take(count):
        got = refs[:count]
        del refs[:count]
        return got

    where, seeds, crossover = take(3)
    map_parts = take(n_dp)
    feat_parts = take(n_ch)
    aff_own, aff_pair = take(n_ch), take(n_ch)
    z_table, conv_w = take(2)
    aff_w, map_b, bias, head, head_t, rgb_w = take(6)
    unit, to_sum, pre_out, hid_out, top_out, picked_out, small, map_out, aff_out = take(9)
    (
        map_full,
        aff_full,
        bias_full,
        feat,
        feat_t,
        kernel_f,
        kernel,
        padded,
        taps,
        shifted,
        wide,
        rows,
        sem_map,
        sem_feat,
        sem_aff,
        sem_z,
        sem_conv,
        sem_out,
    ) = refs
    layers, share, width = map_parts[0].shape
    pixels = side * side
    latents = 2 * samples
    half = aff_own[0].shape[0] - 16
    dp, ch = where[0], where[1]
    pair = lax.rem(dp, 2)

    z_copies = []
    for n in range(latents):
        at = pl.multiple_of((seeds[n] // 8) * 8, 8)
        z_copies.append(pltpu.make_async_copy(z_table.at[pl.ds(at, 8), :], rows.at[n], sem_z.at[n]))
    map_copies = []
    for k in range(n_dp):
        at = pl.multiple_of(lax.bitwise_xor(dp, k) * share, share)
        map_copies.append(
            pltpu.make_async_copy(
                map_parts[k], map_full.at[:, pl.ds(at, share), :], sem_map.at[k]
            )
        )
    aff_copies, feat_copies = [], []
    for k in range(n_ch):
        lane = pl.ds(pl.multiple_of(lax.bitwise_xor(ch, k) * LANES, LANES), LANES)
        mine = pl.ds(pl.multiple_of(pair * half, half), half)
        other = pl.ds(pl.multiple_of((1 - pair) * half, half), half)
        aff_copies.append(
            pltpu.make_async_copy(
                aff_own[k].at[pl.ds(0, half), :], aff_full.at[mine, lane], sem_aff.at[3 * k]
            )
        )
        aff_copies.append(
            pltpu.make_async_copy(
                aff_pair[k].at[pl.ds(0, half), :], aff_full.at[other, lane], sem_aff.at[3 * k + 1]
            )
        )
        aff_copies.append(
            pltpu.make_async_copy(
                aff_own[k].at[pl.ds(half, 16), :], bias_full.at[:, lane], sem_aff.at[3 * k + 2]
            )
        )
        feat_copies.append(
            pltpu.make_async_copy(feat_parts[k], feat.at[:, :, lane], sem_feat.at[k])
        )
    conv_copy = pltpu.make_async_copy(conv_w, kernel_f, sem_conv)
    for copy in z_copies + map_copies + aff_copies + feat_copies + [conv_copy]:
        copy.start()

    hidden_rows = []
    for n in range(latents):
        z_copies[n].wait()
        row = rows[n, pl.ds(lax.rem(seeds[n], 8), 1), :]
        scale = lax.rsqrt(jnp.mean(row * row, axis=1, keepdims=True) + 1e-08)
        hidden_rows.append(row * scale)
    hidden_rows.append(jnp.zeros((16 - latents, width), F32))
    hidden = jnp.concatenate(hidden_rows, axis=0)
    for copy in map_copies:
        copy.wait()
    keep_map = pltpu.make_async_copy(map_full, map_out, sem_out.at[0])
    keep_map.start()
    for layer in range(layers):
        low = hidden.astype(BF16)
        preact = dot(low, map_full[layer]) + map_b[pl.ds(layer, 1), :]
        hid_out[layer] = low.astype(F32)[0:8]
        pre_out[layer] = preact[0:8]
        hidden = preact * jax.nn.sigmoid(preact)
    top_out[...] = hidden[0:8]
    low = hidden.astype(BF16).astype(F32)

    conv_copy.wait()
    square = jnp.zeros((width, LANES), F32)
    for tap in range(TAPS):
        tap_low = kernel_f[tap].astype(BF16)
        kernel[tap // 3, :, pl.ds((tap % 3) * LANES, LANES)] = tap_low
        wide_tap = tap_low.astype(F32)
        square = square + wide_tap * wide_tap
    for copy in feat_copies:
        copy.wait()
    for s in range(samples):
        feat_t[s] = feat[s].T

    for copy in aff_copies:
        copy.wait()
    keep_aff = pltpu.make_async_copy(aff_full, aff_out, sem_out.at[1])
    keep_aff.start()
    for j in range(2):
        chosen = []
        for s in range(samples):
            first = crossover[s] > j
            chosen.append(
                jnp.where(first, low[2 * s : 2 * s + 1, :], low[2 * s + 1 : 2 * s + 2, :])
            )
        chosen.append(jnp.zeros((8 - samples, width), F32))
        picked_out[j] = jnp.concatenate(chosen, axis=0)
    wide_bias = bias_full[...].astype(F32)
    bias_row = wide_bias[0:1] + wide_bias[1:2] + wide_bias[2:3]
    style0 = (dot(picked_out[0].astype(BF16), aff_full[...]) + bias_row).astype(BF16)
    colour_aff = aff_w[1].astype(BF16)
    style1 = dot(picked_out[1].astype(BF16), colour_aff) + bias[1:2, :]
    style0_wide = style0.astype(F32)
    style1 = style1.astype(BF16).astype(F32)
    colour_aff = colour_aff.astype(F32)
    colour = rgb_w[...].astype(BF16)
    colour_wide = colour.astype(F32)
    colour_rows = jnp.concatenate(
        [colour_wide, jnp.zeros((LANES - 3, LANES), F32)], axis=0
    ).astype(BF16)
    conv_bias = bias[2:3, :]
    chunk = min(256, pixels)
    steps = pixels // chunk
    column = lax.rem(lax.broadcasted_iota(jnp.int32, (chunk, LANES), 0), side)
    not_first, not_last = column > 0, column < side - 1
    small[...] = jnp.zeros_like(small)
    to_sum[...] = jnp.zeros_like(to_sum)
    padded[pl.ds(0, side), :] = jnp.zeros((side, width), BF16)
    padded[pl.ds(side + pixels, side), :] = jnp.zeros((side, width), BF16)
    taps[pl.ds(0, 8), :] = jnp.zeros((8, 3 * LANES), F32)
    taps[pl.ds(8 + pixels, 8), :] = jnp.zeros((8, 3 * LANES), F32)
    wide[pl.ds(0, 8), :] = jnp.zeros((8, LANES), F32)
    wide[pl.ds(8 + pixels, 8), :] = jnp.zeros((8, LANES), F32)

    for s in range(samples):
        style_row = style0[s : s + 1, :]
        for r in range(steps):
            padded[pl.ds(side + r * chunk, chunk), :] = feat[s, pl.ds(r * chunk, chunk), :] * style_row
        style_col = jnp.broadcast_to(style0_wide[s : s + 1, :], (LANES, width)).T
        demod = lax.rsqrt(
            jnp.sum(style_col * style_col * square, axis=0, keepdims=True) + 1e-08
        )
        style_colour = style1[s : s + 1, :]
        for r in range(steps):
            total = dot(padded[pl.ds(r * chunk, chunk), :], kernel[0])
            total = total + dot(padded[pl.ds(side + r * chunk, chunk), :], kernel[1])
            total = total + dot(padded[pl.ds(2 * side + r * chunk, chunk), :], kernel[2])
            taps[pl.ds(8 + r * chunk, chunk), :] = total
        mixed = jnp.zeros((3, LANES), F32)
        g_style1 = jnp.zeros((1, LANES), F32)
        g_bias = jnp.zeros((1, LANES), F32)
        g_demod = jnp.zeros((1, LANES), F32)
        for r in range(steps):
            left = taps[pl.ds(7 + r * chunk, chunk), pl.ds(0, LANES)]
            centre = taps[pl.ds(8 + r * chunk, chunk), pl.ds(LANES, LANES)]
            right = taps[pl.ds(9 + r * chunk, chunk), pl.ds(2 * LANES, LANES)]
            conv_out = centre + jnp.where(not_first, left, 0.0) + jnp.where(not_last, right, 0.0)
            scaled = conv_out * demod + conv_bias
            sig = jax.nn.sigmoid(scaled)
            activated = scaled * sig
            act_mod = (activated * style_colour).astype(BF16)
            mixed = mixed + dot(head[:, pl.ds(r * chunk, chunk)], act_mod)
            g_act = dot(head_t[pl.ds(r * chunk, chunk), :], colour_rows)
            g_style1 = g_style1 + jnp.sum(g_act * activated, axis=0, keepdims=True)
            g_scaled = g_act * style_colour * (sig * (1.0 + scaled * (1.0 - sig)))
            g_bias = g_bias + jnp.sum(g_scaled, axis=0, keepdims=True)
            g_demod = g_demod + jnp.sum(g_scaled * conv_out, axis=0, keepdims=True)
            wide[pl.ds(8 + r * chunk, chunk), :] = g_scaled * demod
        for r in range(steps):
            before = jnp.where(not_last, wide[pl.ds(9 + r * chunk, chunk), :], 0.0)
            centre = wide[pl.ds(8 + r * chunk, chunk), :]
            after = jnp.where(not_first, wide[pl.ds(7 + r * chunk, chunk), :], 0.0)
            for dx, value in enumerate((before, centre, after)):
                value = value.astype(BF16)
                for dy in range(3):
                    lane = pl.ds((3 * dy + dx) * LANES, LANES)
                    start = r * chunk + (dy - 1) * side
                    low_at, high_at = max(start, 0), min(start + chunk, pixels)
                    shifted[pl.ds(low_at, high_at - low_at), lane] = value[
                        low_at - start : high_at - start, :
                    ]
        for dx in range(3):
            shifted[pl.ds(pixels - side, side), pl.ds(dx * LANES, LANES)] = jnp.zeros(
                (side, LANES), BF16
            )
            shifted[pl.ds(0, side), pl.ds((6 + dx) * LANES, LANES)] = jnp.zeros(
                (side, LANES), BF16
            )
        factor = g_demod * demod * demod * demod
        g_style = jnp.zeros((width, LANES), F32)
        for first in range(0, TAPS, 2):
            count = min(2, TAPS - first)
            block = dot(feat_t[s], shifted[:, pl.ds(first * LANES, count * LANES)])
            for tap in range(first, first + count):
                raw = block[:, (tap - first) * LANES : (tap - first + 1) * LANES]
                weight = kernel[tap // 3, :, pl.ds((tap % 3) * LANES, LANES)].astype(F32)
                inner = raw - style_col * (weight * factor)
                g_style = g_style + weight * inner
                unit[s, pl.ds(tap * width, width), :] = (style_col * inner).astype(BF16)
        g_style_row = jnp.sum(g_style.T, axis=0, keepdims=True)
        g_colour_row = jnp.sum((colour_aff * g_style1).T, axis=0, keepdims=True)
        logit = jnp.sum(
            jnp.sum(mixed * colour_wide, axis=0, keepdims=True), axis=1, keepdims=True
        )
        to_sum[pl.ds(8 * s, 1), :] = jnp.broadcast_to(logit, (1, width))
        to_sum[pl.ds(8 * s + 1, 1), :] = g_style_row
        to_sum[pl.ds(8 * s + 2, 1), :] = g_colour_row
        small[pl.ds(8 * s, 1), :] = g_style1
        small[pl.ds(8 * s + 1, 1), :] = g_bias
        small[pl.ds(8 * s + 2, 3), :] = mixed
    keep_map.wait()
    keep_aff.wait()


def summed(parts, row):
    values = [part[pl.ds(row, 1), :] for part in parts]
    while len(values) > 1:
        values = [values[i] + values[i + 1] for i in range(0, len(values), 2)]
    return values[0]


def logit_grad(parts, counted, s):
    logit = summed(parts, 8 * s)
    mask = jnp.full(logit.shape, counted[s], jnp.int32).astype(F32)
    return -mask * jax.nn.sigmoid(-logit), mask * jax.nn.softplus(-logit), mask


def scale_kernel(n_ch, samples, where, counted, *refs):
    parts, (unit, kept, sent) = refs[:n_ch], refs[n_ch:]
    pair = lax.rem(where[0], 2)
    half = unit.shape[1] // 2
    grads, total = [], jnp.zeros((1, LANES), F32)
    for s in range(samples):
        grad, _, mask = logit_grad(parts, counted, s)
        grads.append(grad[:, :LANES])
        total = total + mask[:, :LANES]
    block = half // 9
    for out, owner in ((kept, pair), (sent, 1 - pair)):
        for b in range(9):
            at = pl.multiple_of(owner * half + b * block, block)
            value = grads[0] * unit[0, pl.ds(at, block), :].astype(F32)
            for s in range(1, samples):
                value = value + grads[s] * unit[s, pl.ds(at, block), :].astype(F32)
            out[pl.ds(b * block, block), :] = value.astype(BF16)
        out[pl.ds(half, COUNT_ROWS), :] = jnp.broadcast_to(total, (COUNT_ROWS, LANES)).astype(BF16)


def mapping_kernel(n_ch, samples, where, counted, crossover, *refs):
    parts = refs[:n_ch]
    pre, hid, top, picked, small, map_full, aff_full, pack, rows = refs[n_ch:]
    layers, _, width = map_full.shape
    latents = 2 * samples
    ch = where[1]
    grads = [logit_grad(parts, counted, s) for s in range(samples)]
    pack[...] = jnp.zeros_like(pack)
    base = 2 * layers * latents
    style_rows = []
    for s in range(samples):
        grad = grads[s][0]
        style_row = grad * summed(parts, 8 * s + 1)
        rows[pl.ds(s, 1), :] = style_row
        style_rows.append(style_row)
        line = base + latents + 2 * s
        own = rows[pl.ds(s, 1), pl.ds(pl.multiple_of(ch * LANES, LANES), LANES)]
        short = grad[:, :LANES]
        pack[pl.ds(line, 1), pl.ds(0, LANES)] = own
        pack[pl.ds(line, 1), pl.ds(LANES, LANES)] = short * small[pl.ds(8 * s, 1), :]
        pack[pl.ds(line, 1), pl.ds(2 * LANES, LANES)] = short * small[pl.ds(8 * s + 1, 1), :]
        half_lane = lax.broadcasted_iota(jnp.int32, (1, LANES), 1) < LANES // 2
        pack[pl.ds(line, 1), pl.ds(3 * LANES, LANES)] = jnp.where(
            half_lane, grads[s][1][:, :LANES], grads[s][2][:, :LANES]
        )
        for c in range(3):
            pack[pl.ds(line + 1, 1), pl.ds(c * LANES, LANES)] = short * small[
                pl.ds(8 * s + 2 + c, 1), :
            ]
        for j in range(2):
            pack[pl.ds(base + 2 * s + j, 1), :] = picked[j, pl.ds(s, 1), :]
    w_total = top[pl.ds(0, 1), :]
    for n in range(1, latents):
        w_total = w_total + top[pl.ds(n, 1), :]
    pack[pl.ds(base + latents + 2 * samples, 1), :] = w_total

    def back(value, weights):
        hi, lo = pieces(value, 2)
        both = jnp.concatenate([hi.astype(F32), lo.astype(F32)], axis=0).astype(BF16)
        out = dot_nt(both, weights)
        return out[0:8] + out[8:16]

    pad = [jnp.zeros((8 - samples, width), F32)]
    from_conv = back(jnp.concatenate(style_rows + pad, axis=0), aff_full[...])
    g_rows = []
    for s in range(samples):
        conv_row = from_conv[s : s + 1, :]
        colour_row = grads[s][0] * summed(parts, 8 * s + 2)
        to_first = [jnp.full((1, width), crossover[s], jnp.int32) > j for j in range(2)]
        g_rows.append(
            jnp.where(to_first[0], conv_row, 0.0) + jnp.where(to_first[1], colour_row, 0.0)
        )
        g_rows.append(
            jnp.where(to_first[0], 0.0, conv_row) + jnp.where(to_first[1], 0.0, colour_row)
        )
    g_rows.append(jnp.zeros((8 - latents, width), F32))
    g_hidden = jnp.concatenate(g_rows, axis=0)
    for layer in reversed(range(layers)):
        g_pre = g_hidden * silu_slope(pre[layer])
        pack[pl.ds(layer * latents, latents), :] = g_pre[0:latents]
        pack[pl.ds((layers + layer) * latents, latents), :] = hid[layer][0:latents]
        if layer > 0:
            g_hidden = back(g_pre, map_full[layer])


def update_kernel(n_dp, samples, layers, where, *refs):
    packs, refs = refs[:n_dp], refs[n_dp:]
    (map_w, map_m, map_e, aff_w, aff_m, aff_e) = refs[:6]
    (map_b, map_bm, map_be, bias, bias_m, bias_e, rgb, rgb_m, rgb_e, w_avg) = refs[6:16]
    outs, scratch = refs[16:-7], refs[-7:]
    map_outs, aff_outs = outs[0:4], outs[4:8]
    map_b_outs, bias_outs, rgb_outs = outs[8:12], outs[12:16], outs[16:20]
    w_avg_out, loss_out, count_out = outs[20:23]
    g_pre, hid, picked, style, rgb_all, sums, w_sums = scratch
    latents = 2 * samples
    every = n_dp * latents
    dp = where[0]
    step = pl.program_id(0)
    base = 2 * layers * latents
    share = map_w.shape[1]
    width = map_w.shape[2]

    @pl.when(step == 0)
    def _():
        for k in range(n_dp):
            owner = lax.bitwise_xor(dp, k)
            for layer in range(layers):
                for n in range(latents):
                    at = owner * latents + n
                    g_pre[layer, pl.ds(at, 1), :] = packs[k][pl.ds(layer * latents + n, 1), :]
                    hid[layer, pl.ds(at, 1), :] = packs[k][
                        pl.ds((layers + layer) * latents + n, 1), :
                    ]
            for s in range(samples):
                at = owner * samples + s
                line = base + latents + 2 * s
                for j in range(2):
                    picked[j, pl.ds(at, 1), :] = packs[k][pl.ds(base + 2 * s + j, 1), :]
                style[pl.ds(at, 1), :] = packs[k][pl.ds(line, 1), :]
                rgb_all[pl.ds(at, 1), :] = packs[k][pl.ds(line + 1, 1), :]
            w_sums[pl.ds(owner, 1), :] = packs[k][pl.ds(base + latents + 2 * samples, 1), :]
        sums[pl.ds(0, 1), :] = jnp.sum(style[...], axis=0, keepdims=True)
        sums[pl.ds(1, 1), :] = jnp.sum(rgb_all[...], axis=0, keepdims=True)
        total = sums[pl.ds(0, 1), :]
        count = total[:, width - LANES // 2 : width - LANES // 2 + 1]
        inverse = 1.0 / count
        for layer in range(layers):
            grad = jnp.sum(g_pre[layer], axis=0, keepdims=True) * inverse
            new = advance(
                map_b[pl.ds(layer, 1), :], map_bm[pl.ds(layer, 1), :], map_be[pl.ds(layer, 1), :], grad, 30.0
            )
            for out, value in zip(map_b_outs[:3], new[:3]):
                out[pl.ds(layer, 1), :] = value
        map_b_outs[3][...] = map_b_outs[0][...].astype(BF16)
        colour = sums[pl.ds(1, 1), :]
        for c in range(3):
            row = pl.ds(c, 1)
            lane = slice(c * LANES, (c + 1) * LANES)
            new = advance(bias[row, :], bias_m[row, :], bias_e[row, :], total[:, lane] * inverse, 50.0)
            for out, value in zip(bias_outs[:3], new[:3]):
                out[row, :] = value
            new = advance(rgb[row, :], rgb_m[row, :], rgb_e[row, :], colour[:, lane] * inverse, 1.0)
            for out, value in zip(rgb_outs[:3], new[:3]):
                out[row, :] = value
        bias_outs[3][...] = bias_outs[0][...].astype(BF16)
        rgb_outs[3][...] = rgb_outs[0][...].astype(BF16)
        mean = jnp.sum(w_sums[...], axis=0, keepdims=True) * (1.0 / every)
        w_avg_out[...] = w_avg[...] + (1.0 - AVERAGE_BETA) * (mean - w_avg[...])
        loss_out[0] = jnp.sum(total[:, width - LANES : width - LANES + 1])
        count_out[0] = jnp.sum(count)

    count = sums[pl.ds(0, 1), pl.ds(width - LANES, LANES)][:, LANES // 2 : LANES // 2 + 1]
    inverse = 1.0 / count
    own = pltpu.roll(hid[step], lax.rem(width - dp * share, width), 1)[:, :LANES]
    own = jnp.concatenate([own] * 3, axis=0).astype(BF16)
    split = jnp.concatenate([p.astype(F32) for p in pieces(g_pre[step], 3)], axis=0).astype(BF16)
    grad = dot_tn(own, split)[0:share] * inverse
    new = advance(map_w[0], map_m[0], map_e[0], grad, 30.0)
    for out, value in zip(map_outs, new):
        out[0] = value
    depth = aff_w.shape[0]
    per = width // depth
    j = step // per
    start = pl.multiple_of(lax.rem(step, per) * depth, depth)
    chosen = picked[j, :, pl.ds(start, depth)]
    chosen = jnp.concatenate([chosen] * 3, axis=0)
    grad_style = style[:, pl.ds(pl.multiple_of(j * LANES, LANES), LANES)]
    split = jnp.concatenate([p.astype(F32) for p in pieces(grad_style, 3)], axis=0)
    fill = -chosen.shape[0] % 16
    if fill:
        chosen = jnp.concatenate([chosen, jnp.zeros((fill, depth), F32)], axis=0)
        split = jnp.concatenate([split, jnp.zeros((fill, LANES), F32)], axis=0)
    grad = dot_tn(chosen.astype(BF16), split.astype(BF16)) * inverse
    new = advance(aff_w[...], aff_m[...], aff_e[...], grad, 30.0)
    for out, value in zip(aff_outs, new):
        out[...] = value


def conv_kernel(where, mine_a, mine_b, other_a, other_b, param, moment, average, *outs):
    outs, grad = outs[:4], outs[4]
    pair = lax.rem(where[0], 2)
    rows = mine_a.shape[0]
    half = 2 * rows - COUNT_ROWS
    step = pl.program_id(0)

    @pl.when(step == 0)
    def _():
        for first, second, owner in ((mine_a, mine_b, pair), (other_a, other_b, 1 - pair)):
            at = owner * half
            grad[pl.ds(pl.multiple_of(at, 16), rows), :] = first[...]
            grad[pl.ds(pl.multiple_of(at + rows, 16), rows - COUNT_ROWS), :] = second[
                pl.ds(0, rows - COUNT_ROWS), :
            ]

    inverse = 1.0 / mine_b[pl.ds(rows - COUNT_ROWS, 16), :].astype(F32)[0:1]
    depth = param.shape[0]
    at = pl.multiple_of(step * depth, depth)
    value = grad[pl.ds(at, depth), :].astype(F32) * inverse
    new = advance(param[...], moment[...], average[...], value, 5.0)
    for out, item in zip(outs, new):
        out[...] = item


def local(
    features,
    z_table,
    seeds,
    crossover,
    counted,
    head,
    w_avg,
    map_w,
    map_w_mom,
    map_w_ema,
    map_b,
    map_b_mom,
    map_b_ema,
    aff_w,
    aff_w_mom,
    aff_w_ema,
    chan_bias,
    chan_bias_mom,
    chan_bias_ema,
    conv_w,
    conv_w_mom,
    conv_w_ema,
    rgb_w,
    rgb_w_mom,
    rgb_w_ema,
):
    samples, side = features.shape[0], features.shape[1]
    pixels = side * side
    layers, share, width = map_w.shape
    n_dp, n_ch = lax.axis_size("dp"), lax.axis_size("chan")
    latents = 2 * samples
    where = jnp.stack([lax.axis_index("dp"), lax.axis_index("chan")]).astype(jnp.int32)
    flat = lambda a: a.reshape(TAPS * width, LANES)

    half = width // 2
    map_low, aff_part = pl.pallas_call(
        prepare_kernel,
        out_shape=(shape(map_w.shape, BF16), shape((half + 16, LANES), BF16)),
        in_specs=[SMEM, VMEM, VMEM, VMEM],
        out_specs=(VMEM, VMEM),
        compiler_params=params(32),
        name="prepare",
    )(where, map_w, aff_w, chan_bias)
    aff_own = spread_direct(aff_part, "chan")
    map_parts = spread(map_low, "dp")
    feat_parts = spread_direct(features.reshape(samples, pixels, LANES), "chan")
    aff_pair = [swap(part, "dp", 1) for part in aff_own]
    head_t = jnp.pad(head.T, ((0, 0), (0, LANES - 3)))

    main_out = (
        shape((samples, TAPS * width, LANES), BF16),
        shape((8 * samples, width), F32),
        shape((layers, 8, width), F32),
        shape((layers, 8, width), F32),
        shape((8, width), F32),
        shape((2, 8, width), F32),
        shape((8 * samples, LANES), F32),
        shape((layers, width, width), BF16),
        shape((width, width), BF16),
    )
    unit, to_sum, pre, hid, top, picked, small, map_full, aff_full = pl.pallas_call(
        functools.partial(main_kernel, n_dp, n_ch, samples, side),
        out_shape=main_out,
        in_specs=[SMEM] * 3 + [HBM] * (n_dp + 3 * n_ch + 2) + [VMEM] * 6,
        out_specs=(VMEM,) * 7 + (HBM,) * 2,
        scratch_shapes=[
            pltpu.VMEM((layers, width, width), BF16),
            pltpu.VMEM((width, width), BF16),
            pltpu.VMEM((16, width), BF16),
            pltpu.VMEM((samples, pixels, width), BF16),
            pltpu.VMEM((samples, width, pixels), BF16),
            pltpu.VMEM((TAPS, width, LANES), F32),
            pltpu.VMEM((3, width, 3 * LANES), BF16),
            pltpu.VMEM((pixels + 2 * side, width), BF16),
            pltpu.VMEM((pixels + 16, 3 * LANES), F32),
            pltpu.VMEM((pixels, TAPS * LANES), BF16),
            pltpu.VMEM((pixels + 16, LANES), F32),
            pltpu.VMEM((latents, 8, width), F32),
            pltpu.SemaphoreType.DMA((n_dp,)),
            pltpu.SemaphoreType.DMA((n_ch,)),
            pltpu.SemaphoreType.DMA((3 * n_ch,)),
            pltpu.SemaphoreType.DMA((latents,)),
            pltpu.SemaphoreType.DMA,
            pltpu.SemaphoreType.DMA((2,)),
        ],
        compiler_params=params(52),
        name="main",
    )(
        where,
        seeds.reshape(-1),
        crossover,
        *map_parts,
        *feat_parts,
        *aff_own,
        *aff_pair,
        z_table,
        conv_w.reshape(TAPS, width, LANES),
        aff_w,
        map_b,
        chan_bias,
        head,
        head_t,
        rgb_w,
    )

    sum_parts = spread_direct(to_sum, "chan")
    half_rows = TAPS * width // 2 + COUNT_ROWS
    kept, sent = pl.pallas_call(
        functools.partial(scale_kernel, n_ch, samples),
        out_shape=(shape((half_rows, LANES), BF16),) * 2,
        in_specs=[SMEM] * 2 + [VMEM] * (n_ch + 1),
        out_specs=(VMEM, VMEM),
        compiler_params=params(32),
        name="scale",
    )(where, counted, *sum_parts, unit)

    got = swap(sent, "dp", 1)
    total = (kept.astype(F32) + got.astype(F32)).astype(BF16)
    quarter = half_rows // 2
    quarters = [total[:quarter], total[quarter:]]
    bits = [1 << b for b in range(1, n_dp.bit_length() - 1)]
    orders = [bits, bits[::-1]]
    for turn in range(len(bits)):
        got = [swap(quarters[q], "dp", orders[q][turn]) for q in range(2)]
        quarters = [
            (quarters[q].astype(F32) + got[q].astype(F32)).astype(BF16) for q in range(2)
        ]
    others = [swap(quarter_sum, "dp", 1) for quarter_sum in quarters]

    lines = 2 * layers * latents + latents + 2 * samples + 1
    lines = -(-lines // 8) * 8
    pack = pl.pallas_call(
        functools.partial(mapping_kernel, n_ch, samples),
        out_shape=shape((lines, width), F32),
        in_specs=[SMEM] * 3 + [VMEM] * (n_ch + 7),
        out_specs=VMEM,
        scratch_shapes=[pltpu.VMEM((8, width), F32)],
        compiler_params=params(32),
        name="mapping_back",
    )(where, counted, crossover, *sum_parts, pre, hid, top, picked, small, map_full, aff_full)
    packs = spread(pack, "dp")

    whole = lambda a: pl.BlockSpec(a.shape, lambda i: (0,) * len(a.shape))
    map_spec = pl.BlockSpec((1, share, width), lambda i: (i, 0, 0))
    aff_rows = 2 * width // layers
    aff_spec = pl.BlockSpec((aff_rows, LANES), lambda i: (i, 0))
    flat_aff = [a.reshape(2 * width, LANES) for a in (aff_w, aff_w_mom, aff_w_ema)]
    tiny = [
        map_b,
        map_b_mom,
        map_b_ema,
        chan_bias,
        chan_bias_mom,
        chan_bias_ema,
        rgb_w,
        rgb_w_mom,
        rgb_w_ema,
        w_avg.reshape(1, width),
    ]
    types = (F32, F32, F32, BF16)
    out_shape = (
        [shape(map_w.shape, t) for t in types]
        + [shape((2 * width, LANES), t) for t in types]
        + [shape(map_b.shape, t) for t in types]
        + [shape(chan_bias.shape, t) for t in types]
        + [shape(rgb_w.shape, t) for t in types]
        + [shape((1, width), F32), shape((1,), F32), shape((1,), F32)]
    )
    every = n_dp * latents
    outs = pl.pallas_call(
        functools.partial(update_kernel, n_dp, samples, layers),
        grid=(layers,),
        out_shape=out_shape,
        in_specs=[SMEM]
        + [whole(p) for p in packs]
        + [map_spec] * 3
        + [aff_spec] * 3
        + [whole(a) for a in tiny],
        out_specs=[map_spec] * 4
        + [aff_spec] * 4
        + [whole(s) for s in out_shape[8:21]]
        + [SMEM, SMEM],
        scratch_shapes=[
            pltpu.VMEM((layers, every, width), F32),
            pltpu.VMEM((layers, every, width), F32),
            pltpu.VMEM((2, n_dp * samples, width), F32),
            pltpu.VMEM((n_dp * samples, width), F32),
            pltpu.VMEM((n_dp * samples, width), F32),
            pltpu.VMEM((8, width), F32),
            pltpu.VMEM((n_dp, width), F32),
        ],
        compiler_params=params(48),
        name="update",
    )(where, *packs, map_w, map_w_mom, map_w_ema, *flat_aff, *tiny)

    conv_spec = pl.BlockSpec((width, LANES), lambda i: (i, 0))
    conv_outs = pl.pallas_call(
        conv_kernel,
        grid=(TAPS,),
        out_shape=[shape((TAPS * width, LANES), t) for t in types],
        in_specs=[SMEM] + [whole(quarters[0])] * 4 + [conv_spec] * 3,
        out_specs=[conv_spec] * 4,
        scratch_shapes=[pltpu.VMEM((TAPS * width, LANES), BF16)],
        compiler_params=params(32),
        name="conv_update",
    )(where, *quarters, *others, flat(conv_w), flat(conv_w_mom), flat(conv_w_ema))

    map_outs, aff_outs = outs[0:4], [a.reshape(aff_w.shape) for a in outs[4:8]]
    conv_outs = [a.reshape(conv_w.shape) for a in conv_outs]
    return (
        *map_outs,
        *outs[8:12],
        *aff_outs,
        *outs[12:16],
        *conv_outs,
        *outs[16:20],
        outs[20].reshape(width),
        outs[21].reshape(()),
        outs[22].reshape(()),
    )


def solution(mesh):
    in_specs = (
        P("dp", None, None, "chan"),
        P(),
        P("dp", None),
        P("dp"),
        P("dp"),
        P(),
        P(),
        P(None, "dp", None),
        P(None, "dp", None),
        P(None, "dp", None),
        P(),
        P(),
        P(),
        P(None, None, "chan"),
        P(None, None, "chan"),
        P(None, None, "chan"),
        P(None, "chan"),
        P(None, "chan"),
        P(None, "chan"),
        P(None, None, None, "chan"),
        P(None, None, None, "chan"),
        P(None, None, None, "chan"),
        P(None, "chan"),
        P(None, "chan"),
        P(None, "chan"),
    )
    out_specs = (
        P(None, "dp", None),
        P(None, "dp", None),
        P(None, "dp", None),
        P(None, "dp", None),
        P(),
        P(),
        P(),
        P(),
        P(None, None, "chan"),
        P(None, None, "chan"),
        P(None, None, "chan"),
        P(None, None, "chan"),
        P(None, "chan"),
        P(None, "chan"),
        P(None, "chan"),
        P(None, "chan"),
        P(None, None, None, "chan"),
        P(None, None, None, "chan"),
        P(None, None, None, "chan"),
        P(None, None, None, "chan"),
        P(None, "chan"),
        P(None, "chan"),
        P(None, "chan"),
        P(None, "chan"),
        P(),
        P(),
        P(),
    )
    return jax.shard_map(local, mesh=mesh, in_specs=in_specs, out_specs=out_specs, check_vma=False)
```

time: 328 us -> 118 us (0.36)
  waiting for transfers between devices: 167 us -> 38.1 us
  matrix products: 49.9 us -> 0 us
  blocking collectives: 49.8 us -> 0 us
  starting transfers between devices: 0.64 us -> 44.4 us
  other arithmetic: 29.6 us -> 0.55 us
  Pallas kernels: 0 us -> 25.7 us
  between operations: 18.4 us -> 2.42 us
  local copies, waits for them, and re-layouts: 10.8 us -> 6.05 us
    reduce_scatter x1 -> x0, waiting for transfers between devices: 63.7 us -> none  [local(): lax.psum_scatter(weight_terms, 'dp', scatter_dimension=1, tiled=True)]
    dot_general x40 -> x0, matrix products: 45.8 us -> none  [the longest x9 12 us: local(): jnp.einsum('shwi,shwo->io', window, g_conv_out, preferred_element_type=jn...]
    all_gather x2 -> x0, waiting for transfers between devices: 44.8 us -> none  [the longest x1 35.2 us: local(): lax.all_gather(map_w.astype(jnp.bfloat16), 'dp', axis=1, tiled=True)]
    ppermute x0 -> x34, starting transfers between devices: none -> 44.4 us  [swap(): lax.ppermute(value, axis, [(i, i ^ distance) for i in range(lax.axis_size...]
    psum x3 -> x0, blocking collectives: 40 us -> none  [the longest x1 24 us: local(): lax.psum((w_total, local_count, local_loss), 'dp')]
    ppermute x0 -> x34, waiting for transfers between devices: none -> 38.1 us  [swap(): lax.ppermute(value, axis, [(i, i ^ distance) for i in range(lax.axis_size...]
    psum x1 -> x0, waiting for transfers between devices: 32.3 us -> none  [local(): lax.psum((g_affine, g_bias_all, g_kernel, g_colour, g_map_bias), 'dp')]
    unnamed x8 -> x0, waiting for transfers between devices: 25.8 us -> none
  transfers between devices with their start and end apart: 6 -> 34, of which waited for: 5 -> 15; matrix products, arithmetic and copies ran while one was open for 17% -> 2% of each run, Pallas kernels for 0% -> 7%
where the time goes in v1:
time: 118 us; the launch traced here: 117 us
  starting transfers between devices  44.4 us (38%)
  waiting for transfers between devices  38.1 us (32%)
  Pallas kernels  25.7 us (22%)
  local copies, waits for them, and re-layouts  6.05 us (5%)
  between operations  2.42 us (2%)
    ppermute x34, starting transfers between devices, swap(): lax.ppermute(value, axis, [(i, i ^ distance) for i in range(lax.axis_size...  44.4 us
    ppermute x34, waiting for transfers between devices, swap(): lax.ppermute(value, axis, [(i, i ^ distance) for i in range(lax.axis_size...  38.1 us
    pallas_call x1, Pallas kernels, local(): pl.pallas_call(functools.partial(main_kernel, n_dp, n_ch, samples, side),...  10.7 us
    pallas_call x1, Pallas kernels, local(): pl.pallas_call(functools.partial(update_kernel, n_dp, samples, layers), g...  6.03 us
    pallas_call x1, Pallas kernels, local(): pl.pallas_call(conv_kernel, grid=(TAPS,), out_shape=[shape((TAPS * width,...  5.52 us
    unnamed x63, local copies, waits for them, and re-layouts  5.25 us
  transfers between devices with their start and end apart: 34, of which 15 were waited for; matrix products, arithmetic and copies ran while one was open for 2% of the time, Pallas kernels for 7%

profile of v1, /device:TPU:1, one launch (start us, length us, event | category | flops | bytes accessed | tf_op | source)
XLA Modules:
  0.0 117.2 jit_solution(16018886423997972823)
XLA Ops:
  1.8 1.2 %copy-done.4 = f32[8,64,512]{2,1,0:T(8,128)S(1)} copy-done((f32[8,64,512]{2,1,0:T(8,128)S(1)}, f32[8,64,512]{2,1,0:T(8,128)}, u32[]{:S(2)}) %copy-start.4) | copy-done | bytes 1048600
  4.4 2.1 %collective-permute-start.1 = (bf16[8,64,512]{2,1,0:T(8,128)(2,1)S(1)}, bf16[8,64,512]{2,1,0:T(8,128)(2,1)S(1)}, u32[]{:S(2)}, u32[]{:S(2)}) collective-permute-start(bf16[8,64,512]{2,1,0:T(8,128)(2,1)S(1)} %get-tuple-element.67.refs_3_), channel_id=1, source_target_pairs={{0,8},{4,12},{8,0},{12,4},{16,24},{20,28},{24,16},{28,20},{1,9},{5... | collective-permute-start | bytes 1572872 | tf_op jit(solution)/shard_map/ppermute | solution.py:32
  6.5 1.2 %collective-permute-start.3 = (bf16[8,64,512]{2,1,0:T(8,128)(2,1)S(1)}, bf16[8,64,512]{2,1,0:T(8,128)(2,1)S(1)}, u32[]{:S(2)}, u32[]{:S(2)}) collective-permute-start(bf16[8,64,512]{2,1,0:T(8,128)(2,1)S(1)} %get-tuple-element.67.refs_3_), channel_id=1, source_target_pairs={{0,16},{4,20},{8,24},{12,28},{16,0},{20,4},{24,8},{28,12},{1,17},{... | collective-permute-start | bytes 1572872 | tf_op jit(solution)/shard_map/ppermute | solution.py:32
  7.7 1.5 %collective-permute-start.10 = (bf16[272,128]{1,0:T(8,128)(2,1)S(1)}, bf16[272,128]{1,0:T(8,128)(2,1)S(1)}, u32[]{:S(2)}, u32[]{:S(2)}) collective-permute-start(bf16[272,128]{1,0:T(8,128)(2,1)S(1)} %get-tuple-element.68.refs_15_), channel_id=1, source_target_pairs={{0,1},{1,0},{2,3},{3,2},{4,5},{5,4},{6,7},{7,6},{8,9},{9,8},{10,11... | collective-permute-start | bytes 208904 | tf_op jit(solution)/shard_map/ppermute | solution.py:32
  9.2 2.3 %collective-permute-start.11 = (bf16[272,128]{1,0:T(8,128)(2,1)S(1)}, bf16[272,128]{1,0:T(8,128)(2,1)S(1)}, u32[]{:S(2)}, u32[]{:S(2)}) collective-permute-start(bf16[272,128]{1,0:T(8,128)(2,1)S(1)} %get-tuple-element.68.refs_15_), channel_id=1, source_target_pairs={{0,2},{1,3},{2,0},{3,1},{4,6},{5,7},{6,4},{7,5},{8,10},{9,11},{10,... | collective-permute-start | bytes 208904 | tf_op jit(solution)/shard_map/ppermute | solution.py:32
  11.5 3.2 %collective-permute-start.12 = (bf16[272,128]{1,0:T(8,128)(2,1)S(1)}, bf16[272,128]{1,0:T(8,128)(2,1)S(1)}, u32[]{:S(2)}, u32[]{:S(2)}) collective-permute-start(bf16[272,128]{1,0:T(8,128)(2,1)S(1)} %get-tuple-element.68.refs_15_), channel_id=1, source_target_pairs={{0,3},{1,2},{2,1},{3,0},{4,7},{5,6},{6,5},{7,4},{8,11},{9,10},{10,... | collective-permute-start | bytes 208904 | tf_op jit(solution)/shard_map/ppermute | solution.py:32
  14.7 3.7 %collective-permute-start.13 = (bf16[272,128]{1,0:T(8,128)(2,1)S(1)}, bf16[272,128]{1,0:T(8,128)(2,1)S(1)}, u32[]{:S(2)}, u32[]{:S(2)}) collective-permute-start(bf16[272,128]{1,0:T(8,128)(2,1)S(1)} %get-tuple-element.68.refs_15_), channel_id=1, source_target_pairs={{0,4},{4,0},{8,12},{12,8},{16,20},{20,16},{24,28},{28,24},{1,5},{5... | collective-permute-start | bytes 208904 | tf_op jit(solution)/shard_map/ppermute | solution.py:32
  19.3 1.4 %collective-permute-start.14 = (bf16[272,128]{1,0:T(8,128)(2,1)S(1)}, bf16[272,128]{1,0:T(8,128)(2,1)S(1)}, u32[]{:S(2)}, u32[]{:S(2)}) collective-permute-start(bf16[272,128]{1,0:T(8,128)(2,1)S(1)} %collective-permute-done.10.refs_16_), channel_id=1, source_target_pairs={{0,4},{4,0},{8,12},{12,8},{16,20},{20,16},{24,28},{28,24},{1,5},{5... | collective-permute-start | bytes 208904 | tf_op jit(solution)/shard_map/ppermute | solution.py:32
  25.2 2.4 %collective-permute-start.8 = (bf16[1,1024,128]{2,1,0:T(8,128)(2,1)}, bf16[1,1024,128]{2,1,0:T(8,128)(2,1)S(1)}, u32[]{:S(2)}, u32[]{:S(2)}) collective-permute-start(bf16[1,1024,128]{2,1,0:T(8,128)(2,1)} %bitcast.32), channel_id=1, source_target_pairs={{0,2},{1,3},{2,0},{3,1},{4,6},{5,7},{6,4},{7,5},{8,10},{9,11},{10,... | collective-permute-start | bytes 786440 | tf_op jit(solution)/shard_map/ppermute | solution.py:32
  27.5 1.1 collective-permute-start.2
  28.7 3.4 %collective-permute-start.4 = (bf16[8,64,512]{2,1,0:T(8,128)(2,1)S(1)}, bf16[8,64,512]{2,1,0:T(8,128)(2,1)}, u32[]{:S(2)}, u32[]{:S(2)}) collective-permute-start(bf16[8,64,512]{2,1,0:T(8,128)(2,1)S(1)} %collective-permute-done.3.refs_7_), channel_id=1, source_target_pairs={{0,4},{4,0},{8,12},{12,8},{16,20},{20,16},{24,28},{28,24},{1,5},{5... | collective-permute-start | bytes 1572872 | tf_op jit(solution)/shard_map/ppermute | solution.py:32
  32.1 7.9 %collective-permute-done.8.refs_13_ = bf16[1,1024,128]{2,1,0:T(8,128)(2,1)S(1)} collective-permute-done((bf16[1,1024,128]{2,1,0:T(8,128)(2,1)}, bf16[1,1024,128]{2,1,0:T(8,128)(2,1)S(1)}, u32[]{:S(2)}, u32[]{:S(2)}) %collective-permute-start.8) | collective-permute-done | bytes 262176 | tf_op jit(solution)/shard_map/ppermute | solution.py:32
  42.7 6.7 %collective-permute-done.9.refs_14_ = bf16[1,1024,128]{2,1,0:T(8,128)(2,1)S(1)} collective-permute-done((bf16[1,1024,128]{2,1,0:T(8,128)(2,1)}, bf16[1,1024,128]{2,1,0:T(8,128)(2,1)S(1)}, u32[]{:S(2)}, u32[]{:S(2)}) %collective-permute-start.9) | collective-permute-done | bytes 262176 | tf_op jit(solution)/shard_map/ppermute | solution.py:32
  49.6 10.7 %main.1 = (bf16[1,4608,128]{2,1,0:T(8,128)(2,1)}, f32[8,512]{1,0:T(8,128)S(1)}, f32[8,8,512]{2,1,0:T(8,128)S(1)}, f32[8,8,512]{2,1,0:T(8,128)S(1)}, f32[8,512]{1...) custom-call(s32[2]{0:T(128)S(1)} %pad_add_fusion.where.refs_0_, ...), custom_call_target="tpu_custom_call" | custom-call | tf_op jit(solution)/shard_map/main/pallas_call | solution.py:607
  60.3 1.4 %collective-permute-start.17 = (f32[8,512]{1,0:T(8,128)S(1)}, f32[8,512]{1,0:T(8,128)S(1)}, u32[]{:S(2)}, u32[]{:S(2)}) collective-permute-start(f32[8,512]{1,0:T(8,128)S(1)} %get-tuple-element.69.refs_0_), channel_id=1, source_target_pairs={{0,1},{1,0},{2,3},{3,2},{4,5},{5,4},{6,7},{7,6},{8,9},{9,8},{10,11... | collective-permute-start | bytes 49160 | tf_op jit(solution)/shard_map/ppermute | solution.py:32
  61.7 1.9 %collective-permute-start.18 = (f32[8,512]{1,0:T(8,128)S(1)}, f32[8,512]{1,0:T(8,128)S(1)}, u32[]{:S(2)}, u32[]{:S(2)}) collective-permute-start(f32[8,512]{1,0:T(8,128)S(1)} %get-tuple-element.69.refs_0_), channel_id=1, source_target_pairs={{0,2},{1,3},{2,0},{3,1},{4,6},{5,7},{6,4},{7,5},{8,10},{9,11},{10,... | collective-permute-start | bytes 49160 | tf_op jit(solution)/shard_map/ppermute | solution.py:32
  63.6 1.1 collective-permute-start.19
  65.4 2.6 %collective-permute-done.19.refs_3_ = f32[8,512]{1,0:T(8,128)S(1)} collective-permute-done((f32[8,512]{1,0:T(8,128)S(1)}, f32[8,512]{1,0:T(8,128)S(1)}, u32[]{:S(2)}, u32[]{:S(2)}) %collective-permute-start.19) | collective-permute-done | bytes 16416 | tf_op jit(solution)/shard_map/ppermute | solution.py:32
  68.0 1.3 %copy-done.8 = bf16[1,4608,128]{2,1,0:T(8,128)(2,1)S(1)} copy-done((bf16[1,4608,128]{2,1,0:T(8,128)(2,1)S(1)}, bf16[1,4608,128]{2,1,0:T(8,128)(2,1)}, u32[]{:S(2)}) %copy-start.8) | copy-done | bytes 1179672
  70.0 2.8 %collective-permute-start.27 = (bf16[2336,128]{1,0:T(8,128)(2,1)S(1)}, bf16[2336,128]{1,0:T(8,128)(2,1)S(1)}, u32[]{:S(2)}, u32[]{:S(2)}) collective-permute-start(bf16[2336,128]{1,0:T(8,128)(2,1)S(1)} %get-tuple-element.95), channel_id=1, source_target_pairs={{0,4},{4,0},{8,12},{12,8},{16,20},{20,16},{24,28},{28,24},{1,5},{5... | collective-permute-start | bytes 1794056 | tf_op jit(solution)/shard_map/ppermute | solution.py:32
  72.8 1.6 %collective-permute-done.27 = bf16[2336,128]{1,0:T(8,128)(2,1)S(1)} collective-permute-done((bf16[2336,128]{1,0:T(8,128)(2,1)S(1)}, bf16[2336,128]{1,0:T(8,128)(2,1)S(1)}, u32[]{:S(2)}, u32[]{:S(2)}) %collective-permute-start.27) | collective-permute-done | bytes 598048 | tf_op jit(solution)/shard_map/ppermute | solution.py:32
  75.4 1.2 %collective-permute-start.30 = (bf16[1168,128]{1,0:T(8,128)(2,1)S(1)}, bf16[1168,128]{1,0:T(8,128)(2,1)S(1)}, u32[]{:S(2)}, u32[]{:S(2)}) collective-permute-start(bf16[1168,128]{1,0:T(8,128)(2,1)S(1)} %get-tuple-element.109), channel_id=1, source_target_pairs={{0,16},{4,20},{8,24},{12,28},{16,0},{20,4},{24,8},{28,12},{1,17},{... | collective-permute-start | bytes 897032 | tf_op jit(solution)/shard_map/ppermute | solution.py:32
  76.6 6.4 %collective-permute-done.28 = bf16[1168,128]{1,0:T(8,128)(2,1)S(1)} collective-permute-done((bf16[1168,128]{1,0:T(8,128)(2,1)S(1)}, bf16[1168,128]{1,0:T(8,128)(2,1)S(1)}, u32[]{:S(2)}, u32[]{:S(2)}) %collective-permute-start.28) | collective-permute-done | bytes 299040 | tf_op jit(solution)/shard_map/ppermute | solution.py:32
  85.2 5.5 %collective-permute-done.31 = bf16[1168,128]{1,0:T(8,128)(2,1)S(1)} collective-permute-done((bf16[1168,128]{1,0:T(8,128)(2,1)S(1)}, bf16[1168,128]{1,0:T(8,128)(2,1)S(1)}, u32[]{:S(2)}, u32[]{:S(2)}) %collective-permute-start.31) | collective-permute-done | bytes 299040 | tf_op jit(solution)/shard_map/ppermute | solution.py:32
  90.8 2.5 %collective-permute-start.33 = (bf16[1168,128]{1,0:T(8,128)(2,1)S(1)}, bf16[1168,128]{1,0:T(8,128)(2,1)S(1)}, u32[]{:S(2)}, u32[]{:S(2)}) collective-permute-start(bf16[1168,128]{1,0:T(8,128)(2,1)S(1)} %add_convert_fusion.1.mine_b), channel_id=1, source_target_pairs={{0,4},{4,0},{8,12},{12,8},{16,20},{20,16},{24,28},{28,24},{1,5},{5... | collective-permute-start | bytes 897032 | tf_op jit(solution)/shard_map/ppermute | solution.py:32
  94.2 2.1 %mapping_back.1.refs_0_ = f32[40,512]{1,0:T(8,128)S(1)} custom-call(s32[2]{0:T(128)S(1)} %pad_add_fusion.where.refs_0_, s32[1]{0:T(128)S(6)} %copy.54.counted, s32[1]{0:T(128)S(6)} %copy.53.refs_2_.crossover, f32[8,512]{1,0:T(8,128)S(1)} %get-tuple-element.69.refs_0_, f32[8,512]{1,0:T(8,128)S(1)} %collective-permute-done.17.refs_1_, ...), custom_call_target="tpu_custom_call" | custom-call | tf_op jit(solution)/shard_map/mapping_back/pallas_call | solution.py:678
  97.0 1.2 %collective-permute-start.23 = (f32[40,512]{1,0:T(8,128)S(1)}, f32[40,512]{1,0:T(8,128)S(1)}, u32[]{:S(2)}, u32[]{:S(2)}) collective-permute-start(f32[40,512]{1,0:T(8,128)S(1)} %mapping_back.1.refs_0_), channel_id=1, source_target_pairs={{0,16},{4,20},{8,24},{12,28},{16,0},{20,4},{24,8},{28,12},{1,17},{... | collective-permute-start | bytes 245768 | tf_op jit(solution)/shard_map/ppermute | solution.py:32
  99.0 1.4 %collective-permute-done.21.refs_2_ = f32[40,512]{1,0:T(8,128)S(1)} collective-permute-done((f32[40,512]{1,0:T(8,128)S(1)}, f32[40,512]{1,0:T(8,128)S(1)}, u32[]{:S(2)}, u32[]{:S(2)}) %collective-permute-start.21) | collective-permute-done | bytes 81952 | tf_op jit(solution)/shard_map/ppermute | solution.py:32
  101.2 1.5 %collective-permute-start.22 = (f32[40,512]{1,0:T(8,128)S(1)}, f32[40,512]{1,0:T(8,128)S(1)}, u32[]{:S(2)}, u32[]{:S(2)}) collective-permute-start(f32[40,512]{1,0:T(8,128)S(1)} %collective-permute-done.21.refs_2_), channel_id=1, source_target_pairs={{0,4},{4,0},{8,12},{12,8},{16,20},{20,16},{24,28},{28,24},{1,5},{5... | collective-permute-start | bytes 245768 | tf_op jit(solution)/shard_map/ppermute | solution.py:32
  102.7 1.5 %collective-permute-start.24 = (f32[40,512]{1,0:T(8,128)S(1)}, f32[40,512]{1,0:T(8,128)S(1)}, u32[]{:S(2)}, u32[]{:S(2)}) collective-permute-start(f32[40,512]{1,0:T(8,128)S(1)} %collective-permute-done.23.refs_4_), channel_id=1, source_target_pairs={{0,4},{4,0},{8,12},{12,8},{16,20},{20,16},{24,28},{28,24},{1,5},{5... | collective-permute-start | bytes 245768 | tf_op jit(solution)/shard_map/ppermute | solution.py:32
  105.6 6.0 %update.1 = (f32[8,64,512]{2,1,0:T(8,128)}, f32[8,64,512]{2,1,0:T(8,128)}, f32[8,64,512]{2,1,0:T(8,128)}, bf16[8,64,512]{2,1,0:T(8,128)(2,1)}, f32[1024,128]{1,0...) custom-call(s32[2]{0:T(128)S(1)} %pad_add_fusion.where.refs_0_, ...), custom_call_target="tpu_custom_call" | custom-call | tf_op jit(solution)/shard_map/update/pallas_call | solution.py:716
  111.7 5.5 %conv_update.1 = (f32[4608,128]{1,0:T(8,128)}, f32[4608,128]{1,0:T(8,128)}, f32[4608,128]{1,0:T(8,128)}, bf16[4608,128]{1,0:T(8,128)(2,1)}) custom-call(s32[2]{0:T(128)S(1)} %pad_add_fusion.where.refs_0_, bf16[1168,128]{1,0:T(8,128)(2,1)S(1)} %add_convert_fusion.3.mine_a, bf16[1168,128]{1,0:T(8,128)(2,1)S(1)} %add_convert_fusion.1.mine_b, ...), custom_call_target="tpu_custom_call" | custom-call | tf_op jit(solution)/shard_map/conv_update/pallas_call | solution.py:743
  (112 shorter events, 18.2 us)
Async XLA Ops:
  4.4 23.2 %collective-permute-start.1 = (bf16[8,64,512]{2,1,0:T(8,128)(2,1)S(1)}, bf16[8,64,512]{2,1,0:T(8,128)(2,1)S(1)}, u32[]{:S(2)}, u32[]{:S(2)}) collective-permute-start(bf16[8,64,512]{2,1,0:T(8,128)(2,1)S(1)} %get-tuple-element.67.refs_3_), channel_id=1, source_target_pairs={{0,8},{4,12},{8,0},{12,4},{16,24},{20,28},{24,16},{28,20},{1,9},{5... | collective-permute-start | bytes 1572872 | tf_op jit(solution)/shard_map/ppermute | solution.py:32
  6.5 22.2 %collective-permute-start.3 = (bf16[8,64,512]{2,1,0:T(8,128)(2,1)S(1)}, bf16[8,64,512]{2,1,0:T(8,128)(2,1)S(1)}, u32[]{:S(2)}, u32[]{:S(2)}) collective-permute-start(bf16[8,64,512]{2,1,0:T(8,128)(2,1)S(1)} %get-tuple-element.67.refs_3_), channel_id=1, source_target_pairs={{0,16},{4,20},{8,24},{12,28},{16,0},{20,4},{24,8},{28,12},{1,17},{... | collective-permute-start | bytes 1572872 | tf_op jit(solution)/shard_map/ppermute | solution.py:32
  7.7 24.3 %collective-permute-start.5 = (bf16[8,64,512]{2,1,0:T(8,128)(2,1)S(1)}, bf16[8,64,512]{2,1,0:T(8,128)(2,1)}, u32[]{:S(2)}, u32[]{:S(2)}) collective-permute-start(bf16[8,64,512]{2,1,0:T(8,128)(2,1)S(1)} %get-tuple-element.67.refs_3_), channel_id=1, source_target_pairs={{0,24},{4,28},{8,16},{12,20},{16,8},{20,12},{24,0},{28,4},{1,25},{... | collective-permute-start | bytes 1572872 | tf_op jit(solution)/shard_map/ppermute | solution.py:32
  7.7 3.8 %collective-permute-start.10 = (bf16[272,128]{1,0:T(8,128)(2,1)S(1)}, bf16[272,128]{1,0:T(8,128)(2,1)S(1)}, u32[]{:S(2)}, u32[]{:S(2)}) collective-permute-start(bf16[272,128]{1,0:T(8,128)(2,1)S(1)} %get-tuple-element.68.refs_15_), channel_id=1, source_target_pairs={{0,1},{1,0},{2,3},{3,2},{4,5},{5,4},{6,7},{7,6},{8,9},{9,8},{10,11... | collective-permute-start | bytes 208904 | tf_op jit(solution)/shard_map/ppermute | solution.py:32
  9.2 5.5 %collective-permute-start.11 = (bf16[272,128]{1,0:T(8,128)(2,1)S(1)}, bf16[272,128]{1,0:T(8,128)(2,1)S(1)}, u32[]{:S(2)}, u32[]{:S(2)}) collective-permute-start(bf16[272,128]{1,0:T(8,128)(2,1)S(1)} %get-tuple-element.68.refs_15_), channel_id=1, source_target_pairs={{0,2},{1,3},{2,0},{3,1},{4,6},{5,7},{6,4},{7,5},{8,10},{9,11},{10,... | collective-permute-start | bytes 208904 | tf_op jit(solution)/shard_map/ppermute | solution.py:32
  11.5 6.9 %collective-permute-start.12 = (bf16[272,128]{1,0:T(8,128)(2,1)S(1)}, bf16[272,128]{1,0:T(8,128)(2,1)S(1)}, u32[]{:S(2)}, u32[]{:S(2)}) collective-permute-start(bf16[272,128]{1,0:T(8,128)(2,1)S(1)} %get-tuple-element.68.refs_15_), channel_id=1, source_target_pairs={{0,3},{1,2},{2,1},{3,0},{4,7},{5,6},{6,5},{7,4},{8,11},{9,10},{10,... | collective-permute-start | bytes 208904 | tf_op jit(solution)/shard_map/ppermute | solution.py:32
  14.7 4.6 %collective-permute-start.13 = (bf16[272,128]{1,0:T(8,128)(2,1)S(1)}, bf16[272,128]{1,0:T(8,128)(2,1)S(1)}, u32[]{:S(2)}, u32[]{:S(2)}) collective-permute-start(bf16[272,128]{1,0:T(8,128)(2,1)S(1)} %get-tuple-element.68.refs_15_), channel_id=1, source_target_pairs={{0,4},{4,0},{8,12},{12,8},{16,20},{20,16},{24,28},{28,24},{1,5},{5... | collective-permute-start | bytes 208904 | tf_op jit(solution)/shard_map/ppermute | solution.py:32
  18.4 6.7 %collective-permute-start.7 = (bf16[1,1024,128]{2,1,0:T(8,128)(2,1)}, bf16[1,1024,128]{2,1,0:T(8,128)(2,1)S(1)}, u32[]{:S(2)}, u32[]{:S(2)}) collective-permute-start(bf16[1,1024,128]{2,1,0:T(8,128)(2,1)} %bitcast.31), channel_id=1, source_target_pairs={{0,1},{1,0},{2,3},{3,2},{4,5},{5,4},{6,7},{7,6},{8,9},{9,8},{10,11... | collective-permute-start | bytes 786440 | tf_op jit(solution)/shard_map/ppermute | solution.py:32
  19.3 2.4 %collective-permute-start.14 = (bf16[272,128]{1,0:T(8,128)(2,1)S(1)}, bf16[272,128]{1,0:T(8,128)(2,1)S(1)}, u32[]{:S(2)}, u32[]{:S(2)}) collective-permute-start(bf16[272,128]{1,0:T(8,128)(2,1)S(1)} %collective-permute-done.10.refs_16_), channel_id=1, source_target_pairs={{0,4},{4,0},{8,12},{12,8},{16,20},{20,16},{24,28},{28,24},{1,5},{5... | collective-permute-start | bytes 208904 | tf_op jit(solution)/shard_map/ppermute | solution.py:32
  24.2 25.2 %collective-permute-start = (bf16[8,64,512]{2,1,0:T(8,128)(2,1)S(1)}, bf16[8,64,512]{2,1,0:T(8,128)(2,1)}, u32[]{:S(2)}, u32[]{:S(2)}) collective-permute-start(bf16[8,64,512]{2,1,0:T(8,128)(2,1)S(1)} %get-tuple-element.67.refs_3_), channel_id=1, source_target_pairs={{0,4},{4,0},{8,12},{12,8},{16,20},{20,16},{24,28},{28,24},{1,5},{5... | collective-permute-start | bytes 1572872 | tf_op jit(solution)/shard_map/ppermute | solution.py:32
  25.2 14.9 %collective-permute-start.8 = (bf16[1,1024,128]{2,1,0:T(8,128)(2,1)}, bf16[1,1024,128]{2,1,0:T(8,128)(2,1)S(1)}, u32[]{:S(2)}, u32[]{:S(2)}) collective-permute-start(bf16[1,1024,128]{2,1,0:T(8,128)(2,1)} %bitcast.32), channel_id=1, source_target_pairs={{0,2},{1,3},{2,0},{3,1},{4,6},{5,7},{6,4},{7,5},{8,10},{9,11},{10,... | collective-permute-start | bytes 786440 | tf_op jit(solution)/shard_map/ppermute | solution.py:32
  27.5 21.9 %collective-permute-start.2 = (bf16[8,64,512]{2,1,0:T(8,128)(2,1)S(1)}, bf16[8,64,512]{2,1,0:T(8,128)(2,1)}, u32[]{:S(2)}, u32[]{:S(2)}) collective-permute-start(bf16[8,64,512]{2,1,0:T(8,128)(2,1)S(1)} %collective-permute-done.1.refs_5_), channel_id=1, source_target_pairs={{0,4},{4,0},{8,12},{12,8},{16,20},{20,16},{24,28},{28,24},{1,5},{5... | collective-permute-start | bytes 1572872 | tf_op jit(solution)/shard_map/ppermute | solution.py:32
  28.7 20.8 %collective-permute-start.4 = (bf16[8,64,512]{2,1,0:T(8,128)(2,1)S(1)}, bf16[8,64,512]{2,1,0:T(8,128)(2,1)}, u32[]{:S(2)}, u32[]{:S(2)}) collective-permute-start(bf16[8,64,512]{2,1,0:T(8,128)(2,1)S(1)} %collective-permute-done.3.refs_7_), channel_id=1, source_target_pairs={{0,4},{4,0},{8,12},{12,8},{16,20},{20,16},{24,28},{28,24},{1,5},{5... | collective-permute-start | bytes 1572872 | tf_op jit(solution)/shard_map/ppermute | solution.py:32
  32.0 17.4 %collective-permute-start.6 = (bf16[8,64,512]{2,1,0:T(8,128)(2,1)}, bf16[8,64,512]{2,1,0:T(8,128)(2,1)}, u32[]{:S(2)}, u32[]{:S(2)}) collective-permute-start(bf16[8,64,512]{2,1,0:T(8,128)(2,1)} %collective-permute-done.5.refs_9_), channel_id=1, source_target_pairs={{0,4},{4,0},{8,12},{12,8},{16,20},{20,16},{24,28},{28,24},{1,5},{5... | collective-permute-start | bytes 1572872 | tf_op jit(solution)/shard_map/ppermute | solution.py:32
  40.0 9.4 %collective-permute-start.9 = (bf16[1,1024,128]{2,1,0:T(8,128)(2,1)}, bf16[1,1024,128]{2,1,0:T(8,128)(2,1)S(1)}, u32[]{:S(2)}, u32[]{:S(2)}) collective-permute-start(bf16[1,1024,128]{2,1,0:T(8,128)(2,1)} %bitcast.33), channel_id=1, source_target_pairs={{0,3},{1,2},{2,1},{3,0},{4,7},{5,6},{6,5},{7,4},{8,11},{9,10},{10,... | collective-permute-start | bytes 786440 | tf_op jit(solution)/shard_map/ppermute | solution.py:32
  60.3 5.0 %collective-permute-start.17 = (f32[8,512]{1,0:T(8,128)S(1)}, f32[8,512]{1,0:T(8,128)S(1)}, u32[]{:S(2)}, u32[]{:S(2)}) collective-permute-start(f32[8,512]{1,0:T(8,128)S(1)} %get-tuple-element.69.refs_0_), channel_id=1, source_target_pairs={{0,1},{1,0},{2,3},{3,2},{4,5},{5,4},{6,7},{7,6},{8,9},{9,8},{10,11... | collective-permute-start | bytes 49160 | tf_op jit(solution)/shard_map/ppermute | solution.py:32
  61.7 3.7 %collective-permute-start.18 = (f32[8,512]{1,0:T(8,128)S(1)}, f32[8,512]{1,0:T(8,128)S(1)}, u32[]{:S(2)}, u32[]{:S(2)}) collective-permute-start(f32[8,512]{1,0:T(8,128)S(1)} %get-tuple-element.69.refs_0_), channel_id=1, source_target_pairs={{0,2},{1,3},{2,0},{3,1},{4,6},{5,7},{6,4},{7,5},{8,10},{9,11},{10,... | collective-permute-start | bytes 49160 | tf_op jit(solution)/shard_map/ppermute | solution.py:32
  63.6 4.4 %collective-permute-start.19 = (f32[8,512]{1,0:T(8,128)S(1)}, f32[8,512]{1,0:T(8,128)S(1)}, u32[]{:S(2)}, u32[]{:S(2)}) collective-permute-start(f32[8,512]{1,0:T(8,128)S(1)} %get-tuple-element.69.refs_0_), channel_id=1, source_target_pairs={{0,3},{1,2},{2,1},{3,0},{4,7},{5,6},{6,5},{7,4},{8,11},{9,10},{10,... | collective-permute-start | bytes 49160 | tf_op jit(solution)/shard_map/ppermute | solution.py:32
  70.0 4.5 %collective-permute-start.27 = (bf16[2336,128]{1,0:T(8,128)(2,1)S(1)}, bf16[2336,128]{1,0:T(8,128)(2,1)S(1)}, u32[]{:S(2)}, u32[]{:S(2)}) collective-permute-start(bf16[2336,128]{1,0:T(8,128)(2,1)S(1)} %get-tuple-element.95), channel_id=1, source_target_pairs={{0,4},{4,0},{8,12},{12,8},{16,20},{20,16},{24,28},{28,24},{1,5},{5... | collective-permute-start | bytes 1794056 | tf_op jit(solution)/shard_map/ppermute | solution.py:32
  74.7 8.4 %collective-permute-start.28 = (bf16[1168,128]{1,0:T(8,128)(2,1)S(1)}, bf16[1168,128]{1,0:T(8,128)(2,1)S(1)}, u32[]{:S(2)}, u32[]{:S(2)}) collective-permute-start(bf16[1168,128]{1,0:T(8,128)(2,1)S(1)} %get-tuple-element.110), channel_id=1, source_target_pairs={{0,8},{4,12},{8,0},{12,4},{16,24},{20,28},{24,16},{28,20},{1,9},{5... | collective-permute-start | bytes 897032 | tf_op jit(solution)/shard_map/ppermute | solution.py:32
  75.4 8.0 %collective-permute-start.30 = (bf16[1168,128]{1,0:T(8,128)(2,1)S(1)}, bf16[1168,128]{1,0:T(8,128)(2,1)S(1)}, u32[]{:S(2)}, u32[]{:S(2)}) collective-permute-start(bf16[1168,128]{1,0:T(8,128)(2,1)S(1)} %get-tuple-element.109), channel_id=1, source_target_pairs={{0,16},{4,20},{8,24},{12,28},{16,0},{20,4},{24,8},{28,12},{1,17},{... | collective-permute-start | bytes 897032 | tf_op jit(solution)/shard_map/ppermute | solution.py:32
  83.6 7.1 %collective-permute-start.31 = (bf16[1168,128]{1,0:T(8,128)(2,1)S(1)}, bf16[1168,128]{1,0:T(8,128)(2,1)S(1)}, u32[]{:S(2)}, u32[]{:S(2)}) collective-permute-start(bf16[1168,128]{1,0:T(8,128)(2,1)S(1)} %get-tuple-element.107), channel_id=1, source_target_pairs={{0,8},{4,12},{8,0},{12,4},{16,24},{20,28},{24,16},{28,20},{1,9},{5... | collective-permute-start | bytes 897032 | tf_op jit(solution)/shard_map/ppermute | solution.py:32
  84.5 8.8 %collective-permute-start.29 = (bf16[1168,128]{1,0:T(8,128)(2,1)S(1)}, bf16[1168,128]{1,0:T(8,128)(2,1)S(1)}, u32[]{:S(2)}, u32[]{:S(2)}) collective-permute-start(bf16[1168,128]{1,0:T(8,128)(2,1)S(1)} %get-tuple-element.108), channel_id=1, source_target_pairs={{0,16},{4,20},{8,24},{12,28},{16,0},{20,4},{24,8},{28,12},{1,17},{... | collective-permute-start | bytes 897032 | tf_op jit(solution)/shard_map/ppermute | solution.py:32
  90.8 20.9 %collective-permute-start.33 = (bf16[1168,128]{1,0:T(8,128)(2,1)S(1)}, bf16[1168,128]{1,0:T(8,128)(2,1)S(1)}, u32[]{:S(2)}, u32[]{:S(2)}) collective-permute-start(bf16[1168,128]{1,0:T(8,128)(2,1)S(1)} %add_convert_fusion.1.mine_b), channel_id=1, source_target_pairs={{0,4},{4,0},{8,12},{12,8},{16,20},{20,16},{24,28},{28,24},{1,5},{5... | collective-permute-start | bytes 897032 | tf_op jit(solution)/shard_map/ppermute | solution.py:32
  93.4 18.3 %collective-permute-start.32 = (bf16[1168,128]{1,0:T(8,128)(2,1)S(1)}, bf16[1168,128]{1,0:T(8,128)(2,1)S(1)}, u32[]{:S(2)}, u32[]{:S(2)}) collective-permute-start(bf16[1168,128]{1,0:T(8,128)(2,1)S(1)} %add_convert_fusion.3.mine_a), channel_id=1, source_target_pairs={{0,4},{4,0},{8,12},{12,8},{16,20},{20,16},{24,28},{28,24},{1,5},{5... | collective-permute-start | bytes 897032 | tf_op jit(solution)/shard_map/ppermute | solution.py:32
  96.3 4.1 %collective-permute-start.21 = (f32[40,512]{1,0:T(8,128)S(1)}, f32[40,512]{1,0:T(8,128)S(1)}, u32[]{:S(2)}, u32[]{:S(2)}) collective-permute-start(f32[40,512]{1,0:T(8,128)S(1)} %mapping_back.1.refs_0_), channel_id=1, source_target_pairs={{0,8},{4,12},{8,0},{12,4},{16,24},{20,28},{24,16},{28,20},{1,9},{5... | collective-permute-start | bytes 245768 | tf_op jit(solution)/shard_map/ppermute | solution.py:32
  97.0 4.2 %collective-permute-start.23 = (f32[40,512]{1,0:T(8,128)S(1)}, f32[40,512]{1,0:T(8,128)S(1)}, u32[]{:S(2)}, u32[]{:S(2)}) collective-permute-start(f32[40,512]{1,0:T(8,128)S(1)} %mapping_back.1.refs_0_), channel_id=1, source_target_pairs={{0,16},{4,20},{8,24},{12,28},{16,0},{20,4},{24,8},{28,12},{1,17},{... | collective-permute-start | bytes 245768 | tf_op jit(solution)/shard_map/ppermute | solution.py:32
  98.2 4.4 %collective-permute-start.25 = (f32[40,512]{1,0:T(8,128)S(1)}, f32[40,512]{1,0:T(8,128)S(1)}, u32[]{:S(2)}, u32[]{:S(2)}) collective-permute-start(f32[40,512]{1,0:T(8,128)S(1)} %mapping_back.1.refs_0_), channel_id=1, source_target_pairs={{0,24},{4,28},{8,16},{12,20},{16,8},{20,12},{24,0},{28,4},{1,25},{... | collective-permute-start | bytes 245768 | tf_op jit(solution)/shard_map/ppermute | solution.py:32
  100.4 3.8 %collective-permute-start.20 = (f32[40,512]{1,0:T(8,128)S(1)}, f32[40,512]{1,0:T(8,128)S(1)}, u32[]{:S(2)}, u32[]{:S(2)}) collective-permute-start(f32[40,512]{1,0:T(8,128)S(1)} %mapping_back.1.refs_0_), channel_id=1, source_target_pairs={{0,4},{4,0},{8,12},{12,8},{16,20},{20,16},{24,28},{28,24},{1,5},{5... | collective-permute-start | bytes 245768 | tf_op jit(solution)/shard_map/ppermute | solution.py:32
  101.2 3.0 %collective-permute-start.22 = (f32[40,512]{1,0:T(8,128)S(1)}, f32[40,512]{1,0:T(8,128)S(1)}, u32[]{:S(2)}, u32[]{:S(2)}) collective-permute-start(f32[40,512]{1,0:T(8,128)S(1)} %collective-permute-done.21.refs_2_), channel_id=1, source_target_pairs={{0,4},{4,0},{8,12},{12,8},{16,20},{20,16},{24,28},{28,24},{1,5},{5... | collective-permute-start | bytes 245768 | tf_op jit(solution)/shard_map/ppermute | solution.py:32
  102.7 2.4 %collective-permute-start.24 = (f32[40,512]{1,0:T(8,128)S(1)}, f32[40,512]{1,0:T(8,128)S(1)}, u32[]{:S(2)}, u32[]{:S(2)}) collective-permute-start(f32[40,512]{1,0:T(8,128)S(1)} %collective-permute-done.23.refs_4_), channel_id=1, source_target_pairs={{0,4},{4,0},{8,12},{12,8},{16,20},{20,16},{24,28},{28,24},{1,5},{5... | collective-permute-start | bytes 245768 | tf_op jit(solution)/shard_map/ppermute | solution.py:32
  104.2 1.3 %collective-permute-start.26 = (f32[40,512]{1,0:T(8,128)S(1)}, f32[40,512]{1,0:T(8,128)S(1)}, u32[]{:S(2)}, u32[]{:S(2)}) collective-permute-start(f32[40,512]{1,0:T(8,128)S(1)} %collective-permute-done.25.refs_6_), channel_id=1, source_target_pairs={{0,4},{4,0},{8,12},{12,8},{16,20},{20,16},{24,28},{28,24},{1,5},{5... | collective-permute-start | bytes 245768 | tf_op jit(solution)/shard_map/ppermute | solution.py:32
  (33 other events, 637.2 us)

commit v2 on v1

v2 whole, which is shorter than its diff:
```python
import functools

import jax
import jax.numpy as jnp
from jax import lax
from jax.experimental import pallas as pl
from jax.experimental.pallas import tpu as pltpu
from jax.sharding import PartitionSpec as P

MOMENTUM = 0.9
EMA_DECAY = 0.95
AVERAGE_BETA = 0.5
BF16 = jnp.bfloat16
F32 = jnp.float32
TAPS = 9
LANES = 128
COUNT_ROWS = 32
VMEM = pl.BlockSpec(memory_space=pltpu.VMEM)
SMEM = pl.BlockSpec(memory_space=pltpu.SMEM)
ANY = pl.BlockSpec(memory_space=pl.ANY)


def shape(dims, dtype):
    return jax.ShapeDtypeStruct(dims, dtype)


def params(mib):
    return pltpu.CompilerParams(vmem_limit_bytes=mib * 1024 * 1024)


def cost(micros):
    return pl.CostEstimate(flops=0, bytes_accessed=int(micros * 3.5e6), transcendentals=0)


def hbm(*values):
    return [pltpu.with_memory_space_constraint(value, pltpu.HBM) for value in values]


def after(values, *others):
    return lax.optimization_barrier((values, others))[0]


def swap(value, axis, distance):
    return lax.ppermute(
        value, axis, [(i, i ^ distance) for i in range(lax.axis_size(axis))]
    )


def spread(value, axis):
    size = lax.axis_size(axis)
    beside = swap(value, axis, 1)
    if size != 8:
        parts = [(value, [(0, 0)]), (beside, [(1, 1)])]
        for k in range(2, size, 2):
            part = swap(value, axis, k)
            parts += [(part, [(k, k)]), (swap(part, axis, 1), [(k + 1, k + 1)])]
        return parts
    near = jnp.concatenate([value, beside])
    far = crossed(near, axis, 2, 4)
    corner = crossed(far, axis, 4, 2)
    return [
        (near, [(0, 0), (1, 1)]),
        (far, [(2, 4), (3, 5)]),
        (corner, [(6, 6), (7, 7)]),
        (swap(far, axis, 1), [(5, 3), (4, 2)]),
    ]


def spread_direct(value, axis):
    return [value] + [swap(value, axis, k) for k in range(1, lax.axis_size(axis))]


def crossed(value, axis, even_distance, odd_distance):
    size = lax.axis_size(axis)
    pairs = [(i, i ^ (odd_distance if i % 2 else even_distance)) for i in range(size)]
    return lax.ppermute(value, axis, pairs)


def spread_layers(value, axis, others):
    size, layers = lax.axis_size(axis), value.shape[0]
    beside = swap(value, axis, 1)
    if size != 8:
        far = [swap(value, axis, k) for k in range(2, size, 2)]
        parts = [(value, [(0, 0, 0)]), (beside, [(0, 1, 1)])]
        for k, part in zip(range(2, size, 2), far):
            parts.append((part, [(0, k, k)]))
            parts.append((swap(part, axis, 1), [(0, k + 1, k + 1)]))
        return parts
    far = crossed(jnp.concatenate([value, beside]), axis, 2, 4)
    half = layers // 2
    low, high = (crossed(far[at : at + half], axis, 4, 2) for at in (0, half))
    far_low = after(far, others[0])
    low, high = after([low, high], *others[1:])
    return [
        (value, [(0, 0, 0)]),
        (beside, [(0, 1, 1)]),
        (far, [(0, 2, 4), (0, 3, 5)]),
        (low, [(0, 6, 6)]),
        (high, [(half, 6, 6)]),
        (swap(far_low, axis, 1), [(0, 5, 3), (0, 4, 2)]),
        (swap(low, axis, 1), [(0, 7, 7)]),
        (swap(high, axis, 1), [(half, 7, 7)]),
    ]


def silu_slope(preact):
    sig = jax.nn.sigmoid(preact)
    return sig * (1.0 + preact * (1.0 - sig))


def pieces(value, count):
    out = []
    for _ in range(count):
        part = value.astype(BF16)
        out.append(part)
        value = value - part.astype(F32)
    return out


def advance(param, moment, average, grad, rate):
    moment_new = MOMENTUM * moment + grad
    param_new = param - rate * (grad + MOMENTUM * moment_new)
    average_new = EMA_DECAY * average + (1.0 - EMA_DECAY) * param_new
    return param_new, moment_new, average_new, param_new.astype(BF16)


def dot(a, b):
    return jnp.dot(a, b, preferred_element_type=F32)


def dot_nt(a, b):
    return lax.dot_general(a, b, (((1,), (1,)), ((), ())), preferred_element_type=F32)


def dot_tn(a, b):
    return lax.dot_general(a, b, (((0,), (0,)), ((), ())), preferred_element_type=F32)


def prepare_kernel(where, map_w, aff_w, bias, features, map_low, pack, stage, aff_stage, bias_stage, sems):
    layers = map_w.shape[0]
    half = aff_stage.shape[0]
    rows = features.shape[0]
    start = pl.multiple_of(lax.rem(where[0], 2) * half, half)
    copies = [
        pltpu.make_async_copy(map_w.at[layer], stage.at[layer], sems.at[layer])
        for layer in range(layers)
    ]
    aff_copy = pltpu.make_async_copy(aff_w.at[0, pl.ds(start, half), :], aff_stage, sems.at[layers])
    bias_copy = pltpu.make_async_copy(bias, bias_stage, sems.at[layers + 1])
    feat_copy = pltpu.make_async_copy(features, pack.at[pl.ds(0, rows), :], sems.at[layers + 2])
    for copy in copies + [aff_copy, bias_copy, feat_copy]:
        copy.start()
    for layer in range(layers):
        copies[layer].wait()
        map_low[layer] = stage[layer].astype(BF16)
    aff_copy.wait()
    pack[pl.ds(rows, half), :] = aff_stage[...].astype(BF16)
    bias_copy.wait()
    hi, mid, lo = pieces(bias_stage[0:1, :], 3)
    lines = jnp.concatenate(
        [hi.astype(F32), mid.astype(F32), lo.astype(F32), jnp.zeros((13, LANES), F32)], axis=0
    )
    pack[pl.ds(rows + half, 16), :] = lines.astype(BF16)
    feat_copy.wait()


def mapping_kernel(n_dp, samples, places, *refs):
    refs = list(refs)

    def take(count):
        got = refs[:count]
        del refs[:count]
        return got

    where, seeds, crossover = take(3)
    parts = take(len(places))
    z_table, map_b = take(2)
    pre_out, hid_out, top_out, picked_out, map_out = take(5)
    map_full, rows, sem_map, sem_z, sem_out = refs
    layers, share, width = parts[0].shape
    latents = 2 * samples
    dp = where[0]
    z_copies = []
    for n in range(latents):
        at = pl.multiple_of((seeds[n] // 8) * 8, 8)
        z_copies.append(pltpu.make_async_copy(z_table.at[pl.ds(at, 8), :], rows.at[n], sem_z.at[n]))
    map_copies = []
    odd = lax.rem(dp, 2)
    for part, place in zip(parts, places):
        depth = part.shape[0] // len(place)
        for i, (first, even_k, odd_k) in enumerate(place):
            k = jnp.where(odd == 1, odd_k, even_k)
            at = pl.multiple_of(lax.bitwise_xor(dp, k) * share, share)
            map_copies.append(
                pltpu.make_async_copy(
                    part.at[pl.ds(i * depth, depth)],
                    map_full.at[pl.ds(first, depth), pl.ds(at, share), :],
                    sem_map.at[len(map_copies)],
                )
            )
    for copy in z_copies + map_copies:
        copy.start()
    hidden_rows = []
    for n in range(latents):
        z_copies[n].wait()
        row = rows[n, pl.ds(lax.rem(seeds[n], 8), 1), :]
        scale = lax.rsqrt(jnp.mean(row * row, axis=1, keepdims=True) + 1e-08)
        hidden_rows.append(row * scale)
    hidden_rows.append(jnp.zeros((16 - latents, width), F32))
    hidden = jnp.concatenate(hidden_rows, axis=0)
    for copy in map_copies:
        copy.wait()
    keep_map = pltpu.make_async_copy(map_full, map_out, sem_out)
    keep_map.start()
    for layer in range(layers):
        low = hidden.astype(BF16)
        preact = dot(low, map_full[layer]) + map_b[pl.ds(layer, 1), :]
        hid_out[layer] = low.astype(F32)[0:8]
        pre_out[layer] = preact[0:8]
        hidden = preact * jax.nn.sigmoid(preact)
    top_out[...] = hidden[0:8]
    low = hidden.astype(BF16).astype(F32)
    for j in range(2):
        chosen = []
        for s in range(samples):
            first = crossover[s] > j
            chosen.append(
                jnp.where(first, low[2 * s : 2 * s + 1, :], low[2 * s + 1 : 2 * s + 2, :])
            )
        chosen.append(jnp.zeros((8 - samples, width), F32))
        picked_out[j] = jnp.concatenate(chosen, axis=0)
    keep_map.wait()


def main_kernel(n_ch, samples, side, *refs):
    refs = list(refs)

    def take(count):
        got = refs[:count]
        del refs[:count]
        return got

    (where,) = take(1)
    packs = take(n_ch)[::-1]
    pair_packs = take(n_ch)
    (conv_w,) = take(1)
    aff_w, picked, bias, head, rgb_w = take(5)
    unit, to_sum, small, aff_out = take(4)
    (
        aff_full,
        bias_full,
        feat,
        feat_t,
        kernel_f,
        kernel,
        padded,
        taps,
        shifted,
        wide,
        sem_feat,
        sem_aff,
        sem_conv,
        sem_out,
    ) = refs
    width = aff_full.shape[0]
    pixels = side * side
    half = width // 2
    dp, ch = where[0], where[1]
    pair = lax.rem(dp, 2)
    mine = pl.ds(pl.multiple_of(pair * half, half), half)
    other = pl.ds(pl.multiple_of((1 - pair) * half, half), half)

    def arrivals(source, beside, k):
        lane = pl.ds(pl.multiple_of(lax.bitwise_xor(ch, k) * LANES, LANES), LANES)
        copies = [
            pltpu.make_async_copy(
                source.at[pl.ds(s * pixels, pixels), :], feat.at[s, :, lane], sem_feat.at[samples * k + s]
            )
            for s in range(samples)
        ]
        at = samples * pixels
        copies.append(
            pltpu.make_async_copy(
                source.at[pl.ds(at, half), :], aff_full.at[mine, lane], sem_aff.at[3 * k]
            )
        )
        copies.append(
            pltpu.make_async_copy(
                source.at[pl.ds(at + half, 16), :], bias_full.at[:, lane], sem_aff.at[3 * k + 1]
            )
        )
        copies.append(
            pltpu.make_async_copy(
                beside.at[pl.ds(at, half), :], aff_full.at[other, lane], sem_aff.at[3 * k + 2]
            )
        )
        return copies

    conv_copies = [
        pltpu.make_async_copy(conv_w.at[tap], kernel_f.at[tap], sem_conv.at[tap]) for tap in range(TAPS)
    ]
    copies = [copy for k in range(n_ch) for copy in arrivals(packs[k], pair_packs[k], k)]
    for copy in copies + conv_copies:
        copy.start()
    square = jnp.zeros((width, LANES), F32)
    for tap in range(TAPS):
        conv_copies[tap].wait()
        tap_low = kernel_f[tap].astype(BF16)
        kernel[tap // 3, :, pl.ds((tap % 3) * LANES, LANES)] = tap_low
        wide_tap = tap_low.astype(F32)
        square = square + wide_tap * wide_tap
    for copy in copies:
        copy.wait()
    keep_aff = pltpu.make_async_copy(aff_full, aff_out, sem_out)
    keep_aff.start()
    for s in range(samples):
        feat_t[s] = feat[s].T
    wide_bias = bias_full[...].astype(F32)
    bias_row = wide_bias[0:1] + wide_bias[1:2] + wide_bias[2:3]
    style0 = (dot(picked[0].astype(BF16), aff_full[...]) + bias_row).astype(BF16)
    colour_aff = aff_w[1].astype(BF16)
    style1 = dot(picked[1].astype(BF16), colour_aff) + bias[1:2, :]
    style0_wide = style0.astype(F32)
    style1 = style1.astype(BF16).astype(F32)
    colour_aff = colour_aff.astype(F32)
    colour = rgb_w[...].astype(BF16)
    colour_wide = colour.astype(F32)
    colour_rows = jnp.concatenate([colour_wide, jnp.zeros((13, LANES), F32)], axis=0).astype(BF16)
    head_rows = jnp.concatenate(
        [head[...].astype(F32), jnp.zeros((13, pixels), F32)], axis=0
    ).astype(BF16)
    conv_bias = bias[2:3, :]
    chunk = min(256, pixels)
    steps = pixels // chunk
    column = lax.rem(lax.broadcasted_iota(jnp.int32, (chunk, LANES), 0), side)
    not_first, not_last = column > 0, column < side - 1
    small[...] = jnp.zeros_like(small)
    to_sum[...] = jnp.zeros_like(to_sum)
    padded[pl.ds(0, side), :] = jnp.zeros((side, width), BF16)
    padded[pl.ds(side + pixels, side), :] = jnp.zeros((side, width), BF16)
    taps[pl.ds(0, 8), :] = jnp.zeros((8, 3 * LANES), F32)
    taps[pl.ds(8 + pixels, 8), :] = jnp.zeros((8, 3 * LANES), F32)
    wide[pl.ds(0, 8), :] = jnp.zeros((8, LANES), F32)
    wide[pl.ds(8 + pixels, 8), :] = jnp.zeros((8, LANES), F32)

    for s in range(samples):
        style_row = style0[s : s + 1, :]
        for r in range(steps):
            padded[pl.ds(side + r * chunk, chunk), :] = feat[s, pl.ds(r * chunk, chunk), :] * style_row
        style_col = jnp.broadcast_to(style0_wide[s : s + 1, :], (LANES, width)).T
        demod = lax.rsqrt(
            jnp.sum(style_col * style_col * square, axis=0, keepdims=True) + 1e-08
        )
        style_colour = style1[s : s + 1, :]
        for r in range(steps):
            total = dot(padded[pl.ds(r * chunk, chunk), :], kernel[0])
            total = total + dot(padded[pl.ds(side + r * chunk, chunk), :], kernel[1])
            total = total + dot(padded[pl.ds(2 * side + r * chunk, chunk), :], kernel[2])
            taps[pl.ds(8 + r * chunk, chunk), :] = total
        mixed = jnp.zeros((3, LANES), F32)
        g_style1 = jnp.zeros((1, LANES), F32)
        g_bias = jnp.zeros((1, LANES), F32)
        g_demod = jnp.zeros((1, LANES), F32)
        for r in range(steps):
            left = taps[pl.ds(7 + r * chunk, chunk), pl.ds(0, LANES)]
            centre = taps[pl.ds(8 + r * chunk, chunk), pl.ds(LANES, LANES)]
            right = taps[pl.ds(9 + r * chunk, chunk), pl.ds(2 * LANES, LANES)]
            conv_out = centre + jnp.where(not_first, left, 0.0) + jnp.where(not_last, right, 0.0)
            scaled = conv_out * demod + conv_bias
            sig = jax.nn.sigmoid(scaled)
            activated = scaled * sig
            act_mod = (activated * style_colour).astype(BF16)
            mixed = mixed + dot(head_rows[:, r * chunk : (r + 1) * chunk], act_mod)[0:3]
            g_act = dot_tn(head_rows[:, r * chunk : (r + 1) * chunk], colour_rows)
            g_style1 = g_style1 + jnp.sum(g_act * activated, axis=0, keepdims=True)
            g_scaled = g_act * style_colour * (sig * (1.0 + scaled * (1.0 - sig)))
            g_bias = g_bias + jnp.sum(g_scaled, axis=0, keepdims=True)
            g_demod = g_demod + jnp.sum(g_scaled * conv_out, axis=0, keepdims=True)
            wide[pl.ds(8 + r * chunk, chunk), :] = g_scaled * demod
        for r in range(steps):
            before = jnp.where(not_last, wide[pl.ds(9 + r * chunk, chunk), :], 0.0)
            centre = wide[pl.ds(8 + r * chunk, chunk), :]
            after = jnp.where(not_first, wide[pl.ds(7 + r * chunk, chunk), :], 0.0)
            for dx, value in enumerate((before, centre, after)):
                value = value.astype(BF16)
                for dy in range(3):
                    lane = pl.ds((3 * dy + dx) * LANES, LANES)
                    start = r * chunk + (dy - 1) * side
                    low_at, high_at = max(start, 0), min(start + chunk, pixels)
                    shifted[pl.ds(low_at, high_at - low_at), lane] = value[
                        low_at - start : high_at - start, :
                    ]
        for dx in range(3):
            shifted[pl.ds(pixels - side, side), pl.ds(dx * LANES, LANES)] = jnp.zeros(
                (side, LANES), BF16
            )
            shifted[pl.ds(0, side), pl.ds((6 + dx) * LANES, LANES)] = jnp.zeros(
                (side, LANES), BF16
            )
        factor = g_demod * demod * demod * demod
        g_style = jnp.zeros((width, LANES), F32)
        for first in range(0, TAPS, 2):
            count = min(2, TAPS - first)
            block = dot(feat_t[s], shifted[:, pl.ds(first * LANES, count * LANES)])
            for tap in range(first, first + count):
                raw = block[:, (tap - first) * LANES : (tap - first + 1) * LANES]
                weight = kernel[tap // 3, :, pl.ds((tap % 3) * LANES, LANES)].astype(F32)
                inner = raw - style_col * (weight * factor)
                g_style = g_style + weight * inner
                unit[s, pl.ds(tap * width, width), :] = (style_col * inner).astype(BF16)
        g_style_row = jnp.sum(g_style.T, axis=0, keepdims=True)
        g_colour_row = jnp.sum((colour_aff * g_style1).T, axis=0, keepdims=True)
        logit = jnp.sum(
            jnp.sum(mixed * colour_wide, axis=0, keepdims=True), axis=1, keepdims=True
        )
        to_sum[pl.ds(8 * s, 1), :] = jnp.broadcast_to(logit, (1, width))
        to_sum[pl.ds(8 * s + 1, 1), :] = g_style_row
        to_sum[pl.ds(8 * s + 2, 1), :] = g_colour_row
        small[pl.ds(8 * s, 1), :] = g_style1
        small[pl.ds(8 * s + 1, 1), :] = g_bias
        small[pl.ds(8 * s + 2, 3), :] = mixed
    keep_aff.wait()


def summed(parts, row):
    values = [part[pl.ds(row, 1), :] for part in parts]
    while len(values) > 1:
        values = [values[i] + values[i + 1] for i in range(0, len(values), 2)]
    return values[0]


def logit_grad(parts, counted, s):
    logit = summed(parts, 8 * s)
    mask = jnp.full(logit.shape, counted[s], jnp.int32).astype(F32)
    return -mask * jax.nn.sigmoid(-logit), mask * jax.nn.softplus(-logit), mask


def scale_kernel(n_ch, samples, where, counted, *refs):
    parts, (unit, kept, sent) = refs[:n_ch], refs[n_ch:]
    pair = lax.rem(where[0], 2)
    half = unit.shape[1] // 2
    grads, total = [], jnp.zeros((1, LANES), F32)
    for s in range(samples):
        grad, _, mask = logit_grad(parts, counted, s)
        grads.append(grad[:, :LANES])
        total = total + mask[:, :LANES]
    block = half // 9
    for out, owner in ((kept, pair), (sent, 1 - pair)):
        for b in range(9):
            at = pl.multiple_of(owner * half + b * block, block)
            value = grads[0] * unit[0, pl.ds(at, block), :].astype(F32)
            for s in range(1, samples):
                value = value + grads[s] * unit[s, pl.ds(at, block), :].astype(F32)
            out[pl.ds(b * block, block), :] = value.astype(BF16)
        out[pl.ds(half, COUNT_ROWS), :] = jnp.broadcast_to(total, (COUNT_ROWS, LANES)).astype(BF16)


def pack_places(samples, layers):
    latents = 2 * samples
    style = 2 * layers * latents + latents
    colour = style + 2 * samples
    w_total = colour + 2 * samples
    return style, colour, w_total, -(-(w_total + 3) // 16) * 16


def mapping_back_kernel(n_ch, samples, where, counted, crossover, *refs):
    parts = refs[:n_ch]
    pre, hid, top, picked, small, map_full, aff_full, pack_out, rows, pack = refs[n_ch:]
    layers, _, width = map_full.shape
    latents = 2 * samples
    style_at, colour_at, w_at, _ = pack_places(samples, layers)
    ch = where[1]
    grads = [logit_grad(parts, counted, s) for s in range(samples)]
    pack[...] = jnp.zeros_like(pack)

    def put(line, lane, size, value, count):
        for i, part in enumerate(pieces(value, count)):
            pack[pl.ds(line + i, 1), pl.ds(lane, size)] = part.astype(F32)

    style_rows = []
    half_lane = lax.broadcasted_iota(jnp.int32, (1, LANES), 1) < LANES // 2
    for s in range(samples):
        grad = grads[s][0]
        style_row = grad * summed(parts, 8 * s + 1)
        rows[pl.ds(s, 1), :] = style_row
        style_rows.append(style_row)
        own = rows[pl.ds(s, 1), pl.ds(pl.multiple_of(ch * LANES, LANES), LANES)]
        short = grad[:, :LANES]
        put(style_at + 2 * s, 0, LANES, own, 2)
        put(style_at + 2 * s, LANES, LANES, short * small[pl.ds(8 * s, 1), :], 2)
        put(style_at + 2 * s, 2 * LANES, LANES, short * small[pl.ds(8 * s + 1, 1), :], 2)
        loss_count = jnp.where(half_lane, grads[s][1][:, :LANES], grads[s][2][:, :LANES])
        put(style_at + 2 * s, 3 * LANES, LANES, loss_count, 2)
        for c in range(3):
            value = short * small[pl.ds(8 * s + 2 + c, 1), :]
            put(colour_at + 2 * s, c * LANES, LANES, value, 2)
        for j in range(2):
            line = 2 * layers * latents + 2 * s + j
            pack[pl.ds(line, 1), :] = picked[j, pl.ds(s, 1), :]
    w_total = top[pl.ds(0, 1), :]
    for n in range(1, latents):
        w_total = w_total + top[pl.ds(n, 1), :]
    put(w_at, 0, width, w_total, 3)

    def back(value, weights):
        hi, lo = pieces(value, 2)
        both = jnp.concatenate([hi.astype(F32), lo.astype(F32)], axis=0).astype(BF16)
        out = dot_nt(both, weights)
        return out[0:8] + out[8:16]

    pad = [jnp.zeros((8 - samples, width), F32)]
    from_conv = back(jnp.concatenate(style_rows + pad, axis=0), aff_full[...])
    g_rows = []
    for s in range(samples):
        conv_row = from_conv[s : s + 1, :]
        colour_row = grads[s][0] * summed(parts, 8 * s + 2)
        to_first = [jnp.full((1, width), crossover[s], jnp.int32) > j for j in range(2)]
        g_rows.append(
            jnp.where(to_first[0], conv_row, 0.0) + jnp.where(to_first[1], colour_row, 0.0)
        )
        g_rows.append(
            jnp.where(to_first[0], 0.0, conv_row) + jnp.where(to_first[1], 0.0, colour_row)
        )
    g_rows.append(jnp.zeros((8 - latents, width), F32))
    g_hidden = jnp.concatenate(g_rows, axis=0)
    for layer in reversed(range(layers)):
        g_pre = g_hidden * silu_slope(pre[layer])
        pack[pl.ds(layer * latents, latents), :] = g_pre[0:latents]
        pack[pl.ds((layers + layer) * latents, latents), :] = hid[layer][0:latents]
        if layer > 0:
            g_hidden = back(g_pre, map_full[layer])
    pack_out[...] = pack[...].astype(BF16)


def update_kernel(n_dp, samples, layers, places, where, *refs):
    packs, refs = refs[: len(places)], refs[len(places) :]
    (map_w, map_m, map_e, aff_w, aff_m, aff_e) = refs[:6]
    (map_b, map_bm, map_be, bias, bias_m, bias_e, rgb, rgb_m, rgb_e, w_avg) = refs[6:16]
    outs, scratch = refs[16:-7], refs[-7:]
    map_outs, aff_outs = outs[0:4], outs[4:8]
    map_b_outs, bias_outs, rgb_outs = outs[8:12], outs[12:16], outs[16:20]
    w_avg_out, loss_out, count_out = outs[20:23]
    g_pre, hid, picked, style, rgb_all, sums, w_sums = scratch
    latents = 2 * samples
    style_at, colour_at, w_at, lines = pack_places(samples, layers)
    every = n_dp * latents
    dp = where[0]
    step = pl.program_id(0)
    share = map_w.shape[1]
    width = map_w.shape[2]

    @pl.when(step == 0)
    def _():
        odd = lax.rem(dp, 2)
        for part, place in zip(packs, places):
            for index, (even_k, odd_k) in enumerate(place):
                owner = lax.bitwise_xor(dp, jnp.where(odd == 1, odd_k, even_k))
                got = part[pl.ds(index * lines, lines), :].astype(F32)
                for layer in range(layers):
                    for n in range(latents):
                        at = pl.ds(owner * latents + n, 1)
                        line = layer * latents + n
                        g_pre[layer, at, :] = got[line : line + 1]
                        line += layers * latents
                        hid[layer, at, :] = got[line : line + 1]
                for s in range(samples):
                    at = pl.ds(owner * samples + s, 1)
                    line = 2 * layers * latents + 2 * s
                    for j in range(2):
                        picked[j, at, :] = got[line + j : line + j + 1]
                    line = style_at + 2 * s
                    style[at, :] = got[line : line + 1] + got[line + 1 : line + 2]
                    line = colour_at + 2 * s
                    rgb_all[at, :] = got[line : line + 1] + got[line + 1 : line + 2]
                w_sums[pl.ds(owner, 1), :] = (
                    got[w_at : w_at + 1] + got[w_at + 1 : w_at + 2] + got[w_at + 2 : w_at + 3]
                )
        sums[pl.ds(0, 1), :] = jnp.sum(style[...], axis=0, keepdims=True)
        sums[pl.ds(1, 1), :] = jnp.sum(rgb_all[...], axis=0, keepdims=True)
        total = sums[pl.ds(0, 1), :]
        count = total[:, width - LANES // 2 : width - LANES // 2 + 1]
        inverse = 1.0 / count
        for layer in range(layers):
            grad = jnp.sum(g_pre[layer], axis=0, keepdims=True) * inverse
            row = pl.ds(layer, 1)
            new = advance(map_b[row, :], map_bm[row, :], map_be[row, :], grad, 30.0)
            for out, value in zip(map_b_outs[:3], new[:3]):
                out[row, :] = value
        map_b_outs[3][...] = map_b_outs[0][...].astype(BF16)
        colour = sums[pl.ds(1, 1), :]
        for c in range(3):
            row = pl.ds(c, 1)
            lane = slice(c * LANES, (c + 1) * LANES)
            new = advance(bias[row, :], bias_m[row, :], bias_e[row, :], total[:, lane] * inverse, 50.0)
            for out, value in zip(bias_outs[:3], new[:3]):
                out[row, :] = value
            new = advance(rgb[row, :], rgb_m[row, :], rgb_e[row, :], colour[:, lane] * inverse, 1.0)
            for out, value in zip(rgb_outs[:3], new[:3]):
                out[row, :] = value
        bias_outs[3][...] = bias_outs[0][...].astype(BF16)
        rgb_outs[3][...] = rgb_outs[0][...].astype(BF16)
        mean = jnp.sum(w_sums[...], axis=0, keepdims=True) * (1.0 / every)
        w_avg_out[...] = w_avg[...] + (1.0 - AVERAGE_BETA) * (mean - w_avg[...])
        loss_out[0] = jnp.sum(total[:, width - LANES : width - LANES + 1])
        count_out[0] = jnp.sum(count)

    count = sums[pl.ds(0, 1), pl.ds(width - LANES, LANES)][:, LANES // 2 : LANES // 2 + 1]
    inverse = 1.0 / count
    each = map_outs[0].shape[0]
    for index in range(each):
        layer = step * each + index
        own = pltpu.roll(hid[layer], lax.rem(width - dp * share, width), 1)[:, :LANES]
        grad = dot_tn(own.astype(BF16), g_pre[layer].astype(BF16))[0:share] * inverse
        new = advance(map_w[layer], map_m[layer], map_e[layer], grad, 30.0)
        for out, value in zip(map_outs, new):
            out[index] = value
    chosen = jnp.concatenate([picked[step]] * 2, axis=0)
    grad_style = style[:, pl.ds(pl.multiple_of(step * LANES, LANES), LANES)]
    split = jnp.concatenate([p.astype(F32) for p in pieces(grad_style, 2)], axis=0)
    grad = dot_tn(chosen.astype(BF16), split.astype(BF16)) * inverse
    here = pl.ds(pl.multiple_of(step * width, width), width)
    new = advance(aff_w[here, :], aff_m[here, :], aff_e[here, :], grad, 30.0)
    for out, value in zip(aff_outs, new):
        out[...] = value


def conv_kernel(mine, where, grad, param, moment, average, *refs):
    refs = refs if mine else refs[4:]
    outs, buffers, sems = refs[0:4], refs[4:8], refs[8]
    half = grad.shape[0] - COUNT_ROWS
    pair = lax.rem(where[0], 2)
    start = pl.multiple_of((pair if mine else 1 - pair) * half, half)
    inverse = 1.0 / grad[pl.ds(half, 16), :].astype(F32)[0:1]
    chunks = sems.shape[0]
    depth = half // chunks
    copies = []
    for c in range(chunks):
        here = pl.ds(c * depth, depth)
        there = pl.ds(pl.multiple_of(start + c * depth, depth), depth)
        value = grad[here, :].astype(F32) * inverse
        new = advance(param[there, :], moment[there, :], average[there, :], value, 5.0)
        for k in range(4):
            buffers[k][here, :] = new[k]
            copy = pltpu.make_async_copy(buffers[k].at[here, :], outs[k].at[there, :], sems.at[c, k])
            copy.start()
            copies.append(copy)
    for copy in copies:
        copy.wait()


def local(
    features,
    z_table,
    seeds,
    crossover,
    counted,
    head,
    w_avg,
    map_w,
    map_w_mom,
    map_w_ema,
    map_b,
    map_b_mom,
    map_b_ema,
    aff_w,
    aff_w_mom,
    aff_w_ema,
    chan_bias,
    chan_bias_mom,
    chan_bias_ema,
    conv_w,
    conv_w_mom,
    conv_w_ema,
    rgb_w,
    rgb_w_mom,
    rgb_w_ema,
):
    samples, side = features.shape[0], features.shape[1]
    pixels = side * side
    layers, share, width = map_w.shape
    n_dp, n_ch = lax.axis_size("dp"), lax.axis_size("chan")
    latents = 2 * samples
    where = jnp.stack([lax.axis_index("dp"), lax.axis_index("chan")]).astype(jnp.int32)
    flat = lambda a: a.reshape(TAPS * width, LANES)

    half = width // 2
    pack_rows = samples * pixels + half + 16
    map_low, pack = pl.pallas_call(
        prepare_kernel,
        out_shape=(shape(map_w.shape, BF16), shape((pack_rows, LANES), BF16)),
        in_specs=[SMEM] + [ANY] * 4,
        out_specs=(VMEM, VMEM),
        scratch_shapes=[
            pltpu.VMEM(map_w.shape, F32),
            pltpu.VMEM((half, LANES), F32),
            pltpu.VMEM(chan_bias.shape, F32),
            pltpu.SemaphoreType.DMA((layers + 3,)),
        ],
        compiler_params=params(8),
        name="prepare",
    )(where, *hbm(map_w, aff_w, chan_bias, features.reshape(samples * pixels, LANES)))
    packs = spread_direct(pack, "chan")
    blocks = spread_layers(map_low, "dp", packs[1:])
    places = [place for _, place in blocks]

    pre, hid, top, picked, map_full = pl.pallas_call(
        functools.partial(mapping_kernel, n_dp, samples, places),
        out_shape=(
            shape((layers, 8, width), F32),
            shape((layers, 8, width), F32),
            shape((8, width), F32),
            shape((2, 8, width), F32),
            shape((layers, width, width), BF16),
        ),
        in_specs=[SMEM] * 3 + [ANY] * (len(blocks) + 1) + [VMEM],
        out_specs=(VMEM,) * 4 + (ANY,),
        scratch_shapes=[
            pltpu.VMEM((layers, width, width), BF16),
            pltpu.VMEM((latents, 8, width), F32),
            pltpu.SemaphoreType.DMA((sum(len(place) for place in places),)),
            pltpu.SemaphoreType.DMA((latents,)),
            pltpu.SemaphoreType.DMA,
        ],
        compiler_params=params(12),
        cost_estimate=cost(1),
        name="mapping",
    )(where, seeds.reshape(-1), crossover, *[block for block, _ in blocks], *hbm(z_table), map_b)

    pack_pair = [swap(part, "dp", 1) for part in packs]
    unit, to_sum, small, aff_full = pl.pallas_call(
        functools.partial(main_kernel, n_ch, samples, side),
        out_shape=(
            shape((samples, TAPS * width, LANES), BF16),
            shape((8 * samples, width), F32),
            shape((8 * samples, LANES), F32),
            shape((width, width), BF16),
        ),
        in_specs=[SMEM] + [ANY] * (2 * n_ch + 1) + [VMEM] * 5,
        out_specs=(VMEM,) * 3 + (ANY,),
        scratch_shapes=[
            pltpu.VMEM((width, width), BF16),
            pltpu.VMEM((16, width), BF16),
            pltpu.VMEM((samples, pixels, width), BF16),
            pltpu.VMEM((samples, width, pixels), BF16),
            pltpu.VMEM((TAPS, width, LANES), F32),
            pltpu.VMEM((3, width, 3 * LANES), BF16),
            pltpu.VMEM((pixels + 2 * side, width), BF16),
            pltpu.VMEM((pixels + 16, 3 * LANES), F32),
            pltpu.VMEM((pixels, TAPS * LANES), BF16),
            pltpu.VMEM((pixels + 16, LANES), F32),
            pltpu.SemaphoreType.DMA((samples * n_ch,)),
            pltpu.SemaphoreType.DMA((3 * n_ch,)),
            pltpu.SemaphoreType.DMA((TAPS,)),
            pltpu.SemaphoreType.DMA,
        ],
        compiler_params=params(28),
        cost_estimate=cost(8),
        name="main",
    )(
        where,
        *packs[::-1],
        *pack_pair,
        *hbm(conv_w.reshape(TAPS, width, LANES)),
        aff_w,
        picked,
        chan_bias,
        head,
        rgb_w,
    )

    sum_parts = spread_direct(to_sum, "chan")
    half_rows = TAPS * width // 2 + COUNT_ROWS
    kept, sent = pl.pallas_call(
        functools.partial(scale_kernel, n_ch, samples),
        out_shape=(shape((half_rows, LANES), BF16),) * 2,
        in_specs=[SMEM] * 2 + [VMEM] * (n_ch + 1),
        out_specs=(VMEM, VMEM),
        compiler_params=params(8),
        cost_estimate=cost(1),
        name="scale",
    )(where, counted, *sum_parts, unit)

    lines = pack_places(samples, layers)[-1]
    pack = pl.pallas_call(
        functools.partial(mapping_back_kernel, n_ch, samples),
        out_shape=shape((lines, width), BF16),
        in_specs=[SMEM] * 3 + [VMEM] * (n_ch + 7),
        out_specs=VMEM,
        scratch_shapes=[pltpu.VMEM((8, width), F32), pltpu.VMEM((lines, width), F32)],
        compiler_params=params(12),
        cost_estimate=cost(2),
        name="mapping_back",
    )(where, counted, crossover, *sum_parts, pre, hid, top, picked, small, map_full, aff_full)
    spread_pack = spread(pack, "dp")
    packs = [part for part, _ in spread_pack]

    whole = lambda a: pl.BlockSpec(a.shape, lambda i: (0,) * len(a.shape))
    map_spec = pl.BlockSpec((layers // 2, share, width), lambda i: (i, 0, 0))
    aff_spec = pl.BlockSpec((width, LANES), lambda i: (i, 0))
    flat_aff = [a.reshape(2 * width, LANES) for a in (aff_w, aff_w_mom, aff_w_ema)]
    tiny = [
        map_b,
        map_b_mom,
        map_b_ema,
        chan_bias,
        chan_bias_mom,
        chan_bias_ema,
        rgb_w,
        rgb_w_mom,
        rgb_w_ema,
        w_avg.reshape(1, width),
    ]
    types = (F32, F32, F32, BF16)
    out_shape = (
        [shape(map_w.shape, t) for t in types]
        + [shape((2 * width, LANES), t) for t in types]
        + [shape(map_b.shape, t) for t in types]
        + [shape(chan_bias.shape, t) for t in types]
        + [shape(rgb_w.shape, t) for t in types]
        + [shape((1, width), F32), shape((1,), F32), shape((1,), F32)]
    )
    every = n_dp * latents
    update = lambda: pl.pallas_call(
        functools.partial(update_kernel, n_dp, samples, layers, [p for _, p in spread_pack]),
        grid=(2,),
        out_shape=out_shape,
        in_specs=[SMEM]
        + [VMEM] * len(packs)
        + [VMEM] * (6 + len(tiny)),
        out_specs=[map_spec] * 4
        + [aff_spec] * 4
        + [whole(s) for s in out_shape[8:21]]
        + [SMEM, SMEM],
        scratch_shapes=[
            pltpu.VMEM((layers, every, width), F32),
            pltpu.VMEM((layers, every, width), F32),
            pltpu.VMEM((2, n_dp * samples, width), F32),
            pltpu.VMEM((n_dp * samples, width), F32),
            pltpu.VMEM((n_dp * samples, width), F32),
            pltpu.VMEM((8, width), F32),
            pltpu.VMEM((n_dp, width), F32),
        ],
        compiler_params=params(20),
        cost_estimate=cost(5),
        name="update",
    )(where, *packs, map_w, map_w_mom, map_w_ema, *flat_aff, *tiny)

    got = after(swap(sent, "dp", 1), pack)
    total = (kept.astype(F32) + got.astype(F32)).astype(BF16)
    bits = [1 << b for b in range(1, n_dp.bit_length() - 1)]
    for turn, (even_bit, odd_bit) in enumerate(zip(bits, bits[::-1])):
        got = crossed(total, "dp", even_bit, odd_bit)
        if turn == len(bits) - 2:
            got = after(got, packs[1])
        if turn == len(bits) - 1:
            outs = update()
            got = after(got, *outs)
        total = (total.astype(F32) + got.astype(F32)).astype(BF16)
    other = swap(total, "dp", 1)

    conv_params = [flat(conv_w), flat(conv_w_mom), flat(conv_w_ema)]
    half_rows = TAPS * width // 2

    def conv_half(grad, *earlier):
        return pl.pallas_call(
            functools.partial(conv_kernel, not earlier),
            out_shape=[shape((TAPS * width, LANES), t) for t in types],
            in_specs=[SMEM] + [VMEM] * 4 + [ANY] * len(earlier),
            out_specs=[ANY] * 4,
            scratch_shapes=[pltpu.VMEM((half_rows, LANES), t) for t in types]
            + [pltpu.SemaphoreType.DMA((3, 4))],
            input_output_aliases={5 + k: k for k in range(len(earlier))},
            compiler_params=params(12),
            cost_estimate=cost(2),
            name="conv_other" if earlier else "conv_own",
        )(where, grad, *conv_params, *earlier)

    conv_outs = conv_half(other, *conv_half(total))

    map_outs, aff_outs = outs[0:4], [a.reshape(aff_w.shape) for a in outs[4:8]]
    conv_outs = [a.reshape(conv_w.shape) for a in conv_outs]
    return (
        *map_outs,
        *outs[8:12],
        *aff_outs,
        *outs[12:16],
        *conv_outs,
        *outs[16:20],
        outs[20].reshape(width),
        outs[21].reshape(()),
        outs[22].reshape(()),
    )


def solution(mesh):
    in_specs = (
        P("dp", None, None, "chan"),
        P(),
        P("dp", None),
        P("dp"),
        P("dp"),
        P(),
        P(),
        P(None, "dp", None),
        P(None, "dp", None),
        P(None, "dp", None),
        P(),
        P(),
        P(),
        P(None, None, "chan"),
        P(None, None, "chan"),
        P(None, None, "chan"),
        P(None, "chan"),
        P(None, "chan"),
        P(None, "chan"),
        P(None, None, None, "chan"),
        P(None, None, None, "chan"),
        P(None, None, None, "chan"),
        P(None, "chan"),
        P(None, "chan"),
        P(None, "chan"),
    )
    out_specs = (
        P(None, "dp", None),
        P(None, "dp", None),
        P(None, "dp", None),
        P(None, "dp", None),
        P(),
        P(),
        P(),
        P(),
        P(None, None, "chan"),
        P(None, None, "chan"),
        P(None, None, "chan"),
        P(None, None, "chan"),
        P(None, "chan"),
        P(None, "chan"),
        P(None, "chan"),
        P(None, "chan"),
        P(None, None, None, "chan"),
        P(None, None, None, "chan"),
        P(None, None, None, "chan"),
        P(None, None, None, "chan"),
        P(None, "chan"),
        P(None, "chan"),
        P(None, "chan"),
        P(None, "chan"),
        P(),
        P(),
        P(),
    )
    return jax.shard_map(local, mesh=mesh, in_specs=in_specs, out_specs=out_specs, check_vma=False)
```

time: 118 us -> 95.6 us (0.81)
  starting transfers between devices: 44.4 us -> 29.3 us
  local copies, waits for them, and re-layouts: 6.05 us -> 0.16 us
  Pallas kernels: 25.7 us -> 24.4 us
    ppermute x34 -> x18, starting transfers between devices: 44.4 us -> 22.2 us  [swap(): lax.ppermute(value, axis, [(i, i ^ distance) for i in range(lax.axis_size...]
    ppermute x0 -> x7, waiting for transfers between devices: none -> 15 us  [crossed(): return lax.ppermute(value, axis, pairs)]
    ppermute x34 -> x18, waiting for transfers between devices: 38.1 us -> 23.5 us  [swap(): lax.ppermute(value, axis, [(i, i ^ distance) for i in range(lax.axis_size...]
    ppermute x0 -> x7, starting transfers between devices: none -> 7.11 us  [crossed(): return lax.ppermute(value, axis, pairs)]
    unnamed x63 -> x42, local copies, waits for them, and re-layouts: 5.25 us -> 0.13 us
    pallas_call x4 -> x6, Pallas kernels: 24.4 us -> 21.6 us  [the longest x1 6.75 us: local(): pl.pallas_call(functools.partial(main_kernel, n_ch, samples, side), out_s...]
    pallas_call x1, Pallas kernels: 0.61 us -> 2.05 us  [local(): pl.pallas_call(prepare_kernel, out_shape=(shape(map_w.shape, BF16), shape...]
  transfers between devices with their start and end apart: 34 -> 25, of which waited for: 15 -> 9; matrix products, arithmetic and copies ran while one was open for 2% -> 0% of each run, Pallas kernels for 7% -> 13%
where the time goes in v2:
time: 95.6 us; the launch traced here: 95.4 us
  waiting for transfers between devices  38.5 us (40%)
  starting transfers between devices  29.3 us (31%)
  Pallas kernels  24.4 us (26%)
  between operations  2.42 us (3%)
    ppermute x18, waiting for transfers between devices, swap(): lax.ppermute(value, axis, [(i, i ^ distance) for i in range(lax.axis_size...  23.5 us
    ppermute x18, starting transfers between devices, swap(): lax.ppermute(value, axis, [(i, i ^ distance) for i in range(lax.axis_size...  22.2 us
    ppermute x7, waiting for transfers between devices, crossed(): return lax.ppermute(value, axis, pairs)  15 us
    ppermute x7, starting transfers between devices, crossed(): return lax.ppermute(value, axis, pairs)  7.11 us
    pallas_call x1, Pallas kernels, local(): pl.pallas_call(functools.partial(main_kernel, n_ch, samples, side), out_s...  6.75 us
    pallas_call x2, Pallas kernels, conv_half(): pl.pallas_call(functools.partial(conv_kernel, not earlier), out_shape=[sh...  5.46 us
    pallas_call x1, Pallas kernels, local(): pl.pallas_call(functools.partial(update_kernel, n_dp, samples, layers, [p...  4.06 us
    pallas_call x1, Pallas kernels, local(): pl.pallas_call(functools.partial(mapping_kernel, n_dp, samples, places),...  3.21 us
  transfers between devices with their start and end apart: 25, of which 9 were waited for; matrix products, arithmetic and copies ran while one was open for 0% of the time, Pallas kernels for 13%

profile of v2, /device:TPU:1, one launch (start us, length us, event | category | flops | bytes accessed | tf_op | source)
XLA Modules:
  0.0 95.4 jit_solution(11644353730454233593)
XLA Ops:
  0.7 2.0 %prepare.1 = (bf16[8,64,512]{2,1,0:T(8,128)(2,1)S(1)}, bf16[1296,128]{1,0:T(8,128)(2,1)S(1)}) custom-call(s32[2]{0:T(128)S(1)} %pad_add_fusion.where.refs_0_, f32[8,64,512]{2,1,0:T(8,128)} %refs_4_.1, f32[2,512,128]{2,1,0:T(8,128)} %refs_10_.2, f32[3,128]{1,0:T(4,128)} %refs_13_.3, bf16[1024,128]{1,0:T(8,128)(2,1)} %bitcast.39), custom_call_target="tpu_custom_call" | custom-call | tf_op jit(solution)/shard_map/prepare/pallas_call | solution.py:688
  3.0 1.9 %collective-permute-done.7.refs_4_ = bf16[8,64,512]{2,1,0:T(8,128)(2,1)S(1)} collective-permute-done((bf16[8,64,512]{2,1,0:T(8,128)(2,1)S(1)}, bf16[8,64,512]{2,1,0:T(8,128)(2,1)S(1)}, u32[]{:S(2)}, u32[]{:S(2)}) %collective-permute-start.7) | collective-permute-done | bytes 524320 | tf_op jit(solution)/shard_map/ppermute | solution.py:44
  4.9 2.4 %collective-permute-start.8 = (bf16[16,64,512]{2,1,0:T(8,128)(2,1)S(1)}, bf16[16,64,512]{2,1,0:T(8,128)(2,1)S(1)}, u32[]{:S(2)}, u32[]{:S(2)}) collective-permute-start(bf16[16,64,512]{2,1,0:T(8,128)(2,1)S(1)} %pad_maximum_fusion), channel_id=1, source_target_pairs={{0,8},{4,20},{8,0},{12,28},{16,24},{20,4},{24,16},{28,12},{1,9},{5... | collective-permute-start | bytes 3145736 | tf_op jit(solution)/shard_map/ppermute | solution.py:76
  7.3 1.3 %collective-permute-start.2 = (bf16[1296,128]{1,0:T(8,128)(2,1)S(1)}, bf16[1296,128]{1,0:T(8,128)(2,1)S(1)}, u32[]{:S(2)}, u32[]{:S(2)}) collective-permute-start(bf16[1296,128]{1,0:T(8,128)(2,1)S(1)} %get-tuple-element.77.refs_4_), channel_id=1, source_target_pairs={{0,1},{1,0},{2,3},{3,2},{4,5},{5,4},{6,7},{7,6},{8,9},{9,8},{10,11... | collective-permute-start | bytes 995336 | tf_op jit(solution)/shard_map/ppermute | solution.py:44
  8.6 2.3 %collective-permute-start.1 = (bf16[1296,128]{1,0:T(8,128)(2,1)S(1)}, bf16[1296,128]{1,0:T(8,128)(2,1)S(1)}, u32[]{:S(2)}, u32[]{:S(2)}) collective-permute-start(bf16[1296,128]{1,0:T(8,128)(2,1)S(1)} %get-tuple-element.77.refs_4_), channel_id=1, source_target_pairs={{0,2},{1,3},{2,0},{3,1},{4,6},{5,7},{6,4},{7,5},{8,10},{9,11},{10,... | collective-permute-start | bytes 995336 | tf_op jit(solution)/shard_map/ppermute | solution.py:44
  10.9 11.5 %collective-permute-done.2.refs_3_ = bf16[1296,128]{1,0:T(8,128)(2,1)S(1)} collective-permute-done((bf16[1296,128]{1,0:T(8,128)(2,1)S(1)}, bf16[1296,128]{1,0:T(8,128)(2,1)S(1)}, u32[]{:S(2)}, u32[]{:S(2)}) %collective-permute-start.2) | collective-permute-done | bytes 331808 | tf_op jit(solution)/shard_map/ppermute | solution.py:44
  22.4 1.5 %collective-permute-start.11 = (bf16[16,64,512]{2,1,0:T(8,128)(2,1)S(1)}, bf16[16,64,512]{2,1,0:T(8,128)(2,1)S(1)}, u32[]{:S(2)}, u32[]{:S(2)}) collective-permute-start(bf16[16,64,512]{2,1,0:T(8,128)(2,1)S(1)} %collective-permute-done.8.refs_5_), channel_id=1, source_target_pairs={{0,4},{4,0},{8,12},{12,8},{16,20},{20,16},{24,28},{28,24},{1,5},{5... | collective-permute-start | bytes 3145736 | tf_op jit(solution)/shard_map/ppermute | solution.py:44
  24.0 1.2 %collective-permute-start.10 = (bf16[4,64,512]{2,1,0:T(8,128)(2,1)S(1)}, bf16[4,64,512]{2,1,0:T(8,128)(2,1)S(1)}, u32[]{:S(2)}, u32[]{:S(2)}) collective-permute-start(bf16[4,64,512]{2,1,0:T(8,128)(2,1)S(1)} %get-tuple-element.127), channel_id=1, source_target_pairs={{0,16},{4,12},{8,24},{12,4},{16,0},{20,28},{24,8},{28,20},{1,17},{... | collective-permute-start | bytes 786440 | tf_op jit(solution)/shard_map/ppermute | solution.py:76
  25.5 6.9 %collective-permute-done.refs_1_ = bf16[1296,128]{1,0:T(8,128)(2,1)S(1)} collective-permute-done((bf16[1296,128]{1,0:T(8,128)(2,1)S(1)}, bf16[1296,128]{1,0:T(8,128)(2,1)S(1)}, u32[]{:S(2)}, u32[]{:S(2)}) %collective-permute-start) | collective-permute-done | bytes 331808 | tf_op jit(solution)/shard_map/ppermute | solution.py:44
  32.4 3.1 %collective-permute-start.12 = (bf16[4,64,512]{2,1,0:T(8,128)(2,1)S(1)}, bf16[4,64,512]{2,1,0:T(8,128)(2,1)S(1)}, u32[]{:S(2)}, u32[]{:S(2)}) collective-permute-start(bf16[4,64,512]{2,1,0:T(8,128)(2,1)S(1)} %collective-permute-done.9.refs_6_), channel_id=1, source_target_pairs={{0,4},{4,0},{8,12},{12,8},{16,20},{20,16},{24,28},{28,24},{1,5},{5... | collective-permute-start | bytes 786440 | tf_op jit(solution)/shard_map/ppermute | solution.py:44
  35.5 0.4 collective-permute-start.3
  36.0 0.6 collective-permute-done.12.refs_9_
  36.6 0.4 collective-permute-start.5
  38.1 3.2 %mapping.1 = (f32[8,8,512]{2,1,0:T(8,128)S(1)}, f32[8,8,512]{2,1,0:T(8,128)S(1)}, f32[8,512]{1,0:T(8,128)S(1)}, f32[2,8,512]{2,1,0:T(8,128)S(1)}, bf16[8,512,512]{2,1,0:T(8,128)(2,1)S(1)}) custom-call(s32[2]{0:T(128)S(1)} %pad_add_fusion.where.refs_0_, s32[2]{0:T(128)S(1)} %bitcast.34, s32[1]{0:T(128)S(6)} %copy.60.refs_2_.crossover, ...), custom_call_target="tpu_custom_call" | custom-call | bytes 3500000 | tf_op jit(solution)/shard_map/mapping/pallas_call | solution.py:706
  41.4 6.8 %main.1 = (bf16[1,4608,128]{2,1,0:T(8,128)(2,1)S(1)}, f32[8,512]{1,0:T(8,128)S(1)}, f32[8,128]{1,0:T(8,128)S(1)}, bf16[512,512]{1,0:T(8,128)(2,1)S(1)}) custom-call(s32[2]{0:T(128)S(1)} %pad_add_fusion.where.refs_0_, bf16[1296,128]{1,0:T(8,128)(2,1)S(1)} %collective-permute-done.refs_1_, bf16[1296,128]{1,0:T(8,128)(2,1)S(1)} %collective-permute-done.1.refs_2_, ...), custom_call_target="tpu_custom_call" | custom-call | bytes 28000000 | tf_op jit(solution)/shard_map/main/pallas_call | solution.py:730
  48.2 2.3 %collective-permute-start.16 = (f32[8,512]{1,0:T(8,128)S(1)}, f32[8,512]{1,0:T(8,128)S(1)}, u32[]{:S(2)}, u32[]{:S(2)}) collective-permute-start(f32[8,512]{1,0:T(8,128)S(1)} %get-tuple-element.83.refs_0_), channel_id=1, source_target_pairs={{0,3},{1,2},{2,1},{3,0},{4,7},{5,6},{6,5},{7,4},{8,11},{9,10},{10,... | collective-permute-start | bytes 49160 | tf_op jit(solution)/shard_map/ppermute | solution.py:44
  50.4 4.9 %collective-permute-start.15 = (f32[8,512]{1,0:T(8,128)S(1)}, f32[8,512]{1,0:T(8,128)S(1)}, u32[]{:S(2)}, u32[]{:S(2)}) collective-permute-start(f32[8,512]{1,0:T(8,128)S(1)} %get-tuple-element.83.refs_0_), channel_id=1, source_target_pairs={{0,2},{1,3},{2,0},{3,1},{4,6},{5,7},{6,4},{7,5},{8,10},{9,11},{10,... | collective-permute-start | bytes 49160 | tf_op jit(solution)/shard_map/ppermute | solution.py:44
  56.1 0.5 collective-permute-done.15.refs_2_
  56.7 1.3 %collective-permute-done.14.refs_1_ = f32[8,512]{1,0:T(8,128)S(1)} collective-permute-done((f32[8,512]{1,0:T(8,128)S(1)}, f32[8,512]{1,0:T(8,128)S(1)}, u32[]{:S(2)}, u32[]{:S(2)}) %collective-permute-start.14) | collective-permute-done | bytes 16416 | tf_op jit(solution)/shard_map/ppermute | solution.py:44
  58.0 0.7 scale.1
  58.7 1.9 %collective-permute-start.21 = (bf16[2336,128]{1,0:T(8,128)(2,1)S(1)}, bf16[2336,128]{1,0:T(8,128)(2,1)S(1)}, u32[]{:S(2)}, u32[]{:S(2)}) collective-permute-start(bf16[2336,128]{1,0:T(8,128)(2,1)S(1)} %get-tuple-element.108), channel_id=1, source_target_pairs={{0,4},{4,0},{8,12},{12,8},{16,20},{20,16},{24,28},{28,24},{1,5},{5... | collective-permute-start | bytes 1794056 | tf_op jit(solution)/shard_map/ppermute | solution.py:44
  60.6 2.1 %mapping_back.1 = bf16[48,512]{1,0:T(8,128)(2,1)S(1)} custom-call(s32[2]{0:T(128)S(1)} %pad_add_fusion.where.refs_0_, s32[1]{0:T(128)S(6)} %copy.61.counted, s32[1]{0:T(128)S(6)} %copy.60.refs_2_.crossover, f32[8,512]{1,0:T(8,128)S(1)} %get-tuple-element.83.refs_0_, f32[8,512]{1,0:T(8,128)S(1)} %collective-permute-done.14.refs_1_, ...), custom_call_target="tpu_custom_call" | custom-call | bytes 7000000 | tf_op jit(solution)/shard_map/mapping_back/pallas_call | solution.py:784
  63.4 1.3 %collective-permute-start.17 = (bf16[48,512]{1,0:T(8,128)(2,1)S(1)}, bf16[48,512]{1,0:T(8,128)(2,1)S(1)}, u32[]{:S(2)}, u32[]{:S(2)}) collective-permute-start(bf16[48,512]{1,0:T(8,128)(2,1)S(1)} %mapping_back.1), channel_id=1, source_target_pairs={{0,4},{4,0},{8,12},{12,8},{16,20},{20,16},{24,28},{28,24},{1,5},{5... | collective-permute-start | bytes 147464 | tf_op jit(solution)/shard_map/ppermute | solution.py:44
  64.7 0.9 collective-permute-done.17
  65.9 7.4 %collective-permute-done.18.refs_1_ = bf16[96,512]{1,0:T(8,128)(2,1)S(1)} collective-permute-done((bf16[96,512]{1,0:T(8,128)(2,1)S(1)}, bf16[96,512]{1,0:T(8,128)(2,1)S(1)}, u32[]{:S(2)}, u32[]{:S(2)}) %collective-permute-start.18) | collective-permute-done | bytes 98336 | tf_op jit(solution)/shard_map/ppermute | solution.py:76
  73.5 1.3 %collective-permute-start.23 = (bf16[2336,128]{1,0:T(8,128)(2,1)S(1)}, bf16[2336,128]{1,0:T(8,128)(2,1)S(1)}, u32[]{:S(2)}, u32[]{:S(2)}) collective-permute-start(bf16[2336,128]{1,0:T(8,128)(2,1)S(1)} %add_convert_fusion.1), channel_id=1, source_target_pairs={{0,16},{4,12},{8,24},{12,4},{16,0},{20,28},{24,8},{28,20},{1,17},{... | collective-permute-start | bytes 1794056 | tf_op jit(solution)/shard_map/ppermute | solution.py:76
  74.9 1.2 %collective-permute-start.19 = (bf16[96,512]{1,0:T(8,128)(2,1)S(1)}, bf16[96,512]{1,0:T(8,128)(2,1)S(1)}, u32[]{:S(2)}, u32[]{:S(2)}) collective-permute-start(bf16[96,512]{1,0:T(8,128)(2,1)S(1)} %collective-permute-done.18.refs_1_), channel_id=1, source_target_pairs={{0,16},{4,12},{8,24},{12,4},{16,0},{20,28},{24,8},{28,20},{1,17},{... | collective-permute-start | bytes 294920 | tf_op jit(solution)/shard_map/ppermute | solution.py:76
  76.2 7.6 %collective-permute-done.19.refs_2_ = bf16[96,512]{1,0:T(8,128)(2,1)S(1)} collective-permute-done((bf16[96,512]{1,0:T(8,128)(2,1)S(1)}, bf16[96,512]{1,0:T(8,128)(2,1)S(1)}, u32[]{:S(2)}, u32[]{:S(2)}) %collective-permute-start.19) | collective-permute-done | bytes 98336 | tf_op jit(solution)/shard_map/ppermute | solution.py:76
  83.8 4.1 %update.1 = (f32[8,64,512]{2,1,0:T(8,128)}, f32[8,64,512]{2,1,0:T(8,128)}, f32[8,64,512]{2,1,0:T(8,128)}, bf16[8,64,512]{2,1,0:T(8,128)(2,1)}, f32[1024,128]{1,0...) custom-call(s32[2]{0:T(128)S(1)} %pad_add_fusion.where.refs_0_, ...), custom_call_target="tpu_custom_call" | custom-call | bytes 17500000 | tf_op jit(solution)/shard_map/update/pallas_call | solution.py:823
  88.1 1.8 %collective-permute-start.24 = (bf16[2336,128]{1,0:T(8,128)(2,1)S(1)}, bf16[2336,128]{1,0:T(8,128)(2,1)S(1)}, u32[]{:S(2)}, u32[]{:S(2)}) collective-permute-start(bf16[2336,128]{1,0:T(8,128)(2,1)S(1)} %add_convert_fusion.grad), channel_id=1, source_target_pairs={{0,4},{4,0},{8,12},{12,8},{16,20},{20,16},{24,28},{28,24},{1,5},{5... | collective-permute-start | bytes 1794056 | tf_op jit(solution)/shard_map/ppermute | solution.py:44
  89.9 2.7 %conv_own.1 = (f32[4608,128]{1,0:T(8,128)}, f32[4608,128]{1,0:T(8,128)}, f32[4608,128]{1,0:T(8,128)}, bf16[4608,128]{1,0:T(8,128)(2,1)}) custom-call(s32[2]{0:T(128)S(1)} %pad_add_fusion.where.refs_0_, bf16[2336,128]{1,0:T(8,128)(2,1)S(1)} %add_convert_fusion.grad, f32[4608,128]{1,0:T(8,128)S(1)} %bitcast.24, f32[4608,128]{1,0:T(8,128)S(1)} %bitcast.26, ...), custom_call_target="tpu_custom_call" | custom-call | bytes 7000000 | tf_op jit(solution)/shard_map/conv_own/pallas_call | solution.py:865
  92.6 2.7 %conv_other.1 = (f32[4608,128]{1,0:T(8,128)}, f32[4608,128]{1,0:T(8,128)}, f32[4608,128]{1,0:T(8,128)}, bf16[4608,128]{1,0:T(8,128)(2,1)}) custom-call(s32[2]{0:T(128)S(1)} %pad_add_fusion.where.refs_0_, bf16[2336,128]{1,0:T(8,128)(2,1)S(1)} %collective-permute-done.24.grad, ...), custom_call_target="tpu_custom_call", output_to_operand_aliasing={{0}: (5, {}), {1}: (6, {}), {2}: (7, {}), {3}: (8, {})} | custom-call | bytes 7000000 | tf_op jit(solution)/shard_map/conv_other/pallas_call | solution.py:865
  (75 shorter events, 2.8 us)
Async XLA Ops:
  2.8 35.2 %copy-start.9 = (f32[8,512]{1,0:T(8,128)S(1)}, f32[8,512]{1,0:T(8,128)}, u32[]{:S(2)}) copy-start(f32[8,512]{1,0:T(8,128)} %refs_10_.3) | copy-start | bytes 49156
  2.8 35.2 %copy-start.20 = (s32[1,2]{1,0:T(1,128)S(1)}, s32[1,2]{1,0:T(1,128)}, u32[]{:S(2)}) copy-start(s32[1,2]{1,0:T(1,128)} %param.27) | copy-start | bytes 28
  2.8 2.0 %collective-permute-start.7 = (bf16[8,64,512]{2,1,0:T(8,128)(2,1)S(1)}, bf16[8,64,512]{2,1,0:T(8,128)(2,1)S(1)}, u32[]{:S(2)}, u32[]{:S(2)}) collective-permute-start(bf16[8,64,512]{2,1,0:T(8,128)(2,1)S(1)} %get-tuple-element.78.refs_3_), channel_id=1, source_target_pairs={{0,4},{4,0},{8,12},{12,8},{16,20},{20,16},{24,28},{28,24},{1,5},{5... | collective-permute-start | bytes 1572872 | tf_op jit(solution)/shard_map/ppermute | solution.py:44
  4.9 17.5 %collective-permute-start.8 = (bf16[16,64,512]{2,1,0:T(8,128)(2,1)S(1)}, bf16[16,64,512]{2,1,0:T(8,128)(2,1)S(1)}, u32[]{:S(2)}, u32[]{:S(2)}) collective-permute-start(bf16[16,64,512]{2,1,0:T(8,128)(2,1)S(1)} %pad_maximum_fusion), channel_id=1, source_target_pairs={{0,8},{4,20},{8,0},{12,28},{16,24},{20,4},{24,16},{28,12},{1,9},{5... | collective-permute-start | bytes 3145736 | tf_op jit(solution)/shard_map/ppermute | solution.py:76
  7.3 15.1 %collective-permute-start.2 = (bf16[1296,128]{1,0:T(8,128)(2,1)S(1)}, bf16[1296,128]{1,0:T(8,128)(2,1)S(1)}, u32[]{:S(2)}, u32[]{:S(2)}) collective-permute-start(bf16[1296,128]{1,0:T(8,128)(2,1)S(1)} %get-tuple-element.77.refs_4_), channel_id=1, source_target_pairs={{0,1},{1,0},{2,3},{3,2},{4,5},{5,4},{6,7},{7,6},{8,9},{9,8},{10,11... | collective-permute-start | bytes 995336 | tf_op jit(solution)/shard_map/ppermute | solution.py:44
  8.6 16.9 %collective-permute-start.1 = (bf16[1296,128]{1,0:T(8,128)(2,1)S(1)}, bf16[1296,128]{1,0:T(8,128)(2,1)S(1)}, u32[]{:S(2)}, u32[]{:S(2)}) collective-permute-start(bf16[1296,128]{1,0:T(8,128)(2,1)S(1)} %get-tuple-element.77.refs_4_), channel_id=1, source_target_pairs={{0,2},{1,3},{2,0},{3,1},{4,6},{5,7},{6,4},{7,5},{8,10},{9,11},{10,... | collective-permute-start | bytes 995336 | tf_op jit(solution)/shard_map/ppermute | solution.py:44
  10.9 21.4 %collective-permute-start = (bf16[1296,128]{1,0:T(8,128)(2,1)S(1)}, bf16[1296,128]{1,0:T(8,128)(2,1)S(1)}, u32[]{:S(2)}, u32[]{:S(2)}) collective-permute-start(bf16[1296,128]{1,0:T(8,128)(2,1)S(1)} %get-tuple-element.77.refs_4_), channel_id=1, source_target_pairs={{0,3},{1,2},{2,1},{3,0},{4,7},{5,6},{6,5},{7,4},{8,11},{9,10},{10,... | collective-permute-start | bytes 995336 | tf_op jit(solution)/shard_map/ppermute | solution.py:44
  22.4 15.6 %collective-permute-start.11 = (bf16[16,64,512]{2,1,0:T(8,128)(2,1)S(1)}, bf16[16,64,512]{2,1,0:T(8,128)(2,1)S(1)}, u32[]{:S(2)}, u32[]{:S(2)}) collective-permute-start(bf16[16,64,512]{2,1,0:T(8,128)(2,1)S(1)} %collective-permute-done.8.refs_5_), channel_id=1, source_target_pairs={{0,4},{4,0},{8,12},{12,8},{16,20},{20,16},{24,28},{28,24},{1,5},{5... | collective-permute-start | bytes 3145736 | tf_op jit(solution)/shard_map/ppermute | solution.py:44
  24.0 8.4 %collective-permute-start.10 = (bf16[4,64,512]{2,1,0:T(8,128)(2,1)S(1)}, bf16[4,64,512]{2,1,0:T(8,128)(2,1)S(1)}, u32[]{:S(2)}, u32[]{:S(2)}) collective-permute-start(bf16[4,64,512]{2,1,0:T(8,128)(2,1)S(1)} %get-tuple-element.127), channel_id=1, source_target_pairs={{0,16},{4,12},{8,24},{12,4},{16,0},{20,28},{24,8},{28,20},{1,17},{... | collective-permute-start | bytes 786440 | tf_op jit(solution)/shard_map/ppermute | solution.py:76
  25.1 7.2 %collective-permute-start.9 = (bf16[4,64,512]{2,1,0:T(8,128)(2,1)S(1)}, bf16[4,64,512]{2,1,0:T(8,128)(2,1)S(1)}, u32[]{:S(2)}, u32[]{:S(2)}) collective-permute-start(bf16[4,64,512]{2,1,0:T(8,128)(2,1)S(1)} %get-tuple-element.128), channel_id=1, source_target_pairs={{0,16},{4,12},{8,24},{12,4},{16,0},{20,28},{24,8},{28,20},{1,17},{... | collective-permute-start | bytes 786440 | tf_op jit(solution)/shard_map/ppermute | solution.py:76
  32.4 4.3 %collective-permute-start.12 = (bf16[4,64,512]{2,1,0:T(8,128)(2,1)S(1)}, bf16[4,64,512]{2,1,0:T(8,128)(2,1)S(1)}, u32[]{:S(2)}, u32[]{:S(2)}) collective-permute-start(bf16[4,64,512]{2,1,0:T(8,128)(2,1)S(1)} %collective-permute-done.9.refs_6_), channel_id=1, source_target_pairs={{0,4},{4,0},{8,12},{12,8},{16,20},{20,16},{24,28},{28,24},{1,5},{5... | collective-permute-start | bytes 786440 | tf_op jit(solution)/shard_map/ppermute | solution.py:44
  35.5 1.5 %collective-permute-start.13 = (bf16[4,64,512]{2,1,0:T(8,128)(2,1)S(1)}, bf16[4,64,512]{2,1,0:T(8,128)(2,1)S(1)}, u32[]{:S(2)}, u32[]{:S(2)}) collective-permute-start(bf16[4,64,512]{2,1,0:T(8,128)(2,1)S(1)} %collective-permute-done.10.refs_7_), channel_id=1, source_target_pairs={{0,4},{4,0},{8,12},{12,8},{16,20},{20,16},{24,28},{28,24},{1,5},{5... | collective-permute-start | bytes 786440 | tf_op jit(solution)/shard_map/ppermute | solution.py:44
  35.5 5.8 %collective-permute-start.3 = (bf16[1296,128]{1,0:T(8,128)(2,1)S(1)}, bf16[1296,128]{1,0:T(8,128)(2,1)S(1)}, u32[]{:S(2)}, u32[]{:S(2)}) collective-permute-start(bf16[1296,128]{1,0:T(8,128)(2,1)S(1)} %get-tuple-element.77.refs_4_), channel_id=1, source_target_pairs={{0,4},{4,0},{8,12},{12,8},{16,20},{20,16},{24,28},{28,24},{1,5},{5... | collective-permute-start | bytes 995336 | tf_op jit(solution)/shard_map/ppermute | solution.py:44
  36.0 5.4 %collective-permute-start.4 = (bf16[1296,128]{1,0:T(8,128)(2,1)S(1)}, bf16[1296,128]{1,0:T(8,128)(2,1)S(1)}, u32[]{:S(2)}, u32[]{:S(2)}) collective-permute-start(bf16[1296,128]{1,0:T(8,128)(2,1)S(1)} %collective-permute-done.2.refs_3_), channel_id=1, source_target_pairs={{0,4},{4,0},{8,12},{12,8},{16,20},{20,16},{24,28},{28,24},{1,5},{5... | collective-permute-start | bytes 995336 | tf_op jit(solution)/shard_map/ppermute | solution.py:44
  36.6 4.7 %collective-permute-start.5 = (bf16[1296,128]{1,0:T(8,128)(2,1)S(1)}, bf16[1296,128]{1,0:T(8,128)(2,1)S(1)}, u32[]{:S(2)}, u32[]{:S(2)}) collective-permute-start(bf16[1296,128]{1,0:T(8,128)(2,1)S(1)} %collective-permute-done.1.refs_2_), channel_id=1, source_target_pairs={{0,4},{4,0},{8,12},{12,8},{16,20},{20,16},{24,28},{28,24},{1,5},{5... | collective-permute-start | bytes 995336 | tf_op jit(solution)/shard_map/ppermute | solution.py:44
  37.0 4.4 %collective-permute-start.6 = (bf16[1296,128]{1,0:T(8,128)(2,1)S(1)}, bf16[1296,128]{1,0:T(8,128)(2,1)S(1)}, u32[]{:S(2)}, u32[]{:S(2)}) collective-permute-start(bf16[1296,128]{1,0:T(8,128)(2,1)S(1)} %collective-permute-done.refs_1_), channel_id=1, source_target_pairs={{0,4},{4,0},{8,12},{12,8},{16,20},{20,16},{24,28},{28,24},{1,5},{5... | collective-permute-start | bytes 995336 | tf_op jit(solution)/shard_map/ppermute | solution.py:44
  48.2 8.0 %collective-permute-start.16 = (f32[8,512]{1,0:T(8,128)S(1)}, f32[8,512]{1,0:T(8,128)S(1)}, u32[]{:S(2)}, u32[]{:S(2)}) collective-permute-start(f32[8,512]{1,0:T(8,128)S(1)} %get-tuple-element.83.refs_0_), channel_id=1, source_target_pairs={{0,3},{1,2},{2,1},{3,0},{4,7},{5,6},{6,5},{7,4},{8,11},{9,10},{10,... | collective-permute-start | bytes 49160 | tf_op jit(solution)/shard_map/ppermute | solution.py:44
  50.4 6.2 %collective-permute-start.15 = (f32[8,512]{1,0:T(8,128)S(1)}, f32[8,512]{1,0:T(8,128)S(1)}, u32[]{:S(2)}, u32[]{:S(2)}) collective-permute-start(f32[8,512]{1,0:T(8,128)S(1)} %get-tuple-element.83.refs_0_), channel_id=1, source_target_pairs={{0,2},{1,3},{2,0},{3,1},{4,6},{5,7},{6,4},{7,5},{8,10},{9,11},{10,... | collective-permute-start | bytes 49160 | tf_op jit(solution)/shard_map/ppermute | solution.py:44
  55.4 2.6 %collective-permute-start.14 = (f32[8,512]{1,0:T(8,128)S(1)}, f32[8,512]{1,0:T(8,128)S(1)}, u32[]{:S(2)}, u32[]{:S(2)}) collective-permute-start(f32[8,512]{1,0:T(8,128)S(1)} %get-tuple-element.83.refs_0_), channel_id=1, source_target_pairs={{0,1},{1,0},{2,3},{3,2},{4,5},{5,4},{6,7},{7,6},{8,9},{9,8},{10,11... | collective-permute-start | bytes 49160 | tf_op jit(solution)/shard_map/ppermute | solution.py:44
  58.7 4.1 %collective-permute-start.21 = (bf16[2336,128]{1,0:T(8,128)(2,1)S(1)}, bf16[2336,128]{1,0:T(8,128)(2,1)S(1)}, u32[]{:S(2)}, u32[]{:S(2)}) collective-permute-start(bf16[2336,128]{1,0:T(8,128)(2,1)S(1)} %get-tuple-element.108), channel_id=1, source_target_pairs={{0,4},{4,0},{8,12},{12,8},{16,20},{20,16},{24,28},{28,24},{1,5},{5... | collective-permute-start | bytes 1794056 | tf_op jit(solution)/shard_map/ppermute | solution.py:44
  60.6 23.1 %copy-start.8 = (f32[2,512,128]{2,1,0:T(8,128)S(1)}, f32[2,512,128]{2,1,0:T(8,128)}, u32[]{:S(2)}) copy-start(f32[2,512,128]{2,1,0:T(8,128)} %param.40) | copy-start | bytes 1572868
  62.8 20.9 %copy-start.5 = (f32[8,64,512]{2,1,0:T(8,128)S(1)}, f32[8,64,512]{2,1,0:T(8,128)}, u32[]{:S(2)}) copy-start(f32[8,64,512]{2,1,0:T(8,128)} %refs_5_.1) | copy-start | bytes 3145732
  62.8 20.9 %copy-start.6 = (f32[8,64,512]{2,1,0:T(8,128)S(1)}, f32[8,64,512]{2,1,0:T(8,128)}, u32[]{:S(2)}) copy-start(f32[8,64,512]{2,1,0:T(8,128)} %refs_6_.1) | copy-start | bytes 3145732
  63.0 20.8 %copy-start.4 = (f32[8,64,512]{2,1,0:T(8,128)S(1)}, f32[8,64,512]{2,1,0:T(8,128)}, u32[]{:S(2)}) copy-start(f32[8,64,512]{2,1,0:T(8,128)} %refs_4_.1) | copy-start | bytes 3145732
  63.0 20.8 %copy-start.7 = (f32[2,512,128]{2,1,0:T(8,128)S(1)}, f32[2,512,128]{2,1,0:T(8,128)}, u32[]{:S(2)}) copy-start(f32[2,512,128]{2,1,0:T(8,128)} %param.39) | copy-start | bytes 1572868
  63.1 10.2 %collective-permute-start.22 = (bf16[2336,128]{1,0:T(8,128)(2,1)S(1)}, bf16[2336,128]{1,0:T(8,128)(2,1)S(1)}, u32[]{:S(2)}, u32[]{:S(2)}) collective-permute-start(bf16[2336,128]{1,0:T(8,128)(2,1)S(1)} %add_convert_fusion.2), channel_id=1, source_target_pairs={{0,8},{4,20},{8,0},{12,28},{16,24},{20,4},{24,16},{28,12},{1,9},{5... | collective-permute-start | bytes 1794056 | tf_op jit(solution)/shard_map/ppermute | solution.py:76
  63.4 2.2 %collective-permute-start.17 = (bf16[48,512]{1,0:T(8,128)(2,1)S(1)}, bf16[48,512]{1,0:T(8,128)(2,1)S(1)}, u32[]{:S(2)}, u32[]{:S(2)}) collective-permute-start(bf16[48,512]{1,0:T(8,128)(2,1)S(1)} %mapping_back.1), channel_id=1, source_target_pairs={{0,4},{4,0},{8,12},{12,8},{16,20},{20,16},{24,28},{28,24},{1,5},{5... | collective-permute-start | bytes 147464 | tf_op jit(solution)/shard_map/ppermute | solution.py:44
  65.6 7.8 %collective-permute-start.18 = (bf16[96,512]{1,0:T(8,128)(2,1)S(1)}, bf16[96,512]{1,0:T(8,128)(2,1)S(1)}, u32[]{:S(2)}, u32[]{:S(2)}) collective-permute-start(bf16[96,512]{1,0:T(8,128)(2,1)S(1)} %pad_maximum_fusion.1.refs_0_), channel_id=1, source_target_pairs={{0,8},{4,20},{8,0},{12,28},{16,24},{20,4},{24,16},{28,12},{1,9},{5... | collective-permute-start | bytes 294920 | tf_op jit(solution)/shard_map/ppermute | solution.py:76
  73.5 14.4 %collective-permute-start.23 = (bf16[2336,128]{1,0:T(8,128)(2,1)S(1)}, bf16[2336,128]{1,0:T(8,128)(2,1)S(1)}, u32[]{:S(2)}, u32[]{:S(2)}) collective-permute-start(bf16[2336,128]{1,0:T(8,128)(2,1)S(1)} %add_convert_fusion.1), channel_id=1, source_target_pairs={{0,16},{4,12},{8,24},{12,4},{16,0},{20,28},{24,8},{28,20},{1,17},{... | collective-permute-start | bytes 1794056 | tf_op jit(solution)/shard_map/ppermute | solution.py:76
  74.8 1.4 %collective-permute-start.20 = (bf16[96,512]{1,0:T(8,128)(2,1)S(1)}, bf16[96,512]{1,0:T(8,128)(2,1)S(1)}, u32[]{:S(2)}, u32[]{:S(2)}) collective-permute-start(bf16[96,512]{1,0:T(8,128)(2,1)S(1)} %collective-permute-done.18.refs_1_), channel_id=1, source_target_pairs={{0,4},{4,0},{8,12},{12,8},{16,20},{20,16},{24,28},{28,24},{1,5},{5... | collective-permute-start | bytes 294920 | tf_op jit(solution)/shard_map/ppermute | solution.py:44
  74.9 8.8 %collective-permute-start.19 = (bf16[96,512]{1,0:T(8,128)(2,1)S(1)}, bf16[96,512]{1,0:T(8,128)(2,1)S(1)}, u32[]{:S(2)}, u32[]{:S(2)}) collective-permute-start(bf16[96,512]{1,0:T(8,128)(2,1)S(1)} %collective-permute-done.18.refs_1_), channel_id=1, source_target_pairs={{0,16},{4,12},{8,24},{12,4},{16,0},{20,28},{24,8},{28,20},{1,17},{... | collective-permute-start | bytes 294920 | tf_op jit(solution)/shard_map/ppermute | solution.py:76
  88.1 4.5 %collective-permute-start.24 = (bf16[2336,128]{1,0:T(8,128)(2,1)S(1)}, bf16[2336,128]{1,0:T(8,128)(2,1)S(1)}, u32[]{:S(2)}, u32[]{:S(2)}) collective-permute-start(bf16[2336,128]{1,0:T(8,128)(2,1)S(1)} %add_convert_fusion.grad), channel_id=1, source_target_pairs={{0,4},{4,0},{8,12},{12,8},{16,20},{20,16},{24,28},{28,24},{1,5},{5... | collective-permute-start | bytes 1794056 | tf_op jit(solution)/shard_map/ppermute | solution.py:44
  (14 other events, 187.2 us)

commit v3 on v2

--- a/solution.py
+++ b/solution.py
@@ -56,18 +56,41 @@
             parts += [(part, [(k, k)]), (swap(part, axis, 1), [(k + 1, k + 1)])]
         return parts
     near = jnp.concatenate([value, beside])
-    far = crossed(near, axis, 2, 4)
-    corner = crossed(far, axis, 4, 2)
+    far = crossed(near, axis, 4, 2)
+    corner = crossed(far, axis, 2, 4)
     return [
         (near, [(0, 0), (1, 1)]),
-        (far, [(2, 4), (3, 5)]),
+        (far, [(4, 2), (5, 3)]),
         (corner, [(6, 6), (7, 7)]),
-        (swap(far, axis, 1), [(5, 3), (4, 2)]),
+        (swap(far, axis, 1), [(3, 5), (2, 4)]),
     ]
 
 
 def spread_direct(value, axis):
     return [value] + [swap(value, axis, k) for k in range(1, lax.axis_size(axis))]
+
+
+def spread_over_chan(pack, tail, ready):
+    n_dp, n_ch = lax.axis_size("dp"), lax.axis_size("chan")
+    cut = pack.shape[0] - tail
+    other = swap(pack, "dp", 1)
+    both = after(jnp.concatenate([pack, other[cut:], other[:cut]]), ready)
+
+    def joint(value, moves):
+        pairs = [
+            (d * n_ch + a, d * n_ch + b) for d in range(n_dp) for a, b in moves[d % 2]
+        ]
+        return lax.ppermute(value, ("dp", "chan"), pairs)
+
+    first = joint(both, ([(c, c ^ 1) for c in range(4)], [(c, c ^ 2) for c in range(4)]))
+    first_pair = swap(first[cut:], "dp", 1)
+    odd = lax.rem(lax.axis_index("dp"), 2) == 1
+
+    def last_step(*others):
+        value = after(jnp.where(odd, first, both), *others)
+        return joint(value, ([(1, 2), (2, 1)], [(1, 0), (2, 3)]))
+
+    return both, first, first_pair, last_step
 
 
 def crossed(value, axis, even_distance, odd_distance):
@@ -76,31 +99,22 @@
     return lax.ppermute(value, axis, pairs)
 
 
-def spread_layers(value, axis, others):
-    size, layers = lax.axis_size(axis), value.shape[0]
+def spread_layers(value, axis):
+    size = lax.axis_size(axis)
     beside = swap(value, axis, 1)
+    parts = [(value, (0, 0, 0)), (beside, (0, 1, 1))]
     if size != 8:
-        far = [swap(value, axis, k) for k in range(2, size, 2)]
-        parts = [(value, [(0, 0, 0)]), (beside, [(0, 1, 1)])]
-        for k, part in zip(range(2, size, 2), far):
-            parts.append((part, [(0, k, k)]))
-            parts.append((swap(part, axis, 1), [(0, k + 1, k + 1)]))
+        for k in range(2, size, 2):
+            part = swap(value, axis, k)
+            parts += [(part, (0, k, k)), (swap(part, axis, 1), (0, k + 1, k + 1))]
         return parts
-    far = crossed(jnp.concatenate([value, beside]), axis, 2, 4)
-    half = layers // 2
-    low, high = (crossed(far[at : at + half], axis, 4, 2) for at in (0, half))
-    far_low = after(far, others[0])
-    low, high = after([low, high], *others[1:])
-    return [
-        (value, [(0, 0, 0)]),
-        (beside, [(0, 1, 1)]),
-        (far, [(0, 2, 4), (0, 3, 5)]),
-        (low, [(0, 6, 6)]),
-        (high, [(half, 6, 6)]),
-        (swap(far_low, axis, 1), [(0, 5, 3), (0, 4, 2)]),
-        (swap(low, axis, 1), [(0, 7, 7)]),
-        (swap(high, axis, 1), [(half, 7, 7)]),
-    ]
+    far = crossed(value, axis, 2, 4)
+    far_beside = crossed(beside, axis, 2, 4)
+    corner = crossed(far, axis, 4, 2)
+    parts += [(far, (0, 2, 4)), (far_beside, (0, 3, 5)), (corner, (0, 6, 6))]
+    parts += [(swap(far, axis, 1), (0, 5, 3)), (swap(far_beside, axis, 1), (0, 4, 2))]
+    parts += [(swap(corner, axis, 1), (0, 7, 7))]
+    return parts
 
 
 def silu_slope(preact):
@@ -136,32 +150,37 @@
     return lax.dot_general(a, b, (((0,), (0,)), ((), ())), preferred_element_type=F32)
 
 
-def prepare_kernel(where, map_w, aff_w, bias, features, map_low, pack, stage, aff_stage, bias_stage, sems):
-    layers = map_w.shape[0]
+def pack_kernel(where, aff_w, bias, features, pack, aff_stage, bias_stage, sems):
     half = aff_stage.shape[0]
     rows = features.shape[0]
     start = pl.multiple_of(lax.rem(where[0], 2) * half, half)
-    copies = [
-        pltpu.make_async_copy(map_w.at[layer], stage.at[layer], sems.at[layer])
-        for layer in range(layers)
-    ]
-    aff_copy = pltpu.make_async_copy(aff_w.at[0, pl.ds(start, half), :], aff_stage, sems.at[layers])
-    bias_copy = pltpu.make_async_copy(bias, bias_stage, sems.at[layers + 1])
-    feat_copy = pltpu.make_async_copy(features, pack.at[pl.ds(0, rows), :], sems.at[layers + 2])
-    for copy in copies + [aff_copy, bias_copy, feat_copy]:
+    feat_copy = pltpu.make_async_copy(features, pack.at[pl.ds(0, rows), :], sems.at[0])
+    aff_copy = pltpu.make_async_copy(aff_w.at[0, pl.ds(start, half), :], aff_stage, sems.at[1])
+    bias_copy = pltpu.make_async_copy(bias, bias_stage, sems.at[2])
+    for copy in (feat_copy, aff_copy, bias_copy):
         copy.start()
-    for layer in range(layers):
-        copies[layer].wait()
-        map_low[layer] = stage[layer].astype(BF16)
-    aff_copy.wait()
-    pack[pl.ds(rows, half), :] = aff_stage[...].astype(BF16)
     bias_copy.wait()
     hi, mid, lo = pieces(bias_stage[0:1, :], 3)
     lines = jnp.concatenate(
         [hi.astype(F32), mid.astype(F32), lo.astype(F32), jnp.zeros((13, LANES), F32)], axis=0
     )
     pack[pl.ds(rows + half, 16), :] = lines.astype(BF16)
+    aff_copy.wait()
+    pack[pl.ds(rows, half), :] = aff_stage[...].astype(BF16)
     feat_copy.wait()
+
+
+def low_kernel(map_w, map_low, stage, sems):
+    layers = map_w.shape[0]
+    copies = [
+        pltpu.make_async_copy(map_w.at[layer], stage.at[layer], sems.at[layer])
+        for layer in range(layers)
+    ]
+    for copy in copies:
+        copy.start()
+    for layer in range(layers):
+        copies[layer].wait()
+        map_low[layer] = stage[layer].astype(BF16)
 
 
 def mapping_kernel(n_dp, samples, places, *refs):
@@ -175,8 +194,8 @@
     where, seeds, crossover = take(3)
     parts = take(len(places))
     z_table, map_b = take(2)
-    pre_out, hid_out, top_out, picked_out, map_out = take(5)
-    map_full, rows, sem_map, sem_z, sem_out = refs
+    pre_out, hid_out, top_out, picked_out, map_full = take(5)
+    rows, sem_map, sem_z = refs
     layers, share, width = parts[0].shape
     latents = 2 * samples
     dp = where[0]
@@ -184,22 +203,33 @@
     for n in range(latents):
         at = pl.multiple_of((seeds[n] // 8) * 8, 8)
         z_copies.append(pltpu.make_async_copy(z_table.at[pl.ds(at, 8), :], rows.at[n], sem_z.at[n]))
-    map_copies = []
+        z_copies[n].start()
     odd = lax.rem(dp, 2)
-    for part, place in zip(parts, places):
-        depth = part.shape[0] // len(place)
-        for i, (first, even_k, odd_k) in enumerate(place):
-            k = jnp.where(odd == 1, odd_k, even_k)
-            at = pl.multiple_of(lax.bitwise_xor(dp, k) * share, share)
-            map_copies.append(
-                pltpu.make_async_copy(
-                    part.at[pl.ds(i * depth, depth)],
-                    map_full.at[pl.ds(first, depth), pl.ds(at, share), :],
-                    sem_map.at[len(map_copies)],
-                )
+    moves = []
+    for part, (first, even_k, odd_k) in zip(parts, places):
+        k = jnp.where(odd == 1, odd_k, even_k)
+        at = pl.multiple_of(lax.bitwise_xor(dp, k) * share, share)
+        moves.append((part, first, pl.ds(at, share)))
+    whole_tiles = share % 16 == 0
+    if not whole_tiles:
+        copies = [
+            pltpu.make_async_copy(
+                part, map_full.at[pl.ds(first, part.shape[0]), at, :], sem_map.at[i]
             )
-    for copy in z_copies + map_copies:
-        copy.start()
+            for i, (part, first, at) in enumerate(moves)
+        ]
+        for copy in copies:
+            copy.start()
+        for copy in copies:
+            copy.wait()
+
+    def bring(layer):
+        for part, first, at in moves:
+            if whole_tiles and first <= layer < first + part.shape[0]:
+                map_full[layer, at, :] = part[layer - first]
+
+    bring(0)
+    bring(1)
     hidden_rows = []
     for n in range(latents):
         z_copies[n].wait()
@@ -208,13 +238,11 @@
         hidden_rows.append(row * scale)
     hidden_rows.append(jnp.zeros((16 - latents, width), F32))
     hidden = jnp.concatenate(hidden_rows, axis=0)
-    for copy in map_copies:
-        copy.wait()
-    keep_map = pltpu.make_async_copy(map_full, map_out, sem_out)
-    keep_map.start()
     for layer in range(layers):
         low = hidden.astype(BF16)
         preact = dot(low, map_full[layer]) + map_b[pl.ds(layer, 1), :]
+        if layer + 2 < layers:
+            bring(layer + 2)
         hid_out[layer] = low.astype(F32)[0:8]
         pre_out[layer] = preact[0:8]
         hidden = preact * jax.nn.sigmoid(preact)
@@ -229,7 +257,20 @@
             )
         chosen.append(jnp.zeros((8 - samples, width), F32))
         picked_out[j] = jnp.concatenate(chosen, axis=0)
-    keep_map.wait()
+
+
+def weights_kernel(conv_w, kernel, square, stage, sems):
+    copies = [pltpu.make_async_copy(conv_w.at[t], stage.at[t], sems.at[t]) for t in range(TAPS)]
+    for copy in copies:
+        copy.start()
+    total = jnp.zeros(square.shape, F32)
+    for tap in range(TAPS):
+        copies[tap].wait()
+        low = stage[tap].astype(BF16)
+        kernel[tap // 3, :, pl.ds((tap % 3) * LANES, LANES)] = low
+        wide = low.astype(F32)
+        total = total + wide * wide
+    square[...] = total
 
 
 def main_kernel(n_ch, samples, side, *refs):
@@ -241,27 +282,11 @@
         return got
 
     (where,) = take(1)
-    packs = take(n_ch)[::-1]
-    pair_packs = take(n_ch)
-    (conv_w,) = take(1)
+    both, first, first_pair, second, second_pair = take(5)
+    kernel, square_in = take(2)
     aff_w, picked, bias, head, rgb_w = take(5)
-    unit, to_sum, small, aff_out = take(4)
-    (
-        aff_full,
-        bias_full,
-        feat,
-        feat_t,
-        kernel_f,
-        kernel,
-        padded,
-        taps,
-        shifted,
-        wide,
-        sem_feat,
-        sem_aff,
-        sem_conv,
-        sem_out,
-    ) = refs
+    unit, to_sum, small, aff_full = take(4)
+    bias_full, style_rows, late, late_tail, feat_t, padded, taps, shifted, wide = refs
     width = aff_full.shape[0]
     pixels = side * side
     half = width // 2
@@ -270,51 +295,42 @@
     mine = pl.ds(pl.multiple_of(pair * half, half), half)
     other = pl.ds(pl.multiple_of((1 - pair) * half, half), half)
 
-    def arrivals(source, beside, k):
-        lane = pl.ds(pl.multiple_of(lax.bitwise_xor(ch, k) * LANES, LANES), LANES)
-        copies = [
-            pltpu.make_async_copy(
-                source.at[pl.ds(s * pixels, pixels), :], feat.at[s, :, lane], sem_feat.at[samples * k + s]
-            )
-            for s in range(samples)
-        ]
-        at = samples * pixels
-        copies.append(
-            pltpu.make_async_copy(
-                source.at[pl.ds(at, half), :], aff_full.at[mine, lane], sem_aff.at[3 * k]
-            )
-        )
-        copies.append(
-            pltpu.make_async_copy(
-                source.at[pl.ds(at + half, 16), :], bias_full.at[:, lane], sem_aff.at[3 * k + 1]
-            )
-        )
-        copies.append(
-            pltpu.make_async_copy(
-                beside.at[pl.ds(at, half), :], aff_full.at[other, lane], sem_aff.at[3 * k + 2]
-            )
-        )
-        return copies
-
-    conv_copies = [
-        pltpu.make_async_copy(conv_w.at[tap], kernel_f.at[tap], sem_conv.at[tap]) for tap in range(TAPS)
-    ]
-    copies = [copy for k in range(n_ch) for copy in arrivals(packs[k], pair_packs[k], k)]
-    for copy in copies + conv_copies:
-        copy.start()
-    square = jnp.zeros((width, LANES), F32)
-    for tap in range(TAPS):
-        conv_copies[tap].wait()
-        tap_low = kernel_f[tap].astype(BF16)
-        kernel[tap // 3, :, pl.ds((tap % 3) * LANES, LANES)] = tap_low
-        wide_tap = tap_low.astype(F32)
-        square = square + wide_tap * wide_tap
-    for copy in copies:
-        copy.wait()
-    keep_aff = pltpu.make_async_copy(aff_full, aff_out, sem_out)
-    keep_aff.start()
-    for s in range(samples):
-        feat_t[s] = feat[s].T
+    tail_rows = half + 16
+    feats = samples * pixels
+    cut = first.shape[0] - first_pair.shape[0]
+    partner_tail, partner_feats = feats + tail_rows, feats + 2 * tail_rows
+    at_end = jnp.logical_or(ch == 0, ch == n_ch - 1)
+    is_held = at_end == (pair == 1)
+
+    @pl.when(is_held)
+    def _():
+        late[...] = second[pl.ds(0, feats + tail_rows), :]
+        late_tail[...] = second[pl.ds(partner_tail, tail_rows), :]
+
+    @pl.when(jnp.logical_not(is_held))
+    def _():
+        late[pl.ds(0, feats), :] = second_pair[pl.ds(partner_feats - cut, feats), :]
+        late[pl.ds(feats, tail_rows), :] = second_pair[pl.ds(partner_tail - cut, tail_rows), :]
+        late_tail[...] = second_pair[pl.ds(feats - cut, tail_rows), :]
+
+    blocks = []
+    for source, top, tail_at, other_source, other_tail_at, k in (
+        (both, 0, feats, both, partner_tail, 0),
+        (first, 0, feats, first, partner_tail, 1 + pair),
+        (first_pair, partner_feats - cut, partner_tail - cut, first_pair, feats - cut, 2 - pair),
+        (late, 0, feats, late_tail, 0, 3),
+    ):
+        at = pl.multiple_of(lax.bitwise_xor(ch, k) * LANES, LANES)
+        lane = pl.ds(at, LANES)
+        aff_full[mine, lane] = source[pl.ds(tail_at, half), :]
+        aff_full[other, lane] = other_source[pl.ds(other_tail_at, half), :]
+        bias_full[:, lane] = source[pl.ds(tail_at + half, 16), :]
+        for s in range(samples):
+            value = source[pl.ds(top + s * pixels, pixels), :]
+            feat_t[s, lane, :] = value.T
+        blocks.append((source, top, lane))
+    square = square_in[...]
+
     wide_bias = bias_full[...].astype(F32)
     bias_row = wide_bias[0:1] + wide_bias[1:2] + wide_bias[2:3]
     style0 = (dot(picked[0].astype(BF16), aff_full[...]) + bias_row).astype(BF16)
@@ -344,9 +360,12 @@
     wide[pl.ds(8 + pixels, 8), :] = jnp.zeros((8, LANES), F32)
 
     for s in range(samples):
-        style_row = style0[s : s + 1, :]
-        for r in range(steps):
-            padded[pl.ds(side + r * chunk, chunk), :] = feat[s, pl.ds(r * chunk, chunk), :] * style_row
+        style_rows[...] = style0_wide
+        for source, top, lane in blocks:
+            factor_row = style_rows[pl.ds(s, 1), lane].astype(BF16)
+            padded[pl.ds(side, pixels), lane] = (
+                source[pl.ds(top + s * pixels, pixels), :] * factor_row
+            )
         style_col = jnp.broadcast_to(style0_wide[s : s + 1, :], (LANES, width)).T
         demod = lax.rsqrt(
             jnp.sum(style_col * style_col * square, axis=0, keepdims=True) + 1e-08
@@ -419,7 +438,6 @@
         small[pl.ds(8 * s, 1), :] = g_style1
         small[pl.ds(8 * s + 1, 1), :] = g_bias
         small[pl.ds(8 * s + 2, 3), :] = mixed
-    keep_aff.wait()
 
 
 def summed(parts, row):
@@ -685,22 +703,46 @@
 
     half = width // 2
     pack_rows = samples * pixels + half + 16
-    map_low, pack = pl.pallas_call(
-        prepare_kernel,
-        out_shape=(shape(map_w.shape, BF16), shape((pack_rows, LANES), BF16)),
-        in_specs=[SMEM] + [ANY] * 4,
+    pack = pl.pallas_call(
+        pack_kernel,
+        out_shape=shape((pack_rows, LANES), BF16),
+        in_specs=[SMEM] + [ANY] * 3,
+        out_specs=VMEM,
+        scratch_shapes=[
+            pltpu.VMEM((half, LANES), F32),
+            pltpu.VMEM(chan_bias.shape, F32),
+            pltpu.SemaphoreType.DMA((3,)),
+        ],
+        compiler_params=params(4),
+        cost_estimate=cost(1),
+        name="pack",
+    )(where, *hbm(aff_w, chan_bias, features.reshape(samples * pixels, LANES)))
+    map_low = pl.pallas_call(
+        low_kernel,
+        out_shape=shape(map_w.shape, BF16),
+        in_specs=[ANY],
+        out_specs=VMEM,
+        scratch_shapes=[pltpu.VMEM(map_w.shape, F32), pltpu.SemaphoreType.DMA((layers,))],
+        compiler_params=params(8),
+        cost_estimate=cost(1),
+        name="low",
+    )(*hbm(map_w))
+    *chan_packs, last_step = spread_over_chan(pack, half + 16, map_low)
+    blocks = spread_layers(map_low, "dp")
+    kernel, square = pl.pallas_call(
+        weights_kernel,
+        out_shape=(shape((3, width, 3 * LANES), BF16), shape((width, LANES), F32)),
+        in_specs=[ANY],
         out_specs=(VMEM, VMEM),
         scratch_shapes=[
-            pltpu.VMEM(map_w.shape, F32),
-            pltpu.VMEM((half, LANES), F32),
-            pltpu.VMEM(chan_bias.shape, F32),
-            pltpu.SemaphoreType.DMA((layers + 3,)),
+            pltpu.VMEM((TAPS, width, LANES), F32),
+            pltpu.SemaphoreType.DMA((TAPS,)),
         ],
         compiler_params=params(8),
-        name="prepare",
-    )(where, *hbm(map_w, aff_w, chan_bias, features.reshape(samples * pixels, LANES)))
-    packs = spread_direct(pack, "chan")
-    blocks = spread_layers(map_low, "dp", packs[1:])
+        cost_estimate=cost(2),
+        name="weights",
+    )(*hbm(after(conv_w.reshape(TAPS, width, LANES), blocks[1][0])))
+    second = last_step(blocks[2][0], kernel)
     places = [place for _, place in blocks]
 
     pre, hid, top, picked, map_full = pl.pallas_call(
@@ -712,21 +754,19 @@
             shape((2, 8, width), F32),
             shape((layers, width, width), BF16),
         ),
-        in_specs=[SMEM] * 3 + [ANY] * (len(blocks) + 1) + [VMEM],
-        out_specs=(VMEM,) * 4 + (ANY,),
+        in_specs=[SMEM] * 3 + [VMEM] * len(blocks) + [ANY, VMEM],
+        out_specs=(VMEM,) * 5,
         scratch_shapes=[
-            pltpu.VMEM((layers, width, width), BF16),
             pltpu.VMEM((latents, 8, width), F32),
-            pltpu.SemaphoreType.DMA((sum(len(place) for place in places),)),
+            pltpu.SemaphoreType.DMA((len(places),)),
             pltpu.SemaphoreType.DMA((latents,)),
-            pltpu.SemaphoreType.DMA,
         ],
         compiler_params=params(12),
         cost_estimate=cost(1),
         name="mapping",
     )(where, seeds.reshape(-1), crossover, *[block for block, _ in blocks], *hbm(z_table), map_b)
 
-    pack_pair = [swap(part, "dp", 1) for part in packs]
+    chan_packs += [second, swap(after(second, picked)[samples * pixels :], "dp", 1)]
     unit, to_sum, small, aff_full = pl.pallas_call(
         functools.partial(main_kernel, n_ch, samples, side),
         out_shape=(
@@ -735,32 +775,27 @@
             shape((8 * samples, LANES), F32),
             shape((width, width), BF16),
         ),
-        in_specs=[SMEM] + [ANY] * (2 * n_ch + 1) + [VMEM] * 5,
-        out_specs=(VMEM,) * 3 + (ANY,),
+        in_specs=[SMEM] + [VMEM] * 12,
+        out_specs=(VMEM,) * 4,
         scratch_shapes=[
-            pltpu.VMEM((width, width), BF16),
             pltpu.VMEM((16, width), BF16),
-            pltpu.VMEM((samples, pixels, width), BF16),
+            pltpu.VMEM((8, width), F32),
+            pltpu.VMEM((pack_rows, LANES), BF16),
+            pltpu.VMEM((half + 16, LANES), BF16),
             pltpu.VMEM((samples, width, pixels), BF16),
-            pltpu.VMEM((TAPS, width, LANES), F32),
-            pltpu.VMEM((3, width, 3 * LANES), BF16),
             pltpu.VMEM((pixels + 2 * side, width), BF16),
             pltpu.VMEM((pixels + 16, 3 * LANES), F32),
             pltpu.VMEM((pixels, TAPS * LANES), BF16),
             pltpu.VMEM((pixels + 16, LANES), F32),
-            pltpu.SemaphoreType.DMA((samples * n_ch,)),
-            pltpu.SemaphoreType.DMA((3 * n_ch,)),
-            pltpu.SemaphoreType.DMA((TAPS,)),
-            pltpu.SemaphoreType.DMA,
         ],
-        compiler_params=params(28),
+        compiler_params=params(20),
         cost_estimate=cost(8),
         name="main",
     )(
         where,
-        *packs[::-1],
-        *pack_pair,
-        *hbm(conv_w.reshape(TAPS, width, LANES)),
+        *chan_packs,
+        kernel,
+        square,
         aff_w,
         picked,
         chan_bias,

time: 95.6 us -> 81.7 us (0.85)
  waiting for transfers between devices: 38.5 us -> 29 us
  starting transfers between devices: 29.3 us -> 24.3 us
    ppermute x18 -> x14, waiting for transfers between devices: 23.5 us -> 7.42 us  [swap(): lax.ppermute(value, axis, [(i, i ^ distance) for i in range(lax.axis_size...]
    ppermute x18 -> x14, starting transfers between devices: 22.2 us -> 11.5 us  [swap(): lax.ppermute(value, axis, [(i, i ^ distance) for i in range(lax.axis_size...]
    ppermute x0 -> x2, waiting for transfers between devices: none -> 6.85 us  [joint(): return lax.ppermute(value, ('dp', 'chan'), pairs)]
    ppermute x0 -> x2, starting transfers between devices: none -> 4.92 us  [joint(): return lax.ppermute(value, ('dp', 'chan'), pairs)]
    pallas_call x1 -> x3, Pallas kernels: 2.05 us -> 4.62 us  [the longest x1 1.71 us: local(): pl.pallas_call(weights_kernel, out_shape=(shape((3, width, 3 * LANES), BF...]
    pallas_call x1, Pallas kernels: 6.75 us -> 4.98 us  [local(): pl.pallas_call(functools.partial(main_kernel, n_ch, samples, side), out_s...]
  transfers between devices with their start and end apart: 25 -> 23, of which waited for: 9 -> 15; matrix products, arithmetic and copies ran while one was open for 0% -> 0% of each run, Pallas kernels for 13% -> 18%
where the time goes in v3:
time: 81.7 us; the launch traced here: 81.5 us
  waiting for transfers between devices  29 us (35%)
  Pallas kernels  24.9 us (30%)
  starting transfers between devices  24.3 us (30%)
  between operations  2.39 us (3%)
    ppermute x7, waiting for transfers between devices, crossed(): return lax.ppermute(value, axis, pairs)  14.8 us
    ppermute x14, starting transfers between devices, swap(): lax.ppermute(value, axis, [(i, i ^ distance) for i in range(lax.axis_size...  11.5 us
    ppermute x7, starting transfers between devices, crossed(): return lax.ppermute(value, axis, pairs)  7.84 us
    ppermute x14, waiting for transfers between devices, swap(): lax.ppermute(value, axis, [(i, i ^ distance) for i in range(lax.axis_size...  7.42 us
    ppermute x2, waiting for transfers between devices, joint(): return lax.ppermute(value, ('dp', 'chan'), pairs)  6.85 us
    pallas_call x2, Pallas kernels, conv_half(): pl.pallas_call(functools.partial(conv_kernel, not earlier), out_shape=[sh...  5.46 us
    pallas_call x1, Pallas kernels, local(): pl.pallas_call(functools.partial(main_kernel, n_ch, samples, side), out_s...  4.98 us
    ppermute x2, starting transfers between devices, joint(): return lax.ppermute(value, ('dp', 'chan'), pairs)  4.92 us
  transfers between devices with their start and end apart: 23, of which 15 were waited for; matrix products, arithmetic and copies ran while one was open for 0% of the time, Pallas kernels for 18%

profile of v3, /device:TPU:1, one launch (start us, length us, event | category | flops | bytes accessed | tf_op | source)
XLA Modules:
  0.0 81.5 jit_solution(18094301233791487503)
XLA Ops:
  0.7 1.6 %pack.1 = bf16[1296,128]{1,0:T(8,128)(2,1)S(1)} custom-call(s32[2]{0:T(128)S(1)} %pad_add_fusion.where.refs_0_, f32[2,512,128]{2,1,0:T(8,128)} %refs_8_.1, f32[3,128]{1,0:T(4,128)} %refs_13_.1, bf16[1024,128]{1,0:T(8,128)(2,1)} %bitcast.39), custom_call_target="tpu_custom_call" | custom-call | bytes 3500000 | tf_op jit(solution)/shard_map/pack/pallas_call | solution.py:706
  2.4 1.4 %low.1.refs_3_ = bf16[8,64,512]{2,1,0:T(8,128)(2,1)S(1)} custom-call(f32[8,64,512]{2,1,0:T(8,128)} %refs_4_.1), custom_call_target="tpu_custom_call" | custom-call | bytes 3500000 | tf_op jit(solution)/shard_map/low/pallas_call | solution.py:720
  4.1 3.6 %collective-permute-start.1 = (bf16[2592,128]{1,0:T(8,128)(2,1)S(1)}, bf16[2592,128]{1,0:T(8,128)(2,1)S(1)}, u32[]{:S(2)}, u32[]{:S(2)}) collective-permute-start(bf16[2592,128]{1,0:T(8,128)(2,1)S(1)} %pad_maximum_fusion.refs_1_), channel_id=1, source_target_pairs={{0,1},{1,0},{2,3},{3,2},{4,6},{5,7},{6,4},{7,5},{8,9},{9,8},{10,11... | collective-permute-start | bytes 1990664 | tf_op jit(solution)/shard_map/ppermute | solution.py:83
  7.7 1.2 %collective-permute-start.3 = (bf16[8,64,512]{2,1,0:T(8,128)(2,1)S(1)}, bf16[8,64,512]{2,1,0:T(8,128)(2,1)S(1)}, u32[]{:S(2)}, u32[]{:S(2)}) collective-permute-start(bf16[8,64,512]{2,1,0:T(8,128)(2,1)S(1)} %low.1.refs_3_), channel_id=1, source_target_pairs={{0,8},{4,20},{8,0},{12,28},{16,24},{20,4},{24,16},{28,12},{1,9},{5... | collective-permute-start | bytes 1572872 | tf_op jit(solution)/shard_map/ppermute | solution.py:99
  9.6 1.7 %weights.1 = (bf16[3,512,384]{2,1,0:T(8,128)(2,1)S(1)}, f32[512,128]{1,0:T(8,128)S(1)}) custom-call(f32[9,512,128]{2,1,0:T(8,128)} %bitcast.23), custom_call_target="tpu_custom_call" | custom-call | bytes 7000000 | tf_op jit(solution)/shard_map/weights/pallas_call | solution.py:732
  11.4 1.3 %collective-permute-start.6 = (bf16[8,64,512]{2,1,0:T(8,128)(2,1)S(1)}, bf16[8,64,512]{2,1,0:T(8,128)(2,1)S(1)}, u32[]{:S(2)}, u32[]{:S(2)}) collective-permute-start(bf16[8,64,512]{2,1,0:T(8,128)(2,1)S(1)} %collective-permute-done.4.refs_4_), channel_id=1, source_target_pairs={{0,8},{4,20},{8,0},{12,28},{16,24},{20,4},{24,16},{28,12},{1,9},{5... | collective-permute-start | bytes 1572872 | tf_op jit(solution)/shard_map/ppermute | solution.py:99
  12.7 3.4 %collective-permute-done.3.refs_5_ = bf16[8,64,512]{2,1,0:T(8,128)(2,1)S(1)} collective-permute-done((bf16[8,64,512]{2,1,0:T(8,128)(2,1)S(1)}, bf16[8,64,512]{2,1,0:T(8,128)(2,1)S(1)}, u32[]{:S(2)}, u32[]{:S(2)}) %collective-permute-start.3) | collective-permute-done | bytes 524320 | tf_op jit(solution)/shard_map/ppermute | solution.py:99
  16.1 1.2 %collective-permute-start.7 = (bf16[8,64,512]{2,1,0:T(8,128)(2,1)S(1)}, bf16[8,64,512]{2,1,0:T(8,128)(2,1)S(1)}, u32[]{:S(2)}, u32[]{:S(2)}) collective-permute-start(bf16[8,64,512]{2,1,0:T(8,128)(2,1)S(1)} %collective-permute-done.3.refs_5_), channel_id=1, source_target_pairs={{0,16},{4,12},{8,24},{12,4},{16,0},{20,28},{24,8},{28,20},{1,17},{... | collective-permute-start | bytes 1572872 | tf_op jit(solution)/shard_map/ppermute | solution.py:99
  17.3 5.4 %collective-permute-done.1.refs_2_ = bf16[2592,128]{1,0:T(8,128)(2,1)S(1)} collective-permute-done((bf16[2592,128]{1,0:T(8,128)(2,1)S(1)}, bf16[2592,128]{1,0:T(8,128)(2,1)S(1)}, u32[]{:S(2)}, u32[]{:S(2)}) %collective-permute-start.1) | collective-permute-done | bytes 663584 | tf_op jit(solution)/shard_map/ppermute | solution.py:83
  22.8 1.3 %collective-permute-start.5 = (bf16[2592,128]{1,0:T(8,128)(2,1)S(1)}, bf16[2592,128]{1,0:T(8,128)(2,1)S(1)}, u32[]{:S(2)}, u32[]{:S(2)}) collective-permute-start(bf16[2592,128]{1,0:T(8,128)(2,1)S(1)} %broadcast_select_fusion), channel_id=1, source_target_pairs={{1,2},{2,1},{5,4},{6,7},{9,10},{10,9},{13,12},{14,15},{17,18},{18,... | collective-permute-start | bytes 1990664 | tf_op jit(solution)/shard_map/ppermute | solution.py:83
  24.2 2.7 %collective-permute-start.9 = (bf16[8,64,512]{2,1,0:T(8,128)(2,1)S(1)}, bf16[8,64,512]{2,1,0:T(8,128)(2,1)S(1)}, u32[]{:S(2)}, u32[]{:S(2)}) collective-permute-start(bf16[8,64,512]{2,1,0:T(8,128)(2,1)S(1)} %collective-permute-done.6.refs_6_), channel_id=1, source_target_pairs={{0,4},{4,0},{8,12},{12,8},{16,20},{20,16},{24,28},{28,24},{1,5},{5... | collective-permute-start | bytes 1572872 | tf_op jit(solution)/shard_map/ppermute | solution.py:44
  26.8 1.1 %collective-permute-done.7.refs_7_ = bf16[8,64,512]{2,1,0:T(8,128)(2,1)S(1)} collective-permute-done((bf16[8,64,512]{2,1,0:T(8,128)(2,1)S(1)}, bf16[8,64,512]{2,1,0:T(8,128)(2,1)S(1)}, u32[]{:S(2)}, u32[]{:S(2)}) %collective-permute-start.7) | collective-permute-done | bytes 524320 | tf_op jit(solution)/shard_map/ppermute | solution.py:99
  29.9 2.9 %mapping.1 = (f32[8,8,512]{2,1,0:T(8,128)S(1)}, f32[8,8,512]{2,1,0:T(8,128)S(1)}, f32[8,512]{1,0:T(8,128)S(1)}, f32[2,8,512]{2,1,0:T(8,128)S(1)}, bf16[8,512,512]{2,1,0:T(8,128)(2,1)S(1)}) custom-call(s32[2]{0:T(128)S(1)} %pad_add_fusion.where.refs_0_, s32[2]{0:T(128)S(1)} %bitcast.34, s32[1]{0:T(128)S(6)} %copy.60.refs_2_.crossover, ...), custom_call_target="tpu_custom_call" | custom-call | bytes 3500000 | tf_op jit(solution)/shard_map/mapping/pallas_call | solution.py:748
  32.8 1.4 %collective-permute-done.5.refs_4_ = bf16[2592,128]{1,0:T(8,128)(2,1)S(1)} collective-permute-done((bf16[2592,128]{1,0:T(8,128)(2,1)S(1)}, bf16[2592,128]{1,0:T(8,128)(2,1)S(1)}, u32[]{:S(2)}, u32[]{:S(2)}) %collective-permute-start.5) | collective-permute-done | bytes 663584 | tf_op jit(solution)/shard_map/ppermute | solution.py:83
  34.3 1.7 %collective-permute-done.11.refs_5_ = bf16[1568,128]{1,0:T(8,128)(2,1)S(1)} collective-permute-done((bf16[1568,128]{1,0:T(8,128)(2,1)S(1)}, bf16[1568,128]{1,0:T(8,128)(2,1)S(1)}, u32[]{:S(2)}, u32[]{:S(2)}) %collective-permute-start.11) | collective-permute-done | bytes 401440 | tf_op jit(solution)/shard_map/ppermute | solution.py:44
  36.1 5.0 %main.1 = (bf16[1,4608,128]{2,1,0:T(8,128)(2,1)S(1)}, f32[8,512]{1,0:T(8,128)S(1)}, f32[8,128]{1,0:T(8,128)S(1)}, bf16[512,512]{1,0:T(8,128)(2,1)S(1)}) custom-call(s32[2]{0:T(128)S(1)} %pad_add_fusion.where.refs_0_, bf16[2592,128]{1,0:T(8,128)(2,1)S(1)} %pad_maximum_fusion.refs_1_, bf16[2592,128]{1,0:T(8,128)(2,1)S(1)} %collective-permute-done.1.refs_2_, ...), custom_call_target="tpu_custom_call" | custom-call | bytes 28000000 | tf_op jit(solution)/shard_map/main/pallas_call | solution.py:770
  41.0 3.6 %collective-permute-start.14 = (f32[8,512]{1,0:T(8,128)S(1)}, f32[8,512]{1,0:T(8,128)S(1)}, u32[]{:S(2)}, u32[]{:S(2)}) collective-permute-start(f32[8,512]{1,0:T(8,128)S(1)} %get-tuple-element.85.refs_0_), channel_id=1, source_target_pairs={{0,3},{1,2},{2,1},{3,0},{4,7},{5,6},{6,5},{7,4},{8,11},{9,10},{10,... | collective-permute-start | bytes 49160 | tf_op jit(solution)/shard_map/ppermute | solution.py:44
  45.7 2.4 %collective-permute-done.13.refs_2_ = f32[8,512]{1,0:T(8,128)S(1)} collective-permute-done((f32[8,512]{1,0:T(8,128)S(1)}, f32[8,512]{1,0:T(8,128)S(1)}, u32[]{:S(2)}, u32[]{:S(2)}) %collective-permute-start.13) | collective-permute-done | bytes 16416 | tf_op jit(solution)/shard_map/ppermute | solution.py:44
  48.9 1.6 %collective-permute-start.19 = (bf16[2336,128]{1,0:T(8,128)(2,1)S(1)}, bf16[2336,128]{1,0:T(8,128)(2,1)S(1)}, u32[]{:S(2)}, u32[]{:S(2)}) collective-permute-start(bf16[2336,128]{1,0:T(8,128)(2,1)S(1)} %get-tuple-element.110), channel_id=1, source_target_pairs={{0,4},{4,0},{8,12},{12,8},{16,20},{20,16},{24,28},{28,24},{1,5},{5... | collective-permute-start | bytes 1794056 | tf_op jit(solution)/shard_map/ppermute | solution.py:44
  50.5 2.1 %mapping_back.1 = bf16[48,512]{1,0:T(8,128)(2,1)S(1)} custom-call(s32[2]{0:T(128)S(1)} %pad_add_fusion.where.refs_0_, s32[1]{0:T(128)S(6)} %copy.61.counted, s32[1]{0:T(128)S(6)} %copy.60.refs_2_.crossover, f32[8,512]{1,0:T(8,128)S(1)} %get-tuple-element.85.refs_0_, f32[8,512]{1,0:T(8,128)S(1)} %collective-permute-done.12.refs_1_, ...), custom_call_target="tpu_custom_call" | custom-call | bytes 7000000 | tf_op jit(solution)/shard_map/mapping_back/pallas_call | solution.py:819
  52.9 1.3 %collective-permute-start.20 = (bf16[2336,128]{1,0:T(8,128)(2,1)S(1)}, bf16[2336,128]{1,0:T(8,128)(2,1)S(1)}, u32[]{:S(2)}, u32[]{:S(2)}) collective-permute-start(bf16[2336,128]{1,0:T(8,128)(2,1)S(1)} %add_convert_fusion.2), channel_id=1, source_target_pairs={{0,8},{4,20},{8,0},{12,28},{16,24},{20,4},{24,16},{28,12},{1,9},{5... | collective-permute-start | bytes 1794056 | tf_op jit(solution)/shard_map/ppermute | solution.py:99
  54.5 1.0 %collective-permute-done.15 = bf16[48,512]{1,0:T(8,128)(2,1)S(1)} collective-permute-done((bf16[48,512]{1,0:T(8,128)(2,1)S(1)}, bf16[48,512]{1,0:T(8,128)(2,1)S(1)}, u32[]{:S(2)}, u32[]{:S(2)}) %collective-permute-start.15) | collective-permute-done | bytes 49184 | tf_op jit(solution)/shard_map/ppermute | solution.py:44
  55.5 1.3 %collective-permute-start.16 = (bf16[96,512]{1,0:T(8,128)(2,1)S(1)}, bf16[96,512]{1,0:T(8,128)(2,1)S(1)}, u32[]{:S(2)}, u32[]{:S(2)}) collective-permute-start(bf16[96,512]{1,0:T(8,128)(2,1)S(1)} %pad_maximum_fusion.1.refs_0_), channel_id=1, source_target_pairs={{0,16},{4,12},{8,24},{12,4},{16,0},{20,28},{24,8},{28,20},{1,17},{... | collective-permute-start | bytes 294920 | tf_op jit(solution)/shard_map/ppermute | solution.py:99
  56.8 3.7 %collective-permute-done.16.refs_1_ = bf16[96,512]{1,0:T(8,128)(2,1)S(1)} collective-permute-done((bf16[96,512]{1,0:T(8,128)(2,1)S(1)}, bf16[96,512]{1,0:T(8,128)(2,1)S(1)}, u32[]{:S(2)}, u32[]{:S(2)}) %collective-permute-start.16) | collective-permute-done | bytes 98336 | tf_op jit(solution)/shard_map/ppermute | solution.py:99
  60.4 2.7 %collective-permute-done.20 = bf16[2336,128]{1,0:T(8,128)(2,1)S(1)} collective-permute-done((bf16[2336,128]{1,0:T(8,128)(2,1)S(1)}, bf16[2336,128]{1,0:T(8,128)(2,1)S(1)}, u32[]{:S(2)}, u32[]{:S(2)}) %collective-permute-start.20) | collective-permute-done | bytes 598048 | tf_op jit(solution)/shard_map/ppermute | solution.py:99
  63.3 1.3 %collective-permute-start.21 = (bf16[2336,128]{1,0:T(8,128)(2,1)S(1)}, bf16[2336,128]{1,0:T(8,128)(2,1)S(1)}, u32[]{:S(2)}, u32[]{:S(2)}) collective-permute-start(bf16[2336,128]{1,0:T(8,128)(2,1)S(1)} %add_convert_fusion.1), channel_id=1, source_target_pairs={{0,16},{4,12},{8,24},{12,4},{16,0},{20,28},{24,8},{28,20},{1,17},{... | collective-permute-start | bytes 1794056 | tf_op jit(solution)/shard_map/ppermute | solution.py:99
  64.6 1.2 %collective-permute-start.18 = (bf16[96,512]{1,0:T(8,128)(2,1)S(1)}, bf16[96,512]{1,0:T(8,128)(2,1)S(1)}, u32[]{:S(2)}, u32[]{:S(2)}) collective-permute-start(bf16[96,512]{1,0:T(8,128)(2,1)S(1)} %collective-permute-done.16.refs_1_), channel_id=1, source_target_pairs={{0,4},{4,0},{8,12},{12,8},{16,20},{20,16},{24,28},{28,24},{1,5},{5... | collective-permute-start | bytes 294920 | tf_op jit(solution)/shard_map/ppermute | solution.py:44
  66.8 3.9 %collective-permute-done.17.refs_2_ = bf16[96,512]{1,0:T(8,128)(2,1)S(1)} collective-permute-done((bf16[96,512]{1,0:T(8,128)(2,1)S(1)}, bf16[96,512]{1,0:T(8,128)(2,1)S(1)}, u32[]{:S(2)}, u32[]{:S(2)}) %collective-permute-start.17) | collective-permute-done | bytes 98336 | tf_op jit(solution)/shard_map/ppermute | solution.py:99
  70.8 4.1 %update.1 = (f32[8,64,512]{2,1,0:T(8,128)}, f32[8,64,512]{2,1,0:T(8,128)}, f32[8,64,512]{2,1,0:T(8,128)}, bf16[8,64,512]{2,1,0:T(8,128)(2,1)}, f32[1024,128]{1,0...) custom-call(s32[2]{0:T(128)S(1)} %pad_add_fusion.where.refs_0_, ...), custom_call_target="tpu_custom_call" | custom-call | bytes 17500000 | tf_op jit(solution)/shard_map/update/pallas_call | solution.py:858
  75.0 1.0 %collective-permute-start.22 = (bf16[2336,128]{1,0:T(8,128)(2,1)S(1)}, bf16[2336,128]{1,0:T(8,128)(2,1)S(1)}, u32[]{:S(2)}, u32[]{:S(2)}) collective-permute-start(bf16[2336,128]{1,0:T(8,128)(2,1)S(1)} %add_convert_fusion.grad), channel_id=1, source_target_pairs={{0,4},{4,0},{8,12},{12,8},{16,20},{20,16},{24,28},{28,24},{1,5},{5... | collective-permute-start | bytes 1794056 | tf_op jit(solution)/shard_map/ppermute | solution.py:44
  76.0 2.7 %conv_own.1 = (f32[4608,128]{1,0:T(8,128)}, f32[4608,128]{1,0:T(8,128)}, f32[4608,128]{1,0:T(8,128)}, bf16[4608,128]{1,0:T(8,128)(2,1)}) custom-call(s32[2]{0:T(128)S(1)} %pad_add_fusion.where.refs_0_, bf16[2336,128]{1,0:T(8,128)(2,1)S(1)} %add_convert_fusion.grad, f32[4608,128]{1,0:T(8,128)S(1)} %bitcast.24, f32[4608,128]{1,0:T(8,128)S(1)} %bitcast.26, ...), custom_call_target="tpu_custom_call" | custom-call | bytes 7000000 | tf_op jit(solution)/shard_map/conv_own/pallas_call | solution.py:900
  78.7 2.7 %conv_other.1 = (f32[4608,128]{1,0:T(8,128)}, f32[4608,128]{1,0:T(8,128)}, f32[4608,128]{1,0:T(8,128)}, bf16[4608,128]{1,0:T(8,128)(2,1)}) custom-call(s32[2]{0:T(128)S(1)} %pad_add_fusion.where.refs_0_, bf16[2336,128]{1,0:T(8,128)(2,1)S(1)} %collective-permute-done.22.grad, ...), custom_call_target="tpu_custom_call", output_to_operand_aliasing={{0}: (5, {}), {1}: (6, {}), {2}: (7, {}), {3}: (8, {})} | custom-call | bytes 7000000 | tf_op jit(solution)/shard_map/conv_other/pallas_call | solution.py:900
  (77 shorter events, 5.7 us)
Async XLA Ops:
  2.3 1.7 %collective-permute-start = (bf16[1296,128]{1,0:T(8,128)(2,1)S(1)}, bf16[1296,128]{1,0:T(8,128)(2,1)S(1)}, u32[]{:S(2)}, u32[]{:S(2)}) collective-permute-start(bf16[1296,128]{1,0:T(8,128)(2,1)S(1)} %pack.1), channel_id=1, source_target_pairs={{0,4},{4,0},{8,12},{12,8},{16,20},{20,16},{24,28},{28,24},{1,5},{5... | collective-permute-start | bytes 995336 | tf_op jit(solution)/shard_map/ppermute | solution.py:44
  4.1 18.6 %collective-permute-start.1 = (bf16[2592,128]{1,0:T(8,128)(2,1)S(1)}, bf16[2592,128]{1,0:T(8,128)(2,1)S(1)}, u32[]{:S(2)}, u32[]{:S(2)}) collective-permute-start(bf16[2592,128]{1,0:T(8,128)(2,1)S(1)} %pad_maximum_fusion.refs_1_), channel_id=1, source_target_pairs={{0,1},{1,0},{2,3},{3,2},{4,6},{5,7},{6,4},{7,5},{8,9},{9,8},{10,11... | collective-permute-start | bytes 1990664 | tf_op jit(solution)/shard_map/ppermute | solution.py:83
  7.7 1.9 %collective-permute-start.4 = (bf16[8,64,512]{2,1,0:T(8,128)(2,1)S(1)}, bf16[8,64,512]{2,1,0:T(8,128)(2,1)S(1)}, u32[]{:S(2)}, u32[]{:S(2)}) collective-permute-start(bf16[8,64,512]{2,1,0:T(8,128)(2,1)S(1)} %low.1.refs_3_), channel_id=1, source_target_pairs={{0,4},{4,0},{8,12},{12,8},{16,20},{20,16},{24,28},{28,24},{1,5},{5... | collective-permute-start | bytes 1572872 | tf_op jit(solution)/shard_map/ppermute | solution.py:44
  7.7 8.3 %collective-permute-start.3 = (bf16[8,64,512]{2,1,0:T(8,128)(2,1)S(1)}, bf16[8,64,512]{2,1,0:T(8,128)(2,1)S(1)}, u32[]{:S(2)}, u32[]{:S(2)}) collective-permute-start(bf16[8,64,512]{2,1,0:T(8,128)(2,1)S(1)} %low.1.refs_3_), channel_id=1, source_target_pairs={{0,8},{4,20},{8,0},{12,28},{16,24},{20,4},{24,16},{28,12},{1,9},{5... | collective-permute-start | bytes 1572872 | tf_op jit(solution)/shard_map/ppermute | solution.py:99
  11.4 18.5 %copy-start.9 = (f32[8,512]{1,0:T(8,128)S(1)}, f32[8,512]{1,0:T(8,128)}, u32[]{:S(2)}) copy-start(f32[8,512]{1,0:T(8,128)} %refs_10_.3) | copy-start | bytes 49156
  11.4 18.5 %copy-start.20 = (s32[1,2]{1,0:T(1,128)S(1)}, s32[1,2]{1,0:T(1,128)}, u32[]{:S(2)}) copy-start(s32[1,2]{1,0:T(1,128)} %param.27) | copy-start | bytes 28
  11.4 12.8 %collective-permute-start.6 = (bf16[8,64,512]{2,1,0:T(8,128)(2,1)S(1)}, bf16[8,64,512]{2,1,0:T(8,128)(2,1)S(1)}, u32[]{:S(2)}, u32[]{:S(2)}) collective-permute-start(bf16[8,64,512]{2,1,0:T(8,128)(2,1)S(1)} %collective-permute-done.4.refs_4_), channel_id=1, source_target_pairs={{0,8},{4,20},{8,0},{12,28},{16,24},{20,4},{24,16},{28,12},{1,9},{5... | collective-permute-start | bytes 1572872 | tf_op jit(solution)/shard_map/ppermute | solution.py:99
  16.1 11.9 %collective-permute-start.7 = (bf16[8,64,512]{2,1,0:T(8,128)(2,1)S(1)}, bf16[8,64,512]{2,1,0:T(8,128)(2,1)S(1)}, u32[]{:S(2)}, u32[]{:S(2)}) collective-permute-start(bf16[8,64,512]{2,1,0:T(8,128)(2,1)S(1)} %collective-permute-done.3.refs_5_), channel_id=1, source_target_pairs={{0,16},{4,12},{8,24},{12,4},{16,0},{20,28},{24,8},{28,20},{1,17},{... | collective-permute-start | bytes 1572872 | tf_op jit(solution)/shard_map/ppermute | solution.py:99
  22.8 11.4 %collective-permute-start.5 = (bf16[2592,128]{1,0:T(8,128)(2,1)S(1)}, bf16[2592,128]{1,0:T(8,128)(2,1)S(1)}, u32[]{:S(2)}, u32[]{:S(2)}) collective-permute-start(bf16[2592,128]{1,0:T(8,128)(2,1)S(1)} %broadcast_select_fusion), channel_id=1, source_target_pairs={{1,2},{2,1},{5,4},{6,7},{9,10},{10,9},{13,12},{14,15},{17,18},{18,... | collective-permute-start | bytes 1990664 | tf_op jit(solution)/shard_map/ppermute | solution.py:83
  24.1 5.1 %collective-permute-start.8 = (bf16[8,64,512]{2,1,0:T(8,128)(2,1)S(1)}, bf16[8,64,512]{2,1,0:T(8,128)(2,1)S(1)}, u32[]{:S(2)}, u32[]{:S(2)}) collective-permute-start(bf16[8,64,512]{2,1,0:T(8,128)(2,1)S(1)} %collective-permute-done.3.refs_5_), channel_id=1, source_target_pairs={{0,4},{4,0},{8,12},{12,8},{16,20},{20,16},{24,28},{28,24},{1,5},{5... | collective-permute-start | bytes 1572872 | tf_op jit(solution)/shard_map/ppermute | solution.py:44
  24.2 5.0 %collective-permute-start.9 = (bf16[8,64,512]{2,1,0:T(8,128)(2,1)S(1)}, bf16[8,64,512]{2,1,0:T(8,128)(2,1)S(1)}, u32[]{:S(2)}, u32[]{:S(2)}) collective-permute-start(bf16[8,64,512]{2,1,0:T(8,128)(2,1)S(1)} %collective-permute-done.6.refs_6_), channel_id=1, source_target_pairs={{0,4},{4,0},{8,12},{12,8},{16,20},{20,16},{24,28},{28,24},{1,5},{5... | collective-permute-start | bytes 1572872 | tf_op jit(solution)/shard_map/ppermute | solution.py:44
  28.0 1.9 %collective-permute-start.10 = (bf16[8,64,512]{2,1,0:T(8,128)(2,1)S(1)}, bf16[8,64,512]{2,1,0:T(8,128)(2,1)S(1)}, u32[]{:S(2)}, u32[]{:S(2)}) collective-permute-start(bf16[8,64,512]{2,1,0:T(8,128)(2,1)S(1)} %collective-permute-done.7.refs_7_), channel_id=1, source_target_pairs={{0,4},{4,0},{8,12},{12,8},{16,20},{20,16},{24,28},{28,24},{1,5},{5... | collective-permute-start | bytes 1572872 | tf_op jit(solution)/shard_map/ppermute | solution.py:44
  28.7 5.7 %collective-permute-start.2 = (bf16[1568,128]{1,0:T(8,128)(2,1)S(1)}, bf16[1568,128]{1,0:T(8,128)(2,1)S(1)}, u32[]{:S(2)}, u32[]{:S(2)}) collective-permute-start(bf16[1568,128]{1,0:T(8,128)(2,1)S(1)} %slice.18), channel_id=1, source_target_pairs={{0,4},{4,0},{8,12},{12,8},{16,20},{20,16},{24,28},{28,24},{1,5},{5... | collective-permute-start | bytes 1204232 | tf_op jit(solution)/shard_map/ppermute | solution.py:44
  34.3 1.8 %collective-permute-start.11 = (bf16[1568,128]{1,0:T(8,128)(2,1)S(1)}, bf16[1568,128]{1,0:T(8,128)(2,1)S(1)}, u32[]{:S(2)}, u32[]{:S(2)}) collective-permute-start(bf16[1568,128]{1,0:T(8,128)(2,1)S(1)} %slice.15), channel_id=1, source_target_pairs={{0,4},{4,0},{8,12},{12,8},{16,20},{20,16},{24,28},{28,24},{1,5},{5... | collective-permute-start | bytes 1204232 | tf_op jit(solution)/shard_map/ppermute | solution.py:44
  41.0 4.7 %collective-permute-start.14 = (f32[8,512]{1,0:T(8,128)S(1)}, f32[8,512]{1,0:T(8,128)S(1)}, u32[]{:S(2)}, u32[]{:S(2)}) collective-permute-start(f32[8,512]{1,0:T(8,128)S(1)} %get-tuple-element.85.refs_0_), channel_id=1, source_target_pairs={{0,3},{1,2},{2,1},{3,0},{4,7},{5,6},{6,5},{7,4},{8,11},{9,10},{10,... | collective-permute-start | bytes 49160 | tf_op jit(solution)/shard_map/ppermute | solution.py:44
  44.6 3.5 %collective-permute-start.13 = (f32[8,512]{1,0:T(8,128)S(1)}, f32[8,512]{1,0:T(8,128)S(1)}, u32[]{:S(2)}, u32[]{:S(2)}) collective-permute-start(f32[8,512]{1,0:T(8,128)S(1)} %get-tuple-element.85.refs_0_), channel_id=1, source_target_pairs={{0,2},{1,3},{2,0},{3,1},{4,6},{5,7},{6,4},{7,5},{8,10},{9,11},{10,... | collective-permute-start | bytes 49160 | tf_op jit(solution)/shard_map/ppermute | solution.py:44
  44.8 3.3 %collective-permute-start.12 = (f32[8,512]{1,0:T(8,128)S(1)}, f32[8,512]{1,0:T(8,128)S(1)}, u32[]{:S(2)}, u32[]{:S(2)}) collective-permute-start(f32[8,512]{1,0:T(8,128)S(1)} %get-tuple-element.85.refs_0_), channel_id=1, source_target_pairs={{0,1},{1,0},{2,3},{3,2},{4,5},{5,4},{6,7},{7,6},{8,9},{9,8},{10,11... | collective-permute-start | bytes 49160 | tf_op jit(solution)/shard_map/ppermute | solution.py:44
  48.9 3.8 %collective-permute-start.19 = (bf16[2336,128]{1,0:T(8,128)(2,1)S(1)}, bf16[2336,128]{1,0:T(8,128)(2,1)S(1)}, u32[]{:S(2)}, u32[]{:S(2)}) collective-permute-start(bf16[2336,128]{1,0:T(8,128)(2,1)S(1)} %get-tuple-element.110), channel_id=1, source_target_pairs={{0,4},{4,0},{8,12},{12,8},{16,20},{20,16},{24,28},{28,24},{1,5},{5... | collective-permute-start | bytes 1794056 | tf_op jit(solution)/shard_map/ppermute | solution.py:44
  50.5 20.1 %copy-start.8 = (f32[2,512,128]{2,1,0:T(8,128)S(1)}, f32[2,512,128]{2,1,0:T(8,128)}, u32[]{:S(2)}) copy-start(f32[2,512,128]{2,1,0:T(8,128)} %param.40) | copy-start | bytes 1572868
  52.6 18.0 %copy-start.5 = (f32[8,64,512]{2,1,0:T(8,128)S(1)}, f32[8,64,512]{2,1,0:T(8,128)}, u32[]{:S(2)}) copy-start(f32[8,64,512]{2,1,0:T(8,128)} %refs_5_.1) | copy-start | bytes 3145732
  52.7 18.0 %copy-start.6 = (f32[8,64,512]{2,1,0:T(8,128)S(1)}, f32[8,64,512]{2,1,0:T(8,128)}, u32[]{:S(2)}) copy-start(f32[8,64,512]{2,1,0:T(8,128)} %refs_6_.1) | copy-start | bytes 3145732
  52.8 17.8 %copy-start.4 = (f32[8,64,512]{2,1,0:T(8,128)S(1)}, f32[8,64,512]{2,1,0:T(8,128)}, u32[]{:S(2)}) copy-start(f32[8,64,512]{2,1,0:T(8,128)} %refs_4_.1) | copy-start | bytes 3145732
  52.8 17.8 %copy-start.7 = (f32[2,512,128]{2,1,0:T(8,128)S(1)}, f32[2,512,128]{2,1,0:T(8,128)}, u32[]{:S(2)}) copy-start(f32[2,512,128]{2,1,0:T(8,128)} %param.39) | copy-start | bytes 1572868
  52.9 17.8 %copy-start.11 = (f32[8,512]{1,0:T(8,128)S(1)}, f32[8,512]{1,0:T(8,128)}, u32[]{:S(2)}) copy-start(f32[8,512]{1,0:T(8,128)} %refs_11_.5) | copy-start | bytes 49156
  52.9 17.8 %copy-start.12 = (f32[8,512]{1,0:T(8,128)S(1)}, f32[8,512]{1,0:T(8,128)}, u32[]{:S(2)}) copy-start(f32[8,512]{1,0:T(8,128)} %refs_12_.5) | copy-start | bytes 49156
  52.9 10.2 %collective-permute-start.20 = (bf16[2336,128]{1,0:T(8,128)(2,1)S(1)}, bf16[2336,128]{1,0:T(8,128)(2,1)S(1)}, u32[]{:S(2)}, u32[]{:S(2)}) collective-permute-start(bf16[2336,128]{1,0:T(8,128)(2,1)S(1)} %add_convert_fusion.2), channel_id=1, source_target_pairs={{0,8},{4,20},{8,0},{12,28},{16,24},{20,4},{24,16},{28,12},{1,9},{5... | collective-permute-start | bytes 1794056 | tf_op jit(solution)/shard_map/ppermute | solution.py:99
  54.2 1.2 %collective-permute-start.15 = (bf16[48,512]{1,0:T(8,128)(2,1)S(1)}, bf16[48,512]{1,0:T(8,128)(2,1)S(1)}, u32[]{:S(2)}, u32[]{:S(2)}) collective-permute-start(bf16[48,512]{1,0:T(8,128)(2,1)S(1)} %mapping_back.1), channel_id=1, source_target_pairs={{0,4},{4,0},{8,12},{12,8},{16,20},{20,16},{24,28},{28,24},{1,5},{5... | collective-permute-start | bytes 147464 | tf_op jit(solution)/shard_map/ppermute | solution.py:44
  55.5 4.9 %collective-permute-start.16 = (bf16[96,512]{1,0:T(8,128)(2,1)S(1)}, bf16[96,512]{1,0:T(8,128)(2,1)S(1)}, u32[]{:S(2)}, u32[]{:S(2)}) collective-permute-start(bf16[96,512]{1,0:T(8,128)(2,1)S(1)} %pad_maximum_fusion.1.refs_0_), channel_id=1, source_target_pairs={{0,16},{4,12},{8,24},{12,4},{16,0},{20,28},{24,8},{28,20},{1,17},{... | collective-permute-start | bytes 294920 | tf_op jit(solution)/shard_map/ppermute | solution.py:99
  63.3 11.5 %collective-permute-start.21 = (bf16[2336,128]{1,0:T(8,128)(2,1)S(1)}, bf16[2336,128]{1,0:T(8,128)(2,1)S(1)}, u32[]{:S(2)}, u32[]{:S(2)}) collective-permute-start(bf16[2336,128]{1,0:T(8,128)(2,1)S(1)} %add_convert_fusion.1), channel_id=1, source_target_pairs={{0,16},{4,12},{8,24},{12,4},{16,0},{20,28},{24,8},{28,20},{1,17},{... | collective-permute-start | bytes 1794056 | tf_op jit(solution)/shard_map/ppermute | solution.py:99
  64.6 2.1 %collective-permute-start.18 = (bf16[96,512]{1,0:T(8,128)(2,1)S(1)}, bf16[96,512]{1,0:T(8,128)(2,1)S(1)}, u32[]{:S(2)}, u32[]{:S(2)}) collective-permute-start(bf16[96,512]{1,0:T(8,128)(2,1)S(1)} %collective-permute-done.16.refs_1_), channel_id=1, source_target_pairs={{0,4},{4,0},{8,12},{12,8},{16,20},{20,16},{24,28},{28,24},{1,5},{5... | collective-permute-start | bytes 294920 | tf_op jit(solution)/shard_map/ppermute | solution.py:44
  65.8 4.8 %collective-permute-start.17 = (bf16[96,512]{1,0:T(8,128)(2,1)S(1)}, bf16[96,512]{1,0:T(8,128)(2,1)S(1)}, u32[]{:S(2)}, u32[]{:S(2)}) collective-permute-start(bf16[96,512]{1,0:T(8,128)(2,1)S(1)} %collective-permute-done.16.refs_1_), channel_id=1, source_target_pairs={{0,8},{4,20},{8,0},{12,28},{16,24},{20,4},{24,16},{28,12},{1,9},{5... | collective-permute-start | bytes 294920 | tf_op jit(solution)/shard_map/ppermute | solution.py:99
  75.0 3.7 %collective-permute-start.22 = (bf16[2336,128]{1,0:T(8,128)(2,1)S(1)}, bf16[2336,128]{1,0:T(8,128)(2,1)S(1)}, u32[]{:S(2)}, u32[]{:S(2)}) collective-permute-start(bf16[2336,128]{1,0:T(8,128)(2,1)S(1)} %add_convert_fusion.grad), channel_id=1, source_target_pairs={{0,4},{4,0},{8,12},{12,8},{16,20},{20,16},{24,28},{28,24},{1,5},{5... | collective-permute-start | bytes 1794056 | tf_op jit(solution)/shard_map/ppermute | solution.py:44
  (12 other events, 137.0 us)

commit v4 on v3

--- a/solution.py
+++ b/solution.py
@@ -273,32 +273,72 @@
     square[...] = total
 
 
-def main_kernel(n_ch, samples, side, *refs):
-    refs = list(refs)
-
-    def take(count):
-        got = refs[:count]
-        del refs[:count]
-        return got
-
-    (where,) = take(1)
-    both, first, first_pair, second, second_pair = take(5)
-    kernel, square_in = take(2)
-    aff_w, picked, bias, head, rgb_w = take(5)
-    unit, to_sum, small, aff_full = take(4)
-    bias_full, style_rows, late, late_tail, feat_t, padded, taps, shifted, wide = refs
+def bring_blocks(blocks, samples, side, where, picked, bias_full, style_rows, feat_t, aff_full, padded):
     width = aff_full.shape[0]
-    pixels = side * side
-    half = width // 2
+    half, pixels = width // 2, side * side
     dp, ch = where[0], where[1]
     pair = lax.rem(dp, 2)
     mine = pl.ds(pl.multiple_of(pair * half, half), half)
     other = pl.ds(pl.multiple_of((1 - pair) * half, half), half)
-
-    tail_rows = half + 16
-    feats = samples * pixels
+    chosen = picked[0].astype(BF16)
+    for source, top, tail_at, other_source, other_tail_at, k in blocks:
+        lane = pl.ds(pl.multiple_of(lax.bitwise_xor(ch, k) * LANES, LANES), LANES)
+        aff_full[mine, lane] = source[pl.ds(tail_at, half), :]
+        aff_full[other, lane] = other_source[pl.ds(other_tail_at, half), :]
+        bias_full[...] = source[pl.ds(tail_at + half, 16), :].astype(F32)
+        bias_row = bias_full[0:1, :] + bias_full[1:2, :] + bias_full[2:3, :]
+        style = (dot(chosen, aff_full[:, lane]) + bias_row).astype(BF16)
+        style_rows[:, lane] = style.astype(F32)
+        for s in range(samples):
+            value = source[pl.ds(top + s * pixels, pixels), :]
+            feat_t[s, lane, :] = value.T
+            padded[s, pl.ds(side, pixels), lane] = value * style[s : s + 1, :]
+
+
+def begin_kernel(n_ch, samples, side, *refs):
+    where, both, first, first_pair, kernel, picked = refs[:6]
+    feat_t, taps, style_rows, aff_full, bias_full, padded = refs[6:]
+    width = aff_full.shape[0]
+    half, pixels = width // 2, side * side
+    feats, tail_rows = samples * pixels, half + 16
     cut = first.shape[0] - first_pair.shape[0]
     partner_tail, partner_feats = feats + tail_rows, feats + 2 * tail_rows
+    pair = lax.rem(where[0], 2)
+    last = pl.ds(pl.multiple_of(lax.bitwise_xor(where[1], 3) * LANES, LANES), LANES)
+    for s in range(samples):
+        padded[s, pl.ds(0, side), :] = jnp.zeros((side, width), BF16)
+        padded[s, pl.ds(side + pixels, side), :] = jnp.zeros((side, width), BF16)
+        padded[s, pl.ds(side, pixels), last] = jnp.zeros((pixels, LANES), BF16)
+    style_rows[...] = jnp.zeros_like(style_rows)
+    blocks = (
+        (both, 0, feats, both, partner_tail, 0),
+        (first, 0, feats, first, partner_tail, 1 + pair),
+        (first_pair, partner_feats - cut, partner_tail - cut, first_pair, feats - cut, 2 - pair),
+    )
+    bring_blocks(
+        blocks, samples, side, where, picked, bias_full, style_rows, feat_t, aff_full, padded
+    )
+    chunk = min(256, pixels)
+    for s in range(samples):
+        for r in range(pixels // chunk):
+            total = dot(padded[s, pl.ds(r * chunk, chunk), :], kernel[0])
+            total = total + dot(padded[s, pl.ds(side + r * chunk, chunk), :], kernel[1])
+            total = total + dot(padded[s, pl.ds(2 * side + r * chunk, chunk), :], kernel[2])
+            taps[s, pl.ds(r * chunk, chunk), :] = total
+
+
+def main_kernel(n_ch, samples, side, *refs):
+    where, second, second_pair, earlier, kernel, square_in = refs[:6]
+    aff_w, picked, bias, head, rgb_w, counted = refs[6:12]
+    feat_t, style_rows, aff_full, wide, small, loss_rows = refs[15:21]
+    bias_full, late, late_tail, padded, taps = refs[21:]
+    width = aff_full.shape[0]
+    half, pixels = width // 2, side * side
+    feats, tail_rows = samples * pixels, half + 16
+    cut = second.shape[0] - second_pair.shape[0]
+    partner_tail, partner_feats = feats + tail_rows, feats + 2 * tail_rows
+    dp, ch = where[0], where[1]
+    pair = lax.rem(dp, 2)
     at_end = jnp.logical_or(ch == 0, ch == n_ch - 1)
     is_held = at_end == (pair == 1)
 
@@ -313,32 +353,26 @@
         late[pl.ds(feats, tail_rows), :] = second_pair[pl.ds(partner_tail - cut, tail_rows), :]
         late_tail[...] = second_pair[pl.ds(feats - cut, tail_rows), :]
 
-    blocks = []
-    for source, top, tail_at, other_source, other_tail_at, k in (
-        (both, 0, feats, both, partner_tail, 0),
-        (first, 0, feats, first, partner_tail, 1 + pair),
-        (first_pair, partner_feats - cut, partner_tail - cut, first_pair, feats - cut, 2 - pair),
-        (late, 0, feats, late_tail, 0, 3),
-    ):
-        at = pl.multiple_of(lax.bitwise_xor(ch, k) * LANES, LANES)
-        lane = pl.ds(at, LANES)
-        aff_full[mine, lane] = source[pl.ds(tail_at, half), :]
-        aff_full[other, lane] = other_source[pl.ds(other_tail_at, half), :]
-        bias_full[:, lane] = source[pl.ds(tail_at + half, 16), :]
-        for s in range(samples):
-            value = source[pl.ds(top + s * pixels, pixels), :]
-            feat_t[s, lane, :] = value.T
-        blocks.append((source, top, lane))
+    for s in range(samples):
+        padded[s, pl.ds(0, side), :] = jnp.zeros((side, LANES), BF16)
+        padded[s, pl.ds(side + pixels, side), :] = jnp.zeros((side, LANES), BF16)
+    mine = pl.ds(pl.multiple_of(pair * half, half), half)
+    other = pl.ds(pl.multiple_of((1 - pair) * half, half), half)
+    lane = pl.ds(pl.multiple_of(lax.bitwise_xor(ch, 3) * LANES, LANES), LANES)
+    aff_full[mine, lane] = late[pl.ds(feats, half), :]
+    aff_full[other, lane] = late_tail[pl.ds(0, half), :]
+    bias_full[...] = late[pl.ds(feats + half, 16), :].astype(F32)
+    bias_row = bias_full[0:1, :] + bias_full[1:2, :] + bias_full[2:3, :]
+    style = (dot(picked[0].astype(BF16), aff_full[:, lane]) + bias_row).astype(BF16)
+    style_rows[:, lane] = style.astype(F32)
+    for s in range(samples):
+        value = late[pl.ds(s * pixels, pixels), :]
+        feat_t[s, lane, :] = value.T
+        padded[s, pl.ds(side, pixels), :] = value * style[s : s + 1, :]
     square = square_in[...]
-
-    wide_bias = bias_full[...].astype(F32)
-    bias_row = wide_bias[0:1] + wide_bias[1:2] + wide_bias[2:3]
-    style0 = (dot(picked[0].astype(BF16), aff_full[...]) + bias_row).astype(BF16)
     colour_aff = aff_w[1].astype(BF16)
     style1 = dot(picked[1].astype(BF16), colour_aff) + bias[1:2, :]
-    style0_wide = style0.astype(F32)
     style1 = style1.astype(BF16).astype(F32)
-    colour_aff = colour_aff.astype(F32)
     colour = rgb_w[...].astype(BF16)
     colour_wide = colour.astype(F32)
     colour_rows = jnp.concatenate([colour_wide, jnp.zeros((13, LANES), F32)], axis=0).astype(BF16)
@@ -351,30 +385,24 @@
     column = lax.rem(lax.broadcasted_iota(jnp.int32, (chunk, LANES), 0), side)
     not_first, not_last = column > 0, column < side - 1
     small[...] = jnp.zeros_like(small)
-    to_sum[...] = jnp.zeros_like(to_sum)
-    padded[pl.ds(0, side), :] = jnp.zeros((side, width), BF16)
-    padded[pl.ds(side + pixels, side), :] = jnp.zeros((side, width), BF16)
+    loss_rows[...] = jnp.zeros_like(loss_rows)
     taps[pl.ds(0, 8), :] = jnp.zeros((8, 3 * LANES), F32)
     taps[pl.ds(8 + pixels, 8), :] = jnp.zeros((8, 3 * LANES), F32)
-    wide[pl.ds(0, 8), :] = jnp.zeros((8, LANES), F32)
-    wide[pl.ds(8 + pixels, 8), :] = jnp.zeros((8, LANES), F32)
 
     for s in range(samples):
-        style_rows[...] = style0_wide
-        for source, top, lane in blocks:
-            factor_row = style_rows[pl.ds(s, 1), lane].astype(BF16)
-            padded[pl.ds(side, pixels), lane] = (
-                source[pl.ds(top + s * pixels, pixels), :] * factor_row
-            )
-        style_col = jnp.broadcast_to(style0_wide[s : s + 1, :], (LANES, width)).T
+        wide[s, pl.ds(0, 8), :] = jnp.zeros((8, LANES), F32)
+        wide[s, pl.ds(8 + pixels, 8), :] = jnp.zeros((8, LANES), F32)
+        style_col = jnp.broadcast_to(style_rows[pl.ds(s, 1), :], (LANES, width)).T
         demod = lax.rsqrt(
             jnp.sum(style_col * style_col * square, axis=0, keepdims=True) + 1e-08
         )
         style_colour = style1[s : s + 1, :]
         for r in range(steps):
-            total = dot(padded[pl.ds(r * chunk, chunk), :], kernel[0])
-            total = total + dot(padded[pl.ds(side + r * chunk, chunk), :], kernel[1])
-            total = total + dot(padded[pl.ds(2 * side + r * chunk, chunk), :], kernel[2])
+            total = earlier[s, pl.ds(r * chunk, chunk), :]
+            for dy in range(3):
+                total = total + dot(
+                    padded[s, pl.ds(dy * side + r * chunk, chunk), :], kernel[dy, lane, :]
+                )
             taps[pl.ds(8 + r * chunk, chunk), :] = total
         mixed = jnp.zeros((3, LANES), F32)
         g_style1 = jnp.zeros((1, LANES), F32)
@@ -395,12 +423,36 @@
             g_scaled = g_act * style_colour * (sig * (1.0 + scaled * (1.0 - sig)))
             g_bias = g_bias + jnp.sum(g_scaled, axis=0, keepdims=True)
             g_demod = g_demod + jnp.sum(g_scaled * conv_out, axis=0, keepdims=True)
-            wide[pl.ds(8 + r * chunk, chunk), :] = g_scaled * demod
+            wide[s, pl.ds(8 + r * chunk, chunk), :] = g_scaled * demod
+        logit = jnp.sum(
+            jnp.sum(mixed * colour_wide, axis=0, keepdims=True), axis=1, keepdims=True
+        )
+        loss_rows[pl.ds(s, 1), :] = jnp.broadcast_to(logit, (1, LANES))
+        loss_rows[pl.ds(4 * samples + s, 1), :] = jnp.full((1, LANES), counted[s], jnp.int32).astype(F32)
+        small[pl.ds(8 * s, 1), :] = g_style1
+        small[pl.ds(8 * s + 1, 1), :] = g_bias
+        small[pl.ds(8 * s + 2, 3), :] = mixed
+        small[pl.ds(8 * s + 5, 1), :] = g_demod * demod * demod * demod
+
+
+def factor_kernel(samples, side, where, feat_t, wide, small, style_rows, kernel, aff_w, unit, to_sum, shifted):
+    width = feat_t.shape[1]
+    pixels = side * side
+    pair = lax.rem(where[0], 2)
+    half = TAPS * width // 2
+    chunk = min(256, pixels)
+    steps = pixels // chunk
+    column = lax.rem(lax.broadcasted_iota(jnp.int32, (chunk, LANES), 0), side)
+    not_first, not_last = column > 0, column < side - 1
+    to_sum[...] = jnp.zeros_like(to_sum)
+    colour_aff = aff_w[1].astype(BF16).astype(F32)
+    for s in range(samples):
+        style_col = jnp.broadcast_to(style_rows[pl.ds(s, 1), :], (LANES, width)).T
         for r in range(steps):
-            before = jnp.where(not_last, wide[pl.ds(9 + r * chunk, chunk), :], 0.0)
-            centre = wide[pl.ds(8 + r * chunk, chunk), :]
-            after = jnp.where(not_first, wide[pl.ds(7 + r * chunk, chunk), :], 0.0)
-            for dx, value in enumerate((before, centre, after)):
+            before = jnp.where(not_last, wide[s, pl.ds(9 + r * chunk, chunk), :], 0.0)
+            centre = wide[s, pl.ds(8 + r * chunk, chunk), :]
+            after_it = jnp.where(not_first, wide[s, pl.ds(7 + r * chunk, chunk), :], 0.0)
+            for dx, value in enumerate((before, centre, after_it)):
                 value = value.astype(BF16)
                 for dy in range(3):
                     lane = pl.ds((3 * dy + dx) * LANES, LANES)
@@ -410,13 +462,10 @@
                         low_at - start : high_at - start, :
                     ]
         for dx in range(3):
-            shifted[pl.ds(pixels - side, side), pl.ds(dx * LANES, LANES)] = jnp.zeros(
-                (side, LANES), BF16
-            )
-            shifted[pl.ds(0, side), pl.ds((6 + dx) * LANES, LANES)] = jnp.zeros(
-                (side, LANES), BF16
-            )
-        factor = g_demod * demod * demod * demod
+            blank = jnp.zeros((side, LANES), BF16)
+            shifted[pl.ds(pixels - side, side), pl.ds(dx * LANES, LANES)] = blank
+            shifted[pl.ds(0, side), pl.ds((6 + dx) * LANES, LANES)] = blank
+        factor = small[pl.ds(8 * s + 5, 1), :]
         g_style = jnp.zeros((width, LANES), F32)
         for first in range(0, TAPS, 2):
             count = min(2, TAPS - first)
@@ -426,18 +475,19 @@
                 weight = kernel[tap // 3, :, pl.ds((tap % 3) * LANES, LANES)].astype(F32)
                 inner = raw - style_col * (weight * factor)
                 g_style = g_style + weight * inner
-                unit[s, pl.ds(tap * width, width), :] = (style_col * inner).astype(BF16)
-        g_style_row = jnp.sum(g_style.T, axis=0, keepdims=True)
-        g_colour_row = jnp.sum((colour_aff * g_style1).T, axis=0, keepdims=True)
-        logit = jnp.sum(
-            jnp.sum(mixed * colour_wide, axis=0, keepdims=True), axis=1, keepdims=True
-        )
-        to_sum[pl.ds(8 * s, 1), :] = jnp.broadcast_to(logit, (1, width))
-        to_sum[pl.ds(8 * s + 1, 1), :] = g_style_row
-        to_sum[pl.ds(8 * s + 2, 1), :] = g_colour_row
-        small[pl.ds(8 * s, 1), :] = g_style1
-        small[pl.ds(8 * s + 1, 1), :] = g_bias
-        small[pl.ds(8 * s + 2, 3), :] = mixed
+                value = (style_col * inner).astype(BF16)
+                top = tap * width
+                for h in range(2):
+                    low_at, high_at = max(top, h * half), min(top + width, (h + 1) * half)
+                    if low_at < high_at:
+                        slot = 1 - pair if h else pair
+                        unit[s, slot, pl.ds(low_at - h * half, high_at - low_at), :] = value[
+                            low_at - top : high_at - top, :
+                        ]
+        for at, value in ((0, g_style), (4, colour_aff * small[pl.ds(8 * s, 1), :])):
+            row = jnp.sum(value.T, axis=0, keepdims=True)
+            for part in range(width // LANES):
+                to_sum[pl.ds(8 * s + at + part, 1), :] = row[:, part * LANES : (part + 1) * LANES]
 
 
 def summed(parts, row):
@@ -447,30 +497,30 @@
     return values[0]
 
 
-def logit_grad(parts, counted, s):
-    logit = summed(parts, 8 * s)
-    mask = jnp.full(logit.shape, counted[s], jnp.int32).astype(F32)
+def logit_grad(parts, masks, samples, s):
+    at = 4 * samples * (s // samples) + s % samples
+    logit = summed(parts, 8 * samples + at)
+    mask = masks[pl.ds(at, 1), :]
     return -mask * jax.nn.sigmoid(-logit), mask * jax.nn.softplus(-logit), mask
 
 
-def scale_kernel(n_ch, samples, where, counted, *refs):
-    parts, (unit, kept, sent) = refs[:n_ch], refs[n_ch:]
-    pair = lax.rem(where[0], 2)
-    half = unit.shape[1] // 2
+def combine_kernel(n_ch, samples, *refs):
+    parts, (masks, unit, unit_pair, out) = refs[:n_ch], refs[n_ch:]
+    half = unit_pair.shape[1]
     grads, total = [], jnp.zeros((1, LANES), F32)
-    for s in range(samples):
-        grad, _, mask = logit_grad(parts, counted, s)
-        grads.append(grad[:, :LANES])
-        total = total + mask[:, :LANES]
+    for s in range(2 * samples):
+        grad, _, mask = logit_grad(parts, masks, samples, s)
+        grads.append(grad)
+        total = total + mask
     block = half // 9
-    for out, owner in ((kept, pair), (sent, 1 - pair)):
-        for b in range(9):
-            at = pl.multiple_of(owner * half + b * block, block)
-            value = grads[0] * unit[0, pl.ds(at, block), :].astype(F32)
-            for s in range(1, samples):
-                value = value + grads[s] * unit[s, pl.ds(at, block), :].astype(F32)
-            out[pl.ds(b * block, block), :] = value.astype(BF16)
-        out[pl.ds(half, COUNT_ROWS), :] = jnp.broadcast_to(total, (COUNT_ROWS, LANES)).astype(BF16)
+    for b in range(9):
+        here = pl.ds(b * block, block)
+        value = jnp.zeros((block, LANES), F32)
+        for s in range(samples):
+            value = value + grads[s] * unit[s, 0, here, :].astype(F32)
+            value = value + grads[samples + s] * unit_pair[s, here, :].astype(F32)
+        out[here, :] = value.astype(BF16)
+    out[pl.ds(half, COUNT_ROWS), :] = jnp.broadcast_to(total, (COUNT_ROWS, LANES)).astype(BF16)
 
 
 def pack_places(samples, layers):
@@ -481,14 +531,18 @@
     return style, colour, w_total, -(-(w_total + 3) // 16) * 16
 
 
-def mapping_back_kernel(n_ch, samples, where, counted, crossover, *refs):
+def mapping_back_kernel(n_ch, samples, where, crossover, *refs):
     parts = refs[:n_ch]
-    pre, hid, top, picked, small, map_full, aff_full, pack_out, rows, pack = refs[n_ch:]
+    masks, pre, hid, top, picked, small, map_full, aff_full, pack_out, rows, pack = refs[n_ch:]
     layers, _, width = map_full.shape
     latents = 2 * samples
     style_at, colour_at, w_at, _ = pack_places(samples, layers)
     ch = where[1]
-    grads = [logit_grad(parts, counted, s) for s in range(samples)]
+    grads = [logit_grad(parts, masks, samples, s) for s in range(samples)]
+
+    def wide_sum(at):
+        return jnp.concatenate([summed(parts, at + part) for part in range(width // LANES)], axis=1)
+
     pack[...] = jnp.zeros_like(pack)
 
     def put(line, lane, size, value, count):
@@ -499,15 +553,15 @@
     half_lane = lax.broadcasted_iota(jnp.int32, (1, LANES), 1) < LANES // 2
     for s in range(samples):
         grad = grads[s][0]
-        style_row = grad * summed(parts, 8 * s + 1)
+        style_row = grad[:, :1] * wide_sum(8 * s)
         rows[pl.ds(s, 1), :] = style_row
         style_rows.append(style_row)
         own = rows[pl.ds(s, 1), pl.ds(pl.multiple_of(ch * LANES, LANES), LANES)]
-        short = grad[:, :LANES]
+        short = grad
         put(style_at + 2 * s, 0, LANES, own, 2)
         put(style_at + 2 * s, LANES, LANES, short * small[pl.ds(8 * s, 1), :], 2)
         put(style_at + 2 * s, 2 * LANES, LANES, short * small[pl.ds(8 * s + 1, 1), :], 2)
-        loss_count = jnp.where(half_lane, grads[s][1][:, :LANES], grads[s][2][:, :LANES])
+        loss_count = jnp.where(half_lane, grads[s][1], grads[s][2])
         put(style_at + 2 * s, 3 * LANES, LANES, loss_count, 2)
         for c in range(3):
             value = short * small[pl.ds(8 * s + 2 + c, 1), :]
@@ -531,7 +585,7 @@
     g_rows = []
     for s in range(samples):
         conv_row = from_conv[s : s + 1, :]
-        colour_row = grads[s][0] * summed(parts, 8 * s + 2)
+        colour_row = grads[s][0][:, :1] * wide_sum(8 * s + 4)
         to_first = [jnp.full((1, width), crossover[s], jnp.int32) > j for j in range(2)]
         g_rows.append(
             jnp.where(to_first[0], conv_row, 0.0) + jnp.where(to_first[1], colour_row, 0.0)
@@ -554,114 +608,133 @@
     packs, refs = refs[: len(places)], refs[len(places) :]
     (map_w, map_m, map_e, aff_w, aff_m, aff_e) = refs[:6]
     (map_b, map_bm, map_be, bias, bias_m, bias_e, rgb, rgb_m, rgb_e, w_avg) = refs[6:16]
-    outs, scratch = refs[16:-7], refs[-7:]
+    outs, refs = refs[16:39], refs[39:]
+    map_new, aff_new, map_b_new, bias_new, rgb_new = (refs[4 * i : 4 * i + 4] for i in range(5))
+    w_avg_new, loss_new, count_new, g_pre, hid, extra, sems = refs[20:]
     map_outs, aff_outs = outs[0:4], outs[4:8]
     map_b_outs, bias_outs, rgb_outs = outs[8:12], outs[12:16], outs[16:20]
     w_avg_out, loss_out, count_out = outs[20:23]
-    g_pre, hid, picked, style, rgb_all, sums, w_sums = scratch
     latents = 2 * samples
+    depth = layers * latents
     style_at, colour_at, w_at, lines = pack_places(samples, layers)
-    every = n_dp * latents
+    style_at, colour_at, w_at = (at - 2 * depth for at in (style_at, colour_at, w_at))
+    more = lines - 2 * depth
     dp = where[0]
-    step = pl.program_id(0)
-    share = map_w.shape[1]
-    width = map_w.shape[2]
-
-    @pl.when(step == 0)
-    def _():
-        odd = lax.rem(dp, 2)
-        for part, place in zip(packs, places):
-            for index, (even_k, odd_k) in enumerate(place):
-                owner = lax.bitwise_xor(dp, jnp.where(odd == 1, odd_k, even_k))
-                got = part[pl.ds(index * lines, lines), :].astype(F32)
-                for layer in range(layers):
-                    for n in range(latents):
-                        at = pl.ds(owner * latents + n, 1)
-                        line = layer * latents + n
-                        g_pre[layer, at, :] = got[line : line + 1]
-                        line += layers * latents
-                        hid[layer, at, :] = got[line : line + 1]
-                for s in range(samples):
-                    at = pl.ds(owner * samples + s, 1)
-                    line = 2 * layers * latents + 2 * s
-                    for j in range(2):
-                        picked[j, at, :] = got[line + j : line + j + 1]
-                    line = style_at + 2 * s
-                    style[at, :] = got[line : line + 1] + got[line + 1 : line + 2]
-                    line = colour_at + 2 * s
-                    rgb_all[at, :] = got[line : line + 1] + got[line + 1 : line + 2]
-                w_sums[pl.ds(owner, 1), :] = (
-                    got[w_at : w_at + 1] + got[w_at + 1 : w_at + 2] + got[w_at + 2 : w_at + 3]
-                )
-        sums[pl.ds(0, 1), :] = jnp.sum(style[...], axis=0, keepdims=True)
-        sums[pl.ds(1, 1), :] = jnp.sum(rgb_all[...], axis=0, keepdims=True)
-        total = sums[pl.ds(0, 1), :]
-        count = total[:, width - LANES // 2 : width - LANES // 2 + 1]
-        inverse = 1.0 / count
-        for layer in range(layers):
-            grad = jnp.sum(g_pre[layer], axis=0, keepdims=True) * inverse
-            row = pl.ds(layer, 1)
-            new = advance(map_b[row, :], map_bm[row, :], map_be[row, :], grad, 30.0)
-            for out, value in zip(map_b_outs[:3], new[:3]):
-                out[row, :] = value
-        map_b_outs[3][...] = map_b_outs[0][...].astype(BF16)
-        colour = sums[pl.ds(1, 1), :]
-        for c in range(3):
-            row = pl.ds(c, 1)
-            lane = slice(c * LANES, (c + 1) * LANES)
-            new = advance(bias[row, :], bias_m[row, :], bias_e[row, :], total[:, lane] * inverse, 50.0)
-            for out, value in zip(bias_outs[:3], new[:3]):
-                out[row, :] = value
-            new = advance(rgb[row, :], rgb_m[row, :], rgb_e[row, :], colour[:, lane] * inverse, 1.0)
-            for out, value in zip(rgb_outs[:3], new[:3]):
-                out[row, :] = value
-        bias_outs[3][...] = bias_outs[0][...].astype(BF16)
-        rgb_outs[3][...] = rgb_outs[0][...].astype(BF16)
-        mean = jnp.sum(w_sums[...], axis=0, keepdims=True) * (1.0 / every)
-        w_avg_out[...] = w_avg[...] + (1.0 - AVERAGE_BETA) * (mean - w_avg[...])
-        loss_out[0] = jnp.sum(total[:, width - LANES : width - LANES + 1])
-        count_out[0] = jnp.sum(count)
-
-    count = sums[pl.ds(0, 1), pl.ds(width - LANES, LANES)][:, LANES // 2 : LANES // 2 + 1]
+    share, width = map_w.shape[1:]
+
+    odd = lax.rem(dp, 2)
+    for part, place in zip(packs, places):
+        for index, (even_k, odd_k) in enumerate(place):
+            owner = lax.bitwise_xor(dp, jnp.where(odd == 1, odd_k, even_k))
+            top = index * lines
+            for target, start, size in ((g_pre, 0, depth), (hid, depth, depth), (extra, 2 * depth, more)):
+                at = pl.multiple_of(owner * size, size)
+                target[pl.ds(at, size), :] = part[pl.ds(top + start, size), :]
+    every = extra[...].astype(F32)
+    kind = lax.rem(lax.broadcasted_iota(jnp.int32, every.shape, 0), more)
+
+    def total_of(first, count):
+        chosen = jnp.logical_and(kind >= first, kind < first + count)
+        return jnp.sum(jnp.where(chosen, every, 0.0), axis=0, keepdims=True)
+
+    total = total_of(style_at, 2 * samples)
+    count = total[:, width - LANES // 2 : width - LANES // 2 + 1]
     inverse = 1.0 / count
-    each = map_outs[0].shape[0]
-    for index in range(each):
-        layer = step * each + index
-        own = pltpu.roll(hid[layer], lax.rem(width - dp * share, width), 1)[:, :LANES]
-        grad = dot_tn(own.astype(BF16), g_pre[layer].astype(BF16))[0:share] * inverse
-        new = advance(map_w[layer], map_m[layer], map_e[layer], grad, 30.0)
-        for out, value in zip(map_outs, new):
-            out[index] = value
-    chosen = jnp.concatenate([picked[step]] * 2, axis=0)
-    grad_style = style[:, pl.ds(pl.multiple_of(step * LANES, LANES), LANES)]
-    split = jnp.concatenate([p.astype(F32) for p in pieces(grad_style, 2)], axis=0)
-    grad = dot_tn(chosen.astype(BF16), split.astype(BF16)) * inverse
-    here = pl.ds(pl.multiple_of(step * width, width), width)
-    new = advance(aff_w[here, :], aff_m[here, :], aff_e[here, :], grad, 30.0)
-    for out, value in zip(aff_outs, new):
-        out[...] = value
-
-
-def conv_kernel(mine, where, grad, param, moment, average, *refs):
-    refs = refs if mine else refs[4:]
-    outs, buffers, sems = refs[0:4], refs[4:8], refs[8]
-    half = grad.shape[0] - COUNT_ROWS
-    pair = lax.rem(where[0], 2)
-    start = pl.multiple_of((pair if mine else 1 - pair) * half, half)
-    inverse = 1.0 / grad[pl.ds(half, 16), :].astype(F32)[0:1]
-    chunks = sems.shape[0]
-    depth = half // chunks
     copies = []
-    for c in range(chunks):
-        here = pl.ds(c * depth, depth)
-        there = pl.ds(pl.multiple_of(start + c * depth, depth), depth)
-        value = grad[here, :].astype(F32) * inverse
-        new = advance(param[there, :], moment[there, :], average[there, :], value, 5.0)
-        for k in range(4):
-            buffers[k][here, :] = new[k]
-            copy = pltpu.make_async_copy(buffers[k].at[here, :], outs[k].at[there, :], sems.at[c, k])
+
+    def send(buffers, targets, at, sem):
+        for k, (buffer, target) in enumerate(zip(buffers, targets)):
+            if at is not None:
+                buffer, target = buffer.at[at], target.at[at]
+            copy = pltpu.make_async_copy(buffer, target, sems.at[sem, k])
             copy.start()
             copies.append(copy)
+
+    colour = total_of(colour_at, 2 * samples)
+    for c in range(3):
+        row = pl.ds(c, 1)
+        lane = slice(c * LANES, (c + 1) * LANES)
+        new = advance(bias[row, :], bias_m[row, :], bias_e[row, :], total[:, lane] * inverse, 50.0)
+        for out, value in zip(bias_new[:3], new[:3]):
+            out[row, :] = value
+        new = advance(rgb[row, :], rgb_m[row, :], rgb_e[row, :], colour[:, lane] * inverse, 1.0)
+        for out, value in zip(rgb_new[:3], new[:3]):
+            out[row, :] = value
+    bias_new[3][...] = bias_new[0][...].astype(BF16)
+    rgb_new[3][...] = rgb_new[0][...].astype(BF16)
+    mean = total_of(w_at, 3) * (1.0 / (n_dp * latents))
+    w_avg_new[...] = w_avg[...] + (1.0 - AVERAGE_BETA) * (mean - w_avg[...])
+    loss_new[0] = jnp.sum(total[:, width - LANES : width - LANES + 1])
+    count_new[0] = jnp.sum(count)
+    send(bias_new, bias_outs, None, layers // 2 + 2)
+    send(rgb_new, rgb_outs, None, layers // 2 + 3)
+    send((w_avg_new, loss_new, count_new), (w_avg_out, loss_out, count_out), None, layers // 2 + 4)
+
+    own = pltpu.roll(hid[...].astype(F32), lax.rem(width - dp * share, width), 1)[:, :LANES]
+    lane = lax.broadcasted_iota(jnp.int32, own.shape, 1)
+    own = jnp.where(lane < share, own, jnp.where(lane == share, 1.0, 0.0))
+    layer_of = lax.rem(lax.broadcasted_iota(jnp.int32, own.shape, 0), depth) // latents
+    for layer in range(layers):
+        mine = jnp.where(layer_of == layer, own, 0.0).astype(BF16)
+        grads = dot_tn(mine, g_pre[...]) * inverse
+        new = advance(map_w[layer], map_m[layer], map_e[layer], grads[0:share], 30.0)
+        for out, value in zip(map_new, new):
+            out[layer] = value
+        row = pl.ds(layer, 1)
+        new = advance(
+            map_b[row, :], map_bm[row, :], map_be[row, :], grads[share : share + 1], 30.0
+        )
+        for out, value in zip(map_b_new[:3], new[:3]):
+            out[row, :] = value
+        if layer % 2:
+            send(map_new, map_outs, pl.ds(layer - 1, 2), layer // 2)
+    map_b_new[3][...] = map_b_new[0][...].astype(BF16)
+    send(map_b_new, map_b_outs, None, layers // 2 + 5)
+    for j in range(2):
+        chosen = jnp.zeros(every.shape, F32)
+        for piece in range(2):
+            here = jnp.logical_and(kind >= style_at, kind < style_at + 2 * samples)
+            here = jnp.logical_and(here, lax.rem(kind - style_at + 2, 2) == piece)
+            moved = pltpu.roll(every, style_at + piece - j, 0)
+            chosen = jnp.where(here, moved, chosen)
+        grad = dot_tn(chosen.astype(BF16), extra[:, pl.ds(j * LANES, LANES)]) * inverse
+        here = pl.ds(j * width, width)
+        new = advance(aff_w[here, :], aff_m[here, :], aff_e[here, :], grad, 30.0)
+        for out, value in zip(aff_new, new):
+            out[here, :] = value
+        send(aff_new, aff_outs, here, layers // 2 + j)
+    for copy in copies:
+        copy.wait()
+
+
+def conv_kernel(turns, where, *refs):
+    grads, refs = refs[: len(turns)], refs[len(turns) :]
+    param, moment, average = refs[:3]
+    outs, buffers, sems = refs[-9:-5], refs[-5:-1], refs[-1]
+    half = grads[0].shape[0] - COUNT_ROWS
+    depth = half // 9
+    pair = lax.rem(where[0], 2)
+    copies, at = [], 0
+    for turn, (grad, (mine, ninths)) in enumerate(zip(grads, turns)):
+        start = pl.multiple_of((pair if mine else 1 - pair) * half, half)
+        inverse = 1.0 / grad[pl.ds(half, 16), :].astype(F32)[0:1]
+        for n in ninths:
+            here = pl.ds(at * depth, depth)
+            there = pl.ds(pl.multiple_of(start + n * depth, depth), depth)
+            at += 1
+            value = grad[pl.ds(n * depth, depth), :].astype(F32) * inverse
+            new = advance(param[there, :], moment[there, :], average[there, :], value, 5.0)
+            for k in range(4):
+                buffers[k][here, :] = new[k]
+            if n % 3 == 2:
+                for k in range(4):
+                    copy = pltpu.make_async_copy(
+                        buffers[k].at[pl.ds((at - 3) * depth, 3 * depth), :],
+                        outs[k].at[pl.ds(pl.multiple_of(start + (n - 2) * depth, depth), 3 * depth), :],
+                        sems.at[at // 3 - 1, k],
+                    )
+                    copy.start()
+                    copies.append(copy)
     for copy in copies:
         copy.wait()
 
@@ -766,34 +839,54 @@
         name="mapping",
     )(where, seeds.reshape(-1), crossover, *[block for block, _ in blocks], *hbm(z_table), map_b)
 
-    chan_packs += [second, swap(after(second, picked)[samples * pixels :], "dp", 1)]
-    unit, to_sum, small, aff_full = pl.pallas_call(
+    both, first, first_pair = chan_packs
+    feat_t, taps, style_rows, aff_full = pl.pallas_call(
+        functools.partial(begin_kernel, n_ch, samples, side),
+        out_shape=(
+            shape((samples, width, pixels), BF16),
+            shape((samples, pixels, 3 * LANES), F32),
+            shape((8, width), F32),
+            shape((width, width), BF16),
+        ),
+        in_specs=[SMEM] + [VMEM] * 5,
+        out_specs=(VMEM,) * 4,
+        scratch_shapes=[
+            pltpu.VMEM((16, LANES), F32),
+            pltpu.VMEM((samples, pixels + 2 * side, width), BF16),
+        ],
+        compiler_params=params(16),
+        cost_estimate=cost(3),
+        name="begin",
+    )(where, both, first, first_pair, kernel, picked)
+    second_pair = swap(after(second, taps)[samples * pixels :], "dp", 1)
+    feat_t, style_rows, aff_full, wide, small, loss_rows = pl.pallas_call(
         functools.partial(main_kernel, n_ch, samples, side),
         out_shape=(
-            shape((samples, TAPS * width, LANES), BF16),
-            shape((8 * samples, width), F32),
+            shape((samples, width, pixels), BF16),
+            shape((8, width), F32),
+            shape((width, width), BF16),
+            shape((samples, pixels + 16, LANES), F32),
             shape((8 * samples, LANES), F32),
-            shape((width, width), BF16),
+            shape((8 * samples, LANES), F32),
         ),
-        in_specs=[SMEM] + [VMEM] * 12,
-        out_specs=(VMEM,) * 4,
+        in_specs=[SMEM] + [VMEM] * 10 + [SMEM] + [VMEM] * 3,
+        out_specs=(VMEM,) * 6,
         scratch_shapes=[
-            pltpu.VMEM((16, width), BF16),
-            pltpu.VMEM((8, width), F32),
+            pltpu.VMEM((16, LANES), F32),
             pltpu.VMEM((pack_rows, LANES), BF16),
             pltpu.VMEM((half + 16, LANES), BF16),
-            pltpu.VMEM((samples, width, pixels), BF16),
-            pltpu.VMEM((pixels + 2 * side, width), BF16),
+            pltpu.VMEM((samples, pixels + 2 * side, LANES), BF16),
             pltpu.VMEM((pixels + 16, 3 * LANES), F32),
-            pltpu.VMEM((pixels, TAPS * LANES), BF16),
-            pltpu.VMEM((pixels + 16, LANES), F32),
         ],
+        input_output_aliases={12: 0, 13: 1, 14: 2},
         compiler_params=params(20),
-        cost_estimate=cost(8),
+        cost_estimate=cost(3),
         name="main",
     )(
         where,
-        *chan_packs,
+        second,
+        second_pair,
+        taps,
         kernel,
         square,
         aff_w,
@@ -801,37 +894,55 @@
         chan_bias,
         head,
         rgb_w,
+        counted,
+        feat_t,
+        style_rows,
+        aff_full,
     )
-
-    sum_parts = spread_direct(to_sum, "chan")
+    pair_losses = swap(loss_rows, "dp", 1)
+    unit, to_sum = pl.pallas_call(
+        functools.partial(factor_kernel, samples, side),
+        out_shape=(
+            shape((samples, 2, TAPS * width // 2, LANES), BF16),
+            shape((8 * samples, LANES), F32),
+        ),
+        in_specs=[SMEM] + [VMEM] * 6,
+        out_specs=(VMEM,) * 2,
+        scratch_shapes=[pltpu.VMEM((pixels, TAPS * LANES), BF16)],
+        compiler_params=params(16),
+        cost_estimate=cost(2),
+        name="factor",
+    )(where, feat_t, wide, small, style_rows, kernel, aff_w)
+    unit_pair = swap(unit[:, 1], "dp", 1)
+
+    to_send = jnp.concatenate([to_sum, loss_rows[:4 * samples], pair_losses[:4 * samples]])
+    sum_parts = spread_direct(to_send, "chan")
+    masks = jnp.concatenate([loss_rows[4 * samples:], pair_losses[4 * samples:]])
     half_rows = TAPS * width // 2 + COUNT_ROWS
-    kept, sent = pl.pallas_call(
-        functools.partial(scale_kernel, n_ch, samples),
-        out_shape=(shape((half_rows, LANES), BF16),) * 2,
-        in_specs=[SMEM] * 2 + [VMEM] * (n_ch + 1),
-        out_specs=(VMEM, VMEM),
+    total = pl.pallas_call(
+        functools.partial(combine_kernel, n_ch, samples),
+        out_shape=shape((half_rows, LANES), BF16),
+        in_specs=[VMEM] * (n_ch + 3),
+        out_specs=VMEM,
         compiler_params=params(8),
         cost_estimate=cost(1),
-        name="scale",
-    )(where, counted, *sum_parts, unit)
+        name="combine",
+    )(*sum_parts, masks, unit, unit_pair)
 
     lines = pack_places(samples, layers)[-1]
     pack = pl.pallas_call(
         functools.partial(mapping_back_kernel, n_ch, samples),
         out_shape=shape((lines, width), BF16),
-        in_specs=[SMEM] * 3 + [VMEM] * (n_ch + 7),
+        in_specs=[SMEM] * 2 + [VMEM] * (n_ch + 8),
         out_specs=VMEM,
         scratch_shapes=[pltpu.VMEM((8, width), F32), pltpu.VMEM((lines, width), F32)],
         compiler_params=params(12),
         cost_estimate=cost(2),
         name="mapping_back",
-    )(where, counted, crossover, *sum_parts, pre, hid, top, picked, small, map_full, aff_full)
+    )(where, crossover, *after(sum_parts, total), masks, pre, hid, top, picked, small, map_full, aff_full)
     spread_pack = spread(pack, "dp")
     packs = [part for part, _ in spread_pack]
 
-    whole = lambda a: pl.BlockSpec(a.shape, lambda i: (0,) * len(a.shape))
-    map_spec = pl.BlockSpec((layers // 2, share, width), lambda i: (i, 0, 0))
-    aff_spec = pl.BlockSpec((width, LANES), lambda i: (i, 0))
     flat_aff = [a.reshape(2 * width, LANES) for a in (aff_w, aff_w_mom, aff_w_ema)]
     tiny = [
         map_b,
@@ -854,34 +965,26 @@
         + [shape(rgb_w.shape, t) for t in types]
         + [shape((1, width), F32), shape((1,), F32), shape((1,), F32)]
     )
-    every = n_dp * latents
+    depth = layers * latents
     update = lambda: pl.pallas_call(
         functools.partial(update_kernel, n_dp, samples, layers, [p for _, p in spread_pack]),
-        grid=(2,),
         out_shape=out_shape,
-        in_specs=[SMEM]
-        + [VMEM] * len(packs)
-        + [VMEM] * (6 + len(tiny)),
-        out_specs=[map_spec] * 4
-        + [aff_spec] * 4
-        + [whole(s) for s in out_shape[8:21]]
-        + [SMEM, SMEM],
-        scratch_shapes=[
-            pltpu.VMEM((layers, every, width), F32),
-            pltpu.VMEM((layers, every, width), F32),
-            pltpu.VMEM((2, n_dp * samples, width), F32),
-            pltpu.VMEM((n_dp * samples, width), F32),
-            pltpu.VMEM((n_dp * samples, width), F32),
-            pltpu.VMEM((8, width), F32),
-            pltpu.VMEM((n_dp, width), F32),
+        in_specs=[SMEM] + [VMEM] * (len(packs) + 6 + len(tiny)),
+        out_specs=[ANY] * 23,
+        scratch_shapes=[pltpu.VMEM(s.shape, s.dtype) for s in out_shape[:21]]
+        + [
+            pltpu.SMEM((1,), F32),
+            pltpu.SMEM((1,), F32),
+            pltpu.VMEM((n_dp * depth, width), BF16),
+            pltpu.VMEM((n_dp * depth, width), BF16),
+            pltpu.VMEM((n_dp * (lines - 2 * depth), width), BF16),
+            pltpu.SemaphoreType.DMA((layers // 2 + 6, 4)),
         ],
         compiler_params=params(20),
-        cost_estimate=cost(5),
+        cost_estimate=cost(4),
         name="update",
     )(where, *packs, map_w, map_w_mom, map_w_ema, *flat_aff, *tiny)
 
-    got = after(swap(sent, "dp", 1), pack)
-    total = (kept.astype(F32) + got.astype(F32)).astype(BF16)
     bits = [1 << b for b in range(1, n_dp.bit_length() - 1)]
     for turn, (even_bit, odd_bit) in enumerate(zip(bits, bits[::-1])):
         got = crossed(total, "dp", even_bit, odd_bit)
@@ -894,23 +997,24 @@
     other = swap(total, "dp", 1)
 
     conv_params = [flat(conv_w), flat(conv_w_mom), flat(conv_w_ema)]
-    half_rows = TAPS * width // 2
-
-    def conv_half(grad, *earlier):
+
+    def conv_part(turns, grads, earlier):
+        ninths = sum(len(n) for _, n in turns)
         return pl.pallas_call(
-            functools.partial(conv_kernel, not earlier),
+            functools.partial(conv_kernel, turns),
             out_shape=[shape((TAPS * width, LANES), t) for t in types],
-            in_specs=[SMEM] + [VMEM] * 4 + [ANY] * len(earlier),
+            in_specs=[SMEM] + [VMEM] * (len(grads) + 3) + [ANY] * len(earlier),
             out_specs=[ANY] * 4,
-            scratch_shapes=[pltpu.VMEM((half_rows, LANES), t) for t in types]
-            + [pltpu.SemaphoreType.DMA((3, 4))],
-            input_output_aliases={5 + k: k for k in range(len(earlier))},
-            compiler_params=params(12),
+            scratch_shapes=[pltpu.VMEM((ninths * TAPS * width // 18, LANES), t) for t in types]
+            + [pltpu.SemaphoreType.DMA((ninths // 3, 4))],
+            input_output_aliases={4 + len(grads) + k: k for k in range(len(earlier))},
+            compiler_params=params(16),
             cost_estimate=cost(2),
-            name="conv_other" if earlier else "conv_own",
-        )(where, grad, *conv_params, *earlier)
-
-    conv_outs = conv_half(other, *conv_half(total))
+            name="conv_rest" if earlier else "conv_first",
+        )(where, *grads, *conv_params, *earlier)
+
+    first_part = conv_part([(True, range(6))], [total], [])
+    conv_outs = conv_part([(True, range(6, 9)), (False, range(9))], [total, other], first_part)
 
     map_outs, aff_outs = outs[0:4], [a.reshape(aff_w.shape) for a in outs[4:8]]
     conv_outs = [a.reshape(conv_w.shape) for a in conv_outs]

time: 81.7 us -> 79.3 us (0.971)
  waiting for transfers between devices: 29 us -> 24.6 us
  Pallas kernels: 24.9 us -> 26.7 us
    pallas_call x3 -> x5, Pallas kernels: 6.21 us -> 10.9 us  [the longest x2 5.44 us: conv_part(): pl.pallas_call(functools.partial(conv_kernel, turns), out_shape=[shape((T...]
    pallas_call x1, Pallas kernels: 4.98 us -> 2.15 us  [local(): pl.pallas_call(functools.partial(main_kernel, n_ch, samples, side), out_s...]
    ppermute x7, starting transfers between devices: 7.84 us -> 5.88 us  [crossed(): return lax.ppermute(value, axis, pairs)]
    ppermute x14 -> x15, starting transfers between devices: 11.5 us -> 13.4 us  [swap(): lax.ppermute(value, axis, [(i, i ^ distance) for i in range(lax.axis_size...]
    ppermute x7, waiting for transfers between devices: 14.8 us -> 13 us  [crossed(): return lax.ppermute(value, axis, pairs)]
    ppermute x2, waiting for transfers between devices: 6.85 us -> 5.45 us  [joint(): return lax.ppermute(value, ('dp', 'chan'), pairs)]
    ppermute x14 -> x15, waiting for transfers between devices: 7.42 us -> 6.14 us  [swap(): lax.ppermute(value, axis, [(i, i ^ distance) for i in range(lax.axis_size...]
  transfers between devices with their start and end apart: 23 -> 24, of which waited for: 15 -> 13; matrix products, arithmetic and copies ran while one was open for 0% -> 0% of each run, Pallas kernels for 18% -> 25%
where the time goes in v4:
time: 79.3 us; the launch traced here: 78.9 us
  Pallas kernels  26.7 us (34%)
  waiting for transfers between devices  24.6 us (31%)
  starting transfers between devices  24.3 us (31%)
  between operations  2.6 us (3%)
    ppermute x15, starting transfers between devices, swap(): lax.ppermute(value, axis, [(i, i ^ distance) for i in range(lax.axis_size...  13.4 us
    ppermute x7, waiting for transfers between devices, crossed(): return lax.ppermute(value, axis, pairs)  13 us
    ppermute x15, waiting for transfers between devices, swap(): lax.ppermute(value, axis, [(i, i ^ distance) for i in range(lax.axis_size...  6.14 us
    ppermute x7, starting transfers between devices, crossed(): return lax.ppermute(value, axis, pairs)  5.88 us
    ppermute x2, waiting for transfers between devices, joint(): return lax.ppermute(value, ('dp', 'chan'), pairs)  5.45 us
    pallas_call x2, Pallas kernels, conv_part(): pl.pallas_call(functools.partial(conv_kernel, turns), out_shape=[shape((T...  5.44 us
    ppermute x2, starting transfers between devices, joint(): return lax.ppermute(value, ('dp', 'chan'), pairs)  4.92 us
    pallas_call x1, Pallas kernels, local(): pl.pallas_call(functools.partial(update_kernel, n_dp, samples, layers, [p...  3.98 us
  transfers between devices with their start and end apart: 24, of which 13 were waited for; matrix products, arithmetic and copies ran while one was open for 0% of the time, Pallas kernels for 25%

profile of v4, /device:TPU:1, one launch (start us, length us, event | category | flops | bytes accessed | tf_op | source)
XLA Modules:
  0.0 78.9 jit_solution(6126710733761591561)
XLA Ops:
  0.7 1.6 %pack.1 = bf16[1296,128]{1,0:T(8,128)(2,1)S(1)} custom-call(s32[2]{0:T(128)S(1)} %pad_add_fusion.where.refs_0_, f32[2,512,128]{2,1,0:T(8,128)} %aff_w.3, f32[3,128]{1,0:T(4,128)} %refs_13_.1, bf16[1024,128]{1,0:T(8,128)(2,1)} %bitcast.41), custom_call_target="tpu_custom_call" | custom-call | bytes 3500000 | tf_op jit(solution)/shard_map/pack/pallas_call | solution.py:779
  2.4 1.4 %low.1.refs_3_ = bf16[8,64,512]{2,1,0:T(8,128)(2,1)S(1)} custom-call(f32[8,64,512]{2,1,0:T(8,128)} %refs_4_.1), custom_call_target="tpu_custom_call" | custom-call | bytes 3500000 | tf_op jit(solution)/shard_map/low/pallas_call | solution.py:793
  4.1 3.6 %collective-permute-start.1 = (bf16[2592,128]{1,0:T(8,128)(2,1)S(1)}, bf16[2592,128]{1,0:T(8,128)(2,1)S(1)}, u32[]{:S(2)}, u32[]{:S(2)}) collective-permute-start(bf16[2592,128]{1,0:T(8,128)(2,1)S(1)} %pad_maximum_fusion.refs_1_), channel_id=1, source_target_pairs={{0,1},{1,0},{2,3},{3,2},{4,6},{5,7},{6,4},{7,5},{8,9},{9,8},{10,11... | collective-permute-start | bytes 1990664 | tf_op jit(solution)/shard_map/ppermute | solution.py:83
  7.7 1.2 %collective-permute-start.2 = (bf16[8,64,512]{2,1,0:T(8,128)(2,1)S(1)}, bf16[8,64,512]{2,1,0:T(8,128)(2,1)S(1)}, u32[]{:S(2)}, u32[]{:S(2)}) collective-permute-start(bf16[8,64,512]{2,1,0:T(8,128)(2,1)S(1)} %low.1.refs_3_), channel_id=1, source_target_pairs={{0,8},{4,20},{8,0},{12,28},{16,24},{20,4},{24,16},{28,12},{1,9},{5... | collective-permute-start | bytes 1572872 | tf_op jit(solution)/shard_map/ppermute | solution.py:99
  9.6 1.7 %weights.1 = (bf16[3,512,384]{2,1,0:T(8,128)(2,1)S(1)}, f32[512,128]{1,0:T(8,128)S(1)}) custom-call(f32[9,512,128]{2,1,0:T(8,128)} %bitcast.25), custom_call_target="tpu_custom_call" | custom-call | bytes 7000000 | tf_op jit(solution)/shard_map/weights/pallas_call | solution.py:805
  11.4 1.3 %collective-permute-start.6 = (bf16[8,64,512]{2,1,0:T(8,128)(2,1)S(1)}, bf16[8,64,512]{2,1,0:T(8,128)(2,1)S(1)}, u32[]{:S(2)}, u32[]{:S(2)}) collective-permute-start(bf16[8,64,512]{2,1,0:T(8,128)(2,1)S(1)} %collective-permute-done.3.refs_4_), channel_id=1, source_target_pairs={{0,8},{4,20},{8,0},{12,28},{16,24},{20,4},{24,16},{28,12},{1,9},{5... | collective-permute-start | bytes 1572872 | tf_op jit(solution)/shard_map/ppermute | solution.py:99
  12.7 3.4 %collective-permute-done.2.refs_5_ = bf16[8,64,512]{2,1,0:T(8,128)(2,1)S(1)} collective-permute-done((bf16[8,64,512]{2,1,0:T(8,128)(2,1)S(1)}, bf16[8,64,512]{2,1,0:T(8,128)(2,1)S(1)}, u32[]{:S(2)}, u32[]{:S(2)}) %collective-permute-start.2) | collective-permute-done | bytes 524320 | tf_op jit(solution)/shard_map/ppermute | solution.py:99
  16.1 1.2 %collective-permute-start.7 = (bf16[8,64,512]{2,1,0:T(8,128)(2,1)S(1)}, bf16[8,64,512]{2,1,0:T(8,128)(2,1)S(1)}, u32[]{:S(2)}, u32[]{:S(2)}) collective-permute-start(bf16[8,64,512]{2,1,0:T(8,128)(2,1)S(1)} %collective-permute-done.2.refs_5_), channel_id=1, source_target_pairs={{0,16},{4,12},{8,24},{12,4},{16,0},{20,28},{24,8},{28,20},{1,17},{... | collective-permute-start | bytes 1572872 | tf_op jit(solution)/shard_map/ppermute | solution.py:99
  17.3 5.4 %collective-permute-done.1.refs_2_ = bf16[2592,128]{1,0:T(8,128)(2,1)S(1)} collective-permute-done((bf16[2592,128]{1,0:T(8,128)(2,1)S(1)}, bf16[2592,128]{1,0:T(8,128)(2,1)S(1)}, u32[]{:S(2)}, u32[]{:S(2)}) %collective-permute-start.1) | collective-permute-done | bytes 663584 | tf_op jit(solution)/shard_map/ppermute | solution.py:83
  22.8 1.3 %collective-permute-start.4 = (bf16[2592,128]{1,0:T(8,128)(2,1)S(1)}, bf16[2592,128]{1,0:T(8,128)(2,1)S(1)}, u32[]{:S(2)}, u32[]{:S(2)}) collective-permute-start(bf16[2592,128]{1,0:T(8,128)(2,1)S(1)} %broadcast_select_fusion), channel_id=1, source_target_pairs={{1,2},{2,1},{5,4},{6,7},{9,10},{10,9},{13,12},{14,15},{17,18},{18,... | collective-permute-start | bytes 1990664 | tf_op jit(solution)/shard_map/ppermute | solution.py:83
  24.2 2.7 %collective-permute-start.9 = (bf16[8,64,512]{2,1,0:T(8,128)(2,1)S(1)}, bf16[8,64,512]{2,1,0:T(8,128)(2,1)S(1)}, u32[]{:S(2)}, u32[]{:S(2)}) collective-permute-start(bf16[8,64,512]{2,1,0:T(8,128)(2,1)S(1)} %collective-permute-done.6.refs_6_), channel_id=1, source_target_pairs={{0,4},{4,0},{8,12},{12,8},{16,20},{20,16},{24,28},{28,24},{1,5},{5... | collective-permute-start | bytes 1572872 | tf_op jit(solution)/shard_map/ppermute | solution.py:44
  26.8 1.1 %collective-permute-done.7.refs_7_ = bf16[8,64,512]{2,1,0:T(8,128)(2,1)S(1)} collective-permute-done((bf16[8,64,512]{2,1,0:T(8,128)(2,1)S(1)}, bf16[8,64,512]{2,1,0:T(8,128)(2,1)S(1)}, u32[]{:S(2)}, u32[]{:S(2)}) %collective-permute-start.7) | collective-permute-done | bytes 524320 | tf_op jit(solution)/shard_map/ppermute | solution.py:99
  29.9 2.9 %mapping.1 = (f32[8,8,512]{2,1,0:T(8,128)S(1)}, f32[8,8,512]{2,1,0:T(8,128)S(1)}, f32[8,512]{1,0:T(8,128)S(1)}, f32[2,8,512]{2,1,0:T(8,128)S(1)}, bf16[8,512,512]{2,1,0:T(8,128)(2,1)S(1)}) custom-call(s32[2]{0:T(128)S(1)} %pad_add_fusion.where.refs_0_, s32[2]{0:T(128)S(1)} %bitcast.36, s32[1]{0:T(128)S(6)} %copy.66.refs_2_.crossover, ...), custom_call_target="tpu_custom_call" | custom-call | bytes 3500000 | tf_op jit(solution)/shard_map/mapping/pallas_call | solution.py:821
  32.8 2.7 %begin.1 = (bf16[1,512,1024]{2,1,0:T(8,128)(2,1)S(1)}, f32[1,1024,384]{2,1,0:T(8,128)S(1)}, f32[8,512]{1,0:T(8,128)S(1)}, bf16[512,512]{1,0:T(8,128)(2,1)S(1)}) custom-call(s32[2]{0:T(128)S(1)} %pad_add_fusion.where.refs_0_, bf16[2592,128]{1,0:T(8,128)(2,1)S(1)} %pad_maximum_fusion.refs_1_, bf16[2592,128]{1,0:T(8,128)(2,1)S(1)} %collective-permute-done.1.refs_2_, ...), custom_call_target="tpu_custom_call" | custom-call | bytes 10500000 | tf_op jit(solution)/shard_map/begin/pallas_call | solution.py:843
  36.4 0.9 %collective-permute-done.11.refs_2_ = bf16[1568,128]{1,0:T(8,128)(2,1)S(1)} collective-permute-done((bf16[1568,128]{1,0:T(8,128)(2,1)S(1)}, bf16[1568,128]{1,0:T(8,128)(2,1)S(1)}, u32[]{:S(2)}, u32[]{:S(2)}) %collective-permute-start.11) | collective-permute-done | bytes 401440 | tf_op jit(solution)/shard_map/ppermute | solution.py:44
  37.4 2.2 %main.1 = (bf16[1,512,1024]{2,1,0:T(8,128)(2,1)S(1)}, f32[8,512]{1,0:T(8,128)S(1)}, bf16[512,512]{1,0:T(8,128)(2,1)S(1)}, f32[1,1040,128]{2,1,0:T(8,128)S(1)}, f...) custom-call(s32[2]{0:T(128)S(1)} %pad_add_fusion.where.refs_0_, ...), custom_call_target="tpu_custom_call", output_to_operand_aliasing={{0}: (12, {}), {1}: (13, {}), {2}: (14, {})} | custom-call | bytes 10500000 | tf_op jit(solution)/shard_map/main/pallas_call | solution.py:862
  39.7 2.6 %factor.1 = (bf16[1,2,2304,128]{3,2,1,0:T(8,128)(2,1)S(1)}, f32[8,128]{1,0:T(8,128)S(1)}) custom-call(s32[2]{0:T(128)S(1)} %pad_add_fusion.where.refs_0_, bf16[1,512,1024]{2,1,0:T(8,128)(2,1)S(1)} %get-tuple-element.98.feat_t, f32[1,1040,128]{2,1,0:T(8,128)S(1)} %get-tuple-element.99.wide, f32[8,128]{1,0:T(8,128)S(1)} %get-tuple-element.100.small.refs_9_, ...), custom_call_target="tpu_custom_call" | custom-call | bytes 7000000 | tf_op jit(solution)/shard_map/factor/pallas_call | solution.py:903
  42.8 2.3 %collective-permute-start.15 = (f32[16,128]{1,0:T(8,128)S(1)}, f32[16,128]{1,0:T(8,128)S(1)}, u32[]{:S(2)}, u32[]{:S(2)}) collective-permute-start(f32[16,128]{1,0:T(8,128)S(1)} %pad_maximum_fusion.2.refs_0_), channel_id=1, source_target_pairs={{0,3},{1,2},{2,1},{3,0},{4,7},{5,6},{6,5},{7,4},{8,11},{9,10},{10,... | collective-permute-start | bytes 24584 | tf_op jit(solution)/shard_map/ppermute | solution.py:44
  45.4 1.1 %collective-permute-start.13 = (f32[16,128]{1,0:T(8,128)S(1)}, f32[16,128]{1,0:T(8,128)S(1)}, u32[]{:S(2)}, u32[]{:S(2)}) collective-permute-start(f32[16,128]{1,0:T(8,128)S(1)} %pad_maximum_fusion.2.refs_0_), channel_id=1, source_target_pairs={{0,1},{1,0},{2,3},{3,2},{4,5},{5,4},{6,7},{7,6},{8,9},{9,8},{10,11... | collective-permute-start | bytes 24584 | tf_op jit(solution)/shard_map/ppermute | solution.py:44
  46.5 0.8 collective-permute-done.15.refs_3_
  47.2 1.3 %collective-permute-done.14.refs_2_ = f32[16,128]{1,0:T(8,128)S(1)} collective-permute-done((f32[16,128]{1,0:T(8,128)S(1)}, f32[16,128]{1,0:T(8,128)S(1)}, u32[]{:S(2)}, u32[]{:S(2)}) %collective-permute-start.14) | collective-permute-done | bytes 8224 | tf_op jit(solution)/shard_map/ppermute | solution.py:44
  48.8 1.3 %collective-permute-start.21 = (bf16[2336,128]{1,0:T(8,128)(2,1)S(1)}, bf16[2336,128]{1,0:T(8,128)(2,1)S(1)}, u32[]{:S(2)}, u32[]{:S(2)}) collective-permute-start(bf16[2336,128]{1,0:T(8,128)(2,1)S(1)} %combine.1), channel_id=1, source_target_pairs={{0,8},{4,20},{8,0},{12,28},{16,24},{20,4},{24,16},{28,12},{1,9},{5... | collective-permute-start | bytes 1794056 | tf_op jit(solution)/shard_map/ppermute | solution.py:99
  50.1 2.1 %mapping_back.1 = bf16[48,512]{1,0:T(8,128)(2,1)S(1)} custom-call(s32[2]{0:T(128)S(1)} %pad_add_fusion.where.refs_0_, s32[1]{0:T(128)S(6)} %copy.66.refs_2_.crossover, f32[16,128]{1,0:T(8,128)S(1)} %pad_maximum_fusion.2.refs_0_, f32[16,128]{1,0:T(8,128)S(1)} %collective-permute-done.13.refs_1_, f32[16,128]{1,0:T(8,128)S(1)} %collective-permute-done.14.refs_2_, ...), custom_call_target="tpu_custom_call" | custom-call | bytes 7000000 | tf_op jit(solution)/shard_map/mapping_back/pallas_call | solution.py:933
  52.3 1.9 %collective-permute-start.17 = (bf16[48,512]{1,0:T(8,128)(2,1)S(1)}, bf16[48,512]{1,0:T(8,128)(2,1)S(1)}, u32[]{:S(2)}, u32[]{:S(2)}) collective-permute-start(bf16[48,512]{1,0:T(8,128)(2,1)S(1)} %mapping_back.1), channel_id=1, source_target_pairs={{0,4},{4,0},{8,12},{12,8},{16,20},{20,16},{24,28},{28,24},{1,5},{5... | collective-permute-start | bytes 147464 | tf_op jit(solution)/shard_map/ppermute | solution.py:44
  54.2 0.9 %collective-permute-done.17 = bf16[48,512]{1,0:T(8,128)(2,1)S(1)} collective-permute-done((bf16[48,512]{1,0:T(8,128)(2,1)S(1)}, bf16[48,512]{1,0:T(8,128)(2,1)S(1)}, u32[]{:S(2)}, u32[]{:S(2)}) %collective-permute-start.17) | collective-permute-done | bytes 49184 | tf_op jit(solution)/shard_map/ppermute | solution.py:44
  55.4 4.6 %collective-permute-done.18.refs_1_ = bf16[96,512]{1,0:T(8,128)(2,1)S(1)} collective-permute-done((bf16[96,512]{1,0:T(8,128)(2,1)S(1)}, bf16[96,512]{1,0:T(8,128)(2,1)S(1)}, u32[]{:S(2)}, u32[]{:S(2)}) %collective-permute-start.18) | collective-permute-done | bytes 98336 | tf_op jit(solution)/shard_map/ppermute | solution.py:99
  60.5 2.7 %collective-permute-start.20 = (bf16[96,512]{1,0:T(8,128)(2,1)S(1)}, bf16[96,512]{1,0:T(8,128)(2,1)S(1)}, u32[]{:S(2)}, u32[]{:S(2)}) collective-permute-start(bf16[96,512]{1,0:T(8,128)(2,1)S(1)} %collective-permute-done.18.refs_1_), channel_id=1, source_target_pairs={{0,4},{4,0},{8,12},{12,8},{16,20},{20,16},{24,28},{28,24},{1,5},{5... | collective-permute-start | bytes 294920 | tf_op jit(solution)/shard_map/ppermute | solution.py:44
  64.1 3.9 %collective-permute-done.19.refs_2_ = bf16[96,512]{1,0:T(8,128)(2,1)S(1)} collective-permute-done((bf16[96,512]{1,0:T(8,128)(2,1)S(1)}, bf16[96,512]{1,0:T(8,128)(2,1)S(1)}, u32[]{:S(2)}, u32[]{:S(2)}) %collective-permute-start.19) | collective-permute-done | bytes 98336 | tf_op jit(solution)/shard_map/ppermute | solution.py:99
  68.1 4.0 %update.1 = (f32[8,64,512]{2,1,0:T(8,128)}, f32[8,64,512]{2,1,0:T(8,128)}, f32[8,64,512]{2,1,0:T(8,128)}, bf16[8,64,512]{2,1,0:T(8,128)(2,1)}, f32[1024,128]{1,0...) custom-call(s32[2]{0:T(128)S(1)} %pad_add_fusion.where.refs_0_, ...), custom_call_target="tpu_custom_call" | custom-call | bytes 14000000 | tf_op jit(solution)/shard_map/update/pallas_call | solution.py:969
  72.3 1.0 %collective-permute-start.23 = (bf16[2336,128]{1,0:T(8,128)(2,1)S(1)}, bf16[2336,128]{1,0:T(8,128)(2,1)S(1)}, u32[]{:S(2)}, u32[]{:S(2)}) collective-permute-start(bf16[2336,128]{1,0:T(8,128)(2,1)S(1)} %add_convert_fusion.refs_0_), channel_id=1, source_target_pairs={{0,4},{4,0},{8,12},{12,8},{16,20},{20,16},{24,28},{28,24},{1,5},{5... | collective-permute-start | bytes 1794056 | tf_op jit(solution)/shard_map/ppermute | solution.py:44
  73.3 2.2 %conv_first.1 = (f32[4608,128]{1,0:T(8,128)}, f32[4608,128]{1,0:T(8,128)}, f32[4608,128]{1,0:T(8,128)}, bf16[4608,128]{1,0:T(8,128)(2,1)}) custom-call(s32[2]{0:T(128)S(1)} %pad_add_fusion.where.refs_0_, bf16[2336,128]{1,0:T(8,128)(2,1)S(1)} %add_convert_fusion.refs_0_, f32[4608,128]{1,0:T(8,128)S(1)} %bitcast.26, f32[4608,128]{1,0:T(8,128)S(1)} %bitcast.28, ...), custom_call_target="tpu_custom_call" | custom-call | bytes 7000000 | tf_op jit(solution)/shard_map/conv_first/pallas_call | solution.py:1003
  75.6 3.2 %conv_rest.1 = (f32[4608,128]{1,0:T(8,128)}, f32[4608,128]{1,0:T(8,128)}, f32[4608,128]{1,0:T(8,128)}, bf16[4608,128]{1,0:T(8,128)(2,1)}) custom-call(s32[2]{0:T(128)S(1)} %pad_add_fusion.where.refs_0_, bf16[2336,128]{1,0:T(8,128)(2,1)S(1)} %add_convert_fusion.refs_0_, ...), custom_call_target="tpu_custom_call", output_to_operand_aliasing={{0}: (6, {}), {1}: (7, {}), {2}: (8, {}), {3}: (9, {})} | custom-call | bytes 7000000 | tf_op jit(solution)/shard_map/conv_rest/pallas_call | solution.py:1003
  (85 shorter events, 6.0 us)
Async XLA Ops:
  2.3 1.7 %collective-permute-start = (bf16[1296,128]{1,0:T(8,128)(2,1)S(1)}, bf16[1296,128]{1,0:T(8,128)(2,1)S(1)}, u32[]{:S(2)}, u32[]{:S(2)}) collective-permute-start(bf16[1296,128]{1,0:T(8,128)(2,1)S(1)} %pack.1), channel_id=1, source_target_pairs={{0,4},{4,0},{8,12},{12,8},{16,20},{20,16},{24,28},{28,24},{1,5},{5... | collective-permute-start | bytes 995336 | tf_op jit(solution)/shard_map/ppermute | solution.py:44
  4.1 18.6 %collective-permute-start.1 = (bf16[2592,128]{1,0:T(8,128)(2,1)S(1)}, bf16[2592,128]{1,0:T(8,128)(2,1)S(1)}, u32[]{:S(2)}, u32[]{:S(2)}) collective-permute-start(bf16[2592,128]{1,0:T(8,128)(2,1)S(1)} %pad_maximum_fusion.refs_1_), channel_id=1, source_target_pairs={{0,1},{1,0},{2,3},{3,2},{4,6},{5,7},{6,4},{7,5},{8,9},{9,8},{10,11... | collective-permute-start | bytes 1990664 | tf_op jit(solution)/shard_map/ppermute | solution.py:83
  7.7 1.9 %collective-permute-start.3 = (bf16[8,64,512]{2,1,0:T(8,128)(2,1)S(1)}, bf16[8,64,512]{2,1,0:T(8,128)(2,1)S(1)}, u32[]{:S(2)}, u32[]{:S(2)}) collective-permute-start(bf16[8,64,512]{2,1,0:T(8,128)(2,1)S(1)} %low.1.refs_3_), channel_id=1, source_target_pairs={{0,4},{4,0},{8,12},{12,8},{16,20},{20,16},{24,28},{28,24},{1,5},{5... | collective-permute-start | bytes 1572872 | tf_op jit(solution)/shard_map/ppermute | solution.py:44
  7.7 8.3 %collective-permute-start.2 = (bf16[8,64,512]{2,1,0:T(8,128)(2,1)S(1)}, bf16[8,64,512]{2,1,0:T(8,128)(2,1)S(1)}, u32[]{:S(2)}, u32[]{:S(2)}) collective-permute-start(bf16[8,64,512]{2,1,0:T(8,128)(2,1)S(1)} %low.1.refs_3_), channel_id=1, source_target_pairs={{0,8},{4,20},{8,0},{12,28},{16,24},{20,4},{24,16},{28,12},{1,9},{5... | collective-permute-start | bytes 1572872 | tf_op jit(solution)/shard_map/ppermute | solution.py:99
  11.4 18.5 %copy-start.9 = (f32[8,512]{1,0:T(8,128)S(1)}, f32[8,512]{1,0:T(8,128)}, u32[]{:S(2)}) copy-start(f32[8,512]{1,0:T(8,128)} %refs_10_.3) | copy-start | bytes 49156
  11.4 18.5 %copy-start.20 = (s32[1,2]{1,0:T(1,128)S(1)}, s32[1,2]{1,0:T(1,128)}, u32[]{:S(2)}) copy-start(s32[1,2]{1,0:T(1,128)} %param.27) | copy-start | bytes 28
  11.4 12.8 %collective-permute-start.6 = (bf16[8,64,512]{2,1,0:T(8,128)(2,1)S(1)}, bf16[8,64,512]{2,1,0:T(8,128)(2,1)S(1)}, u32[]{:S(2)}, u32[]{:S(2)}) collective-permute-start(bf16[8,64,512]{2,1,0:T(8,128)(2,1)S(1)} %collective-permute-done.3.refs_4_), channel_id=1, source_target_pairs={{0,8},{4,20},{8,0},{12,28},{16,24},{20,4},{24,16},{28,12},{1,9},{5... | collective-permute-start | bytes 1572872 | tf_op jit(solution)/shard_map/ppermute | solution.py:99
  16.1 11.9 %collective-permute-start.7 = (bf16[8,64,512]{2,1,0:T(8,128)(2,1)S(1)}, bf16[8,64,512]{2,1,0:T(8,128)(2,1)S(1)}, u32[]{:S(2)}, u32[]{:S(2)}) collective-permute-start(bf16[8,64,512]{2,1,0:T(8,128)(2,1)S(1)} %collective-permute-done.2.refs_5_), channel_id=1, source_target_pairs={{0,16},{4,12},{8,24},{12,4},{16,0},{20,28},{24,8},{28,20},{1,17},{... | collective-permute-start | bytes 1572872 | tf_op jit(solution)/shard_map/ppermute | solution.py:99
  22.8 12.7 %collective-permute-start.4 = (bf16[2592,128]{1,0:T(8,128)(2,1)S(1)}, bf16[2592,128]{1,0:T(8,128)(2,1)S(1)}, u32[]{:S(2)}, u32[]{:S(2)}) collective-permute-start(bf16[2592,128]{1,0:T(8,128)(2,1)S(1)} %broadcast_select_fusion), channel_id=1, source_target_pairs={{1,2},{2,1},{5,4},{6,7},{9,10},{10,9},{13,12},{14,15},{17,18},{18,... | collective-permute-start | bytes 1990664 | tf_op jit(solution)/shard_map/ppermute | solution.py:83
  24.1 5.1 %collective-permute-start.8 = (bf16[8,64,512]{2,1,0:T(8,128)(2,1)S(1)}, bf16[8,64,512]{2,1,0:T(8,128)(2,1)S(1)}, u32[]{:S(2)}, u32[]{:S(2)}) collective-permute-start(bf16[8,64,512]{2,1,0:T(8,128)(2,1)S(1)} %collective-permute-done.2.refs_5_), channel_id=1, source_target_pairs={{0,4},{4,0},{8,12},{12,8},{16,20},{20,16},{24,28},{28,24},{1,5},{5... | collective-permute-start | bytes 1572872 | tf_op jit(solution)/shard_map/ppermute | solution.py:44
  24.2 5.0 %collective-permute-start.9 = (bf16[8,64,512]{2,1,0:T(8,128)(2,1)S(1)}, bf16[8,64,512]{2,1,0:T(8,128)(2,1)S(1)}, u32[]{:S(2)}, u32[]{:S(2)}) collective-permute-start(bf16[8,64,512]{2,1,0:T(8,128)(2,1)S(1)} %collective-permute-done.6.refs_6_), channel_id=1, source_target_pairs={{0,4},{4,0},{8,12},{12,8},{16,20},{20,16},{24,28},{28,24},{1,5},{5... | collective-permute-start | bytes 1572872 | tf_op jit(solution)/shard_map/ppermute | solution.py:44
  28.0 1.9 %collective-permute-start.10 = (bf16[8,64,512]{2,1,0:T(8,128)(2,1)S(1)}, bf16[8,64,512]{2,1,0:T(8,128)(2,1)S(1)}, u32[]{:S(2)}, u32[]{:S(2)}) collective-permute-start(bf16[8,64,512]{2,1,0:T(8,128)(2,1)S(1)} %collective-permute-done.7.refs_7_), channel_id=1, source_target_pairs={{0,4},{4,0},{8,12},{12,8},{16,20},{20,16},{24,28},{28,24},{1,5},{5... | collective-permute-start | bytes 1572872 | tf_op jit(solution)/shard_map/ppermute | solution.py:44
  28.0 4.8 %collective-permute-start.5 = (bf16[1568,128]{1,0:T(8,128)(2,1)S(1)}, bf16[1568,128]{1,0:T(8,128)(2,1)S(1)}, u32[]{:S(2)}, u32[]{:S(2)}) collective-permute-start(bf16[1568,128]{1,0:T(8,128)(2,1)S(1)} %slice.38), channel_id=1, source_target_pairs={{0,4},{4,0},{8,12},{12,8},{16,20},{20,16},{24,28},{28,24},{1,5},{5... | collective-permute-start | bytes 1204232 | tf_op jit(solution)/shard_map/ppermute | solution.py:44
  35.5 1.8 %collective-permute-start.11 = (bf16[1568,128]{1,0:T(8,128)(2,1)S(1)}, bf16[1568,128]{1,0:T(8,128)(2,1)S(1)}, u32[]{:S(2)}, u32[]{:S(2)}) collective-permute-start(bf16[1568,128]{1,0:T(8,128)(2,1)S(1)} %slice.30), channel_id=1, source_target_pairs={{0,4},{4,0},{8,12},{12,8},{16,20},{20,16},{24,28},{28,24},{1,5},{5... | collective-permute-start | bytes 1204232 | tf_op jit(solution)/shard_map/ppermute | solution.py:44
  39.5 3.3 %collective-permute-start.12 = (f32[8,128]{1,0:T(8,128)S(1)}, f32[8,128]{1,0:T(8,128)S(1)}, u32[]{:S(2)}, u32[]{:S(2)}) collective-permute-start(f32[8,128]{1,0:T(8,128)S(1)} %get-tuple-element.103), channel_id=1, source_target_pairs={{0,4},{4,0},{8,12},{12,8},{16,20},{20,16},{24,28},{28,24},{1,5},{5... | collective-permute-start | bytes 12296 | tf_op jit(solution)/shard_map/ppermute | solution.py:44
  42.4 6.2 %collective-permute-start.16 = (bf16[1,2304,128]{2,1,0:T(8,128)(2,1)S(1)}, bf16[1,2304,128]{2,1,0:T(8,128)(2,1)S(1)}, u32[]{:S(2)}, u32[]{:S(2)}) collective-permute-start(bf16[1,2304,128]{2,1,0:T(8,128)(2,1)S(1)} %slice_bitcast_fusion), channel_id=1, source_target_pairs={{0,4},{4,0},{8,12},{12,8},{16,20},{20,16},{24,28},{28,24},{1,5},{5... | collective-permute-start | bytes 1769480 | tf_op jit(solution)/shard_map/ppermute | solution.py:44
  42.8 4.4 %collective-permute-start.15 = (f32[16,128]{1,0:T(8,128)S(1)}, f32[16,128]{1,0:T(8,128)S(1)}, u32[]{:S(2)}, u32[]{:S(2)}) collective-permute-start(f32[16,128]{1,0:T(8,128)S(1)} %pad_maximum_fusion.2.refs_0_), channel_id=1, source_target_pairs={{0,3},{1,2},{2,1},{3,0},{4,7},{5,6},{6,5},{7,4},{8,11},{9,10},{10,... | collective-permute-start | bytes 24584 | tf_op jit(solution)/shard_map/ppermute | solution.py:44
  45.1 3.4 %collective-permute-start.14 = (f32[16,128]{1,0:T(8,128)S(1)}, f32[16,128]{1,0:T(8,128)S(1)}, u32[]{:S(2)}, u32[]{:S(2)}) collective-permute-start(f32[16,128]{1,0:T(8,128)S(1)} %pad_maximum_fusion.2.refs_0_), channel_id=1, source_target_pairs={{0,2},{1,3},{2,0},{3,1},{4,6},{5,7},{6,4},{7,5},{8,10},{9,11},{10,... | collective-permute-start | bytes 24584 | tf_op jit(solution)/shard_map/ppermute | solution.py:44
  45.4 3.2 %collective-permute-start.13 = (f32[16,128]{1,0:T(8,128)S(1)}, f32[16,128]{1,0:T(8,128)S(1)}, u32[]{:S(2)}, u32[]{:S(2)}) collective-permute-start(f32[16,128]{1,0:T(8,128)S(1)} %pad_maximum_fusion.2.refs_0_), channel_id=1, source_target_pairs={{0,1},{1,0},{2,3},{3,2},{4,5},{5,4},{6,7},{7,6},{8,9},{9,8},{10,11... | collective-permute-start | bytes 24584 | tf_op jit(solution)/shard_map/ppermute | solution.py:44
  48.8 11.2 %collective-permute-start.21 = (bf16[2336,128]{1,0:T(8,128)(2,1)S(1)}, bf16[2336,128]{1,0:T(8,128)(2,1)S(1)}, u32[]{:S(2)}, u32[]{:S(2)}) collective-permute-start(bf16[2336,128]{1,0:T(8,128)(2,1)S(1)} %combine.1), channel_id=1, source_target_pairs={{0,8},{4,20},{8,0},{12,28},{16,24},{20,4},{24,16},{28,12},{1,9},{5... | collective-permute-start | bytes 1794056 | tf_op jit(solution)/shard_map/ppermute | solution.py:99
  50.1 17.9 %copy-start.5 = (f32[8,64,512]{2,1,0:T(8,128)S(1)}, f32[8,64,512]{2,1,0:T(8,128)}, u32[]{:S(2)}) copy-start(f32[8,64,512]{2,1,0:T(8,128)} %refs_5_.1) | copy-start | bytes 3145732
  50.1 17.9 %copy-start.6 = (f32[8,64,512]{2,1,0:T(8,128)S(1)}, f32[8,64,512]{2,1,0:T(8,128)}, u32[]{:S(2)}) copy-start(f32[8,64,512]{2,1,0:T(8,128)} %refs_6_.3) | copy-start | bytes 3145732
  50.1 17.9 %copy-start.8 = (f32[2,512,128]{2,1,0:T(8,128)S(1)}, f32[2,512,128]{2,1,0:T(8,128)}, u32[]{:S(2)}) copy-start(f32[2,512,128]{2,1,0:T(8,128)} %param.40) | copy-start | bytes 1572868
  52.2 15.8 %copy-start.4 = (f32[8,64,512]{2,1,0:T(8,128)S(1)}, f32[8,64,512]{2,1,0:T(8,128)}, u32[]{:S(2)}) copy-start(f32[8,64,512]{2,1,0:T(8,128)} %refs_4_.1) | copy-start | bytes 3145732
  52.2 15.8 %copy-start.7 = (f32[2,512,128]{2,1,0:T(8,128)S(1)}, f32[2,512,128]{2,1,0:T(8,128)}, u32[]{:S(2)}) copy-start(f32[2,512,128]{2,1,0:T(8,128)} %param.39) | copy-start | bytes 1572868
  52.2 15.8 %copy-start.11 = (f32[8,512]{1,0:T(8,128)S(1)}, f32[8,512]{1,0:T(8,128)}, u32[]{:S(2)}) copy-start(f32[8,512]{1,0:T(8,128)} %refs_11_.4) | copy-start | bytes 49156
  52.3 2.8 %collective-permute-start.17 = (bf16[48,512]{1,0:T(8,128)(2,1)S(1)}, bf16[48,512]{1,0:T(8,128)(2,1)S(1)}, u32[]{:S(2)}, u32[]{:S(2)}) collective-permute-start(bf16[48,512]{1,0:T(8,128)(2,1)S(1)} %mapping_back.1), channel_id=1, source_target_pairs={{0,4},{4,0},{8,12},{12,8},{16,20},{20,16},{24,28},{28,24},{1,5},{5... | collective-permute-start | bytes 147464 | tf_op jit(solution)/shard_map/ppermute | solution.py:44
  55.1 4.9 %collective-permute-start.18 = (bf16[96,512]{1,0:T(8,128)(2,1)S(1)}, bf16[96,512]{1,0:T(8,128)(2,1)S(1)}, u32[]{:S(2)}, u32[]{:S(2)}) collective-permute-start(bf16[96,512]{1,0:T(8,128)(2,1)S(1)} %pad_maximum_fusion.1.refs_0_), channel_id=1, source_target_pairs={{0,16},{4,12},{8,24},{12,4},{16,0},{20,28},{24,8},{28,20},{1,17},{... | collective-permute-start | bytes 294920 | tf_op jit(solution)/shard_map/ppermute | solution.py:99
  60.2 11.9 %collective-permute-start.22 = (bf16[2336,128]{1,0:T(8,128)(2,1)S(1)}, bf16[2336,128]{1,0:T(8,128)(2,1)S(1)}, u32[]{:S(2)}, u32[]{:S(2)}) collective-permute-start(bf16[2336,128]{1,0:T(8,128)(2,1)S(1)} %add_convert_fusion.1), channel_id=1, source_target_pairs={{0,16},{4,12},{8,24},{12,4},{16,0},{20,28},{24,8},{28,20},{1,17},{... | collective-permute-start | bytes 1794056 | tf_op jit(solution)/shard_map/ppermute | solution.py:99
  60.5 3.6 %collective-permute-start.20 = (bf16[96,512]{1,0:T(8,128)(2,1)S(1)}, bf16[96,512]{1,0:T(8,128)(2,1)S(1)}, u32[]{:S(2)}, u32[]{:S(2)}) collective-permute-start(bf16[96,512]{1,0:T(8,128)(2,1)S(1)} %collective-permute-done.18.refs_1_), channel_id=1, source_target_pairs={{0,4},{4,0},{8,12},{12,8},{16,20},{20,16},{24,28},{28,24},{1,5},{5... | collective-permute-start | bytes 294920 | tf_op jit(solution)/shard_map/ppermute | solution.py:44
  63.2 4.8 %collective-permute-start.19 = (bf16[96,512]{1,0:T(8,128)(2,1)S(1)}, bf16[96,512]{1,0:T(8,128)(2,1)S(1)}, u32[]{:S(2)}, u32[]{:S(2)}) collective-permute-start(bf16[96,512]{1,0:T(8,128)(2,1)S(1)} %collective-permute-done.18.refs_1_), channel_id=1, source_target_pairs={{0,8},{4,20},{8,0},{12,28},{16,24},{20,4},{24,16},{28,12},{1,9},{5... | collective-permute-start | bytes 294920 | tf_op jit(solution)/shard_map/ppermute | solution.py:99
  72.3 3.2 %collective-permute-start.23 = (bf16[2336,128]{1,0:T(8,128)(2,1)S(1)}, bf16[2336,128]{1,0:T(8,128)(2,1)S(1)}, u32[]{:S(2)}, u32[]{:S(2)}) collective-permute-start(bf16[2336,128]{1,0:T(8,128)(2,1)S(1)} %add_convert_fusion.refs_0_), channel_id=1, source_target_pairs={{0,4},{4,0},{8,12},{12,8},{16,20},{20,16},{24,28},{28,24},{1,5},{5... | collective-permute-start | bytes 1794056 | tf_op jit(solution)/shard_map/ppermute | solution.py:44
  (13 other events, 136.6 us)

commit v5 on v4

--- a/solution.py
+++ b/solution.py
@@ -29,7 +29,7 @@
 
 
 def cost(micros):
-    return pl.CostEstimate(flops=0, bytes_accessed=int(micros * 3.5e6), transcendentals=0)
+    return pl.CostEstimate(flops=int(micros * 1e9), bytes_accessed=0, transcendentals=0)
 
 
 def hbm(*values):
@@ -70,11 +70,10 @@
     return [value] + [swap(value, axis, k) for k in range(1, lax.axis_size(axis))]
 
 
-def spread_over_chan(pack, tail, ready):
+def spread_over_chan(features, pack, ready):
     n_dp, n_ch = lax.axis_size("dp"), lax.axis_size("chan")
-    cut = pack.shape[0] - tail
-    other = swap(pack, "dp", 1)
-    both = after(jnp.concatenate([pack, other[cut:], other[:cut]]), ready)
+    cut = features.shape[0]
+    both = lax.optimization_barrier(jnp.concatenate([pack, swap(features, "dp", 1)]))
 
     def joint(value, moves):
         pairs = [
@@ -151,11 +150,11 @@
 
 
 def pack_kernel(where, aff_w, bias, features, pack, aff_stage, bias_stage, sems):
-    half = aff_stage.shape[0]
+    half = aff_stage.shape[0] // 2
     rows = features.shape[0]
-    start = pl.multiple_of(lax.rem(where[0], 2) * half, half)
+    pair = lax.rem(where[0], 2)
     feat_copy = pltpu.make_async_copy(features, pack.at[pl.ds(0, rows), :], sems.at[0])
-    aff_copy = pltpu.make_async_copy(aff_w.at[0, pl.ds(start, half), :], aff_stage, sems.at[1])
+    aff_copy = pltpu.make_async_copy(aff_w.at[0], aff_stage, sems.at[1])
     bias_copy = pltpu.make_async_copy(bias, bias_stage, sems.at[2])
     for copy in (feat_copy, aff_copy, bias_copy):
         copy.start()
@@ -164,9 +163,12 @@
     lines = jnp.concatenate(
         [hi.astype(F32), mid.astype(F32), lo.astype(F32), jnp.zeros((13, LANES), F32)], axis=0
     )
-    pack[pl.ds(rows + half, 16), :] = lines.astype(BF16)
     aff_copy.wait()
-    pack[pl.ds(rows, half), :] = aff_stage[...].astype(BF16)
+    for turn, owner in enumerate((pair, 1 - pair)):
+        at = rows + turn * (half + 16)
+        start = pl.multiple_of(owner * half, half)
+        pack[pl.ds(at, half), :] = aff_stage[pl.ds(start, half), :].astype(BF16)
+        pack[pl.ds(at + half, 16), :] = lines.astype(BF16)
     feat_copy.wait()
 
 
@@ -191,19 +193,12 @@
         del refs[:count]
         return got
 
-    where, seeds, crossover = take(3)
+    where, crossover = take(2)
     parts = take(len(places))
-    z_table, map_b = take(2)
-    pre_out, hid_out, top_out, picked_out, map_full = take(5)
-    rows, sem_map, sem_z = refs
+    latent_rows, map_b = take(2)
+    pre_out, hid_out, top_out, picked_out, map_full, sem_map = refs
     layers, share, width = parts[0].shape
-    latents = 2 * samples
     dp = where[0]
-    z_copies = []
-    for n in range(latents):
-        at = pl.multiple_of((seeds[n] // 8) * 8, 8)
-        z_copies.append(pltpu.make_async_copy(z_table.at[pl.ds(at, 8), :], rows.at[n], sem_z.at[n]))
-        z_copies[n].start()
     odd = lax.rem(dp, 2)
     moves = []
     for part, (first, even_k, odd_k) in zip(parts, places):
@@ -230,14 +225,7 @@
 
     bring(0)
     bring(1)
-    hidden_rows = []
-    for n in range(latents):
-        z_copies[n].wait()
-        row = rows[n, pl.ds(lax.rem(seeds[n], 8), 1), :]
-        scale = lax.rsqrt(jnp.mean(row * row, axis=1, keepdims=True) + 1e-08)
-        hidden_rows.append(row * scale)
-    hidden_rows.append(jnp.zeros((16 - latents, width), F32))
-    hidden = jnp.concatenate(hidden_rows, axis=0)
+    hidden = latent_rows[...]
     for layer in range(layers):
         low = hidden.astype(BF16)
         preact = dot(low, map_full[layer]) + map_b[pl.ds(layer, 1), :]
@@ -259,9 +247,14 @@
         picked_out[j] = jnp.concatenate(chosen, axis=0)
 
 
-def weights_kernel(conv_w, kernel, square, stage, sems):
+def weights_kernel(samples, seeds, conv_w, z_table, kernel, square, latent_rows, stage, rows, sems, sem_z):
+    latents = 2 * samples
+    z_copies = []
+    for n in range(latents):
+        at = pl.multiple_of((seeds[n] // 8) * 8, 8)
+        z_copies.append(pltpu.make_async_copy(z_table.at[pl.ds(at, 8), :], rows.at[n], sem_z.at[n]))
     copies = [pltpu.make_async_copy(conv_w.at[t], stage.at[t], sems.at[t]) for t in range(TAPS)]
-    for copy in copies:
+    for copy in z_copies + copies:
         copy.start()
     total = jnp.zeros(square.shape, F32)
     for tap in range(TAPS):
@@ -271,6 +264,14 @@
         wide = low.astype(F32)
         total = total + wide * wide
     square[...] = total
+    normed = []
+    for n in range(latents):
+        z_copies[n].wait()
+        row = rows[n, pl.ds(lax.rem(seeds[n], 8), 1), :]
+        scale = lax.rsqrt(jnp.mean(row * row, axis=1, keepdims=True) + 1e-08)
+        normed.append(row * scale)
+    normed.append(jnp.zeros((16 - latents, rows.shape[2]), F32))
+    latent_rows[...] = jnp.concatenate(normed, axis=0)
 
 
 def bring_blocks(blocks, samples, side, where, picked, bias_full, style_rows, feat_t, aff_full, padded):
@@ -776,20 +777,21 @@
 
     half = width // 2
     pack_rows = samples * pixels + half + 16
+    flat_features = features.reshape(samples * pixels, LANES)
     pack = pl.pallas_call(
         pack_kernel,
-        out_shape=shape((pack_rows, LANES), BF16),
+        out_shape=shape((pack_rows + half + 16, LANES), BF16),
         in_specs=[SMEM] + [ANY] * 3,
         out_specs=VMEM,
         scratch_shapes=[
-            pltpu.VMEM((half, LANES), F32),
+            pltpu.VMEM((width, LANES), F32),
             pltpu.VMEM(chan_bias.shape, F32),
             pltpu.SemaphoreType.DMA((3,)),
         ],
         compiler_params=params(4),
-        cost_estimate=cost(1),
+        cost_estimate=cost(0),
         name="pack",
-    )(where, *hbm(aff_w, chan_bias, features.reshape(samples * pixels, LANES)))
+    )(where, *hbm(aff_w, chan_bias, flat_features))
     map_low = pl.pallas_call(
         low_kernel,
         out_shape=shape(map_w.shape, BF16),
@@ -797,24 +799,30 @@
         out_specs=VMEM,
         scratch_shapes=[pltpu.VMEM(map_w.shape, F32), pltpu.SemaphoreType.DMA((layers,))],
         compiler_params=params(8),
-        cost_estimate=cost(1),
+        cost_estimate=cost(0),
         name="low",
-    )(*hbm(map_w))
-    *chan_packs, last_step = spread_over_chan(pack, half + 16, map_low)
+    )(*hbm(after(map_w, pack)))
+    *chan_packs, last_step = spread_over_chan(flat_features, pack, map_low)
     blocks = spread_layers(map_low, "dp")
-    kernel, square = pl.pallas_call(
-        weights_kernel,
-        out_shape=(shape((3, width, 3 * LANES), BF16), shape((width, LANES), F32)),
-        in_specs=[ANY],
-        out_specs=(VMEM, VMEM),
+    kernel, square, latent_rows = pl.pallas_call(
+        functools.partial(weights_kernel, samples),
+        out_shape=(
+            shape((3, width, 3 * LANES), BF16),
+            shape((width, LANES), F32),
+            shape((16, width), F32),
+        ),
+        in_specs=[SMEM, ANY, ANY],
+        out_specs=(VMEM,) * 3,
         scratch_shapes=[
             pltpu.VMEM((TAPS, width, LANES), F32),
+            pltpu.VMEM((latents, 8, width), F32),
             pltpu.SemaphoreType.DMA((TAPS,)),
+            pltpu.SemaphoreType.DMA((latents,)),
         ],
         compiler_params=params(8),
-        cost_estimate=cost(2),
+        cost_estimate=cost(0),
         name="weights",
-    )(*hbm(after(conv_w.reshape(TAPS, width, LANES), blocks[1][0])))
+    )(seeds.reshape(-1), *hbm(after(conv_w.reshape(TAPS, width, LANES), blocks[1][0]), z_table))
     second = last_step(blocks[2][0], kernel)
     places = [place for _, place in blocks]
 
@@ -827,17 +835,13 @@
             shape((2, 8, width), F32),
             shape((layers, width, width), BF16),
         ),
-        in_specs=[SMEM] * 3 + [VMEM] * len(blocks) + [ANY, VMEM],
+        in_specs=[SMEM] * 2 + [VMEM] * (len(blocks) + 2),
         out_specs=(VMEM,) * 5,
-        scratch_shapes=[
-            pltpu.VMEM((latents, 8, width), F32),
-            pltpu.SemaphoreType.DMA((len(places),)),
-            pltpu.SemaphoreType.DMA((latents,)),
-        ],
+        scratch_shapes=[pltpu.SemaphoreType.DMA((len(places),))],
         compiler_params=params(12),
-        cost_estimate=cost(1),
+        cost_estimate=cost(0),
         name="mapping",
-    )(where, seeds.reshape(-1), crossover, *[block for block, _ in blocks], *hbm(z_table), map_b)
+    )(where, crossover, *[block for block, _ in blocks], latent_rows, map_b)
 
     both, first, first_pair = chan_packs
     feat_t, taps, style_rows, aff_full = pl.pallas_call(
@@ -855,7 +859,7 @@
             pltpu.VMEM((samples, pixels + 2 * side, width), BF16),
         ],
         compiler_params=params(16),
-        cost_estimate=cost(3),
+        cost_estimate=cost(0),
         name="begin",
     )(where, both, first, first_pair, kernel, picked)
     second_pair = swap(after(second, taps)[samples * pixels :], "dp", 1)
@@ -880,7 +884,7 @@
         ],
         input_output_aliases={12: 0, 13: 1, 14: 2},
         compiler_params=params(20),
-        cost_estimate=cost(3),
+        cost_estimate=cost(0),
         name="main",
     )(
         where,
@@ -910,7 +914,7 @@
         out_specs=(VMEM,) * 2,
         scratch_shapes=[pltpu.VMEM((pixels, TAPS * LANES), BF16)],
         compiler_params=params(16),
-        cost_estimate=cost(2),
+        cost_estimate=cost(0),
         name="factor",
     )(where, feat_t, wide, small, style_rows, kernel, aff_w)
     unit_pair = swap(unit[:, 1], "dp", 1)
@@ -925,7 +929,7 @@
         in_specs=[VMEM] * (n_ch + 3),
         out_specs=VMEM,
         compiler_params=params(8),
-        cost_estimate=cost(1),
+        cost_estimate=cost(0),
         name="combine",
     )(*sum_parts, masks, unit, unit_pair)
 
@@ -937,7 +941,7 @@
         out_specs=VMEM,
         scratch_shapes=[pltpu.VMEM((8, width), F32), pltpu.VMEM((lines, width), F32)],
         compiler_params=params(12),
-        cost_estimate=cost(2),
+        cost_estimate=cost(0),
         name="mapping_back",
     )(where, crossover, *after(sum_parts, total), masks, pre, hid, top, picked, small, map_full, aff_full)
     spread_pack = spread(pack, "dp")
@@ -981,7 +985,7 @@
             pltpu.SemaphoreType.DMA((layers // 2 + 6, 4)),
         ],
         compiler_params=params(20),
-        cost_estimate=cost(4),
+        cost_estimate=cost(12),
         name="update",
     )(where, *packs, map_w, map_w_mom, map_w_ema, *flat_aff, *tiny)
 
@@ -1009,7 +1013,7 @@
             + [pltpu.SemaphoreType.DMA((ninths // 3, 4))],
             input_output_aliases={4 + len(grads) + k: k for k in range(len(earlier))},
             compiler_params=params(16),
-            cost_estimate=cost(2),
+            cost_estimate=cost(0),
             name="conv_rest" if earlier else "conv_first",
         )(where, *grads, *conv_params, *earlier)
 

time: 79.3 us -> 76.9 us (0.970)
  waiting for transfers between devices: 24.6 us -> 22.1 us
    ppermute x2, waiting for transfers between devices: 5.45 us -> 3.69 us  [joint(): return lax.ppermute(value, ('dp', 'chan'), pairs)]
    ppermute x15, starting transfers between devices: 13.4 us -> 12.1 us  [swap(): lax.ppermute(value, axis, [(i, i ^ distance) for i in range(lax.axis_size...]
    ppermute x15, waiting for transfers between devices: 6.14 us -> 4.79 us  [swap(): lax.ppermute(value, axis, [(i, i ^ distance) for i in range(lax.axis_size...]
    ppermute x7, starting transfers between devices: 5.88 us -> 6.96 us  [crossed(): return lax.ppermute(value, axis, pairs)]
    pallas_call x1, Pallas kernels: 2.88 us -> 2.02 us  [local(): pl.pallas_call(functools.partial(mapping_kernel, n_dp, samples, places),...]
    pallas_call x2, Pallas kernels: 3.26 us -> 4.08 us  [the longest x1 2.47 us: local(): pl.pallas_call(functools.partial(weights_kernel, samples), out_shape=(sha...]
  transfers between devices with their start and end apart: 24 -> 24, of which waited for: 13 -> 13; matrix products, arithmetic and copies ran while one was open for 0% -> 1% of each run, Pallas kernels for 25% -> 28%
where the time goes in v5:
time: 76.9 us; the launch traced here: 76.6 us
  Pallas kernels  27 us (35%)
  starting transfers between devices  24.2 us (31%)
  waiting for transfers between devices  22.1 us (29%)
  between operations  2.59 us (3%)
    ppermute x7, waiting for transfers between devices, crossed(): return lax.ppermute(value, axis, pairs)  13.6 us
    ppermute x15, starting transfers between devices, swap(): lax.ppermute(value, axis, [(i, i ^ distance) for i in range(lax.axis_size...  12.1 us
    ppermute x7, starting transfers between devices, crossed(): return lax.ppermute(value, axis, pairs)  6.96 us
    pallas_call x2, Pallas kernels, conv_part(): pl.pallas_call(functools.partial(conv_kernel, turns), out_shape=[shape((T...  5.44 us
    ppermute x2, starting transfers between devices, joint(): return lax.ppermute(value, ('dp', 'chan'), pairs)  5.11 us
    ppermute x15, waiting for transfers between devices, swap(): lax.ppermute(value, axis, [(i, i ^ distance) for i in range(lax.axis_size...  4.79 us
    pallas_call x1, Pallas kernels, local(): pl.pallas_call(functools.partial(update_kernel, n_dp, samples, layers, [p...  4.35 us
    ppermute x2, waiting for transfers between devices, joint(): return lax.ppermute(value, ('dp', 'chan'), pairs)  3.69 us
  transfers between devices with their start and end apart: 24, of which 13 were waited for; matrix products, arithmetic and copies ran while one was open for 1% of the time, Pallas kernels for 28%

profile of v5, /device:TPU:1, one launch (start us, length us, event | category | flops | bytes accessed | tf_op | source)
XLA Modules:
  0.0 76.6 jit_solution(9748342937467936344)
XLA Ops:
  0.9 1.6 %pack.1 = bf16[1568,128]{1,0:T(8,128)(2,1)S(1)} custom-call(s32[2]{0:T(128)S(1)} %pad_add_fusion.where.refs_0_, f32[2,512,128]{2,1,0:T(8,128)} %aff_w.3, f32[3,128]{1,0:T(4,128)} %refs_13_.1, bf16[1024,128]{1,0:T(8,128)(2,1)} %bitcast.42), custom_call_target="tpu_custom_call" | custom-call | tf_op jit(solution)/shard_map/pack/pallas_call | solution.py:781
  2.6 3.8 %collective-permute-start.1 = (bf16[2592,128]{1,0:T(8,128)(2,1)S(1)}, bf16[2592,128]{1,0:T(8,128)(2,1)S(1)}, u32[]{:S(2)}, u32[]{:S(2)}) collective-permute-start(bf16[2592,128]{1,0:T(8,128)(2,1)S(1)} %pad_maximum_fusion.refs_1_), channel_id=1, source_target_pairs={{0,1},{1,0},{2,3},{3,2},{4,6},{5,7},{6,4},{7,5},{8,9},{9,8},{10,11... | collective-permute-start | bytes 1990664 | tf_op jit(solution)/shard_map/ppermute | solution.py:82
  6.4 1.4 %low.1.refs_2_ = bf16[8,64,512]{2,1,0:T(8,128)(2,1)S(1)} custom-call(f32[8,64,512]{2,1,0:T(8,128)} %refs_4_.1), custom_call_target="tpu_custom_call" | custom-call | tf_op jit(solution)/shard_map/low/pallas_call | solution.py:795
  7.8 1.3 %collective-permute-start.2 = (bf16[8,64,512]{2,1,0:T(8,128)(2,1)S(1)}, bf16[8,64,512]{2,1,0:T(8,128)(2,1)S(1)}, u32[]{:S(2)}, u32[]{:S(2)}) collective-permute-start(bf16[8,64,512]{2,1,0:T(8,128)(2,1)S(1)} %low.1.refs_2_), channel_id=1, source_target_pairs={{0,8},{4,20},{8,0},{12,28},{16,24},{20,4},{24,16},{28,12},{1,9},{5... | collective-permute-start | bytes 1572872 | tf_op jit(solution)/shard_map/ppermute | solution.py:98
  9.7 2.5 %weights.1 = (bf16[3,512,384]{2,1,0:T(8,128)(2,1)S(1)}, f32[512,128]{1,0:T(8,128)S(1)}, f32[16,512]{1,0:T(8,128)S(1)}) custom-call(s32[2]{0:T(128)S(1)} %bitcast.33, f32[9,512,128]{2,1,0:T(8,128)} %bitcast.25, f32[1024,512]{1,0:T(8,128)} %z_table.1), custom_call_target="tpu_custom_call" | custom-call | tf_op jit(solution)/shard_map/weights/pallas_call | solution.py:807
  12.2 1.3 %collective-permute-start.6 = (bf16[8,64,512]{2,1,0:T(8,128)(2,1)S(1)}, bf16[8,64,512]{2,1,0:T(8,128)(2,1)S(1)}, u32[]{:S(2)}, u32[]{:S(2)}) collective-permute-start(bf16[8,64,512]{2,1,0:T(8,128)(2,1)S(1)} %collective-permute-done.3.refs_3_), channel_id=1, source_target_pairs={{0,8},{4,20},{8,0},{12,28},{16,24},{20,4},{24,16},{28,12},{1,9},{5... | collective-permute-start | bytes 1572872 | tf_op jit(solution)/shard_map/ppermute | solution.py:98
  13.5 2.7 %collective-permute-done.2.refs_4_ = bf16[8,64,512]{2,1,0:T(8,128)(2,1)S(1)} collective-permute-done((bf16[8,64,512]{2,1,0:T(8,128)(2,1)S(1)}, bf16[8,64,512]{2,1,0:T(8,128)(2,1)S(1)}, u32[]{:S(2)}, u32[]{:S(2)}) %collective-permute-start.2) | collective-permute-done | bytes 524320 | tf_op jit(solution)/shard_map/ppermute | solution.py:98
  16.2 1.2 %collective-permute-start.7 = (bf16[8,64,512]{2,1,0:T(8,128)(2,1)S(1)}, bf16[8,64,512]{2,1,0:T(8,128)(2,1)S(1)}, u32[]{:S(2)}, u32[]{:S(2)}) collective-permute-start(bf16[8,64,512]{2,1,0:T(8,128)(2,1)S(1)} %collective-permute-done.2.refs_4_), channel_id=1, source_target_pairs={{0,16},{4,12},{8,24},{12,4},{16,0},{20,28},{24,8},{28,20},{1,17},{... | collective-permute-start | bytes 1572872 | tf_op jit(solution)/shard_map/ppermute | solution.py:98
  17.4 3.7 %collective-permute-done.1.refs_2_ = bf16[2592,128]{1,0:T(8,128)(2,1)S(1)} collective-permute-done((bf16[2592,128]{1,0:T(8,128)(2,1)S(1)}, bf16[2592,128]{1,0:T(8,128)(2,1)S(1)}, u32[]{:S(2)}, u32[]{:S(2)}) %collective-permute-start.1) | collective-permute-done | bytes 663584 | tf_op jit(solution)/shard_map/ppermute | solution.py:82
  21.2 1.3 %collective-permute-start.4 = (bf16[2592,128]{1,0:T(8,128)(2,1)S(1)}, bf16[2592,128]{1,0:T(8,128)(2,1)S(1)}, u32[]{:S(2)}, u32[]{:S(2)}) collective-permute-start(bf16[2592,128]{1,0:T(8,128)(2,1)S(1)} %broadcast_select_fusion), channel_id=1, source_target_pairs={{1,2},{2,1},{5,4},{6,7},{9,10},{10,9},{13,12},{14,15},{17,18},{18,... | collective-permute-start | bytes 1990664 | tf_op jit(solution)/shard_map/ppermute | solution.py:82
  22.9 3.9 %collective-permute-start.9 = (bf16[8,64,512]{2,1,0:T(8,128)(2,1)S(1)}, bf16[8,64,512]{2,1,0:T(8,128)(2,1)S(1)}, u32[]{:S(2)}, u32[]{:S(2)}) collective-permute-start(bf16[8,64,512]{2,1,0:T(8,128)(2,1)S(1)} %collective-permute-done.6.refs_5_), channel_id=1, source_target_pairs={{0,4},{4,0},{8,12},{12,8},{16,20},{20,16},{24,28},{28,24},{1,5},{5... | collective-permute-start | bytes 1572872 | tf_op jit(solution)/shard_map/ppermute | solution.py:44
  26.9 1.2 %collective-permute-done.7.refs_6_ = bf16[8,64,512]{2,1,0:T(8,128)(2,1)S(1)} collective-permute-done((bf16[8,64,512]{2,1,0:T(8,128)(2,1)S(1)}, bf16[8,64,512]{2,1,0:T(8,128)(2,1)S(1)}, u32[]{:S(2)}, u32[]{:S(2)}) %collective-permute-start.7) | collective-permute-done | bytes 524320 | tf_op jit(solution)/shard_map/ppermute | solution.py:98
  30.0 2.0 %mapping.1 = (f32[8,8,512]{2,1,0:T(8,128)S(1)}, f32[8,8,512]{2,1,0:T(8,128)S(1)}, f32[8,512]{1,0:T(8,128)S(1)}, f32[2,8,512]{2,1,0:T(8,128)S(1)}, bf16[8,512,512]{2,1,0:T(8,128)(2,1)S(1)}) custom-call(s32[2]{0:T(128)S(1)} %pad_add_fusion.where.refs_0_, s32[1]{0:T(128)S(6)} %copy.66.refs_1_.crossover, bf16[8,64,512]{2,1,0:T(8,128)(2,1)S(1)} %low.1.refs_2_, ...), custom_call_target="tpu_custom_call" | custom-call | tf_op jit(solution)/shard_map/mapping/pallas_call | solution.py:829
  32.0 2.7 %begin.1 = (bf16[1,512,1024]{2,1,0:T(8,128)(2,1)S(1)}, f32[1,1024,384]{2,1,0:T(8,128)S(1)}, f32[8,512]{1,0:T(8,128)S(1)}, bf16[512,512]{1,0:T(8,128)(2,1)S(1)}) custom-call(s32[2]{0:T(128)S(1)} %pad_add_fusion.where.refs_0_, bf16[2592,128]{1,0:T(8,128)(2,1)S(1)} %pad_maximum_fusion.refs_1_, bf16[2592,128]{1,0:T(8,128)(2,1)S(1)} %collective-permute-done.1.refs_2_, ...), custom_call_target="tpu_custom_call" | custom-call | tf_op jit(solution)/shard_map/begin/pallas_call | solution.py:847
  35.6 0.9 %collective-permute-done.11.refs_2_ = bf16[1568,128]{1,0:T(8,128)(2,1)S(1)} collective-permute-done((bf16[1568,128]{1,0:T(8,128)(2,1)S(1)}, bf16[1568,128]{1,0:T(8,128)(2,1)S(1)}, u32[]{:S(2)}, u32[]{:S(2)}) %collective-permute-start.11) | collective-permute-done | bytes 401440 | tf_op jit(solution)/shard_map/ppermute | solution.py:44
  36.6 2.1 %main.1 = (bf16[1,512,1024]{2,1,0:T(8,128)(2,1)S(1)}, f32[8,512]{1,0:T(8,128)S(1)}, bf16[512,512]{1,0:T(8,128)(2,1)S(1)}, f32[1,1040,128]{2,1,0:T(8,128)S(1)}, f...) custom-call(s32[2]{0:T(128)S(1)} %pad_add_fusion.where.refs_0_, ...), custom_call_target="tpu_custom_call", output_to_operand_aliasing={{0}: (12, {}), {1}: (13, {}), {2}: (14, {})} | custom-call | tf_op jit(solution)/shard_map/main/pallas_call | solution.py:866
  38.9 2.6 %factor.1 = (bf16[1,2,2304,128]{3,2,1,0:T(8,128)(2,1)S(1)}, f32[8,128]{1,0:T(8,128)S(1)}) custom-call(s32[2]{0:T(128)S(1)} %pad_add_fusion.where.refs_0_, bf16[1,512,1024]{2,1,0:T(8,128)(2,1)S(1)} %get-tuple-element.100.feat_t, f32[1,1040,128]{2,1,0:T(8,128)S(1)} %get-tuple-element.101.wide, f32[8,128]{1,0:T(8,128)S(1)} %get-tuple-element.102.small.refs_9_, ...), custom_call_target="tpu_custom_call" | custom-call | tf_op jit(solution)/shard_map/factor/pallas_call | solution.py:907
  42.1 1.7 %collective-permute-start.15 = (f32[16,128]{1,0:T(8,128)S(1)}, f32[16,128]{1,0:T(8,128)S(1)}, u32[]{:S(2)}, u32[]{:S(2)}) collective-permute-start(f32[16,128]{1,0:T(8,128)S(1)} %pad_maximum_fusion.2.refs_0_), channel_id=1, source_target_pairs={{0,3},{1,2},{2,1},{3,0},{4,7},{5,6},{6,5},{7,4},{8,11},{9,10},{10,... | collective-permute-start | bytes 24584 | tf_op jit(solution)/shard_map/ppermute | solution.py:44
  43.7 1.2 %collective-permute-start.14 = (f32[16,128]{1,0:T(8,128)S(1)}, f32[16,128]{1,0:T(8,128)S(1)}, u32[]{:S(2)}, u32[]{:S(2)}) collective-permute-start(f32[16,128]{1,0:T(8,128)S(1)} %pad_maximum_fusion.2.refs_0_), channel_id=1, source_target_pairs={{0,2},{1,3},{2,0},{3,1},{4,6},{5,7},{6,4},{7,5},{8,10},{9,11},{10,... | collective-permute-start | bytes 24584 | tf_op jit(solution)/shard_map/ppermute | solution.py:44
  44.9 0.8 %collective-permute-start.13 = (f32[16,128]{1,0:T(8,128)S(1)}, f32[16,128]{1,0:T(8,128)S(1)}, u32[]{:S(2)}, u32[]{:S(2)}) collective-permute-start(f32[16,128]{1,0:T(8,128)S(1)} %pad_maximum_fusion.2.refs_0_), channel_id=1, source_target_pairs={{0,1},{1,0},{2,3},{3,2},{4,5},{5,4},{6,7},{7,6},{8,9},{9,8},{10,11... | collective-permute-start | bytes 24584 | tf_op jit(solution)/shard_map/ppermute | solution.py:44
  46.4 0.9 %collective-permute-done.14.refs_2_ = f32[16,128]{1,0:T(8,128)S(1)} collective-permute-done((f32[16,128]{1,0:T(8,128)S(1)}, f32[16,128]{1,0:T(8,128)S(1)}, u32[]{:S(2)}, u32[]{:S(2)}) %collective-permute-start.14) | collective-permute-done | bytes 8224 | tf_op jit(solution)/shard_map/ppermute | solution.py:44
  47.6 1.3 %collective-permute-start.21 = (bf16[2336,128]{1,0:T(8,128)(2,1)S(1)}, bf16[2336,128]{1,0:T(8,128)(2,1)S(1)}, u32[]{:S(2)}, u32[]{:S(2)}) collective-permute-start(bf16[2336,128]{1,0:T(8,128)(2,1)S(1)} %combine.1), channel_id=1, source_target_pairs={{0,8},{4,20},{8,0},{12,28},{16,24},{20,4},{24,16},{28,12},{1,9},{5... | collective-permute-start | bytes 1794056 | tf_op jit(solution)/shard_map/ppermute | solution.py:98
  48.9 2.1 %mapping_back.1 = bf16[48,512]{1,0:T(8,128)(2,1)S(1)} custom-call(s32[2]{0:T(128)S(1)} %pad_add_fusion.where.refs_0_, s32[1]{0:T(128)S(6)} %copy.66.refs_1_.crossover, f32[16,128]{1,0:T(8,128)S(1)} %pad_maximum_fusion.2.refs_0_, f32[16,128]{1,0:T(8,128)S(1)} %collective-permute-done.13.refs_1_, f32[16,128]{1,0:T(8,128)S(1)} %collective-permute-done.14.refs_2_, ...), custom_call_target="tpu_custom_call" | custom-call | tf_op jit(solution)/shard_map/mapping_back/pallas_call | solution.py:937
  51.2 2.2 %collective-permute-start.17 = (bf16[48,512]{1,0:T(8,128)(2,1)S(1)}, bf16[48,512]{1,0:T(8,128)(2,1)S(1)}, u32[]{:S(2)}, u32[]{:S(2)}) collective-permute-start(bf16[48,512]{1,0:T(8,128)(2,1)S(1)} %mapping_back.1), channel_id=1, source_target_pairs={{0,4},{4,0},{8,12},{12,8},{16,20},{20,16},{24,28},{28,24},{1,5},{5... | collective-permute-start | bytes 147464 | tf_op jit(solution)/shard_map/ppermute | solution.py:44
  53.4 0.9 %collective-permute-done.17 = bf16[48,512]{1,0:T(8,128)(2,1)S(1)} collective-permute-done((bf16[48,512]{1,0:T(8,128)(2,1)S(1)}, bf16[48,512]{1,0:T(8,128)(2,1)S(1)}, u32[]{:S(2)}, u32[]{:S(2)}) %collective-permute-start.17) | collective-permute-done | bytes 49184 | tf_op jit(solution)/shard_map/ppermute | solution.py:44
  54.5 4.6 %collective-permute-done.18.refs_1_ = bf16[96,512]{1,0:T(8,128)(2,1)S(1)} collective-permute-done((bf16[96,512]{1,0:T(8,128)(2,1)S(1)}, bf16[96,512]{1,0:T(8,128)(2,1)S(1)}, u32[]{:S(2)}, u32[]{:S(2)}) %collective-permute-start.18) | collective-permute-done | bytes 98336 | tf_op jit(solution)/shard_map/ppermute | solution.py:98
  59.3 1.2 %collective-permute-start.19 = (bf16[96,512]{1,0:T(8,128)(2,1)S(1)}, bf16[96,512]{1,0:T(8,128)(2,1)S(1)}, u32[]{:S(2)}, u32[]{:S(2)}) collective-permute-start(bf16[96,512]{1,0:T(8,128)(2,1)S(1)} %collective-permute-done.18.refs_1_), channel_id=1, source_target_pairs={{0,8},{4,20},{8,0},{12,28},{16,24},{20,4},{24,16},{28,12},{1,9},{5... | collective-permute-start | bytes 294920 | tf_op jit(solution)/shard_map/ppermute | solution.py:98
  61.0 2.0 %collective-permute-done.19.refs_2_ = bf16[96,512]{1,0:T(8,128)(2,1)S(1)} collective-permute-done((bf16[96,512]{1,0:T(8,128)(2,1)S(1)}, bf16[96,512]{1,0:T(8,128)(2,1)S(1)}, u32[]{:S(2)}, u32[]{:S(2)}) %collective-permute-start.19) | collective-permute-done | bytes 98336 | tf_op jit(solution)/shard_map/ppermute | solution.py:98
  63.2 4.3 %update.1 = (f32[8,64,512]{2,1,0:T(8,128)}, f32[8,64,512]{2,1,0:T(8,128)}, f32[8,64,512]{2,1,0:T(8,128)}, bf16[8,64,512]{2,1,0:T(8,128)(2,1)}, f32[1024,128]{1,0...) custom-call(s32[2]{0:T(128)S(1)} %pad_add_fusion.where.refs_0_, ...), custom_call_target="tpu_custom_call" | custom-call | flops 12000000000 | tf_op jit(solution)/shard_map/update/pallas_call | solution.py:973
  67.5 2.8 %collective-permute-done.22 = bf16[2336,128]{1,0:T(8,128)(2,1)S(1)} collective-permute-done((bf16[2336,128]{1,0:T(8,128)(2,1)S(1)}, bf16[2336,128]{1,0:T(8,128)(2,1)S(1)}, u32[]{:S(2)}, u32[]{:S(2)}) %collective-permute-start.22) | collective-permute-done | bytes 598048 | tf_op jit(solution)/shard_map/ppermute | solution.py:98
  71.0 2.2 %conv_first.1 = (f32[4608,128]{1,0:T(8,128)}, f32[4608,128]{1,0:T(8,128)}, f32[4608,128]{1,0:T(8,128)}, bf16[4608,128]{1,0:T(8,128)(2,1)}) custom-call(s32[2]{0:T(128)S(1)} %pad_add_fusion.where.refs_0_, bf16[2336,128]{1,0:T(8,128)(2,1)S(1)} %add_convert_fusion.refs_0_, f32[4608,128]{1,0:T(8,128)S(1)} %bitcast.26, f32[4608,128]{1,0:T(8,128)S(1)} %bitcast.28, ...), custom_call_target="tpu_custom_call" | custom-call | tf_op jit(solution)/shard_map/conv_first/pallas_call | solution.py:1007
  73.3 3.2 %conv_rest.1 = (f32[4608,128]{1,0:T(8,128)}, f32[4608,128]{1,0:T(8,128)}, f32[4608,128]{1,0:T(8,128)}, bf16[4608,128]{1,0:T(8,128)(2,1)}) custom-call(s32[2]{0:T(128)S(1)} %pad_add_fusion.where.refs_0_, bf16[2336,128]{1,0:T(8,128)(2,1)S(1)} %add_convert_fusion.refs_0_, ...), custom_call_target="tpu_custom_call", output_to_operand_aliasing={{0}: (6, {}), {1}: (7, {}), {2}: (8, {}), {3}: (9, {})} | custom-call | tf_op jit(solution)/shard_map/conv_rest/pallas_call | solution.py:1007
  (83 shorter events, 6.3 us)
Async XLA Ops:
  0.7 1.8 %collective-permute-start = (bf16[1024,128]{1,0:T(8,128)(2,1)}, bf16[1024,128]{1,0:T(8,128)(2,1)S(1)}, u32[]{:S(2)}, u32[]{:S(2)}) collective-permute-start(bf16[1024,128]{1,0:T(8,128)(2,1)} %bitcast.41), channel_id=1, source_target_pairs={{0,4},{4,0},{8,12},{12,8},{16,20},{20,16},{24,28},{28,24},{1,5},{5... | collective-permute-start | bytes 786440 | tf_op jit(solution)/shard_map/ppermute | solution.py:44
  2.6 18.6 %collective-permute-start.1 = (bf16[2592,128]{1,0:T(8,128)(2,1)S(1)}, bf16[2592,128]{1,0:T(8,128)(2,1)S(1)}, u32[]{:S(2)}, u32[]{:S(2)}) collective-permute-start(bf16[2592,128]{1,0:T(8,128)(2,1)S(1)} %pad_maximum_fusion.refs_1_), channel_id=1, source_target_pairs={{0,1},{1,0},{2,3},{3,2},{4,6},{5,7},{6,4},{7,5},{8,9},{9,8},{10,11... | collective-permute-start | bytes 1990664 | tf_op jit(solution)/shard_map/ppermute | solution.py:82
  7.7 2.0 %collective-permute-start.3 = (bf16[8,64,512]{2,1,0:T(8,128)(2,1)S(1)}, bf16[8,64,512]{2,1,0:T(8,128)(2,1)S(1)}, u32[]{:S(2)}, u32[]{:S(2)}) collective-permute-start(bf16[8,64,512]{2,1,0:T(8,128)(2,1)S(1)} %low.1.refs_2_), channel_id=1, source_target_pairs={{0,4},{4,0},{8,12},{12,8},{16,20},{20,16},{24,28},{28,24},{1,5},{5... | collective-permute-start | bytes 1572872 | tf_op jit(solution)/shard_map/ppermute | solution.py:44
  7.8 8.4 %collective-permute-start.2 = (bf16[8,64,512]{2,1,0:T(8,128)(2,1)S(1)}, bf16[8,64,512]{2,1,0:T(8,128)(2,1)S(1)}, u32[]{:S(2)}, u32[]{:S(2)}) collective-permute-start(bf16[8,64,512]{2,1,0:T(8,128)(2,1)S(1)} %low.1.refs_2_), channel_id=1, source_target_pairs={{0,8},{4,20},{8,0},{12,28},{16,24},{20,4},{24,16},{28,12},{1,9},{5... | collective-permute-start | bytes 1572872 | tf_op jit(solution)/shard_map/ppermute | solution.py:98
  12.2 17.8 %copy-start.5 = (f32[8,512]{1,0:T(8,128)S(1)}, f32[8,512]{1,0:T(8,128)}, u32[]{:S(2)}) copy-start(f32[8,512]{1,0:T(8,128)} %refs_10_.3) | copy-start | bytes 49156
  12.2 10.7 %collective-permute-start.6 = (bf16[8,64,512]{2,1,0:T(8,128)(2,1)S(1)}, bf16[8,64,512]{2,1,0:T(8,128)(2,1)S(1)}, u32[]{:S(2)}, u32[]{:S(2)}) collective-permute-start(bf16[8,64,512]{2,1,0:T(8,128)(2,1)S(1)} %collective-permute-done.3.refs_3_), channel_id=1, source_target_pairs={{0,8},{4,20},{8,0},{12,28},{16,24},{20,4},{24,16},{28,12},{1,9},{5... | collective-permute-start | bytes 1572872 | tf_op jit(solution)/shard_map/ppermute | solution.py:98
  16.2 11.8 %collective-permute-start.7 = (bf16[8,64,512]{2,1,0:T(8,128)(2,1)S(1)}, bf16[8,64,512]{2,1,0:T(8,128)(2,1)S(1)}, u32[]{:S(2)}, u32[]{:S(2)}) collective-permute-start(bf16[8,64,512]{2,1,0:T(8,128)(2,1)S(1)} %collective-permute-done.2.refs_4_), channel_id=1, source_target_pairs={{0,16},{4,12},{8,24},{12,4},{16,0},{20,28},{24,8},{28,20},{1,17},{... | collective-permute-start | bytes 1572872 | tf_op jit(solution)/shard_map/ppermute | solution.py:98
  21.2 13.5 %collective-permute-start.4 = (bf16[2592,128]{1,0:T(8,128)(2,1)S(1)}, bf16[2592,128]{1,0:T(8,128)(2,1)S(1)}, u32[]{:S(2)}, u32[]{:S(2)}) collective-permute-start(bf16[2592,128]{1,0:T(8,128)(2,1)S(1)} %broadcast_select_fusion), channel_id=1, source_target_pairs={{1,2},{2,1},{5,4},{6,7},{9,10},{10,9},{13,12},{14,15},{17,18},{18,... | collective-permute-start | bytes 1990664 | tf_op jit(solution)/shard_map/ppermute | solution.py:82
  22.5 6.8 %collective-permute-start.8 = (bf16[8,64,512]{2,1,0:T(8,128)(2,1)S(1)}, bf16[8,64,512]{2,1,0:T(8,128)(2,1)S(1)}, u32[]{:S(2)}, u32[]{:S(2)}) collective-permute-start(bf16[8,64,512]{2,1,0:T(8,128)(2,1)S(1)} %collective-permute-done.2.refs_4_), channel_id=1, source_target_pairs={{0,4},{4,0},{8,12},{12,8},{16,20},{20,16},{24,28},{28,24},{1,5},{5... | collective-permute-start | bytes 1572872 | tf_op jit(solution)/shard_map/ppermute | solution.py:44
  22.9 6.4 %collective-permute-start.9 = (bf16[8,64,512]{2,1,0:T(8,128)(2,1)S(1)}, bf16[8,64,512]{2,1,0:T(8,128)(2,1)S(1)}, u32[]{:S(2)}, u32[]{:S(2)}) collective-permute-start(bf16[8,64,512]{2,1,0:T(8,128)(2,1)S(1)} %collective-permute-done.6.refs_5_), channel_id=1, source_target_pairs={{0,4},{4,0},{8,12},{12,8},{16,20},{20,16},{24,28},{28,24},{1,5},{5... | collective-permute-start | bytes 1572872 | tf_op jit(solution)/shard_map/ppermute | solution.py:44
  28.0 1.9 %collective-permute-start.10 = (bf16[8,64,512]{2,1,0:T(8,128)(2,1)S(1)}, bf16[8,64,512]{2,1,0:T(8,128)(2,1)S(1)}, u32[]{:S(2)}, u32[]{:S(2)}) collective-permute-start(bf16[8,64,512]{2,1,0:T(8,128)(2,1)S(1)} %collective-permute-done.7.refs_6_), channel_id=1, source_target_pairs={{0,4},{4,0},{8,12},{12,8},{16,20},{20,16},{24,28},{28,24},{1,5},{5... | collective-permute-start | bytes 1572872 | tf_op jit(solution)/shard_map/ppermute | solution.py:44
  28.1 3.9 %collective-permute-start.5 = (bf16[1568,128]{1,0:T(8,128)(2,1)S(1)}, bf16[1568,128]{1,0:T(8,128)(2,1)S(1)}, u32[]{:S(2)}, u32[]{:S(2)}) collective-permute-start(bf16[1568,128]{1,0:T(8,128)(2,1)S(1)} %slice.28), channel_id=1, source_target_pairs={{0,4},{4,0},{8,12},{12,8},{16,20},{20,16},{24,28},{28,24},{1,5},{5... | collective-permute-start | bytes 1204232 | tf_op jit(solution)/shard_map/ppermute | solution.py:44
  34.8 1.8 %collective-permute-start.11 = (bf16[1568,128]{1,0:T(8,128)(2,1)S(1)}, bf16[1568,128]{1,0:T(8,128)(2,1)S(1)}, u32[]{:S(2)}, u32[]{:S(2)}) collective-permute-start(bf16[1568,128]{1,0:T(8,128)(2,1)S(1)} %slice.22), channel_id=1, source_target_pairs={{0,4},{4,0},{8,12},{12,8},{16,20},{20,16},{24,28},{28,24},{1,5},{5... | collective-permute-start | bytes 1204232 | tf_op jit(solution)/shard_map/ppermute | solution.py:44
  38.7 3.3 %collective-permute-start.12 = (f32[8,128]{1,0:T(8,128)S(1)}, f32[8,128]{1,0:T(8,128)S(1)}, u32[]{:S(2)}, u32[]{:S(2)}) collective-permute-start(f32[8,128]{1,0:T(8,128)S(1)} %get-tuple-element.105), channel_id=1, source_target_pairs={{0,4},{4,0},{8,12},{12,8},{16,20},{20,16},{24,28},{28,24},{1,5},{5... | collective-permute-start | bytes 12296 | tf_op jit(solution)/shard_map/ppermute | solution.py:44
  41.6 5.8 %collective-permute-start.16 = (bf16[1,2304,128]{2,1,0:T(8,128)(2,1)S(1)}, bf16[1,2304,128]{2,1,0:T(8,128)(2,1)S(1)}, u32[]{:S(2)}, u32[]{:S(2)}) collective-permute-start(bf16[1,2304,128]{2,1,0:T(8,128)(2,1)S(1)} %slice_bitcast_fusion), channel_id=1, source_target_pairs={{0,4},{4,0},{8,12},{12,8},{16,20},{20,16},{24,28},{28,24},{1,5},{5... | collective-permute-start | bytes 1769480 | tf_op jit(solution)/shard_map/ppermute | solution.py:44
  42.1 4.4 %collective-permute-start.15 = (f32[16,128]{1,0:T(8,128)S(1)}, f32[16,128]{1,0:T(8,128)S(1)}, u32[]{:S(2)}, u32[]{:S(2)}) collective-permute-start(f32[16,128]{1,0:T(8,128)S(1)} %pad_maximum_fusion.2.refs_0_), channel_id=1, source_target_pairs={{0,3},{1,2},{2,1},{3,0},{4,7},{5,6},{6,5},{7,4},{8,11},{9,10},{10,... | collective-permute-start | bytes 24584 | tf_op jit(solution)/shard_map/ppermute | solution.py:44
  43.7 3.6 %collective-permute-start.14 = (f32[16,128]{1,0:T(8,128)S(1)}, f32[16,128]{1,0:T(8,128)S(1)}, u32[]{:S(2)}, u32[]{:S(2)}) collective-permute-start(f32[16,128]{1,0:T(8,128)S(1)} %pad_maximum_fusion.2.refs_0_), channel_id=1, source_target_pairs={{0,2},{1,3},{2,0},{3,1},{4,6},{5,7},{6,4},{7,5},{8,10},{9,11},{10,... | collective-permute-start | bytes 24584 | tf_op jit(solution)/shard_map/ppermute | solution.py:44
  44.9 2.5 %collective-permute-start.13 = (f32[16,128]{1,0:T(8,128)S(1)}, f32[16,128]{1,0:T(8,128)S(1)}, u32[]{:S(2)}, u32[]{:S(2)}) collective-permute-start(f32[16,128]{1,0:T(8,128)S(1)} %pad_maximum_fusion.2.refs_0_), channel_id=1, source_target_pairs={{0,1},{1,0},{2,3},{3,2},{4,5},{5,4},{6,7},{7,6},{8,9},{9,8},{10,11... | collective-permute-start | bytes 24584 | tf_op jit(solution)/shard_map/ppermute | solution.py:44
  47.6 12.9 %collective-permute-start.21 = (bf16[2336,128]{1,0:T(8,128)(2,1)S(1)}, bf16[2336,128]{1,0:T(8,128)(2,1)S(1)}, u32[]{:S(2)}, u32[]{:S(2)}) collective-permute-start(bf16[2336,128]{1,0:T(8,128)(2,1)S(1)} %combine.1), channel_id=1, source_target_pairs={{0,8},{4,20},{8,0},{12,28},{16,24},{20,4},{24,16},{28,12},{1,9},{5... | collective-permute-start | bytes 1794056 | tf_op jit(solution)/shard_map/ppermute | solution.py:98
  48.9 14.1 %copy-start.10 = (f32[8,64,512]{2,1,0:T(8,128)S(1)}, f32[8,64,512]{2,1,0:T(8,128)}, u32[]{:S(2)}) copy-start(f32[8,64,512]{2,1,0:T(8,128)} %refs_5_.1) | copy-start | bytes 3145732
  48.9 14.1 %copy-start.11 = (f32[8,64,512]{2,1,0:T(8,128)S(1)}, f32[8,64,512]{2,1,0:T(8,128)}, u32[]{:S(2)}) copy-start(f32[8,64,512]{2,1,0:T(8,128)} %refs_6_.3) | copy-start | bytes 3145732
  48.9 14.1 %copy-start.13 = (f32[2,512,128]{2,1,0:T(8,128)S(1)}, f32[2,512,128]{2,1,0:T(8,128)}, u32[]{:S(2)}) copy-start(f32[2,512,128]{2,1,0:T(8,128)} %param.40) | copy-start | bytes 1572868
  51.1 12.0 %copy-start.4 = (f32[8,64,512]{2,1,0:T(8,128)S(1)}, f32[8,64,512]{2,1,0:T(8,128)}, u32[]{:S(2)}) copy-start(f32[8,64,512]{2,1,0:T(8,128)} %refs_4_.1) | copy-start | bytes 3145732
  51.1 12.0 %copy-start.12 = (f32[2,512,128]{2,1,0:T(8,128)S(1)}, f32[2,512,128]{2,1,0:T(8,128)}, u32[]{:S(2)}) copy-start(f32[2,512,128]{2,1,0:T(8,128)} %param.39) | copy-start | bytes 1572868
  51.1 12.0 %copy-start.14 = (f32[8,512]{1,0:T(8,128)S(1)}, f32[8,512]{1,0:T(8,128)}, u32[]{:S(2)}) copy-start(f32[8,512]{1,0:T(8,128)} %refs_11_.4) | copy-start | bytes 49156
  51.1 12.0 %copy-start.15 = (f32[8,512]{1,0:T(8,128)S(1)}, f32[8,512]{1,0:T(8,128)}, u32[]{:S(2)}) copy-start(f32[8,512]{1,0:T(8,128)} %refs_12_.1) | copy-start | bytes 49156
  51.2 3.1 %collective-permute-start.17 = (bf16[48,512]{1,0:T(8,128)(2,1)S(1)}, bf16[48,512]{1,0:T(8,128)(2,1)S(1)}, u32[]{:S(2)}, u32[]{:S(2)}) collective-permute-start(bf16[48,512]{1,0:T(8,128)(2,1)S(1)} %mapping_back.1), channel_id=1, source_target_pairs={{0,4},{4,0},{8,12},{12,8},{16,20},{20,16},{24,28},{28,24},{1,5},{5... | collective-permute-start | bytes 147464 | tf_op jit(solution)/shard_map/ppermute | solution.py:44
  54.3 4.9 %collective-permute-start.18 = (bf16[96,512]{1,0:T(8,128)(2,1)S(1)}, bf16[96,512]{1,0:T(8,128)(2,1)S(1)}, u32[]{:S(2)}, u32[]{:S(2)}) collective-permute-start(bf16[96,512]{1,0:T(8,128)(2,1)S(1)} %pad_maximum_fusion.1.refs_0_), channel_id=1, source_target_pairs={{0,16},{4,12},{8,24},{12,4},{16,0},{20,28},{24,8},{28,20},{1,17},{... | collective-permute-start | bytes 294920 | tf_op jit(solution)/shard_map/ppermute | solution.py:98
  59.2 1.9 %collective-permute-start.20 = (bf16[96,512]{1,0:T(8,128)(2,1)S(1)}, bf16[96,512]{1,0:T(8,128)(2,1)S(1)}, u32[]{:S(2)}, u32[]{:S(2)}) collective-permute-start(bf16[96,512]{1,0:T(8,128)(2,1)S(1)} %collective-permute-done.18.refs_1_), channel_id=1, source_target_pairs={{0,4},{4,0},{8,12},{12,8},{16,20},{20,16},{24,28},{28,24},{1,5},{5... | collective-permute-start | bytes 294920 | tf_op jit(solution)/shard_map/ppermute | solution.py:44
  59.3 3.8 %collective-permute-start.19 = (bf16[96,512]{1,0:T(8,128)(2,1)S(1)}, bf16[96,512]{1,0:T(8,128)(2,1)S(1)}, u32[]{:S(2)}, u32[]{:S(2)}) collective-permute-start(bf16[96,512]{1,0:T(8,128)(2,1)S(1)} %collective-permute-done.18.refs_1_), channel_id=1, source_target_pairs={{0,8},{4,20},{8,0},{12,28},{16,24},{20,4},{24,16},{28,12},{1,9},{5... | collective-permute-start | bytes 294920 | tf_op jit(solution)/shard_map/ppermute | solution.py:98
  60.7 9.6 %collective-permute-start.22 = (bf16[2336,128]{1,0:T(8,128)(2,1)S(1)}, bf16[2336,128]{1,0:T(8,128)(2,1)S(1)}, u32[]{:S(2)}, u32[]{:S(2)}) collective-permute-start(bf16[2336,128]{1,0:T(8,128)(2,1)S(1)} %add_convert_fusion.1), channel_id=1, source_target_pairs={{0,16},{4,12},{8,24},{12,4},{16,0},{20,28},{24,8},{28,20},{1,17},{... | collective-permute-start | bytes 1794056 | tf_op jit(solution)/shard_map/ppermute | solution.py:98
  70.5 2.8 %collective-permute-start.23 = (bf16[2336,128]{1,0:T(8,128)(2,1)S(1)}, bf16[2336,128]{1,0:T(8,128)(2,1)S(1)}, u32[]{:S(2)}, u32[]{:S(2)}) collective-permute-start(bf16[2336,128]{1,0:T(8,128)(2,1)S(1)} %add_convert_fusion.refs_0_), channel_id=1, source_target_pairs={{0,4},{4,0},{8,12},{12,8},{16,20},{20,16},{24,28},{28,24},{1,5},{5... | collective-permute-start | bytes 1794056 | tf_op jit(solution)/shard_map/ppermute | solution.py:44
  (13 other events, 108.9 us)

commit v6 on v5

--- a/solution.py
+++ b/solution.py
@@ -274,7 +274,9 @@
     latent_rows[...] = jnp.concatenate(normed, axis=0)
 
 
-def bring_blocks(blocks, samples, side, where, picked, bias_full, style_rows, feat_t, aff_full, padded):
+def bring_blocks(
+    blocks, samples, side, where, picked, bias_full, style_rows, feat_t, aff_full, kernel, padded, rows
+):
     width = aff_full.shape[0]
     half, pixels = width // 2, side * side
     dp, ch = where[0], where[1]
@@ -282,57 +284,56 @@
     mine = pl.ds(pl.multiple_of(pair * half, half), half)
     other = pl.ds(pl.multiple_of((1 - pair) * half, half), half)
     chosen = picked[0].astype(BF16)
-    for source, top, tail_at, other_source, other_tail_at, k in blocks:
+    blank = jnp.zeros((side, padded.shape[2]), BF16)
+    for s in range(samples):
+        padded[s, pl.ds(0, side), :] = blank
+        padded[s, pl.ds(side + pixels, side), :] = blank
+    for slot, (source, top, tail_at, other_source, other_tail_at, k) in enumerate(blocks):
         lane = pl.ds(pl.multiple_of(lax.bitwise_xor(ch, k) * LANES, LANES), LANES)
+        place = pl.ds(slot * LANES, LANES)
         aff_full[mine, lane] = source[pl.ds(tail_at, half), :]
         aff_full[other, lane] = other_source[pl.ds(other_tail_at, half), :]
         bias_full[...] = source[pl.ds(tail_at + half, 16), :].astype(F32)
         bias_row = bias_full[0:1, :] + bias_full[1:2, :] + bias_full[2:3, :]
         style = (dot(chosen, aff_full[:, lane]) + bias_row).astype(BF16)
         style_rows[:, lane] = style.astype(F32)
+        for dy in range(3):
+            rows[dy, place, :] = kernel[dy, lane, :]
         for s in range(samples):
             value = source[pl.ds(top + s * pixels, pixels), :]
             feat_t[s, lane, :] = value.T
-            padded[s, pl.ds(side, pixels), lane] = value * style[s : s + 1, :]
+            padded[s, pl.ds(side, pixels), place] = value * style[s : s + 1, :]
 
 
 def begin_kernel(n_ch, samples, side, *refs):
-    where, both, first, first_pair, kernel, picked = refs[:6]
-    feat_t, taps, style_rows, aff_full, bias_full, padded = refs[6:]
+    where, both, first, kernel, picked = refs[:5]
+    feat_t, taps, style_rows, aff_full, bias_full, padded, rows = refs[5:]
     width = aff_full.shape[0]
     half, pixels = width // 2, side * side
     feats, tail_rows = samples * pixels, half + 16
-    cut = first.shape[0] - first_pair.shape[0]
-    partner_tail, partner_feats = feats + tail_rows, feats + 2 * tail_rows
-    pair = lax.rem(where[0], 2)
-    last = pl.ds(pl.multiple_of(lax.bitwise_xor(where[1], 3) * LANES, LANES), LANES)
-    for s in range(samples):
-        padded[s, pl.ds(0, side), :] = jnp.zeros((side, width), BF16)
-        padded[s, pl.ds(side + pixels, side), :] = jnp.zeros((side, width), BF16)
-        padded[s, pl.ds(side, pixels), last] = jnp.zeros((pixels, LANES), BF16)
+    partner_tail = feats + tail_rows
     style_rows[...] = jnp.zeros_like(style_rows)
     blocks = (
         (both, 0, feats, both, partner_tail, 0),
-        (first, 0, feats, first, partner_tail, 1 + pair),
-        (first_pair, partner_feats - cut, partner_tail - cut, first_pair, feats - cut, 2 - pair),
+        (first, 0, feats, first, partner_tail, 1 + lax.rem(where[0], 2)),
     )
     bring_blocks(
-        blocks, samples, side, where, picked, bias_full, style_rows, feat_t, aff_full, padded
+        blocks, samples, side, where, picked, bias_full, style_rows, feat_t, aff_full, kernel, padded, rows
     )
     chunk = min(256, pixels)
     for s in range(samples):
         for r in range(pixels // chunk):
-            total = dot(padded[s, pl.ds(r * chunk, chunk), :], kernel[0])
-            total = total + dot(padded[s, pl.ds(side + r * chunk, chunk), :], kernel[1])
-            total = total + dot(padded[s, pl.ds(2 * side + r * chunk, chunk), :], kernel[2])
+            total = dot(padded[s, pl.ds(r * chunk, chunk), :], rows[0])
+            total = total + dot(padded[s, pl.ds(side + r * chunk, chunk), :], rows[1])
+            total = total + dot(padded[s, pl.ds(2 * side + r * chunk, chunk), :], rows[2])
             taps[s, pl.ds(r * chunk, chunk), :] = total
 
 
 def main_kernel(n_ch, samples, side, *refs):
-    where, second, second_pair, earlier, kernel, square_in = refs[:6]
-    aff_w, picked, bias, head, rgb_w, counted = refs[6:12]
-    feat_t, style_rows, aff_full, wide, small, loss_rows = refs[15:21]
-    bias_full, late, late_tail, padded, taps = refs[21:]
+    where, first_pair, second, second_pair, earlier, kernel, square_in = refs[:7]
+    aff_w, picked, bias, head, rgb_w, counted = refs[7:13]
+    feat_t, style_rows, aff_full, wide, small, loss_rows = refs[16:22]
+    bias_full, late, late_tail, padded, kernel_rows, taps = refs[22:]
     width = aff_full.shape[0]
     half, pixels = width // 2, side * side
     feats, tail_rows = samples * pixels, half + 16
@@ -354,22 +355,13 @@
         late[pl.ds(feats, tail_rows), :] = second_pair[pl.ds(partner_tail - cut, tail_rows), :]
         late_tail[...] = second_pair[pl.ds(feats - cut, tail_rows), :]
 
-    for s in range(samples):
-        padded[s, pl.ds(0, side), :] = jnp.zeros((side, LANES), BF16)
-        padded[s, pl.ds(side + pixels, side), :] = jnp.zeros((side, LANES), BF16)
-    mine = pl.ds(pl.multiple_of(pair * half, half), half)
-    other = pl.ds(pl.multiple_of((1 - pair) * half, half), half)
-    lane = pl.ds(pl.multiple_of(lax.bitwise_xor(ch, 3) * LANES, LANES), LANES)
-    aff_full[mine, lane] = late[pl.ds(feats, half), :]
-    aff_full[other, lane] = late_tail[pl.ds(0, half), :]
-    bias_full[...] = late[pl.ds(feats + half, 16), :].astype(F32)
-    bias_row = bias_full[0:1, :] + bias_full[1:2, :] + bias_full[2:3, :]
-    style = (dot(picked[0].astype(BF16), aff_full[:, lane]) + bias_row).astype(BF16)
-    style_rows[:, lane] = style.astype(F32)
-    for s in range(samples):
-        value = late[pl.ds(s * pixels, pixels), :]
-        feat_t[s, lane, :] = value.T
-        padded[s, pl.ds(side, pixels), :] = value * style[s : s + 1, :]
+    blocks = (
+        (first_pair, partner_feats - cut, partner_tail - cut, first_pair, feats - cut, 2 - pair),
+        (late, 0, feats, late_tail, 0, 3),
+    )
+    bring_blocks(
+        blocks, samples, side, where, picked, bias_full, style_rows, feat_t, aff_full, kernel, padded, kernel_rows
+    )
     square = square_in[...]
     colour_aff = aff_w[1].astype(BF16)
     style1 = dot(picked[1].astype(BF16), colour_aff) + bias[1:2, :]
@@ -402,7 +394,7 @@
             total = earlier[s, pl.ds(r * chunk, chunk), :]
             for dy in range(3):
                 total = total + dot(
-                    padded[s, pl.ds(dy * side + r * chunk, chunk), :], kernel[dy, lane, :]
+                    padded[s, pl.ds(dy * side + r * chunk, chunk), :], kernel_rows[dy]
                 )
             taps[pl.ds(8 + r * chunk, chunk), :] = total
         mixed = jnp.zeros((3, LANES), F32)
@@ -852,16 +844,17 @@
             shape((8, width), F32),
             shape((width, width), BF16),
         ),
-        in_specs=[SMEM] + [VMEM] * 5,
+        in_specs=[SMEM] + [VMEM] * 4,
         out_specs=(VMEM,) * 4,
         scratch_shapes=[
             pltpu.VMEM((16, LANES), F32),
-            pltpu.VMEM((samples, pixels + 2 * side, width), BF16),
+            pltpu.VMEM((samples, pixels + 2 * side, 2 * LANES), BF16),
+            pltpu.VMEM((3, 2 * LANES, 3 * LANES), BF16),
         ],
         compiler_params=params(16),
         cost_estimate=cost(0),
         name="begin",
-    )(where, both, first, first_pair, kernel, picked)
+    )(where, both, first, kernel, picked)
     second_pair = swap(after(second, taps)[samples * pixels :], "dp", 1)
     feat_t, style_rows, aff_full, wide, small, loss_rows = pl.pallas_call(
         functools.partial(main_kernel, n_ch, samples, side),
@@ -873,21 +866,23 @@
             shape((8 * samples, LANES), F32),
             shape((8 * samples, LANES), F32),
         ),
-        in_specs=[SMEM] + [VMEM] * 10 + [SMEM] + [VMEM] * 3,
+        in_specs=[SMEM] + [VMEM] * 11 + [SMEM] + [VMEM] * 3,
         out_specs=(VMEM,) * 6,
         scratch_shapes=[
             pltpu.VMEM((16, LANES), F32),
             pltpu.VMEM((pack_rows, LANES), BF16),
             pltpu.VMEM((half + 16, LANES), BF16),
-            pltpu.VMEM((samples, pixels + 2 * side, LANES), BF16),
+            pltpu.VMEM((samples, pixels + 2 * side, 2 * LANES), BF16),
+            pltpu.VMEM((3, 2 * LANES, 3 * LANES), BF16),
             pltpu.VMEM((pixels + 16, 3 * LANES), F32),
         ],
-        input_output_aliases={12: 0, 13: 1, 14: 2},
+        input_output_aliases={13: 0, 14: 1, 15: 2},
         compiler_params=params(20),
         cost_estimate=cost(0),
         name="main",
     )(
         where,
+        first_pair,
         second,
         second_pair,
         taps,

time: 76.9 us -> 76.6 us (level)
    pallas_call x1, Pallas kernels: 2.67 us -> 1.72 us  [local(): pl.pallas_call(functools.partial(begin_kernel, n_ch, samples, side), out_...]
  transfers between devices with their start and end apart: 24 -> 24, of which waited for: 13 -> 13; matrix products, arithmetic and copies ran while one was open for 1% -> 1% of each run, Pallas kernels for 28% -> 27%
where the time goes in v6:
time: 76.6 us; the launch traced here: 76.4 us
  Pallas kernels  26.3 us (34%)
  starting transfers between devices  24.1 us (31%)
  waiting for transfers between devices  22.6 us (30%)
  between operations  2.58 us (3%)
    ppermute x7, waiting for transfers between devices, crossed(): return lax.ppermute(value, axis, pairs)  13.4 us
    ppermute x15, starting transfers between devices, swap(): lax.ppermute(value, axis, [(i, i ^ distance) for i in range(lax.axis_size...  11.8 us
    ppermute x7, starting transfers between devices, crossed(): return lax.ppermute(value, axis, pairs)  7.17 us
    ppermute x15, waiting for transfers between devices, swap(): lax.ppermute(value, axis, [(i, i ^ distance) for i in range(lax.axis_size...  5.47 us
    pallas_call x2, Pallas kernels, conv_part(): pl.pallas_call(functools.partial(conv_kernel, turns), out_shape=[shape((T...  5.44 us
    ppermute x2, starting transfers between devices, joint(): return lax.ppermute(value, ('dp', 'chan'), pairs)  5.11 us
    pallas_call x1, Pallas kernels, local(): pl.pallas_call(functools.partial(update_kernel, n_dp, samples, layers, [p...  4.35 us
    ppermute x2, waiting for transfers between devices, joint(): return lax.ppermute(value, ('dp', 'chan'), pairs)  3.69 us
  transfers between devices with their start and end apart: 24, of which 13 were waited for; matrix products, arithmetic and copies ran while one was open for 1% of the time, Pallas kernels for 27%

profile of v6, /device:TPU:1, one launch (start us, length us, event | category | flops | bytes accessed | tf_op | source)
XLA Modules:
  0.0 76.4 jit_solution(7454793748408119448)
XLA Ops:
  0.9 1.6 %pack.1 = bf16[1568,128]{1,0:T(8,128)(2,1)S(1)} custom-call(s32[2]{0:T(128)S(1)} %pad_add_fusion.where.refs_0_, f32[2,512,128]{2,1,0:T(8,128)} %aff_w.3, f32[3,128]{1,0:T(4,128)} %refs_13_.1, bf16[1024,128]{1,0:T(8,128)(2,1)} %bitcast.42), custom_call_target="tpu_custom_call" | custom-call | tf_op jit(solution)/shard_map/pack/pallas_call | solution.py:773
  2.6 3.8 %collective-permute-start.1 = (bf16[2592,128]{1,0:T(8,128)(2,1)S(1)}, bf16[2592,128]{1,0:T(8,128)(2,1)S(1)}, u32[]{:S(2)}, u32[]{:S(2)}) collective-permute-start(bf16[2592,128]{1,0:T(8,128)(2,1)S(1)} %pad_maximum_fusion.refs_1_), channel_id=1, source_target_pairs={{0,1},{1,0},{2,3},{3,2},{4,6},{5,7},{6,4},{7,5},{8,9},{9,8},{10,11... | collective-permute-start | bytes 1990664 | tf_op jit(solution)/shard_map/ppermute | solution.py:82
  6.4 1.4 %low.1.refs_2_ = bf16[8,64,512]{2,1,0:T(8,128)(2,1)S(1)} custom-call(f32[8,64,512]{2,1,0:T(8,128)} %refs_4_.1), custom_call_target="tpu_custom_call" | custom-call | tf_op jit(solution)/shard_map/low/pallas_call | solution.py:787
  7.8 1.3 %collective-permute-start.3 = (bf16[8,64,512]{2,1,0:T(8,128)(2,1)S(1)}, bf16[8,64,512]{2,1,0:T(8,128)(2,1)S(1)}, u32[]{:S(2)}, u32[]{:S(2)}) collective-permute-start(bf16[8,64,512]{2,1,0:T(8,128)(2,1)S(1)} %low.1.refs_2_), channel_id=1, source_target_pairs={{0,8},{4,20},{8,0},{12,28},{16,24},{20,4},{24,16},{28,12},{1,9},{5... | collective-permute-start | bytes 1572872 | tf_op jit(solution)/shard_map/ppermute | solution.py:98
  9.7 2.5 %weights.1 = (bf16[3,512,384]{2,1,0:T(8,128)(2,1)S(1)}, f32[512,128]{1,0:T(8,128)S(1)}, f32[16,512]{1,0:T(8,128)S(1)}) custom-call(s32[2]{0:T(128)S(1)} %bitcast.33, f32[9,512,128]{2,1,0:T(8,128)} %bitcast.25, f32[1024,512]{1,0:T(8,128)} %z_table.1), custom_call_target="tpu_custom_call" | custom-call | tf_op jit(solution)/shard_map/weights/pallas_call | solution.py:799
  12.2 1.3 %collective-permute-start.6 = (bf16[8,64,512]{2,1,0:T(8,128)(2,1)S(1)}, bf16[8,64,512]{2,1,0:T(8,128)(2,1)S(1)}, u32[]{:S(2)}, u32[]{:S(2)}) collective-permute-start(bf16[8,64,512]{2,1,0:T(8,128)(2,1)S(1)} %collective-permute-done.4.refs_3_), channel_id=1, source_target_pairs={{0,8},{4,20},{8,0},{12,28},{16,24},{20,4},{24,16},{28,12},{1,9},{5... | collective-permute-start | bytes 1572872 | tf_op jit(solution)/shard_map/ppermute | solution.py:98
  13.5 2.7 %collective-permute-done.3.refs_4_ = bf16[8,64,512]{2,1,0:T(8,128)(2,1)S(1)} collective-permute-done((bf16[8,64,512]{2,1,0:T(8,128)(2,1)S(1)}, bf16[8,64,512]{2,1,0:T(8,128)(2,1)S(1)}, u32[]{:S(2)}, u32[]{:S(2)}) %collective-permute-start.3) | collective-permute-done | bytes 524320 | tf_op jit(solution)/shard_map/ppermute | solution.py:98
  16.2 1.2 %collective-permute-start.7 = (bf16[8,64,512]{2,1,0:T(8,128)(2,1)S(1)}, bf16[8,64,512]{2,1,0:T(8,128)(2,1)S(1)}, u32[]{:S(2)}, u32[]{:S(2)}) collective-permute-start(bf16[8,64,512]{2,1,0:T(8,128)(2,1)S(1)} %collective-permute-done.3.refs_4_), channel_id=1, source_target_pairs={{0,16},{4,12},{8,24},{12,4},{16,0},{20,28},{24,8},{28,20},{1,17},{... | collective-permute-start | bytes 1572872 | tf_op jit(solution)/shard_map/ppermute | solution.py:98
  17.4 3.7 %collective-permute-done.1.refs_2_ = bf16[2592,128]{1,0:T(8,128)(2,1)S(1)} collective-permute-done((bf16[2592,128]{1,0:T(8,128)(2,1)S(1)}, bf16[2592,128]{1,0:T(8,128)(2,1)S(1)}, u32[]{:S(2)}, u32[]{:S(2)}) %collective-permute-start.1) | collective-permute-done | bytes 663584 | tf_op jit(solution)/shard_map/ppermute | solution.py:82
  21.2 1.3 %collective-permute-start.5 = (bf16[2592,128]{1,0:T(8,128)(2,1)S(1)}, bf16[2592,128]{1,0:T(8,128)(2,1)S(1)}, u32[]{:S(2)}, u32[]{:S(2)}) collective-permute-start(bf16[2592,128]{1,0:T(8,128)(2,1)S(1)} %broadcast_select_fusion), channel_id=1, source_target_pairs={{1,2},{2,1},{5,4},{6,7},{9,10},{10,9},{13,12},{14,15},{17,18},{18,... | collective-permute-start | bytes 1990664 | tf_op jit(solution)/shard_map/ppermute | solution.py:82
  22.9 3.9 %collective-permute-start.9 = (bf16[8,64,512]{2,1,0:T(8,128)(2,1)S(1)}, bf16[8,64,512]{2,1,0:T(8,128)(2,1)S(1)}, u32[]{:S(2)}, u32[]{:S(2)}) collective-permute-start(bf16[8,64,512]{2,1,0:T(8,128)(2,1)S(1)} %collective-permute-done.6.refs_5_), channel_id=1, source_target_pairs={{0,4},{4,0},{8,12},{12,8},{16,20},{20,16},{24,28},{28,24},{1,5},{5... | collective-permute-start | bytes 1572872 | tf_op jit(solution)/shard_map/ppermute | solution.py:44
  26.9 1.2 %collective-permute-done.7.refs_6_ = bf16[8,64,512]{2,1,0:T(8,128)(2,1)S(1)} collective-permute-done((bf16[8,64,512]{2,1,0:T(8,128)(2,1)S(1)}, bf16[8,64,512]{2,1,0:T(8,128)(2,1)S(1)}, u32[]{:S(2)}, u32[]{:S(2)}) %collective-permute-start.7) | collective-permute-done | bytes 524320 | tf_op jit(solution)/shard_map/ppermute | solution.py:98
  30.0 2.0 %mapping.1 = (f32[8,8,512]{2,1,0:T(8,128)S(1)}, f32[8,8,512]{2,1,0:T(8,128)S(1)}, f32[8,512]{1,0:T(8,128)S(1)}, f32[2,8,512]{2,1,0:T(8,128)S(1)}, bf16[8,512,512]{2,1,0:T(8,128)(2,1)S(1)}) custom-call(s32[2]{0:T(128)S(1)} %pad_add_fusion.where.refs_0_, s32[1]{0:T(128)S(6)} %copy.66.refs_1_.crossover, bf16[8,64,512]{2,1,0:T(8,128)(2,1)S(1)} %low.1.refs_2_, ...), custom_call_target="tpu_custom_call" | custom-call | tf_op jit(solution)/shard_map/mapping/pallas_call | solution.py:821
  32.0 1.7 %begin.1 = (bf16[1,512,1024]{2,1,0:T(8,128)(2,1)S(1)}, f32[1,1024,384]{2,1,0:T(8,128)S(1)}, f32[8,512]{1,0:T(8,128)S(1)}, bf16[512,512]{1,0:T(8,128)(2,1)S(1)}) custom-call(s32[2]{0:T(128)S(1)} %pad_add_fusion.where.refs_0_, bf16[2592,128]{1,0:T(8,128)(2,1)S(1)} %pad_maximum_fusion.refs_1_, bf16[2592,128]{1,0:T(8,128)(2,1)S(1)} %collective-permute-done.1.refs_2_, ...), custom_call_target="tpu_custom_call" | custom-call | tf_op jit(solution)/shard_map/begin/pallas_call | solution.py:839
  34.7 0.9 %collective-permute-done.11.refs_3_ = bf16[1568,128]{1,0:T(8,128)(2,1)S(1)} collective-permute-done((bf16[1568,128]{1,0:T(8,128)(2,1)S(1)}, bf16[1568,128]{1,0:T(8,128)(2,1)S(1)}, u32[]{:S(2)}, u32[]{:S(2)}) %collective-permute-start.11) | collective-permute-done | bytes 401440 | tf_op jit(solution)/shard_map/ppermute | solution.py:44
  35.6 2.4 %main.1 = (bf16[1,512,1024]{2,1,0:T(8,128)(2,1)S(1)}, f32[8,512]{1,0:T(8,128)S(1)}, bf16[512,512]{1,0:T(8,128)(2,1)S(1)}, f32[1,1040,128]{2,1,0:T(8,128)S(1)}, f...) custom-call(s32[2]{0:T(128)S(1)} %pad_add_fusion.where.refs_0_, ...), custom_call_target="tpu_custom_call", output_to_operand_aliasing={{0}: (13, {}), {1}: (14, {}), {2}: (15, {})} | custom-call | tf_op jit(solution)/shard_map/main/pallas_call | solution.py:859
  38.3 2.6 %factor.1 = (bf16[1,2,2304,128]{3,2,1,0:T(8,128)(2,1)S(1)}, f32[8,128]{1,0:T(8,128)S(1)}) custom-call(s32[2]{0:T(128)S(1)} %pad_add_fusion.where.refs_0_, bf16[1,512,1024]{2,1,0:T(8,128)(2,1)S(1)} %get-tuple-element.100.feat_t, f32[1,1040,128]{2,1,0:T(8,128)S(1)} %get-tuple-element.101.wide, f32[8,128]{1,0:T(8,128)S(1)} %get-tuple-element.102.small.refs_9_, ...), custom_call_target="tpu_custom_call" | custom-call | tf_op jit(solution)/shard_map/factor/pallas_call | solution.py:902
  41.4 2.6 %collective-permute-start.15 = (f32[16,128]{1,0:T(8,128)S(1)}, f32[16,128]{1,0:T(8,128)S(1)}, u32[]{:S(2)}, u32[]{:S(2)}) collective-permute-start(f32[16,128]{1,0:T(8,128)S(1)} %pad_maximum_fusion.2.refs_0_), channel_id=1, source_target_pairs={{0,3},{1,2},{2,1},{3,0},{4,7},{5,6},{6,5},{7,4},{8,11},{9,10},{10,... | collective-permute-start | bytes 24584 | tf_op jit(solution)/shard_map/ppermute | solution.py:44
  44.2 0.8 %collective-permute-start.13 = (f32[16,128]{1,0:T(8,128)S(1)}, f32[16,128]{1,0:T(8,128)S(1)}, u32[]{:S(2)}, u32[]{:S(2)}) collective-permute-start(f32[16,128]{1,0:T(8,128)S(1)} %pad_maximum_fusion.2.refs_0_), channel_id=1, source_target_pairs={{0,1},{1,0},{2,3},{3,2},{4,5},{5,4},{6,7},{7,6},{8,9},{9,8},{10,11... | collective-permute-start | bytes 24584 | tf_op jit(solution)/shard_map/ppermute | solution.py:44
  45.0 0.7 collective-permute-done.15.refs_3_
  45.7 1.7 %collective-permute-done.14.refs_2_ = f32[16,128]{1,0:T(8,128)S(1)} collective-permute-done((f32[16,128]{1,0:T(8,128)S(1)}, f32[16,128]{1,0:T(8,128)S(1)}, u32[]{:S(2)}, u32[]{:S(2)}) %collective-permute-start.14) | collective-permute-done | bytes 8224 | tf_op jit(solution)/shard_map/ppermute | solution.py:44
  47.6 1.3 %collective-permute-start.21 = (bf16[2336,128]{1,0:T(8,128)(2,1)S(1)}, bf16[2336,128]{1,0:T(8,128)(2,1)S(1)}, u32[]{:S(2)}, u32[]{:S(2)}) collective-permute-start(bf16[2336,128]{1,0:T(8,128)(2,1)S(1)} %combine.1), channel_id=1, source_target_pairs={{0,8},{4,20},{8,0},{12,28},{16,24},{20,4},{24,16},{28,12},{1,9},{5... | collective-permute-start | bytes 1794056 | tf_op jit(solution)/shard_map/ppermute | solution.py:98
  48.9 2.1 %mapping_back.1 = bf16[48,512]{1,0:T(8,128)(2,1)S(1)} custom-call(s32[2]{0:T(128)S(1)} %pad_add_fusion.where.refs_0_, s32[1]{0:T(128)S(6)} %copy.66.refs_1_.crossover, f32[16,128]{1,0:T(8,128)S(1)} %pad_maximum_fusion.2.refs_0_, f32[16,128]{1,0:T(8,128)S(1)} %collective-permute-done.13.refs_1_, f32[16,128]{1,0:T(8,128)S(1)} %collective-permute-done.14.refs_2_, ...), custom_call_target="tpu_custom_call" | custom-call | tf_op jit(solution)/shard_map/mapping_back/pallas_call | solution.py:932
  51.2 1.9 %collective-permute-start.17 = (bf16[48,512]{1,0:T(8,128)(2,1)S(1)}, bf16[48,512]{1,0:T(8,128)(2,1)S(1)}, u32[]{:S(2)}, u32[]{:S(2)}) collective-permute-start(bf16[48,512]{1,0:T(8,128)(2,1)S(1)} %mapping_back.1), channel_id=1, source_target_pairs={{0,4},{4,0},{8,12},{12,8},{16,20},{20,16},{24,28},{28,24},{1,5},{5... | collective-permute-start | bytes 147464 | tf_op jit(solution)/shard_map/ppermute | solution.py:44
  53.1 0.9 %collective-permute-done.17 = bf16[48,512]{1,0:T(8,128)(2,1)S(1)} collective-permute-done((bf16[48,512]{1,0:T(8,128)(2,1)S(1)}, bf16[48,512]{1,0:T(8,128)(2,1)S(1)}, u32[]{:S(2)}, u32[]{:S(2)}) %collective-permute-start.17) | collective-permute-done | bytes 49184 | tf_op jit(solution)/shard_map/ppermute | solution.py:44
  54.2 4.6 %collective-permute-done.18.refs_1_ = bf16[96,512]{1,0:T(8,128)(2,1)S(1)} collective-permute-done((bf16[96,512]{1,0:T(8,128)(2,1)S(1)}, bf16[96,512]{1,0:T(8,128)(2,1)S(1)}, u32[]{:S(2)}, u32[]{:S(2)}) %collective-permute-start.18) | collective-permute-done | bytes 98336 | tf_op jit(solution)/shard_map/ppermute | solution.py:98
  59.0 1.2 %collective-permute-start.19 = (bf16[96,512]{1,0:T(8,128)(2,1)S(1)}, bf16[96,512]{1,0:T(8,128)(2,1)S(1)}, u32[]{:S(2)}, u32[]{:S(2)}) collective-permute-start(bf16[96,512]{1,0:T(8,128)(2,1)S(1)} %collective-permute-done.18.refs_1_), channel_id=1, source_target_pairs={{0,8},{4,20},{8,0},{12,28},{16,24},{20,4},{24,16},{28,12},{1,9},{5... | collective-permute-start | bytes 294920 | tf_op jit(solution)/shard_map/ppermute | solution.py:98
  60.9 1.8 %collective-permute-done.19.refs_2_ = bf16[96,512]{1,0:T(8,128)(2,1)S(1)} collective-permute-done((bf16[96,512]{1,0:T(8,128)(2,1)S(1)}, bf16[96,512]{1,0:T(8,128)(2,1)S(1)}, u32[]{:S(2)}, u32[]{:S(2)}) %collective-permute-start.19) | collective-permute-done | bytes 98336 | tf_op jit(solution)/shard_map/ppermute | solution.py:98
  62.9 4.3 %update.1 = (f32[8,64,512]{2,1,0:T(8,128)}, f32[8,64,512]{2,1,0:T(8,128)}, f32[8,64,512]{2,1,0:T(8,128)}, bf16[8,64,512]{2,1,0:T(8,128)(2,1)}, f32[1024,128]{1,0...) custom-call(s32[2]{0:T(128)S(1)} %pad_add_fusion.where.refs_0_, ...), custom_call_target="tpu_custom_call" | custom-call | flops 12000000000 | tf_op jit(solution)/shard_map/update/pallas_call | solution.py:968
  67.3 2.8 %collective-permute-done.22 = bf16[2336,128]{1,0:T(8,128)(2,1)S(1)} collective-permute-done((bf16[2336,128]{1,0:T(8,128)(2,1)S(1)}, bf16[2336,128]{1,0:T(8,128)(2,1)S(1)}, u32[]{:S(2)}, u32[]{:S(2)}) %collective-permute-start.22) | collective-permute-done | bytes 598048 | tf_op jit(solution)/shard_map/ppermute | solution.py:98
  70.7 2.2 %conv_first.1 = (f32[4608,128]{1,0:T(8,128)}, f32[4608,128]{1,0:T(8,128)}, f32[4608,128]{1,0:T(8,128)}, bf16[4608,128]{1,0:T(8,128)(2,1)}) custom-call(s32[2]{0:T(128)S(1)} %pad_add_fusion.where.refs_0_, bf16[2336,128]{1,0:T(8,128)(2,1)S(1)} %add_convert_fusion.refs_0_, f32[4608,128]{1,0:T(8,128)S(1)} %bitcast.26, f32[4608,128]{1,0:T(8,128)S(1)} %bitcast.28, ...), custom_call_target="tpu_custom_call" | custom-call | tf_op jit(solution)/shard_map/conv_first/pallas_call | solution.py:1002
  73.0 3.2 %conv_rest.1 = (f32[4608,128]{1,0:T(8,128)}, f32[4608,128]{1,0:T(8,128)}, f32[4608,128]{1,0:T(8,128)}, bf16[4608,128]{1,0:T(8,128)(2,1)}) custom-call(s32[2]{0:T(128)S(1)} %pad_add_fusion.where.refs_0_, bf16[2336,128]{1,0:T(8,128)(2,1)S(1)} %add_convert_fusion.refs_0_, ...), custom_call_target="tpu_custom_call", output_to_operand_aliasing={{0}: (6, {}), {1}: (7, {}), {2}: (8, {}), {3}: (9, {})} | custom-call | tf_op jit(solution)/shard_map/conv_rest/pallas_call | solution.py:1002
  (83 shorter events, 6.0 us)
Async XLA Ops:
  0.7 1.8 %collective-permute-start = (bf16[1024,128]{1,0:T(8,128)(2,1)}, bf16[1024,128]{1,0:T(8,128)(2,1)S(1)}, u32[]{:S(2)}, u32[]{:S(2)}) collective-permute-start(bf16[1024,128]{1,0:T(8,128)(2,1)} %bitcast.41), channel_id=1, source_target_pairs={{0,4},{4,0},{8,12},{12,8},{16,20},{20,16},{24,28},{28,24},{1,5},{5... | collective-permute-start | bytes 786440 | tf_op jit(solution)/shard_map/ppermute | solution.py:44
  2.6 18.6 %collective-permute-start.1 = (bf16[2592,128]{1,0:T(8,128)(2,1)S(1)}, bf16[2592,128]{1,0:T(8,128)(2,1)S(1)}, u32[]{:S(2)}, u32[]{:S(2)}) collective-permute-start(bf16[2592,128]{1,0:T(8,128)(2,1)S(1)} %pad_maximum_fusion.refs_1_), channel_id=1, source_target_pairs={{0,1},{1,0},{2,3},{3,2},{4,6},{5,7},{6,4},{7,5},{8,9},{9,8},{10,11... | collective-permute-start | bytes 1990664 | tf_op jit(solution)/shard_map/ppermute | solution.py:82
  7.7 2.0 %collective-permute-start.4 = (bf16[8,64,512]{2,1,0:T(8,128)(2,1)S(1)}, bf16[8,64,512]{2,1,0:T(8,128)(2,1)S(1)}, u32[]{:S(2)}, u32[]{:S(2)}) collective-permute-start(bf16[8,64,512]{2,1,0:T(8,128)(2,1)S(1)} %low.1.refs_2_), channel_id=1, source_target_pairs={{0,4},{4,0},{8,12},{12,8},{16,20},{20,16},{24,28},{28,24},{1,5},{5... | collective-permute-start | bytes 1572872 | tf_op jit(solution)/shard_map/ppermute | solution.py:44
  7.8 8.4 %collective-permute-start.3 = (bf16[8,64,512]{2,1,0:T(8,128)(2,1)S(1)}, bf16[8,64,512]{2,1,0:T(8,128)(2,1)S(1)}, u32[]{:S(2)}, u32[]{:S(2)}) collective-permute-start(bf16[8,64,512]{2,1,0:T(8,128)(2,1)S(1)} %low.1.refs_2_), channel_id=1, source_target_pairs={{0,8},{4,20},{8,0},{12,28},{16,24},{20,4},{24,16},{28,12},{1,9},{5... | collective-permute-start | bytes 1572872 | tf_op jit(solution)/shard_map/ppermute | solution.py:98
  12.2 17.8 %copy-start.5 = (f32[8,512]{1,0:T(8,128)S(1)}, f32[8,512]{1,0:T(8,128)}, u32[]{:S(2)}) copy-start(f32[8,512]{1,0:T(8,128)} %refs_10_.3) | copy-start | bytes 49156
  12.2 10.7 %collective-permute-start.6 = (bf16[8,64,512]{2,1,0:T(8,128)(2,1)S(1)}, bf16[8,64,512]{2,1,0:T(8,128)(2,1)S(1)}, u32[]{:S(2)}, u32[]{:S(2)}) collective-permute-start(bf16[8,64,512]{2,1,0:T(8,128)(2,1)S(1)} %collective-permute-done.4.refs_3_), channel_id=1, source_target_pairs={{0,8},{4,20},{8,0},{12,28},{16,24},{20,4},{24,16},{28,12},{1,9},{5... | collective-permute-start | bytes 1572872 | tf_op jit(solution)/shard_map/ppermute | solution.py:98
  16.2 11.8 %collective-permute-start.7 = (bf16[8,64,512]{2,1,0:T(8,128)(2,1)S(1)}, bf16[8,64,512]{2,1,0:T(8,128)(2,1)S(1)}, u32[]{:S(2)}, u32[]{:S(2)}) collective-permute-start(bf16[8,64,512]{2,1,0:T(8,128)(2,1)S(1)} %collective-permute-done.3.refs_4_), channel_id=1, source_target_pairs={{0,16},{4,12},{8,24},{12,4},{16,0},{20,28},{24,8},{28,20},{1,17},{... | collective-permute-start | bytes 1572872 | tf_op jit(solution)/shard_map/ppermute | solution.py:98
  21.2 12.6 %collective-permute-start.5 = (bf16[2592,128]{1,0:T(8,128)(2,1)S(1)}, bf16[2592,128]{1,0:T(8,128)(2,1)S(1)}, u32[]{:S(2)}, u32[]{:S(2)}) collective-permute-start(bf16[2592,128]{1,0:T(8,128)(2,1)S(1)} %broadcast_select_fusion), channel_id=1, source_target_pairs={{1,2},{2,1},{5,4},{6,7},{9,10},{10,9},{13,12},{14,15},{17,18},{18,... | collective-permute-start | bytes 1990664 | tf_op jit(solution)/shard_map/ppermute | solution.py:82
  22.5 6.8 %collective-permute-start.8 = (bf16[8,64,512]{2,1,0:T(8,128)(2,1)S(1)}, bf16[8,64,512]{2,1,0:T(8,128)(2,1)S(1)}, u32[]{:S(2)}, u32[]{:S(2)}) collective-permute-start(bf16[8,64,512]{2,1,0:T(8,128)(2,1)S(1)} %collective-permute-done.3.refs_4_), channel_id=1, source_target_pairs={{0,4},{4,0},{8,12},{12,8},{16,20},{20,16},{24,28},{28,24},{1,5},{5... | collective-permute-start | bytes 1572872 | tf_op jit(solution)/shard_map/ppermute | solution.py:44
  22.9 6.4 %collective-permute-start.9 = (bf16[8,64,512]{2,1,0:T(8,128)(2,1)S(1)}, bf16[8,64,512]{2,1,0:T(8,128)(2,1)S(1)}, u32[]{:S(2)}, u32[]{:S(2)}) collective-permute-start(bf16[8,64,512]{2,1,0:T(8,128)(2,1)S(1)} %collective-permute-done.6.refs_5_), channel_id=1, source_target_pairs={{0,4},{4,0},{8,12},{12,8},{16,20},{20,16},{24,28},{28,24},{1,5},{5... | collective-permute-start | bytes 1572872 | tf_op jit(solution)/shard_map/ppermute | solution.py:44
  28.0 1.9 %collective-permute-start.10 = (bf16[8,64,512]{2,1,0:T(8,128)(2,1)S(1)}, bf16[8,64,512]{2,1,0:T(8,128)(2,1)S(1)}, u32[]{:S(2)}, u32[]{:S(2)}) collective-permute-start(bf16[8,64,512]{2,1,0:T(8,128)(2,1)S(1)} %collective-permute-done.7.refs_6_), channel_id=1, source_target_pairs={{0,4},{4,0},{8,12},{12,8},{16,20},{20,16},{24,28},{28,24},{1,5},{5... | collective-permute-start | bytes 1572872 | tf_op jit(solution)/shard_map/ppermute | solution.py:44
  28.7 5.9 %collective-permute-start.2 = (bf16[1568,128]{1,0:T(8,128)(2,1)S(1)}, bf16[1568,128]{1,0:T(8,128)(2,1)S(1)}, u32[]{:S(2)}, u32[]{:S(2)}) collective-permute-start(bf16[1568,128]{1,0:T(8,128)(2,1)S(1)} %slice.28), channel_id=1, source_target_pairs={{0,4},{4,0},{8,12},{12,8},{16,20},{20,16},{24,28},{28,24},{1,5},{5... | collective-permute-start | bytes 1204232 | tf_op jit(solution)/shard_map/ppermute | solution.py:44
  33.8 1.8 %collective-permute-start.11 = (bf16[1568,128]{1,0:T(8,128)(2,1)S(1)}, bf16[1568,128]{1,0:T(8,128)(2,1)S(1)}, u32[]{:S(2)}, u32[]{:S(2)}) collective-permute-start(bf16[1568,128]{1,0:T(8,128)(2,1)S(1)} %slice.22), channel_id=1, source_target_pairs={{0,4},{4,0},{8,12},{12,8},{16,20},{20,16},{24,28},{28,24},{1,5},{5... | collective-permute-start | bytes 1204232 | tf_op jit(solution)/shard_map/ppermute | solution.py:44
  38.0 3.3 %collective-permute-start.12 = (f32[8,128]{1,0:T(8,128)S(1)}, f32[8,128]{1,0:T(8,128)S(1)}, u32[]{:S(2)}, u32[]{:S(2)}) collective-permute-start(f32[8,128]{1,0:T(8,128)S(1)} %get-tuple-element.105), channel_id=1, source_target_pairs={{0,4},{4,0},{8,12},{12,8},{16,20},{20,16},{24,28},{28,24},{1,5},{5... | collective-permute-start | bytes 12296 | tf_op jit(solution)/shard_map/ppermute | solution.py:44
  40.9 6.5 %collective-permute-start.16 = (bf16[1,2304,128]{2,1,0:T(8,128)(2,1)S(1)}, bf16[1,2304,128]{2,1,0:T(8,128)(2,1)S(1)}, u32[]{:S(2)}, u32[]{:S(2)}) collective-permute-start(bf16[1,2304,128]{2,1,0:T(8,128)(2,1)S(1)} %slice_bitcast_fusion), channel_id=1, source_target_pairs={{0,4},{4,0},{8,12},{12,8},{16,20},{20,16},{24,28},{28,24},{1,5},{5... | collective-permute-start | bytes 1769480 | tf_op jit(solution)/shard_map/ppermute | solution.py:44
  41.4 4.4 %collective-permute-start.15 = (f32[16,128]{1,0:T(8,128)S(1)}, f32[16,128]{1,0:T(8,128)S(1)}, u32[]{:S(2)}, u32[]{:S(2)}) collective-permute-start(f32[16,128]{1,0:T(8,128)S(1)} %pad_maximum_fusion.2.refs_0_), channel_id=1, source_target_pairs={{0,3},{1,2},{2,1},{3,0},{4,7},{5,6},{6,5},{7,4},{8,11},{9,10},{10,... | collective-permute-start | bytes 24584 | tf_op jit(solution)/shard_map/ppermute | solution.py:44
  44.0 3.4 %collective-permute-start.14 = (f32[16,128]{1,0:T(8,128)S(1)}, f32[16,128]{1,0:T(8,128)S(1)}, u32[]{:S(2)}, u32[]{:S(2)}) collective-permute-start(f32[16,128]{1,0:T(8,128)S(1)} %pad_maximum_fusion.2.refs_0_), channel_id=1, source_target_pairs={{0,2},{1,3},{2,0},{3,1},{4,6},{5,7},{6,4},{7,5},{8,10},{9,11},{10,... | collective-permute-start | bytes 24584 | tf_op jit(solution)/shard_map/ppermute | solution.py:44
  44.2 3.2 %collective-permute-start.13 = (f32[16,128]{1,0:T(8,128)S(1)}, f32[16,128]{1,0:T(8,128)S(1)}, u32[]{:S(2)}, u32[]{:S(2)}) collective-permute-start(f32[16,128]{1,0:T(8,128)S(1)} %pad_maximum_fusion.2.refs_0_), channel_id=1, source_target_pairs={{0,1},{1,0},{2,3},{3,2},{4,5},{5,4},{6,7},{7,6},{8,9},{9,8},{10,11... | collective-permute-start | bytes 24584 | tf_op jit(solution)/shard_map/ppermute | solution.py:44
  47.6 12.6 %collective-permute-start.21 = (bf16[2336,128]{1,0:T(8,128)(2,1)S(1)}, bf16[2336,128]{1,0:T(8,128)(2,1)S(1)}, u32[]{:S(2)}, u32[]{:S(2)}) collective-permute-start(bf16[2336,128]{1,0:T(8,128)(2,1)S(1)} %combine.1), channel_id=1, source_target_pairs={{0,8},{4,20},{8,0},{12,28},{16,24},{20,4},{24,16},{28,12},{1,9},{5... | collective-permute-start | bytes 1794056 | tf_op jit(solution)/shard_map/ppermute | solution.py:98
  48.9 13.8 %copy-start.10 = (f32[8,64,512]{2,1,0:T(8,128)S(1)}, f32[8,64,512]{2,1,0:T(8,128)}, u32[]{:S(2)}) copy-start(f32[8,64,512]{2,1,0:T(8,128)} %refs_5_.1) | copy-start | bytes 3145732
  48.9 13.8 %copy-start.11 = (f32[8,64,512]{2,1,0:T(8,128)S(1)}, f32[8,64,512]{2,1,0:T(8,128)}, u32[]{:S(2)}) copy-start(f32[8,64,512]{2,1,0:T(8,128)} %refs_6_.1) | copy-start | bytes 3145732
  48.9 13.8 %copy-start.13 = (f32[2,512,128]{2,1,0:T(8,128)S(1)}, f32[2,512,128]{2,1,0:T(8,128)}, u32[]{:S(2)}) copy-start(f32[2,512,128]{2,1,0:T(8,128)} %param.40) | copy-start | bytes 1572868
  51.1 11.7 %copy-start.4 = (f32[8,64,512]{2,1,0:T(8,128)S(1)}, f32[8,64,512]{2,1,0:T(8,128)}, u32[]{:S(2)}) copy-start(f32[8,64,512]{2,1,0:T(8,128)} %refs_4_.1) | copy-start | bytes 3145732
  51.1 11.7 %copy-start.12 = (f32[2,512,128]{2,1,0:T(8,128)S(1)}, f32[2,512,128]{2,1,0:T(8,128)}, u32[]{:S(2)}) copy-start(f32[2,512,128]{2,1,0:T(8,128)} %param.39) | copy-start | bytes 1572868
  51.1 11.7 %copy-start.14 = (f32[8,512]{1,0:T(8,128)S(1)}, f32[8,512]{1,0:T(8,128)}, u32[]{:S(2)}) copy-start(f32[8,512]{1,0:T(8,128)} %refs_11_.5) | copy-start | bytes 49156
  51.1 11.7 %copy-start.15 = (f32[8,512]{1,0:T(8,128)S(1)}, f32[8,512]{1,0:T(8,128)}, u32[]{:S(2)}) copy-start(f32[8,512]{1,0:T(8,128)} %refs_12_.2) | copy-start | bytes 49156
  51.2 2.8 %collective-permute-start.17 = (bf16[48,512]{1,0:T(8,128)(2,1)S(1)}, bf16[48,512]{1,0:T(8,128)(2,1)S(1)}, u32[]{:S(2)}, u32[]{:S(2)}) collective-permute-start(bf16[48,512]{1,0:T(8,128)(2,1)S(1)} %mapping_back.1), channel_id=1, source_target_pairs={{0,4},{4,0},{8,12},{12,8},{16,20},{20,16},{24,28},{28,24},{1,5},{5... | collective-permute-start | bytes 147464 | tf_op jit(solution)/shard_map/ppermute | solution.py:44
  54.0 4.9 %collective-permute-start.18 = (bf16[96,512]{1,0:T(8,128)(2,1)S(1)}, bf16[96,512]{1,0:T(8,128)(2,1)S(1)}, u32[]{:S(2)}, u32[]{:S(2)}) collective-permute-start(bf16[96,512]{1,0:T(8,128)(2,1)S(1)} %pad_maximum_fusion.1.refs_0_), channel_id=1, source_target_pairs={{0,16},{4,12},{8,24},{12,4},{16,0},{20,28},{24,8},{28,20},{1,17},{... | collective-permute-start | bytes 294920 | tf_op jit(solution)/shard_map/ppermute | solution.py:98
  58.9 2.1 %collective-permute-start.20 = (bf16[96,512]{1,0:T(8,128)(2,1)S(1)}, bf16[96,512]{1,0:T(8,128)(2,1)S(1)}, u32[]{:S(2)}, u32[]{:S(2)}) collective-permute-start(bf16[96,512]{1,0:T(8,128)(2,1)S(1)} %collective-permute-done.18.refs_1_), channel_id=1, source_target_pairs={{0,4},{4,0},{8,12},{12,8},{16,20},{20,16},{24,28},{28,24},{1,5},{5... | collective-permute-start | bytes 294920 | tf_op jit(solution)/shard_map/ppermute | solution.py:44
  59.0 3.8 %collective-permute-start.19 = (bf16[96,512]{1,0:T(8,128)(2,1)S(1)}, bf16[96,512]{1,0:T(8,128)(2,1)S(1)}, u32[]{:S(2)}, u32[]{:S(2)}) collective-permute-start(bf16[96,512]{1,0:T(8,128)(2,1)S(1)} %collective-permute-done.18.refs_1_), channel_id=1, source_target_pairs={{0,8},{4,20},{8,0},{12,28},{16,24},{20,4},{24,16},{28,12},{1,9},{5... | collective-permute-start | bytes 294920 | tf_op jit(solution)/shard_map/ppermute | solution.py:98
  60.4 9.6 %collective-permute-start.22 = (bf16[2336,128]{1,0:T(8,128)(2,1)S(1)}, bf16[2336,128]{1,0:T(8,128)(2,1)S(1)}, u32[]{:S(2)}, u32[]{:S(2)}) collective-permute-start(bf16[2336,128]{1,0:T(8,128)(2,1)S(1)} %add_convert_fusion.1), channel_id=1, source_target_pairs={{0,16},{4,12},{8,24},{12,4},{16,0},{20,28},{24,8},{28,20},{1,17},{... | collective-permute-start | bytes 1794056 | tf_op jit(solution)/shard_map/ppermute | solution.py:98
  70.2 2.8 %collective-permute-start.23 = (bf16[2336,128]{1,0:T(8,128)(2,1)S(1)}, bf16[2336,128]{1,0:T(8,128)(2,1)S(1)}, u32[]{:S(2)}, u32[]{:S(2)}) collective-permute-start(bf16[2336,128]{1,0:T(8,128)(2,1)S(1)} %add_convert_fusion.refs_0_), channel_id=1, source_target_pairs={{0,4},{4,0},{8,12},{12,8},{16,20},{20,16},{24,28},{28,24},{1,5},{5... | collective-permute-start | bytes 1794056 | tf_op jit(solution)/shard_map/ppermute | solution.py:44
  (13 other events, 103.7 us)

commit v7 on v6

--- a/solution.py
+++ b/solution.py
@@ -239,7 +239,7 @@
     for j in range(2):
         chosen = []
         for s in range(samples):
-            first = crossover[s] > j
+            first = crossover[2 + s] > j
             chosen.append(
                 jnp.where(first, low[2 * s : 2 * s + 1, :], low[2 * s + 1 : 2 * s + 2, :])
             )
@@ -421,7 +421,7 @@
             jnp.sum(mixed * colour_wide, axis=0, keepdims=True), axis=1, keepdims=True
         )
         loss_rows[pl.ds(s, 1), :] = jnp.broadcast_to(logit, (1, LANES))
-        loss_rows[pl.ds(4 * samples + s, 1), :] = jnp.full((1, LANES), counted[s], jnp.int32).astype(F32)
+        loss_rows[pl.ds(4 * samples + s, 1), :] = jnp.full((1, LANES), counted[2 + samples + s], jnp.int32).astype(F32)
         small[pl.ds(8 * s, 1), :] = g_style1
         small[pl.ds(8 * s + 1, 1), :] = g_bias
         small[pl.ds(8 * s + 2, 3), :] = mixed
@@ -579,7 +579,7 @@
     for s in range(samples):
         conv_row = from_conv[s : s + 1, :]
         colour_row = grads[s][0][:, :1] * wide_sum(8 * s + 4)
-        to_first = [jnp.full((1, width), crossover[s], jnp.int32) > j for j in range(2)]
+        to_first = [jnp.full((1, width), crossover[2 + s], jnp.int32) > j for j in range(2)]
         g_rows.append(
             jnp.where(to_first[0], conv_row, 0.0) + jnp.where(to_first[1], colour_row, 0.0)
         )
@@ -796,6 +796,7 @@
     )(*hbm(after(map_w, pack)))
     *chan_packs, last_step = spread_over_chan(flat_features, pack, map_low)
     blocks = spread_layers(map_low, "dp")
+    numbers = jnp.concatenate([where, *after([crossover, counted], blocks[1][0])])
     kernel, square, latent_rows = pl.pallas_call(
         functools.partial(weights_kernel, samples),
         out_shape=(
@@ -814,7 +815,7 @@
         compiler_params=params(8),
         cost_estimate=cost(0),
         name="weights",
-    )(seeds.reshape(-1), *hbm(after(conv_w.reshape(TAPS, width, LANES), blocks[1][0]), z_table))
+    )(seeds.reshape(-1), *hbm(after(conv_w.reshape(TAPS, width, LANES), blocks[1][0], numbers), z_table))
     second = last_step(blocks[2][0], kernel)
     places = [place for _, place in blocks]
 
@@ -833,7 +834,7 @@
         compiler_params=params(12),
         cost_estimate=cost(0),
         name="mapping",
-    )(where, crossover, *[block for block, _ in blocks], latent_rows, map_b)
+    )(where, numbers, *[block for block, _ in blocks], latent_rows, map_b)
 
     both, first, first_pair = chan_packs
     feat_t, taps, style_rows, aff_full = pl.pallas_call(
@@ -893,7 +894,7 @@
         chan_bias,
         head,
         rgb_w,
-        counted,
+        numbers,
         feat_t,
         style_rows,
         aff_full,
@@ -938,7 +939,7 @@
         compiler_params=params(12),
         cost_estimate=cost(0),
         name="mapping_back",
-    )(where, crossover, *after(sum_parts, total), masks, pre, hid, top, picked, small, map_full, aff_full)
+    )(where, numbers, *after(sum_parts, total), masks, pre, hid, top, picked, small, map_full, aff_full)
     spread_pack = spread(pack, "dp")
     packs = [part for part, _ in spread_pack]
 

time: 76.6 us -> 76.9 us (level)
  waiting for transfers between devices: 22.6 us -> 27.5 us
  starting transfers between devices: 24.1 us -> 19.4 us
    ppermute x7, waiting for transfers between devices: 13.4 us -> 17.6 us  [crossed(): return lax.ppermute(value, axis, pairs)]
    ppermute x15, starting transfers between devices: 11.8 us -> 8.13 us  [swap(): lax.ppermute(value, axis, [(i, i ^ distance) for i in range(lax.axis_size...]
    ppermute x7, starting transfers between devices: 7.17 us -> 6.16 us  [crossed(): return lax.ppermute(value, axis, pairs)]
    ppermute x15, waiting for transfers between devices: 5.47 us -> 6.26 us  [swap(): lax.ppermute(value, axis, [(i, i ^ distance) for i in range(lax.axis_size...]
  transfers between devices with their start and end apart: 24 -> 24, of which waited for: 13 -> 12; matrix products, arithmetic and copies ran while one was open for 1% -> 1% of each run, Pallas kernels for 27% -> 27%
where the time goes in v7:
time: 76.9 us; the launch traced here: 76.7 us
  waiting for transfers between devices  27.5 us (36%)
  Pallas kernels  26.3 us (34%)
  starting transfers between devices  19.4 us (25%)
  between operations  2.56 us (3%)
    ppermute x7, waiting for transfers between devices, crossed(): return lax.ppermute(value, axis, pairs)  17.6 us
    ppermute x15, starting transfers between devices, swap(): lax.ppermute(value, axis, [(i, i ^ distance) for i in range(lax.axis_size...  8.13 us
    ppermute x15, waiting for transfers between devices, swap(): lax.ppermute(value, axis, [(i, i ^ distance) for i in range(lax.axis_size...  6.26 us
    ppermute x7, starting transfers between devices, crossed(): return lax.ppermute(value, axis, pairs)  6.16 us
    pallas_call x2, Pallas kernels, conv_part(): pl.pallas_call(functools.partial(conv_kernel, turns), out_shape=[shape((T...  5.44 us
    ppermute x2, starting transfers between devices, joint(): return lax.ppermute(value, ('dp', 'chan'), pairs)  5.11 us
    pallas_call x1, Pallas kernels, local(): pl.pallas_call(functools.partial(update_kernel, n_dp, samples, layers, [p...  4.35 us
    ppermute x2, waiting for transfers between devices, joint(): return lax.ppermute(value, ('dp', 'chan'), pairs)  3.69 us
  transfers between devices with their start and end apart: 24, of which 12 were waited for; matrix products, arithmetic and copies ran while one was open for 1% of the time, Pallas kernels for 27%

profile of v7, /device:TPU:1, one launch (start us, length us, event | category | flops | bytes accessed | tf_op | source)
XLA Modules:
  0.0 76.7 jit_solution(5340731113968612772)
XLA Ops:
  0.9 1.6 %pack.1 = bf16[1568,128]{1,0:T(8,128)(2,1)S(1)} custom-call(s32[2]{0:T(128)S(1)} %pad_add_fusion.where.refs_0_, f32[2,512,128]{2,1,0:T(8,128)} %aff_w.3, f32[3,128]{1,0:T(4,128)} %refs_13_.1, bf16[1024,128]{1,0:T(8,128)(2,1)} %bitcast.42), custom_call_target="tpu_custom_call" | custom-call | tf_op jit(solution)/shard_map/pack/pallas_call | solution.py:773
  2.6 3.8 %collective-permute-start.2 = (bf16[2592,128]{1,0:T(8,128)(2,1)S(1)}, bf16[2592,128]{1,0:T(8,128)(2,1)S(1)}, u32[]{:S(2)}, u32[]{:S(2)}) collective-permute-start(bf16[2592,128]{1,0:T(8,128)(2,1)S(1)} %pad_maximum_fusion.refs_1_), channel_id=1, source_target_pairs={{0,1},{1,0},{2,3},{3,2},{4,6},{5,7},{6,4},{7,5},{8,9},{9,8},{10,11... | collective-permute-start | bytes 1990664 | tf_op jit(solution)/shard_map/ppermute | solution.py:82
  6.4 1.4 %low.1.refs_2_ = bf16[8,64,512]{2,1,0:T(8,128)(2,1)S(1)} custom-call(f32[8,64,512]{2,1,0:T(8,128)} %refs_4_.1), custom_call_target="tpu_custom_call" | custom-call | tf_op jit(solution)/shard_map/low/pallas_call | solution.py:787
  7.8 1.3 %collective-permute-start.4 = (bf16[8,64,512]{2,1,0:T(8,128)(2,1)S(1)}, bf16[8,64,512]{2,1,0:T(8,128)(2,1)S(1)}, u32[]{:S(2)}, u32[]{:S(2)}) collective-permute-start(bf16[8,64,512]{2,1,0:T(8,128)(2,1)S(1)} %low.1.refs_2_), channel_id=1, source_target_pairs={{0,8},{4,20},{8,0},{12,28},{16,24},{20,4},{24,16},{28,12},{1,9},{5... | collective-permute-start | bytes 1572872 | tf_op jit(solution)/shard_map/ppermute | solution.py:98
  10.5 2.5 %weights.1 = (bf16[3,512,384]{2,1,0:T(8,128)(2,1)S(1)}, f32[512,128]{1,0:T(8,128)S(1)}, f32[16,512]{1,0:T(8,128)S(1)}) custom-call(s32[2]{0:T(128)S(1)} %bitcast.33, f32[9,512,128]{2,1,0:T(8,128)} %bitcast.25, f32[1024,512]{1,0:T(8,128)} %z_table.1), custom_call_target="tpu_custom_call" | custom-call | tf_op jit(solution)/shard_map/weights/pallas_call | solution.py:800
  13.5 2.7 %collective-permute-done.4.refs_4_ = bf16[8,64,512]{2,1,0:T(8,128)(2,1)S(1)} collective-permute-done((bf16[8,64,512]{2,1,0:T(8,128)(2,1)S(1)}, bf16[8,64,512]{2,1,0:T(8,128)(2,1)S(1)}, u32[]{:S(2)}, u32[]{:S(2)}) %collective-permute-start.4) | collective-permute-done | bytes 524320 | tf_op jit(solution)/shard_map/ppermute | solution.py:98
  16.2 1.2 %collective-permute-start.7 = (bf16[8,64,512]{2,1,0:T(8,128)(2,1)S(1)}, bf16[8,64,512]{2,1,0:T(8,128)(2,1)S(1)}, u32[]{:S(2)}, u32[]{:S(2)}) collective-permute-start(bf16[8,64,512]{2,1,0:T(8,128)(2,1)S(1)} %collective-permute-done.4.refs_4_), channel_id=1, source_target_pairs={{0,16},{4,12},{8,24},{12,4},{16,0},{20,28},{24,8},{28,20},{1,17},{... | collective-permute-start | bytes 1572872 | tf_op jit(solution)/shard_map/ppermute | solution.py:98
  17.4 3.7 %collective-permute-done.2.refs_2_ = bf16[2592,128]{1,0:T(8,128)(2,1)S(1)} collective-permute-done((bf16[2592,128]{1,0:T(8,128)(2,1)S(1)}, bf16[2592,128]{1,0:T(8,128)(2,1)S(1)}, u32[]{:S(2)}, u32[]{:S(2)}) %collective-permute-start.2) | collective-permute-done | bytes 663584 | tf_op jit(solution)/shard_map/ppermute | solution.py:82
  21.2 1.3 %collective-permute-start.5 = (bf16[2592,128]{1,0:T(8,128)(2,1)S(1)}, bf16[2592,128]{1,0:T(8,128)(2,1)S(1)}, u32[]{:S(2)}, u32[]{:S(2)}) collective-permute-start(bf16[2592,128]{1,0:T(8,128)(2,1)S(1)} %broadcast_select_fusion), channel_id=1, source_target_pairs={{1,2},{2,1},{5,4},{6,7},{9,10},{10,9},{13,12},{14,15},{17,18},{18,... | collective-permute-start | bytes 1990664 | tf_op jit(solution)/shard_map/ppermute | solution.py:82
  22.6 5.5 %collective-permute-done.7.refs_6_ = bf16[8,64,512]{2,1,0:T(8,128)(2,1)S(1)} collective-permute-done((bf16[8,64,512]{2,1,0:T(8,128)(2,1)S(1)}, bf16[8,64,512]{2,1,0:T(8,128)(2,1)S(1)}, u32[]{:S(2)}, u32[]{:S(2)}) %collective-permute-start.7) | collective-permute-done | bytes 524320 | tf_op jit(solution)/shard_map/ppermute | solution.py:98
  28.7 1.3 %collective-permute-done.10.refs_9_ = bf16[8,64,512]{2,1,0:T(8,128)(2,1)S(1)} collective-permute-done((bf16[8,64,512]{2,1,0:T(8,128)(2,1)S(1)}, bf16[8,64,512]{2,1,0:T(8,128)(2,1)S(1)}, u32[]{:S(2)}, u32[]{:S(2)}) %collective-permute-start.10) | collective-permute-done | bytes 524320 | tf_op jit(solution)/shard_map/ppermute | solution.py:44
  30.0 0.7 collective-permute-done.9.refs_8_
  30.7 2.0 %mapping.1 = (f32[8,8,512]{2,1,0:T(8,128)S(1)}, f32[8,8,512]{2,1,0:T(8,128)S(1)}, f32[8,512]{1,0:T(8,128)S(1)}, f32[2,8,512]{2,1,0:T(8,128)S(1)}, bf16[8,512,512]{2,1,0:T(8,128)(2,1)S(1)}) custom-call(s32[2]{0:T(128)S(1)} %pad_add_fusion.where.refs_0_, s32[4]{0:T(128)S(1)} %pad_add_fusion.1.refs_1_.refs_12_.crossover, bf16[8,64,512]{2,1,0:T(8,128)(2,1)S(1)} %low.1.refs_2_, ...), custom_call_target="tpu_custom_call" | custom-call | tf_op jit(solution)/shard_map/mapping/pallas_call | solution.py:822
  32.8 1.7 %begin.1 = (bf16[1,512,1024]{2,1,0:T(8,128)(2,1)S(1)}, f32[1,1024,384]{2,1,0:T(8,128)S(1)}, f32[8,512]{1,0:T(8,128)S(1)}, bf16[512,512]{1,0:T(8,128)(2,1)S(1)}) custom-call(s32[2]{0:T(128)S(1)} %pad_add_fusion.where.refs_0_, bf16[2592,128]{1,0:T(8,128)(2,1)S(1)} %pad_maximum_fusion.refs_1_, bf16[2592,128]{1,0:T(8,128)(2,1)S(1)} %collective-permute-done.2.refs_2_, ...), custom_call_target="tpu_custom_call" | custom-call | tf_op jit(solution)/shard_map/begin/pallas_call | solution.py:840
  34.8 1.6 %collective-permute-done.11.refs_3_ = bf16[1568,128]{1,0:T(8,128)(2,1)S(1)} collective-permute-done((bf16[1568,128]{1,0:T(8,128)(2,1)S(1)}, bf16[1568,128]{1,0:T(8,128)(2,1)S(1)}, u32[]{:S(2)}, u32[]{:S(2)}) %collective-permute-start.11) | collective-permute-done | bytes 401440 | tf_op jit(solution)/shard_map/ppermute | solution.py:44
  36.4 2.4 %main.1 = (bf16[1,512,1024]{2,1,0:T(8,128)(2,1)S(1)}, f32[8,512]{1,0:T(8,128)S(1)}, bf16[512,512]{1,0:T(8,128)(2,1)S(1)}, f32[1,1040,128]{2,1,0:T(8,128)S(1)}, f...) custom-call(s32[2]{0:T(128)S(1)} %pad_add_fusion.where.refs_0_, ...), custom_call_target="tpu_custom_call", output_to_operand_aliasing={{0}: (13, {}), {1}: (14, {}), {2}: (15, {})} | custom-call | tf_op jit(solution)/shard_map/main/pallas_call | solution.py:860
  39.0 2.6 %factor.1 = (bf16[1,2,2304,128]{3,2,1,0:T(8,128)(2,1)S(1)}, f32[8,128]{1,0:T(8,128)S(1)}) custom-call(s32[2]{0:T(128)S(1)} %pad_add_fusion.where.refs_0_, bf16[1,512,1024]{2,1,0:T(8,128)(2,1)S(1)} %get-tuple-element.104.feat_t, f32[1,1040,128]{2,1,0:T(8,128)S(1)} %get-tuple-element.105.wide, f32[8,128]{1,0:T(8,128)S(1)} %get-tuple-element.106.small.refs_9_, ...), custom_call_target="tpu_custom_call" | custom-call | tf_op jit(solution)/shard_map/factor/pallas_call | solution.py:903
  42.1 1.9 %collective-permute-start.15 = (f32[16,128]{1,0:T(8,128)S(1)}, f32[16,128]{1,0:T(8,128)S(1)}, u32[]{:S(2)}, u32[]{:S(2)}) collective-permute-start(f32[16,128]{1,0:T(8,128)S(1)} %pad_maximum_fusion.2.refs_0_), channel_id=1, source_target_pairs={{0,3},{1,2},{2,1},{3,0},{4,7},{5,6},{6,5},{7,4},{8,11},{9,10},{10,... | collective-permute-start | bytes 24584 | tf_op jit(solution)/shard_map/ppermute | solution.py:44
  44.0 1.0 %collective-permute-start.14 = (f32[16,128]{1,0:T(8,128)S(1)}, f32[16,128]{1,0:T(8,128)S(1)}, u32[]{:S(2)}, u32[]{:S(2)}) collective-permute-start(f32[16,128]{1,0:T(8,128)S(1)} %pad_maximum_fusion.2.refs_0_), channel_id=1, source_target_pairs={{0,2},{1,3},{2,0},{3,1},{4,6},{5,7},{6,4},{7,5},{8,10},{9,11},{10,... | collective-permute-start | bytes 24584 | tf_op jit(solution)/shard_map/ppermute | solution.py:44
  44.9 0.8 %collective-permute-start.13 = (f32[16,128]{1,0:T(8,128)S(1)}, f32[16,128]{1,0:T(8,128)S(1)}, u32[]{:S(2)}, u32[]{:S(2)}) collective-permute-start(f32[16,128]{1,0:T(8,128)S(1)} %pad_maximum_fusion.2.refs_0_), channel_id=1, source_target_pairs={{0,1},{1,0},{2,3},{3,2},{4,5},{5,4},{6,7},{7,6},{8,9},{9,8},{10,11... | collective-permute-start | bytes 24584 | tf_op jit(solution)/shard_map/ppermute | solution.py:44
  46.5 1.0 %collective-permute-done.14.refs_2_ = f32[16,128]{1,0:T(8,128)S(1)} collective-permute-done((f32[16,128]{1,0:T(8,128)S(1)}, f32[16,128]{1,0:T(8,128)S(1)}, u32[]{:S(2)}, u32[]{:S(2)}) %collective-permute-start.14) | collective-permute-done | bytes 8224 | tf_op jit(solution)/shard_map/ppermute | solution.py:44
  47.7 1.3 %collective-permute-start.21 = (bf16[2336,128]{1,0:T(8,128)(2,1)S(1)}, bf16[2336,128]{1,0:T(8,128)(2,1)S(1)}, u32[]{:S(2)}, u32[]{:S(2)}) collective-permute-start(bf16[2336,128]{1,0:T(8,128)(2,1)S(1)} %combine.1), channel_id=1, source_target_pairs={{0,8},{4,20},{8,0},{12,28},{16,24},{20,4},{24,16},{28,12},{1,9},{5... | collective-permute-start | bytes 1794056 | tf_op jit(solution)/shard_map/ppermute | solution.py:98
  49.0 2.1 %mapping_back.1 = bf16[48,512]{1,0:T(8,128)(2,1)S(1)} custom-call(s32[2]{0:T(128)S(1)} %pad_add_fusion.where.refs_0_, s32[4]{0:T(128)S(1)} %pad_add_fusion.1.refs_1_.refs_12_.crossover, f32[16,128]{1,0:T(8,128)S(1)} %pad_maximum_fusion.2.refs_0_, f32[16,128]{1,0:T(8,128)S(1)} %collective-permute-done.13.refs_1_, ...), custom_call_target="tpu_custom_call" | custom-call | tf_op jit(solution)/shard_map/mapping_back/pallas_call | solution.py:933
  51.3 2.2 %collective-permute-start.17 = (bf16[48,512]{1,0:T(8,128)(2,1)S(1)}, bf16[48,512]{1,0:T(8,128)(2,1)S(1)}, u32[]{:S(2)}, u32[]{:S(2)}) collective-permute-start(bf16[48,512]{1,0:T(8,128)(2,1)S(1)} %mapping_back.1), channel_id=1, source_target_pairs={{0,4},{4,0},{8,12},{12,8},{16,20},{20,16},{24,28},{28,24},{1,5},{5... | collective-permute-start | bytes 147464 | tf_op jit(solution)/shard_map/ppermute | solution.py:44
  53.4 0.9 %collective-permute-done.17 = bf16[48,512]{1,0:T(8,128)(2,1)S(1)} collective-permute-done((bf16[48,512]{1,0:T(8,128)(2,1)S(1)}, bf16[48,512]{1,0:T(8,128)(2,1)S(1)}, u32[]{:S(2)}, u32[]{:S(2)}) %collective-permute-start.17) | collective-permute-done | bytes 49184 | tf_op jit(solution)/shard_map/ppermute | solution.py:44
  54.6 4.6 %collective-permute-done.18.refs_1_ = bf16[96,512]{1,0:T(8,128)(2,1)S(1)} collective-permute-done((bf16[96,512]{1,0:T(8,128)(2,1)S(1)}, bf16[96,512]{1,0:T(8,128)(2,1)S(1)}, u32[]{:S(2)}, u32[]{:S(2)}) %collective-permute-start.18) | collective-permute-done | bytes 98336 | tf_op jit(solution)/shard_map/ppermute | solution.py:98
  59.3 1.2 %collective-permute-start.19 = (bf16[96,512]{1,0:T(8,128)(2,1)S(1)}, bf16[96,512]{1,0:T(8,128)(2,1)S(1)}, u32[]{:S(2)}, u32[]{:S(2)}) collective-permute-start(bf16[96,512]{1,0:T(8,128)(2,1)S(1)} %collective-permute-done.18.refs_1_), channel_id=1, source_target_pairs={{0,8},{4,20},{8,0},{12,28},{16,24},{20,4},{24,16},{28,12},{1,9},{5... | collective-permute-start | bytes 294920 | tf_op jit(solution)/shard_map/ppermute | solution.py:98
  61.1 2.0 %collective-permute-done.19.refs_2_ = bf16[96,512]{1,0:T(8,128)(2,1)S(1)} collective-permute-done((bf16[96,512]{1,0:T(8,128)(2,1)S(1)}, bf16[96,512]{1,0:T(8,128)(2,1)S(1)}, u32[]{:S(2)}, u32[]{:S(2)}) %collective-permute-start.19) | collective-permute-done | bytes 98336 | tf_op jit(solution)/shard_map/ppermute | solution.py:98
  63.2 4.3 %update.1 = (f32[8,64,512]{2,1,0:T(8,128)}, f32[8,64,512]{2,1,0:T(8,128)}, f32[8,64,512]{2,1,0:T(8,128)}, bf16[8,64,512]{2,1,0:T(8,128)(2,1)}, f32[1024,128]{1,0...) custom-call(s32[2]{0:T(128)S(1)} %pad_add_fusion.where.refs_0_, ...), custom_call_target="tpu_custom_call" | custom-call | flops 12000000000 | tf_op jit(solution)/shard_map/update/pallas_call | solution.py:969
  67.6 2.8 %collective-permute-done.22 = bf16[2336,128]{1,0:T(8,128)(2,1)S(1)} collective-permute-done((bf16[2336,128]{1,0:T(8,128)(2,1)S(1)}, bf16[2336,128]{1,0:T(8,128)(2,1)S(1)}, u32[]{:S(2)}, u32[]{:S(2)}) %collective-permute-start.22) | collective-permute-done | bytes 598048 | tf_op jit(solution)/shard_map/ppermute | solution.py:98
  71.0 2.2 %conv_first.1 = (f32[4608,128]{1,0:T(8,128)}, f32[4608,128]{1,0:T(8,128)}, f32[4608,128]{1,0:T(8,128)}, bf16[4608,128]{1,0:T(8,128)(2,1)}) custom-call(s32[2]{0:T(128)S(1)} %pad_add_fusion.where.refs_0_, bf16[2336,128]{1,0:T(8,128)(2,1)S(1)} %add_convert_fusion.refs_0_, f32[4608,128]{1,0:T(8,128)S(1)} %bitcast.26, f32[4608,128]{1,0:T(8,128)S(1)} %bitcast.28, ...), custom_call_target="tpu_custom_call" | custom-call | tf_op jit(solution)/shard_map/conv_first/pallas_call | solution.py:1003
  73.3 3.2 %conv_rest.1 = (f32[4608,128]{1,0:T(8,128)}, f32[4608,128]{1,0:T(8,128)}, f32[4608,128]{1,0:T(8,128)}, bf16[4608,128]{1,0:T(8,128)(2,1)}) custom-call(s32[2]{0:T(128)S(1)} %pad_add_fusion.where.refs_0_, bf16[2336,128]{1,0:T(8,128)(2,1)S(1)} %add_convert_fusion.refs_0_, ...), custom_call_target="tpu_custom_call", output_to_operand_aliasing={{0}: (6, {}), {1}: (7, {}), {2}: (8, {}), {3}: (9, {})} | custom-call | tf_op jit(solution)/shard_map/conv_rest/pallas_call | solution.py:1003
  (84 shorter events, 5.4 us)
Async XLA Ops:
  0.7 1.8 %collective-permute-start.1 = (bf16[1024,128]{1,0:T(8,128)(2,1)}, bf16[1024,128]{1,0:T(8,128)(2,1)S(1)}, u32[]{:S(2)}, u32[]{:S(2)}) collective-permute-start(bf16[1024,128]{1,0:T(8,128)(2,1)} %bitcast.41), channel_id=1, source_target_pairs={{0,4},{4,0},{8,12},{12,8},{16,20},{20,16},{24,28},{28,24},{1,5},{5... | collective-permute-start | bytes 786440 | tf_op jit(solution)/shard_map/ppermute | solution.py:44
  2.6 18.6 %collective-permute-start.2 = (bf16[2592,128]{1,0:T(8,128)(2,1)S(1)}, bf16[2592,128]{1,0:T(8,128)(2,1)S(1)}, u32[]{:S(2)}, u32[]{:S(2)}) collective-permute-start(bf16[2592,128]{1,0:T(8,128)(2,1)S(1)} %pad_maximum_fusion.refs_1_), channel_id=1, source_target_pairs={{0,1},{1,0},{2,3},{3,2},{4,6},{5,7},{6,4},{7,5},{8,9},{9,8},{10,11... | collective-permute-start | bytes 1990664 | tf_op jit(solution)/shard_map/ppermute | solution.py:82
  7.7 2.8 %collective-permute-start = (bf16[8,64,512]{2,1,0:T(8,128)(2,1)S(1)}, bf16[8,64,512]{2,1,0:T(8,128)(2,1)S(1)}, u32[]{:S(2)}, u32[]{:S(2)}) collective-permute-start(bf16[8,64,512]{2,1,0:T(8,128)(2,1)S(1)} %low.1.refs_2_), channel_id=1, source_target_pairs={{0,4},{4,0},{8,12},{12,8},{16,20},{20,16},{24,28},{28,24},{1,5},{5... | collective-permute-start | bytes 1572872 | tf_op jit(solution)/shard_map/ppermute | solution.py:44
  7.8 8.4 %collective-permute-start.4 = (bf16[8,64,512]{2,1,0:T(8,128)(2,1)S(1)}, bf16[8,64,512]{2,1,0:T(8,128)(2,1)S(1)}, u32[]{:S(2)}, u32[]{:S(2)}) collective-permute-start(bf16[8,64,512]{2,1,0:T(8,128)(2,1)S(1)} %low.1.refs_2_), channel_id=1, source_target_pairs={{0,8},{4,20},{8,0},{12,28},{16,24},{20,4},{24,16},{28,12},{1,9},{5... | collective-permute-start | bytes 1572872 | tf_op jit(solution)/shard_map/ppermute | solution.py:98
  13.0 17.7 %copy-start.5 = (f32[8,512]{1,0:T(8,128)S(1)}, f32[8,512]{1,0:T(8,128)}, u32[]{:S(2)}) copy-start(f32[8,512]{1,0:T(8,128)} %refs_10_.3) | copy-start | bytes 49156
  13.0 15.1 %collective-permute-start.6 = (bf16[8,64,512]{2,1,0:T(8,128)(2,1)S(1)}, bf16[8,64,512]{2,1,0:T(8,128)(2,1)S(1)}, u32[]{:S(2)}, u32[]{:S(2)}) collective-permute-start(bf16[8,64,512]{2,1,0:T(8,128)(2,1)S(1)} %collective-permute-done.refs_3_), channel_id=1, source_target_pairs={{0,8},{4,20},{8,0},{12,28},{16,24},{20,4},{24,16},{28,12},{1,9},{5... | collective-permute-start | bytes 1572872 | tf_op jit(solution)/shard_map/ppermute | solution.py:98
  16.2 11.8 %collective-permute-start.7 = (bf16[8,64,512]{2,1,0:T(8,128)(2,1)S(1)}, bf16[8,64,512]{2,1,0:T(8,128)(2,1)S(1)}, u32[]{:S(2)}, u32[]{:S(2)}) collective-permute-start(bf16[8,64,512]{2,1,0:T(8,128)(2,1)S(1)} %collective-permute-done.4.refs_4_), channel_id=1, source_target_pairs={{0,16},{4,12},{8,24},{12,4},{16,0},{20,28},{24,8},{28,20},{1,17},{... | collective-permute-start | bytes 1572872 | tf_op jit(solution)/shard_map/ppermute | solution.py:98
  21.2 13.3 %collective-permute-start.5 = (bf16[2592,128]{1,0:T(8,128)(2,1)S(1)}, bf16[2592,128]{1,0:T(8,128)(2,1)S(1)}, u32[]{:S(2)}, u32[]{:S(2)}) collective-permute-start(bf16[2592,128]{1,0:T(8,128)(2,1)S(1)} %broadcast_select_fusion), channel_id=1, source_target_pairs={{1,2},{2,1},{5,4},{6,7},{9,10},{10,9},{13,12},{14,15},{17,18},{18,... | collective-permute-start | bytes 1990664 | tf_op jit(solution)/shard_map/ppermute | solution.py:82
  22.5 6.2 %collective-permute-start.8 = (bf16[8,64,512]{2,1,0:T(8,128)(2,1)S(1)}, bf16[8,64,512]{2,1,0:T(8,128)(2,1)S(1)}, u32[]{:S(2)}, u32[]{:S(2)}) collective-permute-start(bf16[8,64,512]{2,1,0:T(8,128)(2,1)S(1)} %collective-permute-done.4.refs_4_), channel_id=1, source_target_pairs={{0,4},{4,0},{8,12},{12,8},{16,20},{20,16},{24,28},{28,24},{1,5},{5... | collective-permute-start | bytes 1572872 | tf_op jit(solution)/shard_map/ppermute | solution.py:44
  28.0 1.9 %collective-permute-start.10 = (bf16[8,64,512]{2,1,0:T(8,128)(2,1)S(1)}, bf16[8,64,512]{2,1,0:T(8,128)(2,1)S(1)}, u32[]{:S(2)}, u32[]{:S(2)}) collective-permute-start(bf16[8,64,512]{2,1,0:T(8,128)(2,1)S(1)} %collective-permute-done.7.refs_6_), channel_id=1, source_target_pairs={{0,4},{4,0},{8,12},{12,8},{16,20},{20,16},{24,28},{28,24},{1,5},{5... | collective-permute-start | bytes 1572872 | tf_op jit(solution)/shard_map/ppermute | solution.py:44
  28.1 2.7 %collective-permute-start.9 = (bf16[8,64,512]{2,1,0:T(8,128)(2,1)S(1)}, bf16[8,64,512]{2,1,0:T(8,128)(2,1)S(1)}, u32[]{:S(2)}, u32[]{:S(2)}) collective-permute-start(bf16[8,64,512]{2,1,0:T(8,128)(2,1)S(1)} %collective-permute-done.6.refs_5_), channel_id=1, source_target_pairs={{0,4},{4,0},{8,12},{12,8},{16,20},{20,16},{24,28},{28,24},{1,5},{5... | collective-permute-start | bytes 1572872 | tf_op jit(solution)/shard_map/ppermute | solution.py:44
  28.6 6.2 %collective-permute-start.3 = (bf16[1568,128]{1,0:T(8,128)(2,1)S(1)}, bf16[1568,128]{1,0:T(8,128)(2,1)S(1)}, u32[]{:S(2)}, u32[]{:S(2)}) collective-permute-start(bf16[1568,128]{1,0:T(8,128)(2,1)S(1)} %slice.28), channel_id=1, source_target_pairs={{0,4},{4,0},{8,12},{12,8},{16,20},{20,16},{24,28},{28,24},{1,5},{5... | collective-permute-start | bytes 1204232 | tf_op jit(solution)/shard_map/ppermute | solution.py:44
  34.6 1.8 %collective-permute-start.11 = (bf16[1568,128]{1,0:T(8,128)(2,1)S(1)}, bf16[1568,128]{1,0:T(8,128)(2,1)S(1)}, u32[]{:S(2)}, u32[]{:S(2)}) collective-permute-start(bf16[1568,128]{1,0:T(8,128)(2,1)S(1)} %slice.22), channel_id=1, source_target_pairs={{0,4},{4,0},{8,12},{12,8},{16,20},{20,16},{24,28},{28,24},{1,5},{5... | collective-permute-start | bytes 1204232 | tf_op jit(solution)/shard_map/ppermute | solution.py:44
  38.8 3.3 %collective-permute-start.12 = (f32[8,128]{1,0:T(8,128)S(1)}, f32[8,128]{1,0:T(8,128)S(1)}, u32[]{:S(2)}, u32[]{:S(2)}) collective-permute-start(f32[8,128]{1,0:T(8,128)S(1)} %get-tuple-element.109), channel_id=1, source_target_pairs={{0,4},{4,0},{8,12},{12,8},{16,20},{20,16},{24,28},{28,24},{1,5},{5... | collective-permute-start | bytes 12296 | tf_op jit(solution)/shard_map/ppermute | solution.py:44
  41.6 5.8 %collective-permute-start.16 = (bf16[1,2304,128]{2,1,0:T(8,128)(2,1)S(1)}, bf16[1,2304,128]{2,1,0:T(8,128)(2,1)S(1)}, u32[]{:S(2)}, u32[]{:S(2)}) collective-permute-start(bf16[1,2304,128]{2,1,0:T(8,128)(2,1)S(1)} %slice_bitcast_fusion), channel_id=1, source_target_pairs={{0,4},{4,0},{8,12},{12,8},{16,20},{20,16},{24,28},{28,24},{1,5},{5... | collective-permute-start | bytes 1769480 | tf_op jit(solution)/shard_map/ppermute | solution.py:44
  42.1 4.4 %collective-permute-start.15 = (f32[16,128]{1,0:T(8,128)S(1)}, f32[16,128]{1,0:T(8,128)S(1)}, u32[]{:S(2)}, u32[]{:S(2)}) collective-permute-start(f32[16,128]{1,0:T(8,128)S(1)} %pad_maximum_fusion.2.refs_0_), channel_id=1, source_target_pairs={{0,3},{1,2},{2,1},{3,0},{4,7},{5,6},{6,5},{7,4},{8,11},{9,10},{10,... | collective-permute-start | bytes 24584 | tf_op jit(solution)/shard_map/ppermute | solution.py:44
  44.0 3.4 %collective-permute-start.14 = (f32[16,128]{1,0:T(8,128)S(1)}, f32[16,128]{1,0:T(8,128)S(1)}, u32[]{:S(2)}, u32[]{:S(2)}) collective-permute-start(f32[16,128]{1,0:T(8,128)S(1)} %pad_maximum_fusion.2.refs_0_), channel_id=1, source_target_pairs={{0,2},{1,3},{2,0},{3,1},{4,6},{5,7},{6,4},{7,5},{8,10},{9,11},{10,... | collective-permute-start | bytes 24584 | tf_op jit(solution)/shard_map/ppermute | solution.py:44
  44.9 2.5 %collective-permute-start.13 = (f32[16,128]{1,0:T(8,128)S(1)}, f32[16,128]{1,0:T(8,128)S(1)}, u32[]{:S(2)}, u32[]{:S(2)}) collective-permute-start(f32[16,128]{1,0:T(8,128)S(1)} %pad_maximum_fusion.2.refs_0_), channel_id=1, source_target_pairs={{0,1},{1,0},{2,3},{3,2},{4,5},{5,4},{6,7},{7,6},{8,9},{9,8},{10,11... | collective-permute-start | bytes 24584 | tf_op jit(solution)/shard_map/ppermute | solution.py:44
  47.7 12.9 %collective-permute-start.21 = (bf16[2336,128]{1,0:T(8,128)(2,1)S(1)}, bf16[2336,128]{1,0:T(8,128)(2,1)S(1)}, u32[]{:S(2)}, u32[]{:S(2)}) collective-permute-start(bf16[2336,128]{1,0:T(8,128)(2,1)S(1)} %combine.1), channel_id=1, source_target_pairs={{0,8},{4,20},{8,0},{12,28},{16,24},{20,4},{24,16},{28,12},{1,9},{5... | collective-permute-start | bytes 1794056 | tf_op jit(solution)/shard_map/ppermute | solution.py:98
  49.0 14.1 %copy-start.10 = (f32[8,64,512]{2,1,0:T(8,128)S(1)}, f32[8,64,512]{2,1,0:T(8,128)}, u32[]{:S(2)}) copy-start(f32[8,64,512]{2,1,0:T(8,128)} %refs_5_.1) | copy-start | bytes 3145732
  49.0 14.1 %copy-start.11 = (f32[8,64,512]{2,1,0:T(8,128)S(1)}, f32[8,64,512]{2,1,0:T(8,128)}, u32[]{:S(2)}) copy-start(f32[8,64,512]{2,1,0:T(8,128)} %refs_6_.1) | copy-start | bytes 3145732
  49.0 14.1 %copy-start.13 = (f32[2,512,128]{2,1,0:T(8,128)S(1)}, f32[2,512,128]{2,1,0:T(8,128)}, u32[]{:S(2)}) copy-start(f32[2,512,128]{2,1,0:T(8,128)} %param.40) | copy-start | bytes 1572868
  51.1 12.0 %copy-start.4 = (f32[8,64,512]{2,1,0:T(8,128)S(1)}, f32[8,64,512]{2,1,0:T(8,128)}, u32[]{:S(2)}) copy-start(f32[8,64,512]{2,1,0:T(8,128)} %refs_4_.1) | copy-start | bytes 3145732
  51.2 12.0 %copy-start.12 = (f32[2,512,128]{2,1,0:T(8,128)S(1)}, f32[2,512,128]{2,1,0:T(8,128)}, u32[]{:S(2)}) copy-start(f32[2,512,128]{2,1,0:T(8,128)} %param.39) | copy-start | bytes 1572868
  51.2 12.0 %copy-start.14 = (f32[8,512]{1,0:T(8,128)S(1)}, f32[8,512]{1,0:T(8,128)}, u32[]{:S(2)}) copy-start(f32[8,512]{1,0:T(8,128)} %refs_11_.5) | copy-start | bytes 49156
  51.2 12.0 %copy-start.15 = (f32[8,512]{1,0:T(8,128)S(1)}, f32[8,512]{1,0:T(8,128)}, u32[]{:S(2)}) copy-start(f32[8,512]{1,0:T(8,128)} %refs_12_.1) | copy-start | bytes 49156
  51.3 3.0 %collective-permute-start.17 = (bf16[48,512]{1,0:T(8,128)(2,1)S(1)}, bf16[48,512]{1,0:T(8,128)(2,1)S(1)}, u32[]{:S(2)}, u32[]{:S(2)}) collective-permute-start(bf16[48,512]{1,0:T(8,128)(2,1)S(1)} %mapping_back.1), channel_id=1, source_target_pairs={{0,4},{4,0},{8,12},{12,8},{16,20},{20,16},{24,28},{28,24},{1,5},{5... | collective-permute-start | bytes 147464 | tf_op jit(solution)/shard_map/ppermute | solution.py:44
  54.3 4.9 %collective-permute-start.18 = (bf16[96,512]{1,0:T(8,128)(2,1)S(1)}, bf16[96,512]{1,0:T(8,128)(2,1)S(1)}, u32[]{:S(2)}, u32[]{:S(2)}) collective-permute-start(bf16[96,512]{1,0:T(8,128)(2,1)S(1)} %pad_maximum_fusion.1.refs_0_), channel_id=1, source_target_pairs={{0,16},{4,12},{8,24},{12,4},{16,0},{20,28},{24,8},{28,20},{1,17},{... | collective-permute-start | bytes 294920 | tf_op jit(solution)/shard_map/ppermute | solution.py:98
  59.2 1.9 %collective-permute-start.20 = (bf16[96,512]{1,0:T(8,128)(2,1)S(1)}, bf16[96,512]{1,0:T(8,128)(2,1)S(1)}, u32[]{:S(2)}, u32[]{:S(2)}) collective-permute-start(bf16[96,512]{1,0:T(8,128)(2,1)S(1)} %collective-permute-done.18.refs_1_), channel_id=1, source_target_pairs={{0,4},{4,0},{8,12},{12,8},{16,20},{20,16},{24,28},{28,24},{1,5},{5... | collective-permute-start | bytes 294920 | tf_op jit(solution)/shard_map/ppermute | solution.py:44
  59.3 3.8 %collective-permute-start.19 = (bf16[96,512]{1,0:T(8,128)(2,1)S(1)}, bf16[96,512]{1,0:T(8,128)(2,1)S(1)}, u32[]{:S(2)}, u32[]{:S(2)}) collective-permute-start(bf16[96,512]{1,0:T(8,128)(2,1)S(1)} %collective-permute-done.18.refs_1_), channel_id=1, source_target_pairs={{0,8},{4,20},{8,0},{12,28},{16,24},{20,4},{24,16},{28,12},{1,9},{5... | collective-permute-start | bytes 294920 | tf_op jit(solution)/shard_map/ppermute | solution.py:98
  60.7 9.6 %collective-permute-start.22 = (bf16[2336,128]{1,0:T(8,128)(2,1)S(1)}, bf16[2336,128]{1,0:T(8,128)(2,1)S(1)}, u32[]{:S(2)}, u32[]{:S(2)}) collective-permute-start(bf16[2336,128]{1,0:T(8,128)(2,1)S(1)} %add_convert_fusion.1), channel_id=1, source_target_pairs={{0,16},{4,12},{8,24},{12,4},{16,0},{20,28},{24,8},{28,20},{1,17},{... | collective-permute-start | bytes 1794056 | tf_op jit(solution)/shard_map/ppermute | solution.py:98
  70.5 2.8 %collective-permute-start.23 = (bf16[2336,128]{1,0:T(8,128)(2,1)S(1)}, bf16[2336,128]{1,0:T(8,128)(2,1)S(1)}, u32[]{:S(2)}, u32[]{:S(2)}) collective-permute-start(bf16[2336,128]{1,0:T(8,128)(2,1)S(1)} %add_convert_fusion.refs_0_), channel_id=1, source_target_pairs={{0,4},{4,0},{8,12},{12,8},{16,20},{20,16},{24,28},{28,24},{1,5},{5... | collective-permute-start | bytes 1794056 | tf_op jit(solution)/shard_map/ppermute | solution.py:44
  (13 other events, 105.8 us)
